TPU v7x, 32 devices: a whole 2x2x4 slice. The times are simulated.
32 devices in a mesh: groups: 2 (over y), dp: 4 (over z), tensor: 4 (over x, core).
Axes of the slice: x: 2, y: 2, z: 4, core: 2. Of those that a mesh axis runs over, the one named last changes fastest.
Arguments:
- tokens: bfloat16 [3584, 4096], P(('groups', 'dp'), 'tensor'), parts along dimension 0, may hold values from -6 to 6
- frozen: bfloat16 [4096, 15360], P('dp', 'tensor'), may hold values from -0.09375 to 0.09375
- delta: bfloat16 [16, 128, 128], P('tensor'), may hold values from -0.5 to 0.5
- block_rows: int32 [16], P('tensor'), may hold values from 0 to 31, as said below
- block_cols: int32 [16], P('tensor'), may hold values from 0 to 119, as said below
- owners: int32 [16, 1], P('tensor'), may hold values from 0 to 3; in each aligned block of 4 rows (0 to 3, 4 to 7, ...) at most 2 rows name the same one
- d_out: bfloat16 [3584, 15360], P(('groups', 'dp'), 'tensor'), parts along dimension 0, may hold values from -6 to 6
Outputs:
- activated: bfloat16 [3584, 15360], P(('groups', 'dp'), 'tensor'), parts along dimension 0
- d_tokens: bfloat16 [3584, 4096], P(('groups', 'dp'), 'tensor'), parts along dimension 0
- block_grads: float32 [4, 16, 128, 128], P('tensor', ('groups', 'dp')), parts along dimension 1
There are 2 independent parts, one for each index of `groups`. A program takes and returns all parts, laid end to end along the dimension named above; an argument that names none is the same for every part. Nothing has to cross between parts.
Inputs may be any that keep to these rules, and one draw needn't show every extreme that they name: The blocks 4 j to 4 j + 3 are distinct in (block_rows, block_cols) within that range of blocks. The blocks 4 j to 4 j + 3 have block_cols in j * (30) to (j + 1) * 30 - 1. `owners`: among the 4 blocks 4 j to 4 j + 3 no index is named more than 2 times; in some such range one is named exactly 2 times.
All inputs are finite; a program needn't handle non-finite values.
Results may differ from a plain program's by a relative error of at most 0.012.
Values may be sent and summed in bfloat16 or wider, within the bound.
No kernel may reach another device: no remote copies, remote signals or barrier semaphores. Data moves between devices by JAX's collectives and lax.ppermute only.
A program may use at most 192 MiB of HBM per device.

v0:
```python
import jax
import jax.numpy as jnp
from jax import lax
from jax.sharding import PartitionSpec as P

CAP = 2


def local(tokens, frozen, delta, block_rows, block_cols, owners, d_out):
    rows_here = tokens.shape[0]
    x_full = lax.all_gather(tokens, "tensor", axis=1, tiled=True)
    model_width = x_full.shape[1]
    block_size = delta.shape[1]
    block_count = delta.shape[0]
    slab_width = frozen.shape[1]
    col_blocks = slab_width // block_size
    row_blocks = model_width // block_size
    local_cols = block_cols - lax.axis_index("tensor") * col_blocks
    x_blocks = jnp.take(x_full.reshape(rows_here, row_blocks, block_size), block_rows, axis=1)
    col_pick = (local_cols[:, None] == jnp.arange(col_blocks, dtype=jnp.int32)[None, :]).astype(
        jnp.float32
    )
    row_pick = (block_rows[:, None] == jnp.arange(row_blocks, dtype=jnp.int32)[None, :]).astype(
        jnp.float32
    )
    contrib = jnp.einsum("tnk,nkc->tnc", x_blocks, delta, preferred_element_type=jnp.float32)
    delta_add = jnp.einsum(
        "tnc,nm->tmc", contrib, col_pick, precision=lax.Precision.HIGHEST
    ).reshape(rows_here, slab_width)
    pieces = 3
    piece_width = slab_width // pieces
    d_rows = jnp.zeros((rows_here, model_width), jnp.float32)
    outputs = []
    slopes = []
    for number in range(pieces):
        first_col = number * piece_width
        segment = lax.all_gather(
            frozen[:, first_col : first_col + piece_width], "dp", axis=0, tiled=True
        )
        running = jnp.dot(x_full, segment, preferred_element_type=jnp.float32)
        stored = segment
        running, stored = (running, stored)
        preact = running + delta_add[:, first_col : first_col + piece_width]
        squash = jax.nn.sigmoid(preact)
        outputs.append((preact * squash).astype(jnp.bfloat16))
        d_slope = (
            d_out[:, first_col : first_col + piece_width].astype(jnp.float32)
            * squash
            * (1.0 + preact * (1.0 - squash))
        ).astype(jnp.bfloat16)
        slopes.append(d_slope)
        d_rows = d_rows + lax.dot_general(
            d_slope, stored, (((1,), (1,)), ((), ())), preferred_element_type=jnp.float32
        )
    activated = jnp.concatenate(outputs, axis=1)
    d_pre = jnp.concatenate(slopes, axis=1)
    dy_blocks = jnp.take(d_pre.reshape(rows_here, col_blocks, block_size), local_cols, axis=1)
    back_rows = jnp.einsum("tnc,nkc->tnk", dy_blocks, delta, preferred_element_type=jnp.float32)
    d_rows = d_rows + jnp.einsum(
        "tnk,nr->trk", back_rows, row_pick, precision=lax.Precision.HIGHEST
    ).reshape(rows_here, model_width)
    d_tokens = lax.psum_scatter(
        d_rows.astype(jnp.bfloat16), "tensor", scatter_dimension=1, tiled=True
    )
    partial_grads = jnp.einsum(
        "tnk,tnc->nkc", x_blocks, dy_blocks, preferred_element_type=jnp.float32
    )
    total_rows = rows_here * lax.axis_size("dp")
    norm_scale = float(total_rows) ** (-0.5)
    owner_ids = owners[:, 0]
    positions = jnp.arange(block_count, dtype=jnp.int32)
    earlier = (owner_ids[None, :] == owner_ids[:, None]) & (positions[None, :] < positions[:, None])
    ranking = jnp.sum(earlier.astype(jnp.int32), axis=1)
    self_index = lax.axis_index("dp")
    reduced = (
        lax.psum_scatter(
            partial_grads.astype(jnp.bfloat16), "dp", scatter_dimension=0, tiled=True
        ).astype(jnp.float32)
        * norm_scale
    )
    gathered = lax.all_gather(reduced.astype(jnp.bfloat16), "dp", axis=0, tiled=True).astype(
        reduced.dtype
    )
    wanted = (
        (owner_ids[None, :] == self_index)
        & (ranking[None, :] == jnp.arange(CAP, dtype=jnp.int32)[:, None])
    ).astype(jnp.float32)
    bucket = jnp.einsum("cn,nkl->ckl", wanted, gathered, precision=lax.Precision.HIGHEST)
    return (activated, d_tokens, bucket[None])


def solution(mesh):
    in_specs = (
        P(("groups", "dp"), "tensor"),
        P("dp", "tensor"),
        P("tensor", None, None),
        P("tensor"),
        P("tensor"),
        P("tensor", None),
        P(("groups", "dp"), "tensor"),
    )
    out_specs = (
        P(("groups", "dp"), "tensor"),
        P(("groups", "dp"), "tensor"),
        P("tensor", ("groups", "dp"), None, None),
    )
    return jax.shard_map(local, mesh=mesh, in_specs=in_specs, out_specs=out_specs, check_vma=False)
```

profile of v0, /device:TPU:0, one launch (start us, length us, event | category | flops | bytes accessed | tf_op | source)
XLA Modules:
  0.0 718.4 jit_solution(11246453255186145761)
XLA Ops:
  7.2 0.7 all-gather.5.cloned.1.call-update
  8.0 5.6 fusion.26
  13.6 0.7 all-gather.11.cloned.1.call-update
  14.4 0.5 all-gather.7.cloned.1.call-update
  15.1 28.8 %all-gather.5.cloned.1.call-done = bf16[448,4096]{1,0:T(8,128)(2,1)} async-done(((bf16[448,1024]{1,0:T(8,128)(2,1)}), bf16[448,4096]{1,0:T(8,128)(2,1)}) %all-gather.5.cloned.1.call-update) | async-done | bytes 3670032 | tf_op jit(solution)/shard_map/all_gather | solution.py:11
  43.8 4.9 copy_bitcast_fusion.1
  48.7 2.7 gather_fusion
  51.4 0.3 convolution_bitcast_fusion.1
  51.7 3.3 fusion.3
  55.0 9.4 %copy.45 = f32[56,8,30,128]{3,1,2,0:T(8,128)} copy(f32[56,8,30,128]{3,2,1,0:T(8,128)S(1)} %bitcast.62) | data formatting | bytes 13762560
  64.5 164.9 %all-gather.9.cloned.1.call-done = bf16[4096,1280]{1,0:T(8,128)(2,1)} async-done(((bf16[1024,1280]{1,0:T(8,128)(2,1)}), bf16[4096,1280]{1,0:T(8,128)(2,1)}) %all-gather.9.cloned.1.call-update) | async-done | bytes 10485776 | tf_op jit(solution)/shard_map/all_gather | solution.py:37
  229.3 12.3 %convolution_add_fusion.1 = f32[448,1280]{1,0:T(8,128)} fusion(bf16[448,4096]{1,0:T(8,128)(2,1)} %all-gather.5.cloned.1.call-done, bf16[4096,1280]{1,0:T(8,128)(2,1)} %all-gather.9.cloned.1.call-done, f32[448,3840]{1,0:T(8,128)} %bitcast.64), kind=kOutput, calls=%fused_computation.10 | convolution fusion | flops 4698193920 | bytes 18743296 | tf_op jit(solution)/shard_map/dot_general | solution.py:40
  241.6 171.4 %all-gather.11.cloned.1.call-done = bf16[4096,1280]{1,0:T(8,128)(2,1)} async-done(((bf16[1024,1280]{1,0:T(8,128)(2,1)}), bf16[4096,1280]{1,0:T(8,128)(2,1)}) %all-gather.11.cloned.1.call-update) | async-done | bytes 10485776 | tf_op jit(solution)/shard_map/all_gather | solution.py:37
  413.1 12.1 %convolution_add_fusion = f32[448,1280]{1,0:T(8,128)} fusion(bf16[448,4096]{1,0:T(8,128)(2,1)} %all-gather.5.cloned.1.call-done, bf16[4096,1280]{1,0:T(8,128)(2,1)} %all-gather.11.cloned.1.call-done, f32[448,3840]{1,0:T(8,128)} %bitcast.65), kind=kOutput, calls=%fused_computation.9 | convolution fusion | flops 4698193920 | bytes 18743296 | tf_op jit(solution)/shard_map/dot_general | solution.py:40
  425.1 172.1 %all-gather.7.cloned.1.call-done = bf16[4096,1280]{1,0:T(8,128)(2,1)} async-done(((bf16[1024,1280]{1,0:T(8,128)(2,1)}), bf16[4096,1280]{1,0:T(8,128)(2,1)}) %all-gather.7.cloned.1.call-update) | async-done | bytes 10485776 | tf_op jit(solution)/shard_map/all_gather | solution.py:37
  597.2 14.7 %multiply_convert_fusion.2 = (bf16[448,1280]{1,0:T(8,128)(2,1)S(1)}, bf16[448,1280]{1,0:T(8,128)(2,1)S(1)}, bf16[448,1280]{1,0:T(8,128)(2,1)S(1)}, bf16[448,1280...) fusion(bf16[448,3840]{1,0:T(8,128)(2,1)} %param.13, f32[448,1280]{1,0:T(8,128)} %convolution_add_fusion, ...), kind=kOutput, calls=%fused_computation.14 | convolution fusion | flops 4718837760 | bytes 31358976 | tf_op jit(solution)/shard_map/dot_general | solution.py:40
  611.9 1.0 copy-done.3
  613.2 0.3 copy-done.7
  613.5 2.1 copy_bitcast_fusion.2
  615.6 2.6 gather_fusion.1
  618.5 1.2 convolution_convert_fusion
  619.7 6.2 fusion.1
  626.0 12.3 %fusion.27 = f32[448,4096]{1,0:T(8,128)} fusion(bf16[448,1280]{1,0:T(8,128)(2,1)} %copy-done.7, bf16[4096,1280]{1,0:T(8,128)(2,1)} %all-gather.7.cloned.1.call-done), kind=kOutput, calls=%fused_computation.64 | convolution fusion | flops 4697620480 | bytes 18972672 | tf_op jit(solution)/shard_map/dot_general | solution.py:52
  638.3 12.7 %fusion.28 = f32[448,4096]{1,0:T(8,128)} fusion(bf16[448,1280]{1,0:T(8,128)(2,1)S(1)} %copy-done.6, bf16[4096,1280]{1,0:T(8,128)(2,1)} %all-gather.9.cloned.1.call-done), kind=kOutput, calls=%fused_computation.65 | convolution fusion | flops 4697620480 | bytes 18972672 | tf_op jit(solution)/shard_map/dot_general | solution.py:52
  650.9 20.6 %fusion = bf16[448,4096]{1,0:T(8,128)(2,1)} fusion(f32[56,8,32,128]{3,2,1,0:T(8,128)} %bitcast.63, f32[448,4096]{1,0:T(8,128)} %fusion.27, f32[448,4096]{1,0:T(8,128)} %fusion.28, bf16[448,1280]{1,0:T(8,128)(2,1)S(1)} %copy-done.4, bf16[4096,1280]{1,0:T(8,128)(2,1)} %all-gather.11.cloned.1.call-done), kind=kOutput, calls=%fused_computation.3 | convolution fusion | flops 4704960512 | bytes 37322752 | tf_op jit(solution)/shard_map/dot_general | solution.py:52
  671.6 0.6 copy-done.10
  672.4 0.4 copy-done.2
  672.8 2.9 pad_maximum_fusion
  675.8 0.8 multiply_convert_fusion.6
  676.5 13.5 %all_gather.19 = bf16[4,128,128]{2,1,0:T(8,128)(2,1)S(1)} all-gather(bf16[1,128,128]{2,1,0:T(8,128)(2,1)S(1)} %multiply_convert_fusion.6), channel_id=1, replica_groups=mesh['groups'=2,'dp'=4,'tensor'=4] {'dp'}, dimensions={0}, use_global_device_ids=true | all-gather | bytes 163840 | tf_op jit(solution)/shard_map/all_gather | solution.py:81
  690.2 0.7 copy.30
  690.9 20.2 %reduce-scatter.3.cloned.1.call-done = bf16[448,1024]{1,0:T(8,128)(2,1)} async-done(((bf16[448,4096]{1,0:T(8,128)(2,1)}), bf16[448,1024]{1,0:T(8,128)(2,1)}) %reduce-scatter.3.cloned.1.call-update) | async-done | bytes 917520 | tf_op jit(solution)/shard_map/reduce_scatter | solution.py:62
  (38 shorter events, 1.4 us)
Async XLA Ops:
  7.2 44.2 %copy-start = (bf16[4,128,128]{2,1,0:T(8,128)(2,1)S(1)}, bf16[4,128,128]{2,1,0:T(8,128)(2,1)}, u32[]{:S(2)}) copy-start(bf16[4,128,128]{2,1,0:T(8,128)(2,1)} %param.9) | copy-start | bytes 393220
  7.2 36.6 %all-gather.5.cloned.1.call-start = ((), (), s32[]{:S(2)}) async-start(), calls=%async_computation.2 | async-start | bytes 4587520 | tf_op jit(solution)/shard_map/all_gather | solution.py:11
  7.9 221.4 %all-gather.9.cloned.1.call-start = ((), (), s32[]{:S(2)}) async-start(), calls=%async_computation.4 | async-start | bytes 13107200 | tf_op jit(solution)/shard_map/all_gather | solution.py:37
  13.6 1.4 copy-start.8
  13.6 1.4 copy-start.9
  13.6 399.5 %all-gather.11.cloned.1.call-start = ((), (), s32[]{:S(2)}) async-start(), calls=%async_computation.5 | async-start | bytes 13107200 | tf_op jit(solution)/shard_map/all_gather | solution.py:37
  14.3 582.9 %all-gather.7.cloned.1.call-start = ((), (), s32[]{:S(2)}) async-start(), calls=%async_computation.3 | async-start | bytes 13107200 | tf_op jit(solution)/shard_map/all_gather | solution.py:37
  14.9 660.9 %reduce-scatter.5.cloned.1.call-start = ((), (), s32[]{:S(2)}) async-start(), calls=%async_computation.7 | async-start | bytes 163840 | tf_op jit(solution)/shard_map/reduce_scatter | solution.py:76
  611.9 1.1 copy-start.3
  611.9 1.4 copy-start.5
  611.9 1.7 copy-start.7
  625.9 12.3 %copy-start.6 = (bf16[448,1280]{1,0:T(8,128)(2,1)S(1)}, bf16[448,1280]{1,0:T(8,128)(2,1)}, u32[]{:S(2)}) copy-start(bf16[448,1280]{1,0:T(8,128)(2,1)} %copy-done.5) | copy-start | bytes 3440644
  625.9 85.2 %reduce-scatter.3.cloned.1.call-start = ((), (), s32[]{:S(2)}) async-start(), calls=%async_computation.6 | async-start | bytes 4587520 | tf_op jit(solution)/shard_map/reduce_scatter | solution.py:62
  638.3 12.7 %copy-start.4 = (bf16[448,1280]{1,0:T(8,128)(2,1)S(1)}, bf16[448,1280]{1,0:T(8,128)(2,1)}, u32[]{:S(2)}) copy-start(bf16[448,1280]{1,0:T(8,128)(2,1)} %copy-done.3) | copy-start | bytes 3440644
  671.5 0.7 copy-start.10
  671.5 1.3 copy-start.2
  672.4 38.8 %copy-start.1 = (bf16[4,128,128]{2,1,0:T(8,128)(2,1)S(1)}, bf16[4,128,128]{2,1,0:T(8,128)(2,1)}, u32[]{:S(2)}) copy-start(bf16[4,128,128]{2,1,0:T(8,128)(2,1)} %param.9) | copy-start | bytes 393220
Sparse Core Ops, SparseCore 0:
  9.6 34.1 all-gather.4
  45.4 183.9 all-gather.8
  230.9 182.0 all-gather.10
  415.1 182.1 all-gather.6
  626.1 17.3 reduce-scatter.4
  671.7 39.4 reduce-scatter.2
where the time goes:
time: 728 us; the launch traced here: 718 us
  waiting for transfers between devices  559 us (77%)
  matrix products  96.1 us (13%)
  local copies, waits for them, and re-layouts  28.6 us (4%)
  between operations  14.7 us (2%)
  blocking collectives  13.5 us (2%)
    all_gather x3, waiting for transfers between devices, local(): lax.all_gather(frozen[:, first_col:first_col + piece_width], 'dp', axis=0...  508 us
    dot_general x3, matrix products, local(): lax.dot_general(d_slope, stored, (((1,), (1,)), ((), ())), preferred_elem...  45.5 us
    dot_general x3, matrix products, local(): running = jnp.dot(x_full, segment, preferred_element_type=jnp.float32)  39 us
    all_gather x1, waiting for transfers between devices, local(): x_full = lax.all_gather(tokens, 'tensor', axis=1, tiled=True)  28.8 us
    reduce_scatter x1, waiting for transfers between devices, local(): lax.psum_scatter(d_rows.astype(jnp.bfloat16), 'tensor', scatter_dimension...  20.2 us
  transfers between devices with their start and end apart: 6, of which 5 were waited for; matrix products, arithmetic and copies ran while one was open for 14% of the time, Pallas kernels for 0%

commit v1 on v0

v1 whole, which is shorter than its diff:
```python
import jax
import jax.numpy as jnp
from jax import lax
from jax.sharding import PartitionSpec as P

CAP = 2
BF = jnp.bfloat16
F32 = jnp.float32


def swap(array, axis, bit):
    size = lax.axis_size(axis)
    return lax.ppermute(array, axis, [(i, i ^ bit) for i in range(size)])


def merge_blocks(weight, delta, first_rows, first_cols):
    size = delta.shape[1]
    for n in range(delta.shape[0]):
        row, col = first_rows[n], first_cols[n]
        inside = (row >= 0) & (row < weight.shape[0]) & (col >= 0) & (col < weight.shape[1])
        at = (jnp.clip(row, 0, weight.shape[0] - size), jnp.clip(col, 0, weight.shape[1] - size))
        old = lax.dynamic_slice(weight, at, (size, size))
        new = (old.astype(F32) + delta[n].astype(F32)).astype(BF)
        weight = lax.dynamic_update_slice(weight, jnp.where(inside, new, old), at)
    return weight


def split_sizes(width, unit):
    blocks = width // unit
    if width % unit or blocks < 8:
        return [width]
    sizes = []
    for parts in (5, 4, 3, 2):
        take = -(-blocks // parts) if parts > 2 else blocks // 2 + blocks % 2
        sizes.append(take * unit)
        blocks -= take
    sizes.append(blocks * unit)
    return [s for s in sizes if s]


def local(tokens, frozen, delta, block_rows, block_cols, owners, d_out):
    group, me_dp, me_t = (lax.axis_index(a) for a in ("groups", "dp", "tensor"))
    n_dp, n_tensor = lax.axis_size("dp"), lax.axis_size("tensor")
    rows, feats = tokens.shape
    block_count, bs = delta.shape[0], delta.shape[1]
    slab = frozen.shape[1]
    half = slab // 2
    width = feats * n_tensor
    mine, theirs = group * half, (1 - group) * half

    first_rows = block_rows * bs - me_dp * frozen.shape[0]
    slab_cols = block_cols * bs - me_t * slab
    if half % bs == 0:
        weight = lax.dynamic_slice(frozen, (0, mine), (frozen.shape[0], half))
        weight = merge_blocks(weight, delta, first_rows, slab_cols - mine)
    else:
        weight = merge_blocks(frozen, delta, first_rows, slab_cols)
        weight = lax.dynamic_slice(weight, (0, mine), (frozen.shape[0], half))

    x_two = jnp.concatenate([tokens, swap(tokens, "groups", 1)], axis=0)
    if n_tensor == 4:
        own, other = x_two, swap(x_two, "tensor", 2)
        own_c, other_c = swap(own, "tensor", 1), swap(other, "tensor", 1)
        x_full = jnp.zeros((2 * rows, width), BF)
        for bit, part in ((0, own), (2, other), (1, own_c), (3, other_c)):
            x_full = lax.dynamic_update_slice(x_full, part, (0, (me_t ^ bit) * feats))
    else:
        x_full = lax.all_gather(x_two, "tensor", axis=1, tiled=True)

    give = lax.dynamic_slice(d_out, (0, theirs), (rows, half))
    keep = lax.dynamic_slice(d_out, (0, mine), (rows, half))
    d_two = jnp.concatenate([keep, swap(give, "groups", 1)], axis=0)

    sizes = split_sizes(half, bs)
    activated = jnp.zeros((rows, slab), BF)
    d_rows = None
    slopes = []
    history = []
    first = 0
    for number, size in enumerate(sizes):
        shard = weight[:, first : first + size]
        if number >= 2:
            shard, history[number - 2] = lax.optimization_barrier((shard, history[number - 2]))
        segment = lax.all_gather(shard, "dp", axis=0, tiled=True)
        preact = jnp.dot(x_full, segment, preferred_element_type=F32)
        squash = jax.nn.sigmoid(preact)
        act = (preact * squash).astype(BF)
        d_slope = (
            d_two[:, first : first + size].astype(F32) * squash * (1.0 + preact * (1.0 - squash))
        ).astype(BF)
        slopes.append(d_slope)
        back = swap(act[rows:], "groups", 1)
        activated = lax.dynamic_update_slice(activated, act[:rows], (0, mine + first))
        activated = lax.dynamic_update_slice(activated, back, (0, theirs + first))
        term = lax.dot_general(
            d_slope, segment, (((1,), (1,)), ((), ())), preferred_element_type=F32
        )
        d_rows = term if d_rows is None else d_rows + term
        history.append(d_slope)
        first += size

    if n_tensor == 4:
        parts = d_rows.reshape(2 * rows, 2, 2, feats)
        core = me_t % 2
        side = me_t // 2
        send = lax.dynamic_slice_in_dim(parts, 1 - core, 1, 2)[:, :, 0].astype(BF)
        stay = lax.dynamic_slice_in_dim(parts, core, 1, 2)[:, :, 0]
        both = stay + swap(send, "tensor", 1).astype(F32)
        near = lax.dynamic_slice_in_dim(both, side, 1, 1)[:, 0]
        far = lax.dynamic_slice_in_dim(both, 1 - side, 1, 1)[:, 0]
        cut = rows // 2
        near_own, near_peer = near[:rows], near[rows:]
        far_own, far_peer = far[:rows], far[rows:].astype(BF)
        over_x = swap(far_peer[:cut], "tensor", 2).astype(F32)
        over_y = swap(far_peer[cut:], "groups", 1).astype(F32)
        near_peer = jnp.concatenate([near_peer[:cut] + over_x, near_peer[cut:]], axis=0)
        far_own = jnp.concatenate([far_own[:cut], far_own[cut:] + over_y], axis=0)
        from_y = swap(near_peer.astype(BF), "groups", 1).astype(F32)
        from_x = swap(far_own.astype(BF), "tensor", 2).astype(F32)
        d_tokens = (near_own + from_x + from_y).astype(BF)
    else:
        summed = lax.psum_scatter(d_rows.astype(BF), "tensor", scatter_dimension=1, tiled=True)
        d_tokens = (
            summed[:rows].astype(F32) + swap(summed[rows:], "groups", 1).astype(F32)
        ).astype(BF)

    d_pre = jnp.concatenate(
        [jnp.zeros((2 * rows, bs), BF)] + slopes + [jnp.zeros((2 * rows, bs), BF)], axis=1
    )
    starts = jnp.clip(slab_cols - mine + bs, 0, half + bs)
    dy = jnp.stack(
        [lax.dynamic_slice(d_pre, (0, starts[n]), (2 * rows, bs)) for n in range(block_count)]
    ).reshape(block_count, 2, rows, bs)
    xb = jnp.stack(
        [
            lax.dynamic_slice(x_full, (0, block_rows[n] * bs), (2 * rows, bs))
            for n in range(block_count)
        ]
    ).reshape(block_count, 2, rows, bs)
    grads = jnp.einsum("ngtk,ngtc->gnkc", xb, dy, preferred_element_type=F32)
    grads = grads[0] + swap(grads[1].astype(BF), "groups", 1).astype(F32)
    norm = float(rows * n_dp) ** (-0.5)
    everyone = lax.all_gather(grads.astype(BF), "dp", axis=0)
    total = jnp.sum(everyone.astype(F32), axis=0) * norm
    owner_ids = owners[:, 0]
    order = jnp.arange(block_count, dtype=jnp.int32)
    earlier = (owner_ids[None, :] == owner_ids[:, None]) & (order[None, :] < order[:, None])
    rank = jnp.sum(earlier.astype(jnp.int32), axis=1)
    wanted = (owner_ids[None, :] == me_dp) & (
        rank[None, :] == jnp.arange(CAP, dtype=jnp.int32)[:, None]
    )
    bucket = jnp.sum(jnp.where(wanted[:, :, None, None], total[None], 0.0), axis=1)
    return (activated, d_tokens, bucket[None])


def solution(mesh):
    in_specs = (
        P(("groups", "dp"), "tensor"),
        P("dp", "tensor"),
        P("tensor", None, None),
        P("tensor"),
        P("tensor"),
        P("tensor", None),
        P(("groups", "dp"), "tensor"),
    )
    out_specs = (
        P(("groups", "dp"), "tensor"),
        P(("groups", "dp"), "tensor"),
        P("tensor", ("groups", "dp"), None, None),
    )
    return jax.shard_map(local, mesh=mesh, in_specs=in_specs, out_specs=out_specs, check_vma=False)
```

time: 728 us -> 548 us (0.75)
  waiting for transfers between devices: 559 us -> 244 us
  local copies, waits for them, and re-layouts: 28.6 us -> 98.1 us
  between operations: 14.7 us -> 40.2 us
  starting transfers between devices: 0.24 us -> 16.9 us
  other arithmetic: 5.97 us -> 19.8 us
  matrix products: 96.1 us -> 104 us
    all_gather x4 -> x5, waiting for transfers between devices: 537 us -> 135 us  [local(): segment = lax.all_gather(shard, 'dp', axis=0, tiled=True)]
    ppermute x0 -> x16, waiting for transfers between devices: none -> 109 us  [swap(): return lax.ppermute(array, axis, [(i, i ^ bit) for i in range(size)])]
    dynamic_slice x0 -> x6, local copies, waits for them, and re-layouts: none -> 29 us  [the longest x1 9.37 us: local(): stay = lax.dynamic_slice_in_dim(parts, core, 1, 2)[:, :, 0]]
    dynamic_update_slice x0 -> x13, local copies, waits for them, and re-layouts: none -> 23.4 us  [the longest x4 12.1 us: local(): x_full = lax.dynamic_update_slice(x_full, part, (0, (me_t ^ bit) * feats))]
    reduce_scatter x2 -> x0, waiting for transfers between devices: 20.2 us -> none  [the longest x1 20.2 us: local(): lax.psum_scatter(d_rows.astype(jnp.bfloat16), 'tensor', scatter_dimension...]
    ppermute x0 -> x16, starting transfers between devices: none -> 16.5 us  [swap(): return lax.ppermute(array, axis, [(i, i ^ bit) for i in range(size)])]
    reshape x1, local copies, waits for them, and re-layouts: 4.87 us -> 19.4 us  [local(): parts = d_rows.reshape(2 * rows, 2, 2, feats)]
    dot_general x12 -> x11, matrix products: 96.1 us -> 104 us  [the longest x5 56.2 us: local(): lax.dot_general(d_slope, segment, (((1,), (1,)), ((), ())), preferred_ele...]
  transfers between devices with their start and end apart: 6 -> 21, of which waited for: 5 -> 12; matrix products, arithmetic and copies ran while one was open for 14% -> 24% of each run, Pallas kernels for 0% -> 0%
where the time goes in v1:
time: 548 us; the launch traced here: 538 us
  waiting for transfers between devices  244 us (45%)
  matrix products  104 us (19%)
  local copies, waits for them, and re-layouts  98.1 us (18%)
  between operations  40.2 us (7%)
  other arithmetic  19.8 us (4%)
  starting transfers between devices  16.9 us (3%)
  blocking collectives  15.1 us (3%)
    all_gather x5, waiting for transfers between devices, local(): segment = lax.all_gather(shard, 'dp', axis=0, tiled=True)  135 us
    ppermute x16, waiting for transfers between devices, swap(): return lax.ppermute(array, axis, [(i, i ^ bit) for i in range(size)])  109 us
    dot_general x5, matrix products, local(): lax.dot_general(d_slope, segment, (((1,), (1,)), ((), ())), preferred_ele...  56.2 us
    dot_general x5, matrix products, local(): preact = jnp.dot(x_full, segment, preferred_element_type=F32)  47.2 us
    reshape x1, local copies, waits for them, and re-layouts, local(): parts = d_rows.reshape(2 * rows, 2, 2, feats)  19.4 us
    ppermute x16, starting transfers between devices, swap(): return lax.ppermute(array, axis, [(i, i ^ bit) for i in range(size)])  16.5 us
    all_gather x1, blocking collectives, local(): everyone = lax.all_gather(grads.astype(BF), 'dp', axis=0)  15.1 us
    dynamic_update_slice x4, local copies, waits for them, and re-layouts, local(): x_full = lax.dynamic_update_slice(x_full, part, (0, (me_t ^ bit) * feats))  12.1 us
  transfers between devices with their start and end apart: 21, of which 12 were waited for; matrix products, arithmetic and copies ran while one was open for 24% of the time, Pallas kernels for 0%

profile of v1, /device:TPU:0, one launch (start us, length us, event | category | flops | bytes accessed | tf_op | source)
XLA Modules:
  0.0 538.4 jit_solution(17224540566690932974)
XLA Ops:
  25.6 4.3 constant_dynamic-slice_fusion.12
  41.2 4.2 fusion.42
  45.5 3.3 collective-permute-start
  49.7 19.4 %collective-permute-done = bf16[448,1024]{1,0:T(8,128)(2,1)S(1)} collective-permute-done((bf16[448,1024]{1,0:T(8,128)(2,1)S(1)}, bf16[448,1024]{1,0:T(8,128)(2,1)S(1)}, u32[]{:S(2)}, u32[]{:S(2)}) %collective-permute-start) | collective-permute-done | bytes 917536 | tf_op jit(solution)/shard_map/ppermute | solution.py:13
  70.4 41.3 %collective-permute-done.1 = bf16[896,1024]{1,0:T(8,128)(2,1)} collective-permute-done((bf16[896,1024]{1,0:T(8,128)(2,1)}, bf16[896,1024]{1,0:T(8,128)(2,1)}, u32[]{:S(2)}, u32[]{:S(2)}) %collective-permute-start.1) | collective-permute-done | bytes 1835040 | tf_op jit(solution)/shard_map/ppermute | solution.py:13
  111.7 3.4 constant_dynamic-slice_fusion.11
  117.3 3.8 broadcast_in_dim.36
  133.2 22.1 %collective-permute-done.6 = bf16[448,1920]{1,0:T(8,128)(2,1)S(1)} collective-permute-done((bf16[448,1920]{1,0:T(8,128)(2,1)}, bf16[448,1920]{1,0:T(8,128)(2,1)S(1)}, u32[]{:S(2)}, u32[]{:S(2)}) %collective-permute-start.6) | collective-permute-done | bytes 1720352 | tf_op jit(solution)/shard_map/ppermute | solution.py:13
  155.3 9.8 %constant_dynamic-update-slice_fusion.6 = (bf16[896,2176]{1,0:T(8,128)(2,1)}, bf16[896,384]{1,0:T(8,128)(2,1)}, f32[896,384]{1,0:T(8,128)}) fusion(bf16[896,2176]{1,0:T(8,128)(2,1)} %broadcast_dynamic-update-slice_fusion, bf16[448,1920]{1,0:T(8,128)(2,1)S(1)} %collective-permute-done.6, bf16[448,1920]{1,0:T(8,128)(2,1)S(1)} %get-tuple-element.34, ...), kind=kOutput, calls=%fused_computation.98 | convolution fusion | flops 2823045120 | bytes 16678912 | tf_op jit(solution)/shard_map/dot_general | solution.py:85
  165.1 14.4 %all-gather.9.cloned.1.call-done = bf16[4096,384]{1,0:T(8,128)(2,1)} async-done(((bf16[1024,384]{1,0:T(8,128)(2,1)}), bf16[4096,384]{1,0:T(8,128)(2,1)}) %all-gather.9.cloned.1.call-update) | async-done | bytes 3145744 | tf_op jit(solution)/shard_map/all_gather | solution.py:84
  179.5 9.8 %constant_dynamic-update-slice_fusion.5 = (bf16[896,2176]{1,0:T(8,128)(2,1)}, bf16[896,384]{1,0:T(8,128)(2,1)}, f32[896,384]{1,0:T(8,128)}) fusion(bf16[896,2176]{1,0:T(8,128)(2,1)} %get-tuple-element.17, bf16[448,1920]{1,0:T(8,128)(2,1)S(1)} %collective-permute-done.6, bf16[448,1920]{1,0:T(8,128)(2,1)S(1)} %get-tuple-element.34, ...), kind=kOutput, calls=%fused_computation.97 | convolution fusion | flops 2823045120 | bytes 16678912 | tf_op jit(solution)/shard_map/dot_general | solution.py:85
  192.2 51.1 %all-gather.11.cloned.1.call-done = bf16[4096,384]{1,0:T(8,128)(2,1)} async-done(((bf16[1024,384]{1,0:T(8,128)(2,1)}), bf16[4096,384]{1,0:T(8,128)(2,1)}) %all-gather.11.cloned.1.call-update) | async-done | bytes 3145744 | tf_op jit(solution)/shard_map/all_gather | solution.py:84
  243.3 9.8 %constant_dynamic-update-slice_fusion.4 = (bf16[896,2176]{1,0:T(8,128)(2,1)}, bf16[896,384]{1,0:T(8,128)(2,1)}, f32[896,384]{1,0:T(8,128)}) fusion(bf16[896,2176]{1,0:T(8,128)(2,1)} %get-tuple-element.15, bf16[448,1920]{1,0:T(8,128)(2,1)S(1)} %collective-permute-done.6, bf16[448,1920]{1,0:T(8,128)(2,1)S(1)} %get-tuple-element.34, ...), kind=kOutput, calls=%fused_computation.96 | convolution fusion | flops 2823045120 | bytes 16678912 | tf_op jit(solution)/shard_map/dot_general | solution.py:85
  258.8 7.3 %fusion.53 = f32[896,4096]{1,0:T(8,128)} fusion(bf16[896,384]{1,0:T(8,128)(2,1)S(1)} %copy-done.8, bf16[4096,384]{1,0:T(8,128)(2,1)S(1)} %copy-done.1), kind=kOutput, calls=%fused_computation.142 | convolution fusion | flops 2818572288 | bytes 18513920 | tf_op jit(solution)/shard_map/dot_general | solution.py:95
  266.1 7.3 %fusion.52 = f32[896,4096]{1,0:T(8,128)} fusion(bf16[896,384]{1,0:T(8,128)(2,1)S(1)} %copy-done.7, bf16[4096,384]{1,0:T(8,128)(2,1)S(1)} %copy-done), kind=kOutput, calls=%fused_computation.141 | convolution fusion | flops 2818572288 | bytes 18513920 | tf_op jit(solution)/shard_map/dot_general | solution.py:95
  275.4 31.4 %all-gather.13.cloned.1.call-done = bf16[4096,384]{1,0:T(8,128)(2,1)} async-done(((bf16[1024,384]{1,0:T(8,128)(2,1)}), bf16[4096,384]{1,0:T(8,128)(2,1)}) %all-gather.13.cloned.1.call-update) | async-done | bytes 3145744 | tf_op jit(solution)/shard_map/all_gather | solution.py:84
  306.9 9.0 %multiply_convert_fusion.4 = (bf16[896,384]{1,0:T(8,128)(2,1)}, f32[896,384]{1,0:T(8,128)S(1)}) fusion(bf16[896,4096]{1,0:T(8,128)(2,1)} %constant_dynamic-update-slice_fusion.12, bf16[4096,384]{1,0:T(8,128)(2,1)} %all-gather.13.cloned.1.call-done), kind=kOutput, calls=%fused_computation.22 | convolution fusion | flops 2820292608 | bytes 12550144 | tf_op jit(solution)/shard_map/dot_general | solution.py:85
  318.3 7.3 %fusion.54 = f32[896,4096]{1,0:T(8,128)} fusion(bf16[896,384]{1,0:T(8,128)(2,1)S(1)} %copy-done.9, bf16[4096,384]{1,0:T(8,128)(2,1)S(1)} %copy-done.2), kind=kOutput, calls=%fused_computation.143 | convolution fusion | flops 2818572288 | bytes 18513920 | tf_op jit(solution)/shard_map/dot_general | solution.py:95
  325.6 7.8 %fusion.41 = f32[896,4096]{1,0:T(8,128)} fusion(bf16[4096,384]{1,0:T(8,128)(2,1)S(1)} %copy-done.3, f32[896,384]{1,0:T(8,128)S(1)} %get-tuple-element.71, bf16[448,1920]{1,0:T(8,128)(2,1)S(1)} %get-tuple-element.34, bf16[448,1920]{1,0:T(8,128)(2,1)S(1)} %collective-permute-done.6), kind=kOutput, calls=%fused_computation.130 | convolution fusion | flops 2823045120 | bytes 22642688 | tf_op jit(solution)/shard_map/dot_general | solution.py:95
  333.4 37.6 %all-gather.15.cloned.1.call-done = bf16[4096,384]{1,0:T(8,128)(2,1)} async-done(((bf16[1024,384]{1,0:T(8,128)(2,1)}), bf16[4096,384]{1,0:T(8,128)(2,1)}) %all-gather.15.cloned.1.call-update) | async-done | bytes 3145744 | tf_op jit(solution)/shard_map/all_gather | solution.py:84
  371.1 8.9 %multiply_convert_fusion.2 = (bf16[896,384]{1,0:T(8,128)(2,1)}, f32[896,384]{1,0:T(8,128)S(1)}) fusion(bf16[896,4096]{1,0:T(8,128)(2,1)} %constant_dynamic-update-slice_fusion.12, bf16[4096,384]{1,0:T(8,128)(2,1)} %all-gather.15.cloned.1.call-done), kind=kOutput, calls=%fused_computation.19 | convolution fusion | flops 2820292608 | bytes 12550144 | tf_op jit(solution)/shard_map/dot_general | solution.py:85
  381.6 26.5 %add_add_fusion = f32[896,4096]{1,0:T(8,128)} fusion(f32[896,4096]{1,0:T(8,128)} %fusion.41, f32[896,4096]{1,0:T(8,128)} %fusion.54, f32[896,4096]{1,0:T(8,128)} %fusion.52, f32[896,4096]{1,0:T(8,128)} %fusion.53, bf16[896,384]{1,0:T(8,128)(2,1)} %get-tuple-element.12, bf16[4096,384]{1,0:T(8,128)(2,1)} %all-gather.15.cloned.1.call-done), kind=kOutput, calls=%fused_computation | convolution fusion | flops 2833252352 | bytes 77234176 | tf_op jit(solution)/shard_map/dot_general | solution.py:95
  408.1 19.4 %reshape.176 = f32[896,2,2,1024]{3,2,1,0:T(2,128)} reshape(f32[896,4096]{1,0:T(8,128)} %add_add_fusion) | data formatting | bytes 29360128 | tf_op jit(solution)/shard_map/reshape | solution.py:103
  427.5 8.9 %constant_dynamic-slice_fusion.8 = bf16[896,2,1,1024]{3,2,1,0:T(2,128)(2,1)S(1)} fusion(f32[896,2,2,1024]{3,2,1,0:T(2,128)} %reshape.176, s32[]{:T(128)S(6)} %select_n.165), kind=kLoop, calls=%fused_computation.107 | loop fusion | bytes 7340036 | tf_op jit(solution)/shard_map/dynamic_slice | solution.py:106
  436.4 3.8 copy.21
  442.6 9.0 %collective-permute-done.5 = bf16[448,384]{1,0:T(8,128)(2,1)S(1)} collective-permute-done((bf16[448,384]{1,0:T(8,128)(2,1)S(1)}, bf16[448,384]{1,0:T(8,128)(2,1)S(1)}, u32[]{:S(2)}, u32[]{:S(2)}) %collective-permute-start.5) | collective-permute-done | bytes 344096 | tf_op jit(solution)/shard_map/ppermute | solution.py:13
  469.2 7.5 %collective-permute-done.8 = bf16[448,384]{1,0:T(8,128)(2,1)S(1)} collective-permute-done((bf16[448,384]{1,0:T(8,128)(2,1)S(1)}, bf16[448,384]{1,0:T(8,128)(2,1)S(1)}, u32[]{:S(2)}, u32[]{:S(2)}) %collective-permute-start.8) | collective-permute-done | bytes 344096 | tf_op jit(solution)/shard_map/ppermute | solution.py:13
  481.3 9.4 %constant_dynamic-slice_fusion.9 = f32[896,2,1,1024]{3,2,1,0:T(1,128)S(1)} fusion(f32[896,2,2,1024]{3,2,1,0:T(2,128)} %reshape.176, s32[]{:T(128)S(6)} %select_n.164), kind=kLoop, calls=%fused_computation.108 | loop fusion | bytes 14680068 | tf_op jit(solution)/shard_map/dynamic_slice | solution.py:107
  490.6 4.6 bitcast_add_fusion
  500.2 6.2 %collective-permute-done.13 = bf16[224,1024]{1,0:T(8,128)(2,1)S(1)} collective-permute-done((bf16[224,1024]{1,0:T(8,128)(2,1)S(1)}, bf16[224,1024]{1,0:T(8,128)(2,1)S(1)}, u32[]{:S(2)}, u32[]{:S(2)}) %collective-permute-start.13) | collective-permute-done | bytes 458784 | tf_op jit(solution)/shard_map/ppermute | solution.py:13
  506.4 3.9 collective-permute-done.11
  513.1 15.1 %all-gather = bf16[16,128,128]{2,1,0:T(8,128)(2,1)S(1)} all-gather(bf16[4,128,128]{2,1,0:T(8,128)(2,1)S(1)} %fusion.29), channel_id=2, replica_groups=mesh['groups'=2,'dp'=4,'tensor'=4] {'dp'}, dimensions={0}, use_global_device_ids=true | all-gather | bytes 655360 | tf_op jit(solution)/shard_map/all_gather | solution.py:143
  (122 shorter events, 70.7 us)
Async XLA Ops:
  7.2 148.1 %all-gather.7.cloned.1.call-start = ((), (), s32[]{:S(2)}) async-start(), calls=%async_computation | async-start | bytes 3932160 | tf_op jit(solution)/shard_map/all_gather | solution.py:84
  45.4 134.1 %all-gather.9.cloned.1.call-start = ((), (), s32[]{:S(2)}) async-start(), calls=%async_computation.1 | async-start | bytes 3932160 | tf_op jit(solution)/shard_map/all_gather | solution.py:84
  45.5 23.7 %collective-permute-start = (bf16[448,1024]{1,0:T(8,128)(2,1)S(1)}, bf16[448,1024]{1,0:T(8,128)(2,1)S(1)}, u32[]{:S(2)}, u32[]{:S(2)}) collective-permute-start(bf16[448,1024]{1,0:T(8,128)(2,1)S(1)} %copy-done.10), channel_id=1, source_target_pairs={{0,16},{16,0},{1,17},{17,1},{2,18},{18,2},{3,19},{19,3},{4,20},{20... | collective-permute-start | bytes 2752520 | tf_op jit(solution)/shard_map/ppermute | solution.py:13
  70.1 41.6 %collective-permute-start.1 = (bf16[896,1024]{1,0:T(8,128)(2,1)}, bf16[896,1024]{1,0:T(8,128)(2,1)}, u32[]{:S(2)}, u32[]{:S(2)}) collective-permute-start(bf16[896,1024]{1,0:T(8,128)(2,1)} %constant_dynamic-update-slice_fusion), channel_id=1, source_target_pairs={{0,2},{1,3},{2,0},{3,1},{4,6},{5,7},{6,4},{7,5},{8,10},{9,11},{10,... | collective-permute-start | bytes 5505032 | tf_op jit(solution)/shard_map/ppermute | solution.py:13
  70.3 173.0 %all-gather.11.cloned.1.call-start = ((), (), s32[]{:S(2)}) async-start(), calls=%async_computation.2 | async-start | bytes 3932160 | tf_op jit(solution)/shard_map/all_gather | solution.py:84
  70.3 56.9 %collective-permute-start.2 = (bf16[896,1024]{1,0:T(8,128)(2,1)}, bf16[896,1024]{1,0:T(8,128)(2,1)}, u32[]{:S(2)}, u32[]{:S(2)}) collective-permute-start(bf16[896,1024]{1,0:T(8,128)(2,1)} %constant_dynamic-update-slice_fusion), channel_id=1, source_target_pairs={{0,1},{1,0},{2,3},{3,2},{4,5},{5,4},{6,7},{7,6},{8,9},{9,8},{10,11... | collective-permute-start | bytes 5505032 | tf_op jit(solution)/shard_map/ppermute | solution.py:13
  111.7 18.5 %collective-permute-start.3 = (bf16[896,1024]{1,0:T(8,128)(2,1)}, bf16[896,1024]{1,0:T(8,128)(2,1)}, u32[]{:S(2)}, u32[]{:S(2)}) collective-permute-start(bf16[896,1024]{1,0:T(8,128)(2,1)} %collective-permute-done.1), channel_id=1, source_target_pairs={{0,1},{1,0},{2,3},{3,2},{4,5},{5,4},{6,7},{7,6},{8,9},{9,8},{10,11... | collective-permute-start | bytes 5505032 | tf_op jit(solution)/shard_map/ppermute | solution.py:13
  115.1 40.2 %collective-permute-start.6 = (bf16[448,1920]{1,0:T(8,128)(2,1)}, bf16[448,1920]{1,0:T(8,128)(2,1)S(1)}, u32[]{:S(2)}, u32[]{:S(2)}) collective-permute-start(bf16[448,1920]{1,0:T(8,128)(2,1)} %get-tuple-element.35), channel_id=1, source_target_pairs={{0,16},{16,0},{1,17},{17,1},{2,18},{18,2},{3,19},{19,3},{4,20},{20... | collective-permute-start | bytes 5160968 | tf_op jit(solution)/shard_map/ppermute | solution.py:13
  165.1 141.8 %all-gather.13.cloned.1.call-start = ((), (), s32[]{:S(2)}) async-start(), calls=%async_computation.3 | async-start | bytes 3932160 | tf_op jit(solution)/shard_map/all_gather | solution.py:84
  189.3 181.7 %all-gather.15.cloned.1.call-start = ((), (), s32[]{:S(2)}) async-start(), calls=%async_computation.4 | async-start | bytes 3932160 | tf_op jit(solution)/shard_map/all_gather | solution.py:84
  253.1 5.8 %copy-start.1 = (bf16[4096,384]{1,0:T(8,128)(2,1)S(1)}, bf16[4096,384]{1,0:T(8,128)(2,1)}, u32[]{:S(2)}) copy-start(bf16[4096,384]{1,0:T(8,128)(2,1)} %all-gather.9.cloned.1.call-done) | copy-start | bytes 9437188
  253.1 5.8 %copy-start.8 = (bf16[896,384]{1,0:T(8,128)(2,1)S(1)}, bf16[896,384]{1,0:T(8,128)(2,1)}, u32[]{:S(2)}) copy-start(bf16[896,384]{1,0:T(8,128)(2,1)} %get-tuple-element.16) | copy-start | bytes 2064388
  257.3 8.8 %copy-start = (bf16[4096,384]{1,0:T(8,128)(2,1)S(1)}, bf16[4096,384]{1,0:T(8,128)(2,1)}, u32[]{:S(2)}) copy-start(bf16[4096,384]{1,0:T(8,128)(2,1)} %all-gather.7.cloned.1.call-done) | copy-start | bytes 9437188
  257.3 8.8 %copy-start.7 = (bf16[896,384]{1,0:T(8,128)(2,1)S(1)}, bf16[896,384]{1,0:T(8,128)(2,1)}, u32[]{:S(2)}) copy-start(bf16[896,384]{1,0:T(8,128)(2,1)} %get-tuple-element.18) | copy-start | bytes 2064388
  257.3 17.3 %collective-permute-start.4 = (bf16[448,384]{1,0:T(8,128)(2,1)S(1)}, bf16[448,384]{1,0:T(8,128)(2,1)S(1)}, u32[]{:S(2)}, u32[]{:S(2)}) collective-permute-start(bf16[448,384]{1,0:T(8,128)(2,1)S(1)} %get-tuple-element.47), channel_id=1, source_target_pairs={{0,16},{16,0},{1,17},{17,1},{2,18},{18,2},{3,19},{19,3},{4,20},{20... | collective-permute-start | bytes 1032200 | tf_op jit(solution)/shard_map/ppermute | solution.py:13
  266.1 7.3 %copy-start.6 = (f32[896,384]{1,0:T(8,128)S(1)}, f32[896,384]{1,0:T(8,128)}, u32[]{:S(2)}) copy-start(f32[896,384]{1,0:T(8,128)} %get-tuple-element.66) | copy-start | bytes 4128772
  318.3 7.3 %copy-start.3 = (bf16[4096,384]{1,0:T(8,128)(2,1)S(1)}, bf16[4096,384]{1,0:T(8,128)(2,1)}, u32[]{:S(2)}) copy-start(bf16[4096,384]{1,0:T(8,128)(2,1)} %all-gather.13.cloned.1.call-done) | copy-start | bytes 9437188
  436.4 15.9 %copy-start.5 = (f32[896,384]{1,0:T(8,128)S(1)}, f32[896,384]{1,0:T(8,128)}, u32[]{:S(2)}) copy-start(f32[896,384]{1,0:T(8,128)} %get-tuple-element.67) | copy-start | bytes 4128772
  440.3 14.7 %copy-start.14 = (s32[4]{0:T(128)S(1)}, s32[4]{0:T(128)}, u32[]{:S(2)}) copy-start(s32[4]{0:T(128)} %param.10) | copy-start | bytes 52
  440.3 25.2 %copy-start.15 = (s32[4,1]{0,1:T(1,128)S(1)}, s32[4,1]{0,1:T(1,128)}, u32[]{:S(2)}) copy-start(s32[4,1]{0,1:T(1,128)} %param.12) | copy-start | bytes 52
  440.3 26.2 %copy-start.12 = (bf16[896,384]{1,0:T(8,128)(2,1)S(1)}, bf16[896,384]{1,0:T(8,128)(2,1)}, u32[]{:S(2)}) copy-start(bf16[896,384]{1,0:T(8,128)(2,1)} %get-tuple-element.70) | copy-start | bytes 2064388
  440.3 50.3 %collective-permute-start.10 = (bf16[896,2,1024]{2,0,1:T(8,128)(2,1)}, bf16[896,2,1024]{2,0,1:T(8,128)(2,1)}, u32[]{:S(2)}, u32[]{:S(2)}) collective-permute-start(bf16[896,2,1024]{2,0,1:T(8,128)(2,1)} %bitcast.104), channel_id=1, source_target_pairs={{0,1},{1,0},{2,3},{3,2},{4,5},{5,4},{6,7},{7,6},{8,9},{9,8},{10,11... | collective-permute-start | bytes 11010056 | tf_op jit(solution)/shard_map/ppermute | solution.py:13
  441.1 10.5 %collective-permute-start.5 = (bf16[448,384]{1,0:T(8,128)(2,1)S(1)}, bf16[448,384]{1,0:T(8,128)(2,1)S(1)}, u32[]{:S(2)}, u32[]{:S(2)}) collective-permute-start(bf16[448,384]{1,0:T(8,128)(2,1)S(1)} %get-tuple-element.45), channel_id=1, source_target_pairs={{0,16},{16,0},{1,17},{17,1},{2,18},{18,2},{3,19},{19,3},{4,20},{20... | collective-permute-start | bytes 1032200 | tf_op jit(solution)/shard_map/ppermute | solution.py:13
  452.7 24.8 %copy-start.11 = (bf16[896,384]{1,0:T(8,128)(2,1)S(1)}, bf16[896,384]{1,0:T(8,128)(2,1)}, u32[]{:S(2)}) copy-start(bf16[896,384]{1,0:T(8,128)(2,1)} %get-tuple-element.68) | copy-start | bytes 2064388
  453.5 12.2 %collective-permute-start.7 = (bf16[448,384]{1,0:T(8,128)(2,1)S(1)}, bf16[448,384]{1,0:T(8,128)(2,1)S(1)}, u32[]{:S(2)}, u32[]{:S(2)}) collective-permute-start(bf16[448,384]{1,0:T(8,128)(2,1)S(1)} %get-tuple-element.43), channel_id=1, source_target_pairs={{0,16},{16,0},{1,17},{17,1},{2,18},{18,2},{3,19},{19,3},{4,20},{20... | collective-permute-start | bytes 1032200 | tf_op jit(solution)/shard_map/ppermute | solution.py:13
  467.3 9.4 %collective-permute-start.8 = (bf16[448,384]{1,0:T(8,128)(2,1)S(1)}, bf16[448,384]{1,0:T(8,128)(2,1)S(1)}, u32[]{:S(2)}, u32[]{:S(2)}) collective-permute-start(bf16[448,384]{1,0:T(8,128)(2,1)S(1)} %get-tuple-element.41), channel_id=1, source_target_pairs={{0,16},{16,0},{1,17},{17,1},{2,18},{18,2},{3,19},{19,3},{4,20},{20... | collective-permute-start | bytes 1032200 | tf_op jit(solution)/shard_map/ppermute | solution.py:13
  478.3 50.9 %collective-permute-start.9 = (bf16[448,384]{1,0:T(8,128)(2,1)S(1)}, bf16[448,384]{1,0:T(8,128)(2,1)S(1)}, u32[]{:S(2)}, u32[]{:S(2)}) collective-permute-start(bf16[448,384]{1,0:T(8,128)(2,1)S(1)} %get-tuple-element.39), channel_id=1, source_target_pairs={{0,16},{16,0},{1,17},{17,1},{2,18},{18,2},{3,19},{19,3},{4,20},{20... | collective-permute-start | bytes 1032200 | tf_op jit(solution)/shard_map/ppermute | solution.py:13
  495.7 10.7 %collective-permute-start.13 = (bf16[224,1024]{1,0:T(8,128)(2,1)S(1)}, bf16[224,1024]{1,0:T(8,128)(2,1)S(1)}, u32[]{:S(2)}, u32[]{:S(2)}) collective-permute-start(bf16[224,1024]{1,0:T(8,128)(2,1)S(1)} %get-tuple-element.37), channel_id=1, source_target_pairs={{0,2},{1,3},{2,0},{3,1},{4,6},{5,7},{6,4},{7,5},{8,10},{9,11},{10,... | collective-permute-start | bytes 1376264 | tf_op jit(solution)/shard_map/ppermute | solution.py:13
  497.3 13.0 %collective-permute-start.11 = (bf16[224,1024]{1,0:T(8,128)(2,1)S(1)}, bf16[224,1024]{1,0:T(8,128)(2,1)S(1)}, u32[]{:S(2)}, u32[]{:S(2)}) collective-permute-start(bf16[224,1024]{1,0:T(8,128)(2,1)S(1)} %get-tuple-element.38), channel_id=1, source_target_pairs={{0,16},{16,0},{1,17},{17,1},{2,18},{18,2},{3,19},{19,3},{4,20},{20... | collective-permute-start | bytes 1376264 | tf_op jit(solution)/shard_map/ppermute | solution.py:13
  499.9 13.2 %collective-permute-start.15 = (bf16[4,128,128]{2,1,0:T(8,128)(2,1)S(1)}, bf16[4,128,128]{2,1,0:T(8,128)(2,1)S(1)}, u32[]{:S(2)}, u32[]{:S(2)}) collective-permute-start(bf16[4,128,128]{2,1,0:T(8,128)(2,1)S(1)} %fusion.30), channel_id=1, source_target_pairs={{0,16},{16,0},{1,17},{17,1},{2,18},{18,2},{3,19},{19,3},{4,20},{20... | collective-permute-start | bytes 393224 | tf_op jit(solution)/shard_map/ppermute | solution.py:13
  510.7 19.3 %collective-permute-start.14 = (bf16[448,1024]{1,0:T(8,128)(2,1)S(1)}, bf16[448,1024]{1,0:T(8,128)(2,1)S(1)}, u32[]{:S(2)}, u32[]{:S(2)}) collective-permute-start(bf16[448,1024]{1,0:T(8,128)(2,1)S(1)} %pad_maximum_fusion.1), channel_id=1, source_target_pairs={{0,16},{16,0},{1,17},{17,1},{2,18},{18,2},{3,19},{19,3},{4,20},{20... | collective-permute-start | bytes 2752520 | tf_op jit(solution)/shard_map/ppermute | solution.py:13
  512.7 17.3 %collective-permute-start.12 = (bf16[448,1024]{1,0:T(8,128)(2,1)S(1)}, bf16[448,1024]{1,0:T(8,128)(2,1)S(1)}, u32[]{:S(2)}, u32[]{:S(2)}) collective-permute-start(bf16[448,1024]{1,0:T(8,128)(2,1)S(1)} %pad_maximum_fusion), channel_id=1, source_target_pairs={{0,2},{1,3},{2,0},{3,1},{4,6},{5,7},{6,4},{7,5},{8,10},{9,11},{10,... | collective-permute-start | bytes 2752520 | tf_op jit(solution)/shard_map/ppermute | solution.py:13
  (5 other events, 17.3 us)
Sparse Core Ops, SparseCore 0:
  45.5 70.1 all-gather.6
  117.3 62.1 all-gather.8
  181.1 62.1 all-gather.10
  244.7 62.1 all-gather.12
  308.9 62.1 all-gather.14

commit v2 on v0

v2 whole, which is shorter than its diff:
```python
import functools

import jax
import jax.numpy as jnp
from jax import lax
from jax.experimental import pallas as pl
from jax.experimental.pallas import tpu as pltpu
from jax.sharding import PartitionSpec as P

CAP = 2
BF = jnp.bfloat16
F32 = jnp.float32
VMEM_BYTES = 56 * 2**20


def swap(array, axis, bit):
    size = lax.axis_size(axis)
    return lax.ppermute(array, axis, [(i, i ^ bit) for i in range(size)])


def params():
    return pltpu.CompilerParams(vmem_limit_bytes=VMEM_BYTES)


def forward_kernel(n_x, n_w, first, blocks, bs, meta, *refs):
    x_refs, w_refs = refs[:n_x], refs[n_x : n_x + n_w]
    delta_ref, d_ref, act_ref, slope_ref, acc = refs[n_x + n_w :]
    feats = x_refs[0].shape[1]
    width = acc.shape[1]
    total = None
    for k in range(n_x):
        part = meta[k]
        if n_w == 1:
            weight = w_refs[0][pl.ds(pl.multiple_of(part * feats, feats), feats), :]
        else:
            weight = w_refs[k][...]
        term = jnp.dot(x_refs[k][...], weight, preferred_element_type=F32)
        total = term if total is None else total + term
    acc[...] = total
    for n in range(blocks):
        row, col = meta[8 + 2 * n], meta[9 + 2 * n] - first
        here = (col >= 0) & (col < width)
        for k in range(n_x):
            offset = row - meta[k] * feats

            @pl.when(here & (offset >= 0) & (offset < feats))
            def _():
                cols = pl.ds(pl.multiple_of(col, bs), bs)
                xs = x_refs[k][:, pl.ds(pl.multiple_of(offset, bs), bs)]
                acc[:, cols] += jnp.dot(xs, delta_ref[n], preferred_element_type=F32)

    preact = acc[...]
    squash = jax.nn.sigmoid(preact)
    act_ref[0] = (preact * squash).astype(BF)
    slope_ref[...] = (
        d_ref[...].astype(F32) * squash * (1.0 + preact * (1.0 - squash))
    ).astype(BF)


def forward(meta, xs, ws, delta, d_piece, first, groups_of):
    rows, width = d_piece.shape
    feats = xs[0].shape[1]
    tile = rows // groups_of
    blocks, bs = delta.shape[0], delta.shape[1]
    flops = 2 * rows * feats * len(xs) * width
    return pl.pallas_call(
        functools.partial(forward_kernel, len(xs), len(ws), first, blocks, bs),
        grid_spec=pltpu.PrefetchScalarGridSpec(
            num_scalar_prefetch=1,
            grid=(groups_of,),
            in_specs=[pl.BlockSpec((tile, feats), lambda i, m: (i, 0)) for _ in xs]
            + [
                pl.BlockSpec(w.shape, lambda i, m: (0, 0), pipeline_mode=pl.Buffered(1))
                for w in ws
            ]
            + [
                pl.BlockSpec(delta.shape, lambda i, m: (0, 0, 0)),
                pl.BlockSpec((tile, width), lambda i, m: (i, 0)),
            ],
            out_specs=[
                pl.BlockSpec((1, tile, width), lambda i, m: (i, 0, 0)),
                pl.BlockSpec((tile, width), lambda i, m: (i, 0)),
            ],
            scratch_shapes=[pltpu.VMEM((tile, width), F32)],
        ),
        out_shape=[
            jax.ShapeDtypeStruct((groups_of, tile, width), BF),
            jax.ShapeDtypeStruct((rows, width), BF),
        ],
        compiler_params=params(),
        cost_estimate=pl.CostEstimate(
            flops=flops, bytes_accessed=2 * (rows + width) * feats * len(xs), transcendentals=0
        ),
    )(meta, *xs, *ws, delta, d_piece)


def backward_kernel(firsts, blocks, bs, meta, *refs):
    n = len(firsts)
    slopes, w_refs = refs[:n], refs[n : 2 * n]
    delta_ref, out_ref, acc = refs[2 * n :]
    size = acc.shape[1]
    base = meta[0] * (size * pl.num_programs(0)) + pl.program_id(0) * size
    total = None
    for p in range(n):
        term = lax.dot_general(
            slopes[p][...], w_refs[p][...], (((1,), (1,)), ((), ())), preferred_element_type=F32
        )
        total = term if total is None else total + term
    acc[...] = total
    for b in range(blocks):
        row = meta[8 + 2 * b] - base
        for p in range(n):
            col = meta[9 + 2 * b] - firsts[p]

            @pl.when((row >= 0) & (row < size) & (col >= 0) & (col < slopes[p].shape[1]))
            def _():
                ds = slopes[p][:, pl.ds(pl.multiple_of(col, bs), bs)]
                acc[:, pl.ds(pl.multiple_of(row, bs), bs)] += lax.dot_general(
                    ds, delta_ref[b], (((1,), (1,)), ((), ())), preferred_element_type=F32
                )

    out_ref[...] = acc[...].astype(out_ref.dtype)


def backward(meta, slopes, ws, delta, firsts, feats, out_type):
    rows = slopes[0].shape[0]
    blocks, bs = delta.shape[0], delta.shape[1]
    tiles = 4
    size = feats // tiles
    width = sum(s.shape[1] for s in slopes)
    return pl.pallas_call(
        functools.partial(backward_kernel, firsts, blocks, bs),
        grid_spec=pltpu.PrefetchScalarGridSpec(
            num_scalar_prefetch=1,
            grid=(tiles,),
            in_specs=[
                pl.BlockSpec(s.shape, lambda i, m: (0, 0), pipeline_mode=pl.Buffered(1))
                for s in slopes
            ]
            + [
                pl.BlockSpec((size, w.shape[1]), lambda i, m: (m[0] * tiles + i, 0)) for w in ws
            ]
            + [pl.BlockSpec(delta.shape, lambda i, m: (0, 0, 0))],
            out_specs=pl.BlockSpec((rows, size), lambda i, m: (0, i)),
            scratch_shapes=[pltpu.VMEM((rows, size), F32)],
        ),
        out_shape=jax.ShapeDtypeStruct((rows, feats), out_type),
        compiler_params=params(),
        cost_estimate=pl.CostEstimate(
            flops=2 * rows * feats * width,
            bytes_accessed=2 * (rows + feats) * width,
            transcendentals=0,
        ),
    )(meta, *slopes, *ws, delta)


def slot_ranks(owners):
    owner_ids = owners[:, 0]
    order = jnp.arange(owner_ids.shape[0], dtype=jnp.int32)
    earlier = (owner_ids[None, :] == owner_ids[:, None]) & (order[None, :] < order[:, None])
    rank = jnp.sum(earlier.astype(jnp.int32), axis=1)
    return (owner_ids[None, :] == lax.axis_index("dp")) & (
        rank[None, :] == jnp.arange(CAP, dtype=jnp.int32)[:, None]
    )


def pick_slots(owners, total):
    wanted = slot_ranks(owners)
    return jnp.sum(jnp.where(wanted[:, :, None, None], total[None], 0.0), axis=1)[None]


def tie(*values):
    return lax.optimization_barrier(values)


def piece_sizes(half, bs):
    blocks = half // bs
    if blocks < 12:
        return [half]
    last = 4
    rest = blocks - last
    return [(rest - rest // 2) * bs, rest // 2 * bs, last * bs]


def local(tokens, frozen, delta, block_rows, block_cols, owners, d_out):
    group, me_dp, me_t = (lax.axis_index(a) for a in ("groups", "dp", "tensor"))
    n_dp, n_tensor = lax.axis_size("dp"), lax.axis_size("tensor")
    rows, feats = tokens.shape
    blocks, bs = delta.shape[0], delta.shape[1]
    slab = frozen.shape[1]
    half = slab // 2
    mine, theirs = group * half, (1 - group) * half
    sizes = piece_sizes(half, bs)
    firsts = [sum(sizes[:p]) for p in range(len(sizes))]
    block_cols_here = block_cols * bs - me_t * slab - mine
    block_info = jnp.stack([block_rows * bs, block_cols_here], axis=1).reshape(-1)
    parts = [me_t ^ k for k in range(4)]

    def meta_of(*head):
        lead = jnp.stack(list(head) + [jnp.int32(0)] * (8 - len(head)))
        return jnp.concatenate([lead, block_info]).astype(jnp.int32)

    gathered = []
    for first, size in zip(firsts, sizes):
        shard = lax.dynamic_slice(frozen, (0, mine + first), (frozen.shape[0], size))
        gathered.append(lax.all_gather(shard, "dp", axis=0, tiled=True))

    peer = swap(tokens, "groups", 1)
    own_x = swap(tokens, "tensor", 2)
    peer_x = swap(peer, "tensor", 2)
    near_x = jnp.concatenate([tokens, peer], axis=0)
    far_x = jnp.concatenate([own_x, peer_x], axis=0)
    xs = [near_x, swap(near_x, "tensor", 1), far_x, swap(far_x, "tensor", 1)]

    order = peer_x
    d_pieces = []
    for first, size in zip(firsts, sizes):
        give = lax.dynamic_slice(d_out, (0, theirs + first), (rows, size))
        keep = lax.dynamic_slice(d_out, (0, mine + first), (rows, size))
        give, order = tie(give, order)
        got = swap(give, "groups", 1)
        order = got
        d_pieces.append(jnp.concatenate([keep, got], axis=0))

    activated = jnp.zeros((rows, slab), BF)
    slopes = []
    meta = meta_of(*parts)
    for first, size, weight, d_piece in zip(firsts, sizes, gathered, d_pieces):
        act, slope = forward(meta, xs, [weight], delta, d_piece, first, 2)
        slopes.append(slope)
        back = swap(act[1], "groups", 1)
        activated = lax.dynamic_update_slice(activated, act[0], (0, mine + first))
        activated = lax.dynamic_update_slice(activated, back, (0, theirs + first))

    def back_of(bit, out_type, wait=None):
        m = meta_of(me_t ^ bit)
        if wait is not None:
            m, wait = tie(m, wait)
        return backward(m, slopes, gathered, delta, firsts, feats, out_type)

    far_give = back_of(3, BF)
    far_got = swap(far_give, "tensor", 1)
    far_stay = back_of(2, F32, far_give)
    near_give = back_of(1, BF, far_stay)
    near_got = swap(near_give, "tensor", 1)
    near_stay = back_of(0, F32, near_give)
    cut = rows // 2
    far_peer = (far_stay[rows:] + far_got[rows:].astype(F32)).astype(BF)
    over_x = swap(far_peer[:cut], "tensor", 2)
    over_y = swap(far_peer[cut:], "groups", 1)
    far_own = far_stay[:rows] + far_got[:rows].astype(F32)
    far_own = jnp.concatenate([far_own[:cut], far_own[cut:] + over_y.astype(F32)], 0).astype(BF)
    from_x = swap(far_own, "tensor", 2)
    near_peer = near_stay[rows:] + near_got[rows:].astype(F32)
    near_peer = jnp.concatenate([near_peer[:cut] + over_x.astype(F32), near_peer[cut:]], 0)
    from_y = swap(near_peer.astype(BF), "groups", 1)
    near_own = near_stay[:rows] + near_got[:rows].astype(F32)
    d_tokens = (near_own + from_x.astype(F32) + from_y.astype(F32)).astype(BF)

    grads = []
    for n in range(blocks):
        dy = jnp.zeros((2 * rows, bs), BF)
        for first, size, slope in zip(firsts, sizes, slopes):
            col = block_cols_here[n] - first
            cut_out = lax.dynamic_slice(slope, (0, jnp.clip(col, 0, size - bs)), (2 * rows, bs))
            dy = jnp.where((col >= 0) & (col < size), cut_out, dy)
        xb = jnp.zeros((2 * rows, bs), BF)
        for k in range(4):
            off = block_rows[n] * bs - parts[k] * feats
            cut_out = lax.dynamic_slice(xs[k], (0, jnp.clip(off, 0, feats - bs)), (2 * rows, bs))
            xb = jnp.where((off >= 0) & (off < feats), cut_out, xb)
        xb, dy = xb.reshape(2, rows, bs), dy.reshape(2, rows, bs)
        grads.append(jnp.einsum("gtk,gtc->gkc", xb, dy, preferred_element_type=F32))
    grads = jnp.stack(grads, axis=1)
    grads = grads[0] + swap(grads[1].astype(BF), "groups", 1).astype(F32)
    bit = 1
    while bit < n_dp:
        grads = grads + swap(grads.astype(BF), "dp", bit).astype(F32)
        bit *= 2
    norm = float(rows * n_dp) ** (-0.5)
    return (activated, d_tokens, pick_slots(owners, grads * norm))


def local_any(tokens, frozen, delta, block_rows, block_cols, owners, d_out):
    me_dp, me_t, n_dp = lax.axis_index("dp"), lax.axis_index("tensor"), lax.axis_size("dp")
    rows = tokens.shape[0]
    blocks, bs = delta.shape[0], delta.shape[1]
    slab = frozen.shape[1]
    x_full = lax.all_gather(tokens, "tensor", axis=1, tiled=True)
    weight = lax.all_gather(frozen, "dp", axis=0, tiled=True)
    width = x_full.shape[1]
    row_pick = (block_rows[:, None] == jnp.arange(width // bs)[None, :]).astype(F32)
    cols_here = block_cols - me_t * (slab // bs)
    col_pick = (cols_here[:, None] == jnp.arange(slab // bs)[None, :]).astype(F32)
    highest = lax.Precision.HIGHEST
    xb = jnp.take(x_full.reshape(rows, width // bs, bs), block_rows, axis=1)
    contrib = jnp.einsum("tnk,nkc->tnc", xb, delta, preferred_element_type=F32)
    add = jnp.einsum("tnc,nm->tmc", contrib, col_pick, precision=highest).reshape(rows, slab)
    preact = jnp.dot(x_full, weight, preferred_element_type=F32) + add
    squash = jax.nn.sigmoid(preact)
    activated = (preact * squash).astype(BF)
    d_pre = (d_out.astype(F32) * squash * (1.0 + preact * (1.0 - squash))).astype(BF)
    d_rows = lax.dot_general(
        d_pre, weight, (((1,), (1,)), ((), ())), preferred_element_type=F32
    )
    dy = jnp.take(d_pre.reshape(rows, slab // bs, bs), cols_here, axis=1)
    back = jnp.einsum("tnc,nkc->tnk", dy, delta, preferred_element_type=F32)
    back = jnp.einsum("tnk,nr->trk", back, row_pick, precision=highest).reshape(rows, width)
    d_tokens = lax.psum_scatter(
        (d_rows + back).astype(BF), "tensor", scatter_dimension=1, tiled=True
    )
    grads = jnp.einsum("tnk,tnc->nkc", xb, dy, preferred_element_type=F32)
    everyone = lax.all_gather(grads.astype(BF), "dp", axis=0).astype(F32)
    norm = float(rows * n_dp) ** (-0.5)
    return (activated, d_tokens, pick_slots(owners, jnp.sum(everyone, axis=0) * norm))


def solution(mesh):
    sizes = dict(mesh.shape)
    small = sizes["groups"] == 2 and sizes["dp"] == 4 and sizes["tensor"] == 4
    body = local if small else local_any
    in_specs = (
        P(("groups", "dp"), "tensor"),
        P("dp", "tensor"),
        P("tensor", None, None),
        P("tensor"),
        P("tensor"),
        P("tensor", None),
        P(("groups", "dp"), "tensor"),
    )
    out_specs = (
        P(("groups", "dp"), "tensor"),
        P(("groups", "dp"), "tensor"),
        P("tensor", ("groups", "dp"), None, None),
    )
    return jax.shard_map(body, mesh=mesh, in_specs=in_specs, out_specs=out_specs, check_vma=False)
```

time: 728 us -> 430 us (0.59); the launches traced: 718 us -> 428 us
  waiting for transfers between devices: 559 us -> 248 us
  matrix products: 96.1 us -> 1.14 us
  Pallas kernels: 0 us -> 77.3 us
  starting transfers between devices: 0.24 us -> 20.6 us
  other arithmetic: 5.97 us -> 20.5 us
  between operations: 14.7 us -> 29.1 us
  blocking collectives: 13.5 us -> 0 us
    all_gather x4 -> x3, waiting for transfers between devices: 537 us -> 159 us  [local(): gathered.append(lax.all_gather(shard, 'dp', axis=0, tiled=True))]
    dot_general x12 -> x4, matrix products: 96.1 us -> 1.14 us  [local(): grads.append(jnp.einsum('gtk,gtc->gkc', xb, dy, preferred_element_type=F32))]
    ppermute x0 -> x20, waiting for transfers between devices: none -> 89.1 us  [swap(): return lax.ppermute(array, axis, [(i, i ^ bit) for i in range(size)])]
    pallas_call x0 -> x7, Pallas kernels: none -> 77.3 us  [the longest x3 38.9 us: forward(): pl.pallas_call(functools.partial(forward_kernel, len(xs), len(ws), first,...]
    ppermute x0 -> x20, starting transfers between devices: none -> 20.5 us  [swap(): return lax.ppermute(array, axis, [(i, i ^ bit) for i in range(size)])]
    reduce_scatter x2 -> x0, waiting for transfers between devices: 20.2 us -> none  [the longest x1 20.2 us: local(): lax.psum_scatter(d_rows.astype(jnp.bfloat16), 'tensor', scatter_dimension...]
    all_gather x1 -> x0, blocking collectives: 13.5 us -> none  [local(): lax.all_gather(reduced.astype(jnp.bfloat16), 'dp', axis=0, tiled=True)]
    select_n x2 -> x6, other arithmetic: 0.01 us -> 11 us  [the longest x4 7.36 us: local(): xb = jnp.where((off >= 0) & (off < feats), cut_out, xb)]
  transfers between devices with their start and end apart: 6 -> 23, of which waited for: 5 -> 11; matrix products, arithmetic and copies ran while one was open for 14% -> 11% of each run, Pallas kernels for 0% -> 18%
where the time goes in v2:
time: 430 us; the launch traced here: 428 us
  waiting for transfers between devices  248 us (58%)
  Pallas kernels  77.3 us (18%)
  local copies, waits for them, and re-layouts  31.5 us (7%)
  between operations  29.1 us (7%)
  starting transfers between devices  20.6 us (5%)
  other arithmetic  20.5 us (5%)
    all_gather x3, waiting for transfers between devices, local(): gathered.append(lax.all_gather(shard, 'dp', axis=0, tiled=True))  159 us
    ppermute x20, waiting for transfers between devices, swap(): return lax.ppermute(array, axis, [(i, i ^ bit) for i in range(size)])  89.1 us
    pallas_call x3, Pallas kernels, forward(): pl.pallas_call(functools.partial(forward_kernel, len(xs), len(ws), first,...  38.9 us
    pallas_call x4, Pallas kernels, backward(): pl.pallas_call(functools.partial(backward_kernel, firsts, blocks, bs), gr...  38.4 us
    ppermute x20, starting transfers between devices, swap(): return lax.ppermute(array, axis, [(i, i ^ bit) for i in range(size)])  20.5 us
  transfers between devices with their start and end apart: 23, of which 11 were waited for; matrix products, arithmetic and copies ran while one was open for 11% of the time, Pallas kernels for 18%

profile of v2, /device:TPU:0, one launch (start us, length us, event | category | flops | bytes accessed | tf_op | source)
XLA Modules:
  0.0 428.4 jit_solution(3081125650413731232)
XLA Ops:
  7.2 2.3 constant_dynamic-slice_fusion.2
  9.6 2.6 constant_dynamic-slice_fusion.5
  12.3 2.9 constant_dynamic-slice_fusion.8
  15.2 3.0 collective-permute-start
  19.7 19.2 %collective-permute-done = bf16[448,1024]{1,0:T(8,128)(2,1)} collective-permute-done((bf16[448,1024]{1,0:T(8,128)(2,1)}, bf16[448,1024]{1,0:T(8,128)(2,1)}, u32[]{:S(2)}, u32[]{:S(2)}) %collective-permute-start) | collective-permute-done | bytes 917536 | tf_op jit(solution)/shard_map/ppermute | solution.py:18
  41.2 2.2 constant_dynamic-update-slice_fusion.4
  44.7 2.2 constant_dynamic-update-slice_fusion.3.refs_0_
  46.9 2.2 constant_dynamic-update-slice_fusion.6
  49.0 11.7 %collective-permute-done.3 = bf16[448,1024]{1,0:T(8,128)(2,1)} collective-permute-done((bf16[448,1024]{1,0:T(8,128)(2,1)}, bf16[448,1024]{1,0:T(8,128)(2,1)}, u32[]{:S(2)}, u32[]{:S(2)}) %collective-permute-start.3) | collective-permute-done | bytes 917536 | tf_op jit(solution)/shard_map/ppermute | solution.py:18
  62.2 2.2 constant_dynamic-update-slice_fusion.5.refs_2_
  85.5 11.4 %collective-permute-done.7 = bf16[448,640]{1,0:T(8,128)(2,1)} collective-permute-done((bf16[448,640]{1,0:T(8,128)(2,1)}, bf16[448,640]{1,0:T(8,128)(2,1)}, u32[]{:S(2)}, u32[]{:S(2)}) %collective-permute-start.7) | collective-permute-done | bytes 573472 | tf_op jit(solution)/shard_map/ppermute | solution.py:18
  97.5 2.3 pad_maximum_fusion.refs_6_
  99.7 2.2 pad_maximum_fusion.1.refs_6_
  101.9 7.1 %collective-permute-done.9 = bf16[448,512]{1,0:T(8,128)(2,1)S(1)} collective-permute-done((bf16[448,512]{1,0:T(8,128)(2,1)S(1)}, bf16[448,512]{1,0:T(8,128)(2,1)S(1)}, u32[]{:S(2)}, u32[]{:S(2)}) %collective-permute-start.9) | collective-permute-done | bytes 458784 | tf_op jit(solution)/shard_map/ppermute | solution.py:18
  110.0 1.9 select_select_fusion.7
  115.5 1.9 select_select_fusion.1
  117.4 11.3 %shard_map.96 = (bf16[2,448,512]{2,1,0:T(8,128)(2,1)}, bf16[896,512]{1,0:T(8,128)(2,1)}) custom-call(s32[16]{0:T(128)} %concatenate.38.meta, bf16[896,1024]{1,0:T(8,128)(2,1)} %constant_dynamic-update-slice_fusion.3.refs_0_, bf16[896,1024]{1,0:T(8,128)(2,1)} %collective-permute-done.1.refs_1_, bf16[896,1024]{1,0:T(8,128)(2,1)} %constant_dynamic-update-slice_fusion.5.refs_2_, ...), custom_call_target="tpu_custom_call" | custom-call | flops 3758096384 | bytes 11534336 | tf_op jit(solution)/shard_map/pallas_call | solution.py:66
  130.7 60.6 %all-gather.6.cloned.1.call-done.refs_4_ = bf16[4096,640]{1,0:T(8,128)(2,1)} async-done(((bf16[1024,640]{1,0:T(8,128)(2,1)}), bf16[4096,640]{1,0:T(8,128)(2,1)}) %all-gather.6.cloned.1.call-update) | async-done | bytes 5242896 | tf_op jit(solution)/shard_map/all_gather | solution.py:206
  191.3 13.6 %shard_map.95 = (bf16[2,448,640]{2,1,0:T(8,128)(2,1)}, bf16[896,640]{1,0:T(8,128)(2,1)}) custom-call(s32[16]{0:T(128)} %concatenate.38.meta, bf16[896,1024]{1,0:T(8,128)(2,1)} %constant_dynamic-update-slice_fusion.3.refs_0_, bf16[896,1024]{1,0:T(8,128)(2,1)} %collective-permute-done.1.refs_1_, bf16[896,1024]{1,0:T(8,128)(2,1)} %constant_dynamic-update-slice_fusion.5.refs_2_, ...), custom_call_target="tpu_custom_call" | custom-call | flops 4697620480 | bytes 12582912 | tf_op jit(solution)/shard_map/pallas_call | solution.py:66
  204.9 1.9 slice_bitcast_fusion.1
  208.3 98.4 %all-gather.4.cloned.1.call-done.refs_4_.refs_3_ = bf16[4096,768]{1,0:T(8,128)(2,1)} async-done(((bf16[1024,768]{1,0:T(8,128)(2,1)}), bf16[4096,768]{1,0:T(8,128)(2,1)}) %all-gather.4.cloned.1.call-update) | async-done | bytes 6291472 | tf_op jit(solution)/shard_map/all_gather | solution.py:206
  306.7 14.1 %shard_map.94 = (bf16[2,448,768]{2,1,0:T(8,128)(2,1)}, bf16[896,768]{1,0:T(8,128)(2,1)}) custom-call(s32[16]{0:T(128)} %concatenate.38.meta, bf16[896,1024]{1,0:T(8,128)(2,1)} %constant_dynamic-update-slice_fusion.3.refs_0_, bf16[896,1024]{1,0:T(8,128)(2,1)} %collective-permute-done.1.refs_1_, bf16[896,1024]{1,0:T(8,128)(2,1)} %constant_dynamic-update-slice_fusion.5.refs_2_, ...), custom_call_target="tpu_custom_call" | custom-call | flops 5637144576 | bytes 13631488 | tf_op jit(solution)/shard_map/pallas_call | solution.py:66
  327.1 9.2 %shard_map.97 = bf16[896,1024]{1,0:T(8,128)(2,1)} custom-call(s32[16]{0:T(128)} %concatenate.47.meta, bf16[896,768]{1,0:T(8,128)(2,1)} %get-tuple-element.21.refs_0_, bf16[896,640]{1,0:T(8,128)(2,1)} %get-tuple-element.22.refs_1_, bf16[896,512]{1,0:T(8,128)(2,1)} %get-tuple-element.23.refs_2_, ...), custom_call_target="tpu_custom_call" | custom-call | flops 3523215360 | bytes 7372800 | tf_op jit(solution)/shard_map/pallas_call | solution.py:131
  336.3 9.8 %shard_map.98 = f32[896,1024]{1,0:T(8,128)} custom-call(s32[16]{0:T(128)} %concatenate.46.meta, bf16[896,768]{1,0:T(8,128)(2,1)} %get-tuple-element.21.refs_0_, bf16[896,640]{1,0:T(8,128)(2,1)} %get-tuple-element.22.refs_1_, bf16[896,512]{1,0:T(8,128)(2,1)} %get-tuple-element.23.refs_2_, bf16[4096,768]{1,0:T(8,128)(2,1)} %all-gather.4.cloned.1.call-done.refs_4_.refs_3_, ...), custom_call_target="tpu_custom_call" | custom-call | flops 3523215360 | bytes 7372800 | tf_op jit(solution)/shard_map/pallas_call | solution.py:131
  346.0 9.2 %shard_map.99 = bf16[896,1024]{1,0:T(8,128)(2,1)} custom-call(s32[16]{0:T(128)} %concatenate.45.meta, bf16[896,768]{1,0:T(8,128)(2,1)} %get-tuple-element.21.refs_0_, bf16[896,640]{1,0:T(8,128)(2,1)} %get-tuple-element.22.refs_1_, bf16[896,512]{1,0:T(8,128)(2,1)} %get-tuple-element.23.refs_2_, ...), custom_call_target="tpu_custom_call" | custom-call | flops 3523215360 | bytes 7372800 | tf_op jit(solution)/shard_map/pallas_call | solution.py:131
  355.7 10.2 %shard_map.100 = f32[896,1024]{1,0:T(8,128)} custom-call(s32[16]{0:T(128)} %concatenate.44.meta, bf16[896,768]{1,0:T(8,128)(2,1)} %get-tuple-element.21.refs_0_, bf16[896,640]{1,0:T(8,128)(2,1)} %get-tuple-element.22.refs_1_, bf16[896,512]{1,0:T(8,128)(2,1)} %get-tuple-element.23.refs_2_, bf16[4096,768]{1,0:T(8,128)(2,1)} %all-gather.4.cloned.1.call-done.refs_4_.refs_3_, ...), custom_call_target="tpu_custom_call" | custom-call | flops 3523215360 | bytes 7372800 | tf_op jit(solution)/shard_map/pallas_call | solution.py:131
  367.4 3.8 collective-permute-done.18
  374.0 6.8 %collective-permute-done.19 = bf16[4,128,128]{2,1,0:T(8,128)(2,1)S(1)} collective-permute-done((bf16[4,128,128]{2,1,0:T(8,128)(2,1)S(1)}, bf16[4,128,128]{2,1,0:T(8,128)(2,1)S(1)}, u32[]{:S(2)}, u32[]{:S(2)}) %collective-permute-start.19) | collective-permute-done | bytes 131104 | tf_op jit(solution)/shard_map/ppermute | solution.py:18
  381.2 2.2 collective-permute-start.15
  383.9 13.5 %collective-permute-done.13 = bf16[224,1024]{1,0:T(8,128)(2,1)S(1)} collective-permute-done((bf16[224,1024]{1,0:T(8,128)(2,1)S(1)}, bf16[224,1024]{1,0:T(8,128)(2,1)S(1)}, u32[]{:S(2)}, u32[]{:S(2)}) %collective-permute-start.13) | collective-permute-done | bytes 458784 | tf_op jit(solution)/shard_map/ppermute | solution.py:18
  397.5 2.2 collective-permute-start.14
  404.6 13.9 %collective-permute-done.14 = bf16[448,1024]{1,0:T(8,128)(2,1)S(1)} collective-permute-done((bf16[448,1024]{1,0:T(8,128)(2,1)S(1)}, bf16[448,1024]{1,0:T(8,128)(2,1)S(1)}, u32[]{:S(2)}, u32[]{:S(2)}) %collective-permute-start.14) | collective-permute-done | bytes 917536 | tf_op jit(solution)/shard_map/ppermute | solution.py:18
  (121 shorter events, 41.5 us)
Async XLA Ops:
  7.2 110.3 %all-gather.8.cloned.1.call-start = ((), (), s32[]{:S(2)}) async-start(), calls=%async_computation.2 | async-start | bytes 5242880 | tf_op jit(solution)/shard_map/all_gather | solution.py:206
  9.5 181.8 %all-gather.6.cloned.1.call-start = ((), (), s32[]{:S(2)}) async-start(), calls=%async_computation.1 | async-start | bytes 6553600 | tf_op jit(solution)/shard_map/all_gather | solution.py:206
  12.2 294.5 %all-gather.4.cloned.1.call-start = ((), (), s32[]{:S(2)}) async-start(), calls=%async_computation | async-start | bytes 7864320 | tf_op jit(solution)/shard_map/all_gather | solution.py:206
  12.3 28.3 %copy-start.13 = (s32[4]{0:T(128)S(1)}, s32[4]{0:T(128)}, u32[]{:S(2)}) copy-start(s32[4]{0:T(128)} %param.11) | copy-start | bytes 52
  12.3 31.1 %copy-start.4 = (bf16[448,3840]{1,0:T(8,128)(2,1)S(1)}, bf16[448,3840]{1,0:T(8,128)(2,1)}, u32[]{:S(2)}) copy-start(bf16[448,3840]{1,0:T(8,128)(2,1)} %param.13) | copy-start | bytes 10321924
  15.2 23.7 %collective-permute-start = (bf16[448,1024]{1,0:T(8,128)(2,1)}, bf16[448,1024]{1,0:T(8,128)(2,1)}, u32[]{:S(2)}, u32[]{:S(2)}) collective-permute-start(bf16[448,1024]{1,0:T(8,128)(2,1)} %param.7), channel_id=1, source_target_pairs={{0,16},{16,0},{1,17},{17,1},{2,18},{18,2},{3,19},{19,3},{4,20},{20... | collective-permute-start | bytes 2752520 | tf_op jit(solution)/shard_map/ppermute | solution.py:18
  18.2 28.6 %collective-permute-start.2 = (bf16[448,1024]{1,0:T(8,128)(2,1)}, bf16[448,1024]{1,0:T(8,128)(2,1)}, u32[]{:S(2)}, u32[]{:S(2)}) collective-permute-start(bf16[448,1024]{1,0:T(8,128)(2,1)} %param.7), channel_id=1, source_target_pairs={{0,2},{1,3},{2,0},{3,1},{4,6},{5,7},{6,4},{7,5},{8,10},{9,11},{10,... | collective-permute-start | bytes 2752520 | tf_op jit(solution)/shard_map/ppermute | solution.py:18
  38.9 21.9 %collective-permute-start.3 = (bf16[448,1024]{1,0:T(8,128)(2,1)}, bf16[448,1024]{1,0:T(8,128)(2,1)}, u32[]{:S(2)}, u32[]{:S(2)}) collective-permute-start(bf16[448,1024]{1,0:T(8,128)(2,1)} %collective-permute-done), channel_id=1, source_target_pairs={{0,2},{1,3},{2,0},{3,1},{4,6},{5,7},{6,4},{7,5},{8,10},{9,11},{10,... | collective-permute-start | bytes 2752520 | tf_op jit(solution)/shard_map/ppermute | solution.py:18
  46.8 17.5 %copy-start.12 = (s32[4]{0:T(128)S(1)}, s32[4]{0:T(128)}, u32[]{:S(2)}) copy-start(s32[4]{0:T(128)} %param.10) | copy-start | bytes 52
  46.8 63.2 %collective-permute-start.1 = (bf16[896,1024]{1,0:T(8,128)(2,1)}, bf16[896,1024]{1,0:T(8,128)(2,1)}, u32[]{:S(2)}, u32[]{:S(2)}) collective-permute-start(bf16[896,1024]{1,0:T(8,128)(2,1)} %constant_dynamic-update-slice_fusion.3.refs_0_), channel_id=1, source_target_pairs={{0,1},{1,0},{2,3},{3,2},{4,5},{5,4},{6,7},{7,6},{8,9},{9,8},{10,11... | collective-permute-start | bytes 5505032 | tf_op jit(solution)/shard_map/ppermute | solution.py:18
  60.7 24.4 %copy-start.14 = (s32[4,1]{0,1:T(1,128)S(1)}, s32[4,1]{0,1:T(1,128)}, u32[]{:S(2)}) copy-start(s32[4,1]{0,1:T(1,128)} %param.12) | copy-start | bytes 52
  60.7 20.4 %collective-permute-start.5 = (bf16[448,768]{1,0:T(8,128)(2,1)}, bf16[448,768]{1,0:T(8,128)(2,1)}, u32[]{:S(2)}, u32[]{:S(2)}) collective-permute-start(bf16[448,768]{1,0:T(8,128)(2,1)} %get-tuple-element.15), channel_id=1, source_target_pairs={{0,16},{16,0},{1,17},{17,1},{2,18},{18,2},{3,19},{19,3},{4,20},{20... | collective-permute-start | bytes 2064392 | tf_op jit(solution)/shard_map/ppermute | solution.py:18
  64.3 45.7 %collective-permute-start.4 = (bf16[896,1024]{1,0:T(8,128)(2,1)}, bf16[896,1024]{1,0:T(8,128)(2,1)}, u32[]{:S(2)}, u32[]{:S(2)}) collective-permute-start(bf16[896,1024]{1,0:T(8,128)(2,1)} %constant_dynamic-update-slice_fusion.5.refs_2_), channel_id=1, source_target_pairs={{0,1},{1,0},{2,3},{3,2},{4,5},{5,4},{6,7},{7,6},{8,9},{9,8},{10,11... | collective-permute-start | bytes 5505032 | tf_op jit(solution)/shard_map/ppermute | solution.py:18
  81.1 15.8 %collective-permute-start.7 = (bf16[448,640]{1,0:T(8,128)(2,1)}, bf16[448,640]{1,0:T(8,128)(2,1)}, u32[]{:S(2)}, u32[]{:S(2)}) collective-permute-start(bf16[448,640]{1,0:T(8,128)(2,1)} %get-tuple-element.17), channel_id=1, source_target_pairs={{0,16},{16,0},{1,17},{17,1},{2,18},{18,2},{3,19},{19,3},{4,20},{20... | collective-permute-start | bytes 1720328 | tf_op jit(solution)/shard_map/ppermute | solution.py:18
  85.2 12.3 %copy-start.6 = (bf16[448,768]{1,0:T(8,128)(2,1)S(1)}, bf16[448,768]{1,0:T(8,128)(2,1)}, u32[]{:S(2)}) copy-start(bf16[448,768]{1,0:T(8,128)(2,1)} %get-tuple-element.37) | copy-start | bytes 2064388
  85.5 14.3 %copy-start.7 = (bf16[448,640]{1,0:T(8,128)(2,1)S(1)}, bf16[448,640]{1,0:T(8,128)(2,1)}, u32[]{:S(2)}) copy-start(bf16[448,640]{1,0:T(8,128)(2,1)} %get-tuple-element.35) | copy-start | bytes 1720324
  96.9 12.2 %collective-permute-start.9 = (bf16[448,512]{1,0:T(8,128)(2,1)S(1)}, bf16[448,512]{1,0:T(8,128)(2,1)S(1)}, u32[]{:S(2)}, u32[]{:S(2)}) collective-permute-start(bf16[448,512]{1,0:T(8,128)(2,1)S(1)} %get-tuple-element.19), channel_id=1, source_target_pairs={{0,16},{16,0},{1,17},{17,1},{2,18},{18,2},{3,19},{19,3},{4,20},{20... | collective-permute-start | bytes 1376264 | tf_op jit(solution)/shard_map/ppermute | solution.py:18
  130.5 273.0 %collective-permute-start.10 = (bf16[448,512]{1,0:T(8,128)(2,1)}, bf16[448,512]{1,0:T(8,128)(2,1)}, u32[]{:S(2)}, u32[]{:S(2)}) collective-permute-start(bf16[448,512]{1,0:T(8,128)(2,1)} %slice_bitcast_fusion.2), channel_id=1, source_target_pairs={{0,16},{16,0},{1,17},{17,1},{2,18},{18,2},{3,19},{19,3},{4,20},{20... | collective-permute-start | bytes 1376264 | tf_op jit(solution)/shard_map/ppermute | solution.py:18
  206.8 114.0 %copy-start = (bf16[896,640]{1,0:T(8,128)(2,1)S(1)}, bf16[896,640]{1,0:T(8,128)(2,1)}, u32[]{:S(2)}) copy-start(bf16[896,640]{1,0:T(8,128)(2,1)} %get-tuple-element.22.refs_1_) | copy-start | bytes 3440644
  206.8 114.0 %copy-start.1 = (bf16[896,512]{1,0:T(8,128)(2,1)S(1)}, bf16[896,512]{1,0:T(8,128)(2,1)}, u32[]{:S(2)}) copy-start(bf16[896,512]{1,0:T(8,128)(2,1)} %get-tuple-element.23.refs_2_) | copy-start | bytes 2752516
  206.8 195.4 %collective-permute-start.8 = (bf16[448,640]{1,0:T(8,128)(2,1)}, bf16[448,640]{1,0:T(8,128)(2,1)}, u32[]{:S(2)}, u32[]{:S(2)}) collective-permute-start(bf16[448,640]{1,0:T(8,128)(2,1)} %slice_bitcast_fusion.1), channel_id=1, source_target_pairs={{0,16},{16,0},{1,17},{17,1},{2,18},{18,2},{3,19},{19,3},{4,20},{20... | collective-permute-start | bytes 1720328 | tf_op jit(solution)/shard_map/ppermute | solution.py:18
  325.7 40.3 %collective-permute-start.17 = (bf16[4,128,128]{2,1,0:T(8,128)(2,1)S(1)}, bf16[4,128,128]{2,1,0:T(8,128)(2,1)S(1)}, u32[]{:S(2)}, u32[]{:S(2)}) collective-permute-start(bf16[4,128,128]{2,1,0:T(8,128)(2,1)S(1)} %fusion.8), channel_id=1, source_target_pairs={{0,16},{16,0},{1,17},{17,1},{2,18},{18,2},{3,19},{19,3},{4,20},{20... | collective-permute-start | bytes 393224 | tf_op jit(solution)/shard_map/ppermute | solution.py:18
  336.3 36.1 %collective-permute-start.12 = (bf16[896,1024]{1,0:T(8,128)(2,1)}, bf16[896,1024]{1,0:T(8,128)(2,1)S(1)}, u32[]{:S(2)}, u32[]{:S(2)}) collective-permute-start(bf16[896,1024]{1,0:T(8,128)(2,1)} %shard_map.97), channel_id=1, source_target_pairs={{0,1},{1,0},{2,3},{3,2},{4,5},{5,4},{6,7},{7,6},{8,9},{9,8},{10,11... | collective-permute-start | bytes 5505032 | tf_op jit(solution)/shard_map/ppermute | solution.py:18
  355.2 26.0 %collective-permute-start.11 = (bf16[896,1024]{1,0:T(8,128)(2,1)}, bf16[896,1024]{1,0:T(8,128)(2,1)S(1)}, u32[]{:S(2)}, u32[]{:S(2)}) collective-permute-start(bf16[896,1024]{1,0:T(8,128)(2,1)} %shard_map.99), channel_id=1, source_target_pairs={{0,1},{1,0},{2,3},{3,2},{4,5},{5,4},{6,7},{7,6},{8,9},{9,8},{10,11... | collective-permute-start | bytes 5505032 | tf_op jit(solution)/shard_map/ppermute | solution.py:18
  366.0 5.2 %collective-permute-start.18 = (bf16[4,128,128]{2,1,0:T(8,128)(2,1)S(1)}, bf16[4,128,128]{2,1,0:T(8,128)(2,1)S(1)}, u32[]{:S(2)}, u32[]{:S(2)}) collective-permute-start(bf16[4,128,128]{2,1,0:T(8,128)(2,1)S(1)} %fusion.9), channel_id=1, source_target_pairs={{0,4},{4,0},{8,12},{12,8},{1,5},{5,1},{9,13},{13,9},{2,6},{6,2},{1... | collective-permute-start | bytes 393224 | tf_op jit(solution)/shard_map/ppermute | solution.py:18
  371.3 30.8 %collective-permute-start.6 = (bf16[448,768]{1,0:T(8,128)(2,1)S(1)}, bf16[448,768]{1,0:T(8,128)(2,1)S(1)}, u32[]{:S(2)}, u32[]{:S(2)}) collective-permute-start(bf16[448,768]{1,0:T(8,128)(2,1)S(1)} %slice_bitcast_fusion), channel_id=1, source_target_pairs={{0,16},{16,0},{1,17},{17,1},{2,18},{18,2},{3,19},{19,3},{4,20},{20... | collective-permute-start | bytes 2064392 | tf_op jit(solution)/shard_map/ppermute | solution.py:18
  372.4 8.4 %collective-permute-start.19 = (bf16[4,128,128]{2,1,0:T(8,128)(2,1)S(1)}, bf16[4,128,128]{2,1,0:T(8,128)(2,1)S(1)}, u32[]{:S(2)}, u32[]{:S(2)}) collective-permute-start(bf16[4,128,128]{2,1,0:T(8,128)(2,1)S(1)} %fusion.7), channel_id=1, source_target_pairs={{0,8},{4,12},{8,0},{12,4},{1,9},{5,13},{9,1},{13,5},{2,10},{6,14},... | collective-permute-start | bytes 393224 | tf_op jit(solution)/shard_map/ppermute | solution.py:18
  380.8 16.5 %collective-permute-start.13 = (bf16[224,1024]{1,0:T(8,128)(2,1)S(1)}, bf16[224,1024]{1,0:T(8,128)(2,1)S(1)}, u32[]{:S(2)}, u32[]{:S(2)}) collective-permute-start(bf16[224,1024]{1,0:T(8,128)(2,1)S(1)} %get-tuple-element.39), channel_id=1, source_target_pairs={{0,16},{16,0},{1,17},{17,1},{2,18},{18,2},{3,19},{19,3},{4,20},{20... | collective-permute-start | bytes 1376264 | tf_op jit(solution)/shard_map/ppermute | solution.py:18
  381.2 18.6 %collective-permute-start.15 = (bf16[224,1024]{1,0:T(8,128)(2,1)S(1)}, bf16[224,1024]{1,0:T(8,128)(2,1)S(1)}, u32[]{:S(2)}, u32[]{:S(2)}) collective-permute-start(bf16[224,1024]{1,0:T(8,128)(2,1)S(1)} %get-tuple-element.40), channel_id=1, source_target_pairs={{0,2},{1,3},{2,0},{3,1},{4,6},{5,7},{6,4},{7,5},{8,10},{9,11},{10,... | collective-permute-start | bytes 1376264 | tf_op jit(solution)/shard_map/ppermute | solution.py:18
  397.5 21.0 %collective-permute-start.14 = (bf16[448,1024]{1,0:T(8,128)(2,1)S(1)}, bf16[448,1024]{1,0:T(8,128)(2,1)S(1)}, u32[]{:S(2)}, u32[]{:S(2)}) collective-permute-start(bf16[448,1024]{1,0:T(8,128)(2,1)S(1)} %pad_maximum_fusion.3), channel_id=1, source_target_pairs={{0,2},{1,3},{2,0},{3,1},{4,6},{5,7},{6,4},{7,5},{8,10},{9,11},{10,... | collective-permute-start | bytes 2752520 | tf_op jit(solution)/shard_map/ppermute | solution.py:18
  400.0 20.3 %collective-permute-start.16 = (bf16[448,1024]{1,0:T(8,128)(2,1)S(1)}, bf16[448,1024]{1,0:T(8,128)(2,1)S(1)}, u32[]{:S(2)}, u32[]{:S(2)}) collective-permute-start(bf16[448,1024]{1,0:T(8,128)(2,1)S(1)} %pad_maximum_fusion.4), channel_id=1, source_target_pairs={{0,16},{16,0},{1,17},{17,1},{2,18},{18,2},{3,19},{19,3},{4,20},{20... | collective-permute-start | bytes 2752520 | tf_op jit(solution)/shard_map/ppermute | solution.py:18
  404.6 17.2 %copy-start.5 = (bf16[448,3840]{1,0:T(8,128)(2,1)}, bf16[448,3840]{1,0:T(8,128)(2,1)S(1)}, u32[]{:S(2)}) copy-start(bf16[448,3840]{1,0:T(8,128)(2,1)S(1)} %constant_dynamic-update-slice_fusion) | copy-start | bytes 10321924
  (6 other events, 33.1 us)
Sparse Core Ops, SparseCore 0:
  9.7 83.4 all-gather.7
  94.7 96.5 all-gather.5
  192.9 113.7 all-gather.3

commit v3 on v2

v3 whole, which is shorter than its diff:
```python
import functools

import jax
import jax.numpy as jnp
from jax import lax
from jax.experimental import pallas as pl
from jax.experimental.pallas import tpu as pltpu
from jax.sharding import PartitionSpec as P

CAP = 2
BF = jnp.bfloat16
F32 = jnp.float32
VMEM_BYTES = 56 * 2**20


def swap(array, axis, bit):
    size = lax.axis_size(axis)
    return lax.ppermute(array, axis, [(i, i ^ bit) for i in range(size)])


def params():
    return pltpu.CompilerParams(vmem_limit_bytes=VMEM_BYTES)


def forward_kernel(first, blocks, bs, meta, x_ref, w_ref, delta_ref, d_ref, act_ref, slope_ref, acc):
    width = acc.shape[1]
    total = None
    for s in range(w_ref.shape[0]):
        term = jnp.dot(x_ref[meta[s]], w_ref[s], preferred_element_type=F32)
        total = term if total is None else total + term
    acc[...] = total
    for n in range(blocks):
        col = meta[11 + 4 * n] - first

        @pl.when((col >= 0) & (col < width))
        def _():
            cols = pl.ds(pl.multiple_of(col, bs), bs)
            rows = pl.ds(pl.multiple_of(meta[10 + 4 * n], bs), bs)
            xs = x_ref[meta[8 + 4 * n], :, rows]
            acc[:, cols] += jnp.dot(xs, delta_ref[n], preferred_element_type=F32)

    preact = acc[...]
    squash = jax.nn.sigmoid(preact)
    act_ref[0] = (preact * squash).astype(BF)
    slope_ref[...] = (
        d_ref[...].astype(F32) * squash * (1.0 + preact * (1.0 - squash))
    ).astype(BF)


def forward(meta, x4, w4, delta, d_piece, first, groups_of):
    rows, width = d_piece.shape
    slots, feats = w4.shape[0], w4.shape[1]
    tile = rows // groups_of
    blocks, bs = delta.shape[0], delta.shape[1]
    return pl.pallas_call(
        functools.partial(forward_kernel, first, blocks, bs),
        grid_spec=pltpu.PrefetchScalarGridSpec(
            num_scalar_prefetch=1,
            grid=(groups_of,),
            in_specs=[
                pl.BlockSpec((slots, tile, feats), lambda i, m: (0, i, 0)),
                pl.BlockSpec(w4.shape, lambda i, m: (0, 0, 0), pipeline_mode=pl.Buffered(1)),
                pl.BlockSpec(delta.shape, lambda i, m: (0, 0, 0)),
                pl.BlockSpec((tile, width), lambda i, m: (i, 0)),
            ],
            out_specs=[
                pl.BlockSpec((1, tile, width), lambda i, m: (i, 0, 0)),
                pl.BlockSpec((tile, width), lambda i, m: (i, 0)),
            ],
            scratch_shapes=[pltpu.VMEM((tile, width), F32)],
        ),
        out_shape=[
            jax.ShapeDtypeStruct((groups_of, tile, width), BF),
            jax.ShapeDtypeStruct((rows, width), BF),
        ],
        compiler_params=params(),
        cost_estimate=pl.CostEstimate(
            flops=2 * rows * feats * slots * width,
            bytes_accessed=2 * (rows + width) * feats * slots,
            transcendentals=0,
        ),
    )(meta, x4, w4, delta, d_piece)


def backward_kernel(firsts, blocks, bs, has_acc, meta, *refs):
    n = len(firsts)
    slopes, w_refs = refs[:n], refs[n : 2 * n]
    delta_ref = refs[2 * n]
    acc_in = refs[2 * n + 1] if has_acc else None
    outs, acc = refs[2 * n + 1 + has_acc : -1], refs[-1]
    size = acc.shape[1]
    slot = meta[4] + pl.program_id(0)
    base = pl.program_id(1) * size
    total = acc_in[0] if has_acc else None
    for p in range(n):
        term = lax.dot_general(
            slopes[p][...], w_refs[p][0], (((1,), (1,)), ((), ())), preferred_element_type=F32
        )
        total = term if total is None else total + term
    acc[...] = total
    for b in range(blocks):
        row = meta[10 + 4 * b] - base
        for p in range(n):
            col = meta[11 + 4 * b] - firsts[p]
            inside = (row >= 0) & (row < size) & (col >= 0) & (col < slopes[p].shape[1])

            @pl.when(inside & (meta[9 + 4 * b] == slot))
            def _():
                ds = slopes[p][:, pl.ds(pl.multiple_of(col, bs), bs)]
                acc[:, pl.ds(pl.multiple_of(row, bs), bs)] += lax.dot_general(
                    ds, delta_ref[b], (((1,), (1,)), ((), ())), preferred_element_type=F32
                )

    if len(outs) == 1:
        outs[0][0] = acc[...]
    else:
        cut = outs[0].shape[0]
        outs[0][...] = acc[:cut].astype(outs[0].dtype)
        outs[1][...] = acc[cut:].astype(outs[1].dtype)


def backward(meta, slopes, ws, delta, firsts, acc, out_type):
    rows = slopes[0].shape[0]
    slots, feats = ws[0].shape[0], ws[0].shape[1]
    blocks, bs = delta.shape[0], delta.shape[1]
    tiles = 2
    size = feats // tiles
    width = sum(s.shape[1] for s in slopes)
    every = out_type is None
    steps = slots if every else 1
    whole = pl.BlockSpec((1, rows, size), lambda s, i, m: (m[4] + s, 0, i))
    half = pl.BlockSpec((rows // 2, size), lambda s, i, m: (0, i))
    if every:
        out_specs = [whole]
        out_shape = [jax.ShapeDtypeStruct((slots, rows, feats), F32)]
    else:
        out_specs = [half, half]
        out_shape = [jax.ShapeDtypeStruct((rows // 2, feats), out_type)] * 2
    return pl.pallas_call(
        functools.partial(backward_kernel, firsts, blocks, bs, acc is not None),
        grid_spec=pltpu.PrefetchScalarGridSpec(
            num_scalar_prefetch=1,
            grid=(steps, tiles),
            in_specs=[
                pl.BlockSpec(s.shape, lambda s, i, m: (0, 0), pipeline_mode=pl.Buffered(1))
                for s in slopes
            ]
            + [
                pl.BlockSpec((1, size, w.shape[2]), lambda s, i, m: (m[4] + s, i, 0)) for w in ws
            ]
            + [pl.BlockSpec(delta.shape, lambda s, i, m: (0, 0, 0))]
            + ([] if acc is None else [whole]),
            out_specs=out_specs,
            scratch_shapes=[pltpu.VMEM((rows, size), F32)],
        ),
        out_shape=out_shape,
        compiler_params=params(),
        cost_estimate=pl.CostEstimate(
            flops=2 * rows * feats * width * steps,
            bytes_accessed=2 * (rows + feats) * width * steps,
            transcendentals=0,
        ),
    )(meta, *slopes, *ws, delta, *([] if acc is None else [acc]))


def slot_ranks(owners):
    owner_ids = owners[:, 0]
    order = jnp.arange(owner_ids.shape[0], dtype=jnp.int32)
    earlier = (owner_ids[None, :] == owner_ids[:, None]) & (order[None, :] < order[:, None])
    rank = jnp.sum(earlier.astype(jnp.int32), axis=1)
    return (owner_ids[None, :] == lax.axis_index("dp")) & (
        rank[None, :] == jnp.arange(CAP, dtype=jnp.int32)[:, None]
    )


def pick_slots(owners, total):
    wanted = slot_ranks(owners)
    return jnp.sum(jnp.where(wanted[:, :, None, None], total[None], 0.0), axis=1)[None]


def tie(value, *after):
    return lax.optimization_barrier((value,) + after)[0]


def piece_sizes(half, bs):
    blocks = half // bs
    last = max(blocks // 7, 1)
    sizes = []
    for left in (3, 2, 1):
        take = -(-(blocks - last - sum(sizes)) // left)
        sizes.append(take)
    return [s * bs for s in sizes + [last]]


def gather_line(shards):
    pairs = [(0, 1), (1, 0), (2, 3), (3, 2)]
    middle = [(1, 2), (2, 1)]
    outward = [(1, 0), (2, 3)]
    flights = []
    centre = []
    out = []

    def outer(value, route):
        if len(flights) >= 2:
            value = tie(value, flights[-2])
        got = lax.ppermute(value, "dp", route)
        flights.append(got)
        return got

    def inner(value):
        if len(centre) >= 2:
            value = tie(value, centre[-2])
        got = lax.ppermute(value, "dp", middle)
        centre.append(got)
        return got

    for shard in shards:
        a = outer(shard, pairs)
        b = inner(shard)
        c = inner(a)
        e = outer(b, outward)
        f = outer(c, outward)
        out.append(jnp.stack([shard, a, c + e, b + f]))
    return out


def local(tokens, frozen, delta, block_rows, block_cols, owners, d_out):
    group, me_dp, me_t = (lax.axis_index(a) for a in ("groups", "dp", "tensor"))
    n_dp = lax.axis_size("dp")
    rows, feats = tokens.shape
    blocks, bs = delta.shape[0], delta.shape[1]
    slab = frozen.shape[1]
    half = slab // 2
    mine, theirs = group * half, (1 - group) * half
    sizes = piece_sizes(half, bs)
    firsts = [sum(sizes[:p]) for p in range(len(sizes))]
    cols_here = block_cols * bs - me_t * slab - mine
    row_part = block_rows * bs // feats
    block_info = jnp.stack(
        [row_part ^ me_t, row_part ^ me_dp, block_rows * bs % feats, cols_here], axis=1
    ).reshape(-1)

    def meta_of(slot):
        head = [me_dp ^ me_t ^ s for s in range(4)] + [slot] + [jnp.int32(0)] * 3
        return jnp.concatenate([jnp.stack(head), block_info]).astype(jnp.int32)

    shards = [
        lax.dynamic_slice(frozen, (0, mine + first), (frozen.shape[0], size))
        for first, size in zip(firsts, sizes)
    ]
    gathered = gather_line(shards)

    peer = swap(tokens, "groups", 1)
    own_x = swap(tokens, "tensor", 2)
    peer_x = swap(peer, "tensor", 2)
    near_x = jnp.concatenate([tokens, peer], axis=0)
    far_x = jnp.concatenate([own_x, peer_x], axis=0)
    x4 = jnp.stack([near_x, swap(near_x, "tensor", 1), far_x, swap(far_x, "tensor", 1)])

    order = peer_x
    d_pieces = []
    for first, size in zip(firsts, sizes):
        give = lax.dynamic_slice(d_out, (0, theirs + first), (rows, size))
        keep = lax.dynamic_slice(d_out, (0, mine + first), (rows, size))
        got = swap(tie(give, order), "groups", 1)
        order = got
        d_pieces.append(jnp.concatenate([keep, got], axis=0))

    activated = jnp.zeros((rows, slab), BF)
    slopes = []
    meta = meta_of(jnp.int32(0))
    early = None
    for p, (first, size) in enumerate(zip(firsts, sizes)):
        if p == 3:
            meta = tie(meta, early)
        act, slope = forward(meta, x4, gathered[p], delta, d_pieces[p], first, 2)
        slopes.append(slope)
        back = swap(act[1], "groups", 1)
        activated = lax.dynamic_update_slice(activated, act[0], (0, mine + first))
        activated = lax.dynamic_update_slice(activated, back, (0, theirs + first))
        if p == 1:
            (early,) = backward(meta, slopes, gathered[:2], delta, firsts[:2], None, None)

    def back_of(bit, out_type, *wait):
        m = meta_of(me_t ^ bit ^ me_dp)
        if wait:
            m = tie(m, *wait)
        return backward(m, slopes[2:], gathered[2:], delta, firsts[2:], early, out_type)

    far_own_give, far_peer_give = back_of(3, BF)
    far_peer_got = swap(far_peer_give, "tensor", 1)
    far_own_got = swap(far_own_give, "tensor", 1)
    far_own, far_peer = back_of(2, F32, far_peer_give)
    near_own_give, near_peer_give = back_of(1, BF, far_own)
    near_peer_got = swap(near_peer_give, "tensor", 1)
    near_own_got = swap(near_own_give, "tensor", 1)
    near_own, near_peer = back_of(0, F32, near_peer_give)
    cut = rows // 2
    far_peer = (far_peer + far_peer_got.astype(F32)).astype(BF)
    over_x = swap(far_peer[:cut], "tensor", 2).astype(F32)
    over_y = swap(far_peer[cut:], "groups", 1).astype(F32)
    far_own = far_own + far_own_got.astype(F32)
    far_own = jnp.concatenate([far_own[:cut], far_own[cut:] + over_y], axis=0).astype(BF)
    from_x = swap(far_own, "tensor", 2)
    near_peer = near_peer + near_peer_got.astype(F32)
    near_peer = jnp.concatenate([near_peer[:cut] + over_x, near_peer[cut:]], axis=0).astype(BF)
    from_y = swap(near_peer, "groups", 1)
    near_own = near_own + near_own_got.astype(F32)
    d_tokens = (near_own + from_x.astype(F32) + from_y.astype(F32)).astype(BF)

    last_slope = tie(slopes[-1], near_own)
    grads = []
    for n in range(blocks):
        dy = jnp.zeros((2 * rows, bs), BF)
        for first, size, slope in zip(firsts, sizes, slopes[:-1] + [last_slope]):
            col = cols_here[n] - first
            cut_out = lax.dynamic_slice(slope, (0, jnp.clip(col, 0, size - bs)), (2 * rows, bs))
            dy = jnp.where((col >= 0) & (col < size), cut_out, dy)
        xb = lax.dynamic_slice(
            x4, (row_part[n] ^ me_t, 0, block_rows[n] * bs % feats), (1, 2 * rows, bs)
        )
        xb, dy = xb.reshape(2, rows, bs), dy.reshape(2, rows, bs)
        grads.append(jnp.einsum("gtk,gtc->gkc", xb, dy, preferred_element_type=F32))
    grads = jnp.stack(grads, axis=1)
    grads = grads[0] + swap(grads[1].astype(BF), "groups", 1).astype(F32)
    bit = 1
    while bit < n_dp:
        grads = grads + swap(grads.astype(BF), "dp", bit).astype(F32)
        bit *= 2
    norm = float(rows * n_dp) ** (-0.5)
    return (activated, d_tokens, pick_slots(owners, grads * norm))


def local_any(tokens, frozen, delta, block_rows, block_cols, owners, d_out):
    me_dp, me_t, n_dp = lax.axis_index("dp"), lax.axis_index("tensor"), lax.axis_size("dp")
    rows = tokens.shape[0]
    blocks, bs = delta.shape[0], delta.shape[1]
    slab = frozen.shape[1]
    x_full = lax.all_gather(tokens, "tensor", axis=1, tiled=True)
    weight = lax.all_gather(frozen, "dp", axis=0, tiled=True)
    width = x_full.shape[1]
    row_pick = (block_rows[:, None] == jnp.arange(width // bs)[None, :]).astype(F32)
    cols_here = block_cols - me_t * (slab // bs)
    col_pick = (cols_here[:, None] == jnp.arange(slab // bs)[None, :]).astype(F32)
    highest = lax.Precision.HIGHEST
    xb = jnp.take(x_full.reshape(rows, width // bs, bs), block_rows, axis=1)
    contrib = jnp.einsum("tnk,nkc->tnc", xb, delta, preferred_element_type=F32)
    add = jnp.einsum("tnc,nm->tmc", contrib, col_pick, precision=highest).reshape(rows, slab)
    preact = jnp.dot(x_full, weight, preferred_element_type=F32) + add
    squash = jax.nn.sigmoid(preact)
    activated = (preact * squash).astype(BF)
    d_pre = (d_out.astype(F32) * squash * (1.0 + preact * (1.0 - squash))).astype(BF)
    d_rows = lax.dot_general(
        d_pre, weight, (((1,), (1,)), ((), ())), preferred_element_type=F32
    )
    dy = jnp.take(d_pre.reshape(rows, slab // bs, bs), cols_here, axis=1)
    back = jnp.einsum("tnc,nkc->tnk", dy, delta, preferred_element_type=F32)
    back = jnp.einsum("tnk,nr->trk", back, row_pick, precision=highest).reshape(rows, width)
    d_tokens = lax.psum_scatter(
        (d_rows + back).astype(BF), "tensor", scatter_dimension=1, tiled=True
    )
    grads = jnp.einsum("tnk,tnc->nkc", xb, dy, preferred_element_type=F32)
    everyone = lax.all_gather(grads.astype(BF), "dp", axis=0).astype(F32)
    norm = float(rows * n_dp) ** (-0.5)
    return (activated, d_tokens, pick_slots(owners, jnp.sum(everyone, axis=0) * norm))


def solution(mesh):
    sizes = dict(mesh.shape)
    small = sizes["groups"] == 2 and sizes["dp"] == 4 and sizes["tensor"] == 4
    body = local if small else local_any
    in_specs = (
        P(("groups", "dp"), "tensor"),
        P("dp", "tensor"),
        P("tensor", None, None),
        P("tensor"),
        P("tensor"),
        P("tensor", None),
        P(("groups", "dp"), "tensor"),
    )
    out_specs = (
        P(("groups", "dp"), "tensor"),
        P(("groups", "dp"), "tensor"),
        P("tensor", ("groups", "dp"), None, None),
    )
    return jax.shard_map(body, mesh=mesh, in_specs=in_specs, out_specs=out_specs, check_vma=False)
```

time: 430 us -> 413 us (0.960)
  waiting for transfers between devices: 248 us -> 182 us
  starting transfers between devices: 20.6 us -> 45.6 us
  other arithmetic: 20.5 us -> 41.1 us
  between operations: 29.1 us -> 21 us
  local copies, waits for them, and re-layouts: 31.5 us -> 37.9 us
  Pallas kernels: 77.3 us -> 82.8 us
    all_gather x3 -> x0, waiting for transfers between devices: 159 us -> none  [local(): gathered.append(lax.all_gather(shard, 'dp', axis=0, tiled=True))]
    ppermute x0 -> x20, waiting for transfers between devices: none -> 113 us  [the longest x12 113 us: outer(): got = lax.ppermute(value, 'dp', route)]
    another operation x5 -> x19, other arithmetic: 0.25 us -> 26.7 us  [the longest x12 19.8 us: gather_line(): out.append(jnp.stack([shard, a, c + e, b + f]))]
    ppermute x0 -> x20, starting transfers between devices: none -> 24.2 us  [the longest x12 13.6 us: outer(): got = lax.ppermute(value, 'dp', route)]
    ppermute x20 -> x24, waiting for transfers between devices: 89.1 us -> 68.7 us  [swap(): return lax.ppermute(array, axis, [(i, i ^ bit) for i in range(size)])]
    select_n x4 -> x0, other arithmetic: 7.36 us -> none  [local(): xb = jnp.where((off >= 0) & (off < feats), cut_out, xb)]
    pallas_call x7 -> x9, Pallas kernels: 77.3 us -> 82.8 us  [the longest x5 43.3 us: backward(): pl.pallas_call(functools.partial(backward_kernel, firsts, blocks, bs, acc...]
    dynamic_slice x3, local copies, waits for them, and re-layouts: 2.57 us -> 6.94 us  [local(): keep = lax.dynamic_slice(d_out, (0, mine + first), (rows, size))]
  transfers between devices with their start and end apart: 23 -> 44, of which waited for: 11 -> 18; matrix products, arithmetic and copies ran while one was open for 11% -> 18% of each run, Pallas kernels for 18% -> 17%
where the time goes in v3:
time: 413 us; the launch traced here: 411 us
  waiting for transfers between devices  182 us (44%)
  Pallas kernels  82.8 us (20%)
  starting transfers between devices  45.6 us (11%)
  other arithmetic  41.1 us (10%)
  local copies, waits for them, and re-layouts  37.9 us (9%)
  between operations  21 us (5%)
    ppermute x12, waiting for transfers between devices, outer(): got = lax.ppermute(value, 'dp', route)  113 us
    ppermute x24, waiting for transfers between devices, swap(): return lax.ppermute(array, axis, [(i, i ^ bit) for i in range(size)])  68.7 us
    pallas_call x5, Pallas kernels, backward(): pl.pallas_call(functools.partial(backward_kernel, firsts, blocks, bs, acc...  43.3 us
    pallas_call x4, Pallas kernels, forward(): pl.pallas_call(functools.partial(forward_kernel, first, blocks, bs), grid...  39.5 us
    ppermute x24, starting transfers between devices, swap(): return lax.ppermute(array, axis, [(i, i ^ bit) for i in range(size)])  21.4 us
    another operation x12, other arithmetic, gather_line(): out.append(jnp.stack([shard, a, c + e, b + f]))  19.8 us
    ppermute x12, starting transfers between devices, outer(): got = lax.ppermute(value, 'dp', route)  13.6 us
    ppermute x8, starting transfers between devices, inner(): got = lax.ppermute(value, 'dp', middle)  10.6 us
  transfers between devices with their start and end apart: 44, of which 18 were waited for; matrix products, arithmetic and copies ran while one was open for 18% of the time, Pallas kernels for 17%

profile of v3, /device:TPU:0, one launch (start us, length us, event | category | flops | bytes accessed | tf_op | source)
XLA Modules:
  0.0 411.4 jit_solution(17798513863313108676)
XLA Ops:
  0.6 2.5 constant_dynamic-slice_fusion.15
  4.9 3.0 collective-permute-start
  7.9 3.3 collective-permute-start.5
  12.7 2.7 constant_dynamic-slice_fusion.8
  16.9 11.7 %collective-permute-done = bf16[448,1024]{1,0:T(8,128)(2,1)} collective-permute-done((bf16[448,1024]{1,0:T(8,128)(2,1)}, bf16[448,1024]{1,0:T(8,128)(2,1)}, u32[]{:S(2)}, u32[]{:S(2)}) %collective-permute-start) | collective-permute-done | bytes 917536 | tf_op jit(solution)/shard_map/ppermute | solution.py:18
  39.9 12.6 %collective-permute-done.3 = bf16[448,1024]{1,0:T(8,128)(2,1)} collective-permute-done((bf16[448,1024]{1,0:T(8,128)(2,1)}, bf16[448,1024]{1,0:T(8,128)(2,1)}, u32[]{:S(2)}, u32[]{:S(2)}) %collective-permute-start.3) | collective-permute-done | bytes 917536 | tf_op jit(solution)/shard_map/ppermute | solution.py:18
  58.4 9.8 %collective-permute-done.8 = bf16[1024,640]{1,0:T(8,128)(2,1)S(1)} collective-permute-done((bf16[1024,640]{1,0:T(8,128)(2,1)}, bf16[1024,640]{1,0:T(8,128)(2,1)S(1)}, u32[]{:S(2)}, u32[]{:S(2)}) %collective-permute-start.8) | collective-permute-done | bytes 1310752 | tf_op jit(solution)/shard_map/ppermute | solution.py:206
  118.8 40.0 %collective-permute-done.9 = bf16[1024,640]{1,0:T(8,128)(2,1)} collective-permute-done((bf16[1024,640]{1,0:T(8,128)(2,1)}, bf16[1024,640]{1,0:T(8,128)(2,1)}, u32[]{:S(2)}, u32[]{:S(2)}) %collective-permute-start.9) | collective-permute-done | bytes 1310752 | tf_op jit(solution)/shard_map/ppermute | solution.py:206
  163.7 6.6 %pad_maximum_fusion.x_ref = bf16[4,896,1024]{2,1,0:T(8,128)(2,1)} fusion(bf16[1,896,1024]{2,1,0:T(8,128)(2,1)} %bitcast.11, bf16[1,896,1024]{2,1,0:T(8,128)(2,1)} %bitcast.10, bf16[1,896,1024]{2,1,0:T(8,128)(2,1)} %bitcast.9, bf16[1,896,1024]{2,1,0:T(8,128)(2,1)} %bitcast.8), kind=kLoop, calls=%fused_computation | loop fusion | flops 11010048 | bytes 14680064 | tf_op jit(solution)/shard_map/stack | solution.py:258
  170.3 18.2 %collective-permute-done.15 = bf16[1024,512]{1,0:T(8,128)(2,1)S(1)} collective-permute-done((bf16[1024,512]{1,0:T(8,128)(2,1)}, bf16[1024,512]{1,0:T(8,128)(2,1)S(1)}, u32[]{:S(2)}, u32[]{:S(2)}) %collective-permute-start.15) | collective-permute-done | bytes 1048608 | tf_op jit(solution)/shard_map/ppermute | solution.py:206
  190.3 20.6 %collective-permute-done.16 = bf16[1024,512]{1,0:T(8,128)(2,1)S(1)} collective-permute-done((bf16[1024,512]{1,0:T(8,128)(2,1)S(1)}, bf16[1024,512]{1,0:T(8,128)(2,1)S(1)}, u32[]{:S(2)}, u32[]{:S(2)}) %collective-permute-start.16) | collective-permute-done | bytes 1048608 | tf_op jit(solution)/shard_map/ppermute | solution.py:206
  213.2 4.1 pad_maximum_fusion.1.w_ref.refs_2_
  217.2 12.7 %shard_map.94 = (bf16[2,448,640]{2,1,0:T(8,128)(2,1)}, bf16[896,640]{1,0:T(8,128)(2,1)}) custom-call(s32[24]{0:T(128)} %concatenate.41.meta, bf16[4,896,1024]{2,1,0:T(8,128)(2,1)} %pad_maximum_fusion.x_ref, bf16[4,1024,640]{2,1,0:T(8,128)(2,1)} %pad_maximum_fusion.1.w_ref.refs_2_, bf16[4,128,128]{2,1,0:T(8,128)(2,1)} %refs_4_.9, ...), custom_call_target="tpu_custom_call" | custom-call | flops 4697620480 | bytes 12582912 | tf_op jit(solution)/shard_map/pallas_call | solution.py:55
  229.9 3.6 collective-permute-done.19
  235.7 17.2 %collective-permute-done.22 = bf16[1024,512]{1,0:T(8,128)(2,1)S(1)} collective-permute-done((bf16[1024,512]{1,0:T(8,128)(2,1)}, bf16[1024,512]{1,0:T(8,128)(2,1)S(1)}, u32[]{:S(2)}, u32[]{:S(2)}) %collective-permute-start.22) | collective-permute-done | bytes 1048608 | tf_op jit(solution)/shard_map/ppermute | solution.py:206
  252.9 3.3 pad_maximum_fusion.2.w_ref.refs_3_
  256.2 9.8 %shard_map.95 = (bf16[2,448,512]{2,1,0:T(8,128)(2,1)}, bf16[896,512]{1,0:T(8,128)(2,1)}) custom-call(s32[24]{0:T(128)} %concatenate.41.meta, bf16[4,896,1024]{2,1,0:T(8,128)(2,1)} %pad_maximum_fusion.x_ref, bf16[4,1024,512]{2,1,0:T(8,128)(2,1)} %pad_maximum_fusion.2.w_ref.refs_3_, bf16[4,128,128]{2,1,0:T(8,128)(2,1)} %refs_4_.9, ...), custom_call_target="tpu_custom_call" | custom-call | flops 3758096384 | bytes 11534336 | tf_op jit(solution)/shard_map/pallas_call | solution.py:55
  268.2 17.9 %shard_map.97.refs_5_ = f32[4,896,1024]{2,1,0:T(8,128)} custom-call(s32[24]{0:T(128)} %concatenate.41.meta, bf16[896,640]{1,0:T(8,128)(2,1)} %get-tuple-element.61.refs_0_, bf16[896,512]{1,0:T(8,128)(2,1)} %get-tuple-element.62.refs_1_, bf16[4,1024,640]{2,1,0:T(8,128)(2,1)} %pad_maximum_fusion.1.w_ref.refs_2_, ...), custom_call_target="tpu_custom_call" | custom-call | flops 8455716864 | bytes 17694720 | tf_op jit(solution)/shard_map/pallas_call | solution.py:139
  290.2 3.3 pad_maximum_fusion.3.w_ref.refs_2_
  293.5 10.2 %shard_map.96 = (bf16[2,448,512]{2,1,0:T(8,128)(2,1)}, bf16[896,512]{1,0:T(8,128)(2,1)}) custom-call(s32[24]{0:T(128)} %concatenate.41.meta, bf16[4,896,1024]{2,1,0:T(8,128)(2,1)} %pad_maximum_fusion.x_ref, bf16[4,1024,512]{2,1,0:T(8,128)(2,1)} %pad_maximum_fusion.3.w_ref.refs_2_, bf16[4,128,128]{2,1,0:T(8,128)(2,1)} %refs_4_.9, ...), custom_call_target="tpu_custom_call" | custom-call | flops 3758096384 | bytes 11534336 | tf_op jit(solution)/shard_map/pallas_call | solution.py:55
  304.8 3.9 collective-permute-done.29
  310.4 6.8 %shard_map.98 = (bf16[2,448,256]{2,1,0:T(8,128)(2,1)}, bf16[896,256]{1,0:T(8,128)(2,1)}) custom-call(s32[24]{0:T(128)} %concatenate.41.meta, bf16[4,896,1024]{2,1,0:T(8,128)(2,1)} %pad_maximum_fusion.x_ref, bf16[4,1024,256]{2,1,0:T(8,128)(2,1)} %pad_maximum_fusion.4.w_ref.refs_3_, bf16[4,128,128]{2,1,0:T(8,128)(2,1)} %refs_4_.9, ...), custom_call_target="tpu_custom_call" | custom-call | flops 1879048192 | bytes 9437184 | tf_op jit(solution)/shard_map/pallas_call | solution.py:55
  317.2 6.2 %shard_map.99 = (bf16[448,1024]{1,0:T(8,128)(2,1)}, bf16[448,1024]{1,0:T(8,128)(2,1)}) custom-call(s32[24]{0:T(128)} %concatenate.51.meta, bf16[896,512]{1,0:T(8,128)(2,1)} %get-tuple-element.71.refs_0_, bf16[896,256]{1,0:T(8,128)(2,1)} %get-tuple-element.84.refs_1_, bf16[4,1024,512]{2,1,0:T(8,128)(2,1)} %pad_maximum_fusion.3.w_ref.refs_2_, ...), custom_call_target="tpu_custom_call" | custom-call | flops 1409286144 | bytes 2949120 | tf_op jit(solution)/shard_map/pallas_call | solution.py:139
  328.4 6.7 %shard_map.100 = (f32[448,1024]{1,0:T(8,128)}, f32[448,1024]{1,0:T(8,128)}) custom-call(s32[24]{0:T(128)} %concatenate.50.meta, bf16[896,512]{1,0:T(8,128)(2,1)} %get-tuple-element.71.refs_0_, bf16[896,256]{1,0:T(8,128)(2,1)} %get-tuple-element.84.refs_1_, bf16[4,1024,512]{2,1,0:T(8,128)(2,1)} %pad_maximum_fusion.3.w_ref.refs_2_, ...), custom_call_target="tpu_custom_call" | custom-call | flops 1409286144 | bytes 2949120 | tf_op jit(solution)/shard_map/pallas_call | solution.py:139
  335.1 6.0 %shard_map.101 = (bf16[448,1024]{1,0:T(8,128)(2,1)}, bf16[448,1024]{1,0:T(8,128)(2,1)}) custom-call(s32[24]{0:T(128)} %concatenate.49.meta, bf16[896,512]{1,0:T(8,128)(2,1)} %get-tuple-element.71.refs_0_, bf16[896,256]{1,0:T(8,128)(2,1)} %get-tuple-element.84.refs_1_, bf16[4,1024,512]{2,1,0:T(8,128)(2,1)} %pad_maximum_fusion.3.w_ref.refs_2_, ...), custom_call_target="tpu_custom_call" | custom-call | flops 1409286144 | bytes 2949120 | tf_op jit(solution)/shard_map/pallas_call | solution.py:139
  341.6 6.5 %shard_map.102 = (f32[448,1024]{1,0:T(8,128)}, f32[448,1024]{1,0:T(8,128)}) custom-call(s32[24]{0:T(128)} %concatenate.48.meta, bf16[896,512]{1,0:T(8,128)(2,1)} %get-tuple-element.71.refs_0_, bf16[896,256]{1,0:T(8,128)(2,1)} %get-tuple-element.84.refs_1_, bf16[4,1024,512]{2,1,0:T(8,128)(2,1)} %pad_maximum_fusion.3.w_ref.refs_2_, ...), custom_call_target="tpu_custom_call" | custom-call | flops 1409286144 | bytes 2949120 | tf_op jit(solution)/shard_map/pallas_call | solution.py:139
  353.4 8.2 %collective-permute-done.36 = bf16[224,1024]{1,0:T(8,128)(2,1)S(1)} collective-permute-done((bf16[224,1024]{1,0:T(8,128)(2,1)S(1)}, bf16[224,1024]{1,0:T(8,128)(2,1)S(1)}, u32[]{:S(2)}, u32[]{:S(2)}) %collective-permute-start.36) | collective-permute-done | bytes 458784 | tf_op jit(solution)/shard_map/ppermute | solution.py:18
  367.6 16.2 %collective-permute-done.37 = bf16[448,1024]{1,0:T(8,128)(2,1)S(1)} collective-permute-done((bf16[448,1024]{1,0:T(8,128)(2,1)S(1)}, bf16[448,1024]{1,0:T(8,128)(2,1)S(1)}, u32[]{:S(2)}, u32[]{:S(2)}) %collective-permute-start.37) | collective-permute-done | bytes 917536 | tf_op jit(solution)/shard_map/ppermute | solution.py:18
  383.9 3.1 collective-permute-done.40
  393.1 3.7 collective-permute-done.25
  399.8 3.6 collective-permute-done.42
  405.1 5.5 %collective-permute-done.43 = bf16[4,128,128]{2,1,0:T(8,128)(2,1)S(1)} collective-permute-done((bf16[4,128,128]{2,1,0:T(8,128)(2,1)S(1)}, bf16[4,128,128]{2,1,0:T(8,128)(2,1)S(1)}, u32[]{:S(2)}, u32[]{:S(2)}) %collective-permute-start.43) | collective-permute-done | bytes 131104 | tf_op jit(solution)/shard_map/ppermute | solution.py:18
  (209 shorter events, 101.0 us)
Async XLA Ops:
  3.1 29.5 %collective-permute-start.7 = (bf16[1024,640]{1,0:T(8,128)(2,1)}, bf16[1024,640]{1,0:T(8,128)(2,1)}, u32[]{:S(2)}, u32[]{:S(2)}) collective-permute-start(bf16[1024,640]{1,0:T(8,128)(2,1)} %constant_dynamic-slice_fusion.15), channel_id=1, source_target_pairs={{4,8},{8,4},{5,9},{9,5},{6,10},{10,6},{7,11},{11,7},{20,24},{24,20... | collective-permute-start | bytes 3932168 | tf_op jit(solution)/shard_map/ppermute | solution.py:213
  4.9 23.6 %collective-permute-start = (bf16[448,1024]{1,0:T(8,128)(2,1)}, bf16[448,1024]{1,0:T(8,128)(2,1)}, u32[]{:S(2)}, u32[]{:S(2)}) collective-permute-start(bf16[448,1024]{1,0:T(8,128)(2,1)} %param.7), channel_id=1, source_target_pairs={{0,16},{16,0},{1,17},{17,1},{2,18},{18,2},{3,19},{19,3},{4,20},{20... | collective-permute-start | bytes 2752520 | tf_op jit(solution)/shard_map/ppermute | solution.py:18
  7.9 45.1 %collective-permute-start.5 = (bf16[1024,640]{1,0:T(8,128)(2,1)}, bf16[1024,640]{1,0:T(8,128)(2,1)}, u32[]{:S(2)}, u32[]{:S(2)}) collective-permute-start(bf16[1024,640]{1,0:T(8,128)(2,1)} %constant_dynamic-slice_fusion.15), channel_id=1, source_target_pairs={{0,4},{4,0},{8,12},{12,8},{1,5},{5,1},{9,13},{13,9},{2,6},{6,2},{1... | collective-permute-start | bytes 3932168 | tf_op jit(solution)/shard_map/ppermute | solution.py:206
  11.2 62.2 %collective-permute-start.2 = (bf16[448,1024]{1,0:T(8,128)(2,1)}, bf16[448,1024]{1,0:T(8,128)(2,1)}, u32[]{:S(2)}, u32[]{:S(2)}) collective-permute-start(bf16[448,1024]{1,0:T(8,128)(2,1)} %param.7), channel_id=1, source_target_pairs={{0,2},{1,3},{2,0},{3,1},{4,6},{5,7},{6,4},{7,5},{8,10},{9,11},{10,... | collective-permute-start | bytes 2752520 | tf_op jit(solution)/shard_map/ppermute | solution.py:18
  28.6 23.9 %collective-permute-start.3 = (bf16[448,1024]{1,0:T(8,128)(2,1)}, bf16[448,1024]{1,0:T(8,128)(2,1)}, u32[]{:S(2)}, u32[]{:S(2)}) collective-permute-start(bf16[448,1024]{1,0:T(8,128)(2,1)} %collective-permute-done), channel_id=1, source_target_pairs={{0,2},{1,3},{2,0},{3,1},{4,6},{5,7},{6,4},{7,5},{8,10},{9,11},{10,... | collective-permute-start | bytes 2752520 | tf_op jit(solution)/shard_map/ppermute | solution.py:18
  32.6 35.6 %collective-permute-start.8 = (bf16[1024,640]{1,0:T(8,128)(2,1)}, bf16[1024,640]{1,0:T(8,128)(2,1)S(1)}, u32[]{:S(2)}, u32[]{:S(2)}) collective-permute-start(bf16[1024,640]{1,0:T(8,128)(2,1)} %collective-permute-done.7), channel_id=1, source_target_pairs={{4,0},{8,12},{5,1},{9,13},{6,2},{10,14},{7,3},{11,15},{20,16},{24,... | collective-permute-start | bytes 3932168 | tf_op jit(solution)/shard_map/ppermute | solution.py:206
  53.0 32.1 %collective-permute-start.6 = (bf16[1024,640]{1,0:T(8,128)(2,1)}, bf16[1024,640]{1,0:T(8,128)(2,1)}, u32[]{:S(2)}, u32[]{:S(2)}) collective-permute-start(bf16[1024,640]{1,0:T(8,128)(2,1)} %collective-permute-done.5), channel_id=1, source_target_pairs={{4,8},{8,4},{5,9},{9,5},{6,10},{10,6},{7,11},{11,7},{20,24},{24,20... | collective-permute-start | bytes 3932168 | tf_op jit(solution)/shard_map/ppermute | solution.py:213
  56.6 26.9 %collective-permute-start.14 = (bf16[1024,512]{1,0:T(8,128)(2,1)S(1)}, bf16[1024,512]{1,0:T(8,128)(2,1)}, u32[]{:S(2)}, u32[]{:S(2)}) collective-permute-start(bf16[1024,512]{1,0:T(8,128)(2,1)S(1)} %get-tuple-element.47), channel_id=1, source_target_pairs={{4,8},{8,4},{5,9},{9,5},{6,10},{10,6},{7,11},{11,7},{20,24},{24,20... | collective-permute-start | bytes 3145736 | tf_op jit(solution)/shard_map/ppermute | solution.py:213
  68.2 38.6 %collective-permute-start.12 = (bf16[1024,512]{1,0:T(8,128)(2,1)S(1)}, bf16[1024,512]{1,0:T(8,128)(2,1)}, u32[]{:S(2)}, u32[]{:S(2)}) collective-permute-start(bf16[1024,512]{1,0:T(8,128)(2,1)S(1)} %get-tuple-element.47), channel_id=1, source_target_pairs={{0,4},{4,0},{8,12},{12,8},{1,5},{5,1},{9,13},{13,9},{2,6},{6,2},{1... | collective-permute-start | bytes 3145736 | tf_op jit(solution)/shard_map/ppermute | solution.py:206
  73.5 90.2 %collective-permute-start.1 = (bf16[896,1024]{1,0:T(8,128)(2,1)}, bf16[896,1024]{1,0:T(8,128)(2,1)}, u32[]{:S(2)}, u32[]{:S(2)}) collective-permute-start(bf16[896,1024]{1,0:T(8,128)(2,1)} %constant_dynamic-update-slice_fusion), channel_id=1, source_target_pairs={{0,1},{1,0},{2,3},{3,2},{4,5},{5,4},{6,7},{7,6},{8,9},{9,8},{10,11... | collective-permute-start | bytes 5505032 | tf_op jit(solution)/shard_map/ppermute | solution.py:18
  80.0 83.7 %collective-permute-start.4 = (bf16[896,1024]{1,0:T(8,128)(2,1)}, bf16[896,1024]{1,0:T(8,128)(2,1)}, u32[]{:S(2)}, u32[]{:S(2)}) collective-permute-start(bf16[896,1024]{1,0:T(8,128)(2,1)} %constant_dynamic-update-slice_fusion.2), channel_id=1, source_target_pairs={{0,1},{1,0},{2,3},{3,2},{4,5},{5,4},{6,7},{7,6},{8,9},{9,8},{10,11... | collective-permute-start | bytes 5505032 | tf_op jit(solution)/shard_map/ppermute | solution.py:18
  83.5 26.0 %collective-permute-start.24 = (bf16[448,512]{1,0:T(8,128)(2,1)}, bf16[448,512]{1,0:T(8,128)(2,1)}, u32[]{:S(2)}, u32[]{:S(2)}) collective-permute-start(bf16[448,512]{1,0:T(8,128)(2,1)} %get-tuple-element.59), channel_id=1, source_target_pairs={{0,16},{16,0},{1,17},{17,1},{2,18},{18,2},{3,19},{19,3},{4,20},{20... | collective-permute-start | bytes 1376264 | tf_op jit(solution)/shard_map/ppermute | solution.py:18
  85.1 29.1 %collective-permute-start.21 = (bf16[1024,512]{1,0:T(8,128)(2,1)S(1)}, bf16[1024,512]{1,0:T(8,128)(2,1)}, u32[]{:S(2)}, u32[]{:S(2)}) collective-permute-start(bf16[1024,512]{1,0:T(8,128)(2,1)S(1)} %get-tuple-element.54), channel_id=1, source_target_pairs={{4,8},{8,4},{5,9},{9,5},{6,10},{10,6},{7,11},{11,7},{20,24},{24,20... | collective-permute-start | bytes 3145736 | tf_op jit(solution)/shard_map/ppermute | solution.py:213
  106.8 51.9 %collective-permute-start.9 = (bf16[1024,640]{1,0:T(8,128)(2,1)}, bf16[1024,640]{1,0:T(8,128)(2,1)}, u32[]{:S(2)}, u32[]{:S(2)}) collective-permute-start(bf16[1024,640]{1,0:T(8,128)(2,1)} %collective-permute-done.6), channel_id=1, source_target_pairs={{4,0},{8,12},{5,1},{9,13},{6,2},{10,14},{7,3},{11,15},{20,16},{24,... | collective-permute-start | bytes 3932168 | tf_op jit(solution)/shard_map/ppermute | solution.py:206
  109.5 52.9 %collective-permute-start.13 = (bf16[1024,512]{1,0:T(8,128)(2,1)}, bf16[1024,512]{1,0:T(8,128)(2,1)S(1)}, u32[]{:S(2)}, u32[]{:S(2)}) collective-permute-start(bf16[1024,512]{1,0:T(8,128)(2,1)} %collective-permute-done.12), channel_id=1, source_target_pairs={{4,8},{8,4},{5,9},{9,5},{6,10},{10,6},{7,11},{11,7},{20,24},{24,20... | collective-permute-start | bytes 3145736 | tf_op jit(solution)/shard_map/ppermute | solution.py:213
  114.2 46.1 %collective-permute-start.31 = (bf16[448,256]{1,0:T(8,128)(2,1)S(1)}, bf16[448,256]{1,0:T(8,128)(2,1)S(1)}, u32[]{:S(2)}, u32[]{:S(2)}) collective-permute-start(bf16[448,256]{1,0:T(8,128)(2,1)S(1)} %copy-done.24), channel_id=1, source_target_pairs={{0,16},{16,0},{1,17},{17,1},{2,18},{18,2},{3,19},{19,3},{4,20},{20... | collective-permute-start | bytes 688136 | tf_op jit(solution)/shard_map/ppermute | solution.py:18
  158.8 128.8 %collective-permute-start.28 = (bf16[1024,256]{1,0:T(8,128)(2,1)}, bf16[1024,256]{1,0:T(8,128)(2,1)}, u32[]{:S(2)}, u32[]{:S(2)}) collective-permute-start(bf16[1024,256]{1,0:T(8,128)(2,1)} %constant_dynamic-slice_fusion.6), channel_id=1, source_target_pairs={{4,8},{8,4},{5,9},{9,5},{6,10},{10,6},{7,11},{11,7},{20,24},{24,20... | collective-permute-start | bytes 1572872 | tf_op jit(solution)/shard_map/ppermute | solution.py:213
  160.2 28.2 %collective-permute-start.15 = (bf16[1024,512]{1,0:T(8,128)(2,1)}, bf16[1024,512]{1,0:T(8,128)(2,1)S(1)}, u32[]{:S(2)}, u32[]{:S(2)}) collective-permute-start(bf16[1024,512]{1,0:T(8,128)(2,1)} %collective-permute-done.14), channel_id=1, source_target_pairs={{4,0},{8,12},{5,1},{9,13},{6,2},{10,14},{7,3},{11,15},{20,16},{24,... | collective-permute-start | bytes 3145736 | tf_op jit(solution)/shard_map/ppermute | solution.py:206
  162.4 48.5 %collective-permute-start.16 = (bf16[1024,512]{1,0:T(8,128)(2,1)S(1)}, bf16[1024,512]{1,0:T(8,128)(2,1)S(1)}, u32[]{:S(2)}, u32[]{:S(2)}) collective-permute-start(bf16[1024,512]{1,0:T(8,128)(2,1)S(1)} %collective-permute-done.13), channel_id=1, source_target_pairs={{4,0},{8,12},{5,1},{9,13},{6,2},{10,14},{7,3},{11,15},{20,16},{24,... | collective-permute-start | bytes 3145736 | tf_op jit(solution)/shard_map/ppermute | solution.py:206
  188.4 45.0 %collective-permute-start.19 = (bf16[1024,512]{1,0:T(8,128)(2,1)S(1)}, bf16[1024,512]{1,0:T(8,128)(2,1)}, u32[]{:S(2)}, u32[]{:S(2)}) collective-permute-start(bf16[1024,512]{1,0:T(8,128)(2,1)S(1)} %get-tuple-element.54), channel_id=1, source_target_pairs={{0,4},{4,0},{8,12},{12,8},{1,5},{5,1},{9,13},{13,9},{2,6},{6,2},{1... | collective-permute-start | bytes 3145736 | tf_op jit(solution)/shard_map/ppermute | solution.py:206
  211.9 41.0 %collective-permute-start.22 = (bf16[1024,512]{1,0:T(8,128)(2,1)}, bf16[1024,512]{1,0:T(8,128)(2,1)S(1)}, u32[]{:S(2)}, u32[]{:S(2)}) collective-permute-start(bf16[1024,512]{1,0:T(8,128)(2,1)} %collective-permute-done.21), channel_id=1, source_target_pairs={{4,0},{8,12},{5,1},{9,13},{6,2},{10,14},{7,3},{11,15},{20,16},{24,... | collective-permute-start | bytes 3145736 | tf_op jit(solution)/shard_map/ppermute | solution.py:206
  233.5 32.6 %collective-permute-start.20 = (bf16[1024,512]{1,0:T(8,128)(2,1)}, bf16[1024,512]{1,0:T(8,128)(2,1)S(1)}, u32[]{:S(2)}, u32[]{:S(2)}) collective-permute-start(bf16[1024,512]{1,0:T(8,128)(2,1)} %collective-permute-done.19), channel_id=1, source_target_pairs={{4,8},{8,4},{5,9},{9,5},{6,10},{10,6},{7,11},{11,7},{20,24},{24,20... | collective-permute-start | bytes 3145736 | tf_op jit(solution)/shard_map/ppermute | solution.py:213
  266.0 21.5 %collective-permute-start.23 = (bf16[1024,512]{1,0:T(8,128)(2,1)S(1)}, bf16[1024,512]{1,0:T(8,128)(2,1)S(1)}, u32[]{:S(2)}, u32[]{:S(2)}) collective-permute-start(bf16[1024,512]{1,0:T(8,128)(2,1)S(1)} %collective-permute-done.20), channel_id=1, source_target_pairs={{4,0},{8,12},{5,1},{9,13},{6,2},{10,14},{7,3},{11,15},{20,16},{24,... | collective-permute-start | bytes 3145736 | tf_op jit(solution)/shard_map/ppermute | solution.py:206
  287.6 21.2 %collective-permute-start.29 = (bf16[1024,256]{1,0:T(8,128)(2,1)}, bf16[1024,256]{1,0:T(8,128)(2,1)S(1)}, u32[]{:S(2)}, u32[]{:S(2)}) collective-permute-start(bf16[1024,256]{1,0:T(8,128)(2,1)} %collective-permute-done.28), channel_id=1, source_target_pairs={{4,0},{8,12},{5,1},{9,13},{6,2},{10,14},{7,3},{11,15},{20,16},{24,... | collective-permute-start | bytes 1572872 | tf_op jit(solution)/shard_map/ppermute | solution.py:206
  323.4 24.8 %collective-permute-start.35 = (bf16[448,1024]{1,0:T(8,128)(2,1)}, bf16[448,1024]{1,0:T(8,128)(2,1)S(1)}, u32[]{:S(2)}, u32[]{:S(2)}) collective-permute-start(bf16[448,1024]{1,0:T(8,128)(2,1)} %get-tuple-element.73), channel_id=1, source_target_pairs={{0,1},{1,0},{2,3},{3,2},{4,5},{5,4},{6,7},{7,6},{8,9},{9,8},{10,11... | collective-permute-start | bytes 2752520 | tf_op jit(solution)/shard_map/ppermute | solution.py:18
  326.3 38.2 %collective-permute-start.11 = (bf16[448,640]{1,0:T(8,128)(2,1)}, bf16[448,640]{1,0:T(8,128)(2,1)}, u32[]{:S(2)}, u32[]{:S(2)}) collective-permute-start(bf16[448,640]{1,0:T(8,128)(2,1)} %slice_bitcast_fusion), channel_id=1, source_target_pairs={{0,16},{16,0},{1,17},{17,1},{2,18},{18,2},{3,19},{19,3},{4,20},{20... | collective-permute-start | bytes 1720328 | tf_op jit(solution)/shard_map/ppermute | solution.py:18
  326.5 39.4 %collective-permute-start.18 = (bf16[448,512]{1,0:T(8,128)(2,1)S(1)}, bf16[448,512]{1,0:T(8,128)(2,1)S(1)}, u32[]{:S(2)}, u32[]{:S(2)}) collective-permute-start(bf16[448,512]{1,0:T(8,128)(2,1)S(1)} %slice_bitcast_fusion.2), channel_id=1, source_target_pairs={{0,16},{16,0},{1,17},{17,1},{2,18},{18,2},{3,19},{19,3},{4,20},{20... | collective-permute-start | bytes 1376264 | tf_op jit(solution)/shard_map/ppermute | solution.py:18
  328.4 20.2 %collective-permute-start.34 = (bf16[448,1024]{1,0:T(8,128)(2,1)}, bf16[448,1024]{1,0:T(8,128)(2,1)S(1)}, u32[]{:S(2)}, u32[]{:S(2)}) collective-permute-start(bf16[448,1024]{1,0:T(8,128)(2,1)} %get-tuple-element.81), channel_id=1, source_target_pairs={{0,1},{1,0},{2,3},{3,2},{4,5},{5,4},{6,7},{7,6},{8,9},{9,8},{10,11... | collective-permute-start | bytes 2752520 | tf_op jit(solution)/shard_map/ppermute | solution.py:18
  348.2 19.5 %collective-permute-start.33 = (bf16[448,1024]{1,0:T(8,128)(2,1)}, bf16[448,1024]{1,0:T(8,128)(2,1)S(1)}, u32[]{:S(2)}, u32[]{:S(2)}) collective-permute-start(bf16[448,1024]{1,0:T(8,128)(2,1)} %get-tuple-element.80), channel_id=1, source_target_pairs={{0,1},{1,0},{2,3},{3,2},{4,5},{5,4},{6,7},{7,6},{8,9},{9,8},{10,11... | collective-permute-start | bytes 2752520 | tf_op jit(solution)/shard_map/ppermute | solution.py:18
  361.9 22.0 %collective-permute-start.37 = (bf16[448,1024]{1,0:T(8,128)(2,1)S(1)}, bf16[448,1024]{1,0:T(8,128)(2,1)S(1)}, u32[]{:S(2)}, u32[]{:S(2)}) collective-permute-start(bf16[448,1024]{1,0:T(8,128)(2,1)S(1)} %pad_maximum_fusion.8), channel_id=1, source_target_pairs={{0,2},{1,3},{2,0},{3,1},{4,6},{5,7},{6,4},{7,5},{8,10},{9,11},{10,... | collective-permute-start | bytes 2752520 | tf_op jit(solution)/shard_map/ppermute | solution.py:18
  363.7 23.3 %collective-permute-start.40 = (bf16[448,1024]{1,0:T(8,128)(2,1)S(1)}, bf16[448,1024]{1,0:T(8,128)(2,1)S(1)}, u32[]{:S(2)}, u32[]{:S(2)}) collective-permute-start(bf16[448,1024]{1,0:T(8,128)(2,1)S(1)} %pad_maximum_fusion.9), channel_id=1, source_target_pairs={{0,16},{16,0},{1,17},{17,1},{2,18},{18,2},{3,19},{19,3},{4,20},{20... | collective-permute-start | bytes 2752520 | tf_op jit(solution)/shard_map/ppermute | solution.py:18
  366.0 30.9 %collective-permute-start.25 = (bf16[448,512]{1,0:T(8,128)(2,1)S(1)}, bf16[448,512]{1,0:T(8,128)(2,1)S(1)}, u32[]{:S(2)}, u32[]{:S(2)}) collective-permute-start(bf16[448,512]{1,0:T(8,128)(2,1)S(1)} %slice_bitcast_fusion.1), channel_id=1, source_target_pairs={{0,16},{16,0},{1,17},{17,1},{2,18},{18,2},{3,19},{19,3},{4,20},{20... | collective-permute-start | bytes 1376264 | tf_op jit(solution)/shard_map/ppermute | solution.py:18
  (40 other events, 379.0 us)

commit v4 on v3

--- a/solution.py
+++ b/solution.py
@@ -50,13 +50,14 @@
 def forward(meta, x4, w4, delta, d_piece, first, groups_of):
     rows, width = d_piece.shape
     slots, feats = w4.shape[0], w4.shape[1]
-    tile = rows // groups_of
+    cuts = 2
+    tile = rows // groups_of // cuts
     blocks, bs = delta.shape[0], delta.shape[1]
     return pl.pallas_call(
         functools.partial(forward_kernel, first, blocks, bs),
         grid_spec=pltpu.PrefetchScalarGridSpec(
             num_scalar_prefetch=1,
-            grid=(groups_of,),
+            grid=(groups_of * cuts,),
             in_specs=[
                 pl.BlockSpec((slots, tile, feats), lambda i, m: (0, i, 0)),
                 pl.BlockSpec(w4.shape, lambda i, m: (0, 0, 0), pipeline_mode=pl.Buffered(1)),
@@ -64,13 +65,13 @@
                 pl.BlockSpec((tile, width), lambda i, m: (i, 0)),
             ],
             out_specs=[
-                pl.BlockSpec((1, tile, width), lambda i, m: (i, 0, 0)),
+                pl.BlockSpec((1, tile, width), lambda i, m: (i // cuts, i % cuts, 0)),
                 pl.BlockSpec((tile, width), lambda i, m: (i, 0)),
             ],
             scratch_shapes=[pltpu.VMEM((tile, width), F32)],
         ),
         out_shape=[
-            jax.ShapeDtypeStruct((groups_of, tile, width), BF),
+            jax.ShapeDtypeStruct((groups_of, rows // groups_of, width), BF),
             jax.ShapeDtypeStruct((rows, width), BF),
         ],
         compiler_params=params(),
@@ -119,11 +120,15 @@
         outs[1][...] = acc[cut:].astype(outs[1].dtype)
 
 
+def weight_block(piece, step, tile, meta):
+    return jnp.bitwise_xor(meta[4] + step, meta[5 + piece]), tile, 0
+
+
 def backward(meta, slopes, ws, delta, firsts, acc, out_type):
     rows = slopes[0].shape[0]
     slots, feats = ws[0].shape[0], ws[0].shape[1]
     blocks, bs = delta.shape[0], delta.shape[1]
-    tiles = 2
+    tiles = 4
     size = feats // tiles
     width = sum(s.shape[1] for s in slopes)
     every = out_type is None
@@ -146,7 +151,8 @@
                 for s in slopes
             ]
             + [
-                pl.BlockSpec((1, size, w.shape[2]), lambda s, i, m: (m[4] + s, i, 0)) for w in ws
+                pl.BlockSpec((1, size, w.shape[2]), functools.partial(weight_block, p))
+                for p, w in enumerate(ws)
             ]
             + [pl.BlockSpec(delta.shape, lambda s, i, m: (0, 0, 0))]
             + ([] if acc is None else [whole]),
@@ -182,46 +188,21 @@
     return lax.optimization_barrier((value,) + after)[0]
 
 
+def chain_line(shard):
+    middle = [(1, 2), (2, 1)]
+    outward = [(1, 0), (2, 3)]
+    a = lax.ppermute(shard, "dp", [(0, 1), (1, 0), (2, 3), (3, 2)])
+    b = lax.ppermute(shard, "dp", middle)
+    c = lax.ppermute(a, "dp", middle)
+    e = lax.ppermute(b, "dp", outward)
+    f = lax.ppermute(c, "dp", outward)
+    return jnp.stack([shard, a, c + e, b + f])
+
+
 def piece_sizes(half, bs):
     blocks = half // bs
-    last = max(blocks // 7, 1)
-    sizes = []
-    for left in (3, 2, 1):
-        take = -(-(blocks - last - sum(sizes)) // left)
-        sizes.append(take)
-    return [s * bs for s in sizes + [last]]
-
-
-def gather_line(shards):
-    pairs = [(0, 1), (1, 0), (2, 3), (3, 2)]
-    middle = [(1, 2), (2, 1)]
-    outward = [(1, 0), (2, 3)]
-    flights = []
-    centre = []
-    out = []
-
-    def outer(value, route):
-        if len(flights) >= 2:
-            value = tie(value, flights[-2])
-        got = lax.ppermute(value, "dp", route)
-        flights.append(got)
-        return got
-
-    def inner(value):
-        if len(centre) >= 2:
-            value = tie(value, centre[-2])
-        got = lax.ppermute(value, "dp", middle)
-        centre.append(got)
-        return got
-
-    for shard in shards:
-        a = outer(shard, pairs)
-        b = inner(shard)
-        c = inner(a)
-        e = outer(b, outward)
-        f = outer(c, outward)
-        out.append(jnp.stack([shard, a, c + e, b + f]))
-    return out
+    chain, last = max(blocks // 3, 1), max(blocks // 5, 1)
+    return [chain * bs, (blocks - chain - last) * bs, last * bs]
 
 
 def local(tokens, frozen, delta, block_rows, block_cols, owners, d_out):
@@ -237,18 +218,24 @@
     cols_here = block_cols * bs - me_t * slab - mine
     row_part = block_rows * bs // feats
     block_info = jnp.stack(
-        [row_part ^ me_t, row_part ^ me_dp, block_rows * bs % feats, cols_here], axis=1
+        [row_part ^ me_t, row_part, block_rows * bs % feats, cols_here], axis=1
     ).reshape(-1)
-
-    def meta_of(slot):
-        head = [me_dp ^ me_t ^ s for s in range(4)] + [slot] + [jnp.int32(0)] * 3
+    zero = jnp.int32(0)
+
+    def meta_of(mask, slot, *masks):
+        head = [mask ^ me_t ^ s for s in range(4)] + [slot] + list(masks)
+        head += [zero] * (8 - len(head))
         return jnp.concatenate([jnp.stack(head), block_info]).astype(jnp.int32)
 
-    shards = [
+    chain, first_shard, last_shard = [
         lax.dynamic_slice(frozen, (0, mine + first), (frozen.shape[0], size))
         for first, size in zip(firsts, sizes)
     ]
-    gathered = gather_line(shards)
+    gather_a = lax.all_gather(first_shard, "dp")
+    chained = chain_line(chain)
+    gather_b = lax.all_gather(tie(last_shard, gather_a, chained), "dp")
+    gathered = [chained, gather_a, gather_b]
+    masks = [me_dp, zero, zero]
 
     peer = swap(tokens, "groups", 1)
     own_x = swap(tokens, "tensor", 2)
@@ -268,45 +255,36 @@
 
     activated = jnp.zeros((rows, slab), BF)
     slopes = []
-    meta = meta_of(jnp.int32(0))
-    early = None
     for p, (first, size) in enumerate(zip(firsts, sizes)):
-        if p == 3:
-            meta = tie(meta, early)
+        meta = meta_of(masks[p], zero)
+        if p == 2:
+            both = meta_of(zero, zero, *masks[:2])
+            (early,) = backward(both, slopes, gathered[:2], delta, firsts[:2], None, None)
+            meta = tie(meta, early, activated)
         act, slope = forward(meta, x4, gathered[p], delta, d_pieces[p], first, 2)
         slopes.append(slope)
         back = swap(act[1], "groups", 1)
         activated = lax.dynamic_update_slice(activated, act[0], (0, mine + first))
         activated = lax.dynamic_update_slice(activated, back, (0, theirs + first))
-        if p == 1:
-            (early,) = backward(meta, slopes, gathered[:2], delta, firsts[:2], None, None)
 
     def back_of(bit, out_type, *wait):
-        m = meta_of(me_t ^ bit ^ me_dp)
+        m = meta_of(zero, me_t ^ bit, masks[2])
         if wait:
             m = tie(m, *wait)
         return backward(m, slopes[2:], gathered[2:], delta, firsts[2:], early, out_type)
 
+    cut = rows // 2
     far_own_give, far_peer_give = back_of(3, BF)
     far_peer_got = swap(far_peer_give, "tensor", 1)
     far_own_got = swap(far_own_give, "tensor", 1)
     far_own, far_peer = back_of(2, F32, far_peer_give)
-    near_own_give, near_peer_give = back_of(1, BF, far_own)
+    far_peer = (far_peer + far_peer_got.astype(F32)).astype(BF)
+    over_x = swap(far_peer[:cut], "tensor", 2)
+    over_y = swap(far_peer[cut:], "groups", 1)
+    near_own_give, near_peer_give = back_of(1, BF, far_peer)
     near_peer_got = swap(near_peer_give, "tensor", 1)
     near_own_got = swap(near_own_give, "tensor", 1)
     near_own, near_peer = back_of(0, F32, near_peer_give)
-    cut = rows // 2
-    far_peer = (far_peer + far_peer_got.astype(F32)).astype(BF)
-    over_x = swap(far_peer[:cut], "tensor", 2).astype(F32)
-    over_y = swap(far_peer[cut:], "groups", 1).astype(F32)
-    far_own = far_own + far_own_got.astype(F32)
-    far_own = jnp.concatenate([far_own[:cut], far_own[cut:] + over_y], axis=0).astype(BF)
-    from_x = swap(far_own, "tensor", 2)
-    near_peer = near_peer + near_peer_got.astype(F32)
-    near_peer = jnp.concatenate([near_peer[:cut] + over_x, near_peer[cut:]], axis=0).astype(BF)
-    from_y = swap(near_peer, "groups", 1)
-    near_own = near_own + near_own_got.astype(F32)
-    d_tokens = (near_own + from_x.astype(F32) + from_y.astype(F32)).astype(BF)
 
     last_slope = tie(slopes[-1], near_own)
     grads = []
@@ -322,11 +300,22 @@
         xb, dy = xb.reshape(2, rows, bs), dy.reshape(2, rows, bs)
         grads.append(jnp.einsum("gtk,gtc->gkc", xb, dy, preferred_element_type=F32))
     grads = jnp.stack(grads, axis=1)
-    grads = grads[0] + swap(grads[1].astype(BF), "groups", 1).astype(F32)
-    bit = 1
-    while bit < n_dp:
-        grads = grads + swap(grads.astype(BF), "dp", bit).astype(F32)
-        bit *= 2
+    grads_got = swap(grads[1].astype(BF), "groups", 1)
+
+    far_own = far_own + far_own_got.astype(F32)
+    far_own = jnp.concatenate([far_own[:cut], far_own[cut:] + over_y.astype(F32)], axis=0)
+    from_x = swap(far_own.astype(BF), "tensor", 2)
+    near_peer = near_peer + near_peer_got.astype(F32)
+    near_peer = jnp.concatenate([near_peer[:cut] + over_x.astype(F32), near_peer[cut:]], axis=0)
+    from_y = swap(near_peer.astype(BF), "groups", 1)
+    grads = grads[0] + grads_got.astype(F32)
+    sent = grads.astype(BF)
+    shares = [swap(sent, "dp", bit) for bit in range(1, n_dp)]
+    near_own = near_own + near_own_got.astype(F32)
+    near_own = tie(near_own, *shares)
+    d_tokens = (near_own + from_x.astype(F32) + from_y.astype(F32)).astype(BF)
+    for share in shares:
+        grads = grads + share.astype(F32)
     norm = float(rows * n_dp) ** (-0.5)
     return (activated, d_tokens, pick_slots(owners, grads * norm))
 

time: 413 us -> 431 us (1.044)
  waiting for transfers between devices: 182 us -> 204 us
  starting transfers between devices: 45.6 us -> 30.8 us
  between operations: 21 us -> 32.3 us
  other arithmetic: 41.1 us -> 30.3 us
  Pallas kernels: 82.8 us -> 90 us
    ppermute x20 -> x5, waiting for transfers between devices: 113 us -> 158 us  [the longest x1 57.6 us: chain_line(): e = lax.ppermute(b, 'dp', outward)]
    ppermute x24 -> x23, waiting for transfers between devices: 68.7 us -> 46.4 us  [swap(): return lax.ppermute(array, axis, [(i, i ^ bit) for i in range(size)])]
    ppermute x20 -> x5, starting transfers between devices: 24.2 us -> 9.21 us  [the longest x1 3.09 us: chain_line(): a = lax.ppermute(shard, 'dp', [(0, 1), (1, 0), (2, 3), (3, 2)])]
    another operation x18 -> x9, other arithmetic: 20.1 us -> 8.26 us  [the longest x3 7.99 us: chain_line(): return jnp.stack([shard, a, c + e, b + f])]
    pallas_call x5, Pallas kernels: 43.3 us -> 50.8 us  [backward(): pl.pallas_call(functools.partial(backward_kernel, firsts, blocks, bs, acc...]
    pallas_call x4 -> x3, Pallas kernels: 39.5 us -> 39.3 us  [forward(): pl.pallas_call(functools.partial(forward_kernel, first, blocks, bs), grid...]
    ppermute x24 -> x23, starting transfers between devices: 21.4 us -> 21.5 us  [swap(): return lax.ppermute(array, axis, [(i, i ^ bit) for i in range(size)])]
  transfers between devices with their start and end apart: 44 -> 30, of which waited for: 18 -> 10; matrix products, arithmetic and copies ran while one was open for 18% -> 15% of each run, Pallas kernels for 17% -> 17%
where the time goes in v4:
time: 431 us; the launch traced here: 429 us
  waiting for transfers between devices  204 us (47%)
  Pallas kernels  90 us (21%)
  local copies, waits for them, and re-layouts  39.9 us (9%)
  between operations  32.3 us (7%)
  starting transfers between devices  30.8 us (7%)
  other arithmetic  30.3 us (7%)
    ppermute x1, waiting for transfers between devices, chain_line(): e = lax.ppermute(b, 'dp', outward)  57.6 us
    ppermute x1, waiting for transfers between devices, chain_line(): a = lax.ppermute(shard, 'dp', [(0, 1), (1, 0), (2, 3), (3, 2)])  56.3 us
    pallas_call x5, Pallas kernels, backward(): pl.pallas_call(functools.partial(backward_kernel, firsts, blocks, bs, acc...  50.8 us
    ppermute x23, waiting for transfers between devices, swap(): return lax.ppermute(array, axis, [(i, i ^ bit) for i in range(size)])  46.4 us
    ppermute x1, waiting for transfers between devices, chain_line(): f = lax.ppermute(c, 'dp', outward)  43.8 us
    pallas_call x3, Pallas kernels, forward(): pl.pallas_call(functools.partial(forward_kernel, first, blocks, bs), grid...  39.3 us
    ppermute x23, starting transfers between devices, swap(): return lax.ppermute(array, axis, [(i, i ^ bit) for i in range(size)])  21.5 us
  transfers between devices with their start and end apart: 30, of which 10 were waited for; matrix products, arithmetic and copies ran while one was open for 15% of the time, Pallas kernels for 17%

profile of v4, /device:TPU:0, one launch (start us, length us, event | category | flops | bytes accessed | tf_op | source)
XLA Modules:
  0.0 428.6 jit_solution(13086121357886133486)
XLA Ops:
  7.2 2.9 constant_dynamic-slice_fusion.9
  11.6 3.1 collective-permute-start.5
  20.9 2.5 constant_dynamic-slice_fusion.11
  23.5 56.3 %collective-permute-done.5 = bf16[1024,640]{1,0:T(8,128)(2,1)} collective-permute-done((bf16[1024,640]{1,0:T(8,128)(2,1)S(1)}, bf16[1024,640]{1,0:T(8,128)(2,1)}, u32[]{:S(2)}, u32[]{:S(2)}) %collective-permute-start.5) | collective-permute-done | bytes 1310752 | tf_op jit(solution)/shard_map/ppermute | solution.py:194
  81.5 2.2 collective-permute-start.3
  83.7 2.2 constant_dynamic-slice_fusion.6
  90.9 10.8 %collective-permute-done.3 = bf16[448,1024]{1,0:T(8,128)(2,1)} collective-permute-done((bf16[448,1024]{1,0:T(8,128)(2,1)}, bf16[448,1024]{1,0:T(8,128)(2,1)}, u32[]{:S(2)}, u32[]{:S(2)}) %collective-permute-start.3) | collective-permute-done | bytes 917536 | tf_op jit(solution)/shard_map/ppermute | solution.py:18
  105.7 2.2 constant_dynamic-update-slice_fusion.3
  107.8 2.2 constant_dynamic-update-slice_fusion.2
  111.1 2.7 constant_dynamic-slice_fusion.8
  115.3 2.3 pad_maximum_fusion.3.d_ref
  117.7 57.6 %collective-permute-done.8 = bf16[1024,640]{1,0:T(8,128)(2,1)} collective-permute-done((bf16[1024,640]{1,0:T(8,128)(2,1)}, bf16[1024,640]{1,0:T(8,128)(2,1)}, u32[]{:S(2)}, u32[]{:S(2)}) %collective-permute-start.8) | collective-permute-done | bytes 1310752 | tf_op jit(solution)/shard_map/ppermute | solution.py:197
  179.1 43.8 %collective-permute-done.9 = bf16[1024,640]{1,0:T(8,128)(2,1)} collective-permute-done((bf16[1024,640]{1,0:T(8,128)(2,1)}, bf16[1024,640]{1,0:T(8,128)(2,1)}, u32[]{:S(2)}, u32[]{:S(2)}) %collective-permute-start.9) | collective-permute-done | bytes 1310752 | tf_op jit(solution)/shard_map/ppermute | solution.py:198
  224.8 4.3 pad_maximum_fusion.1.w_ref.refs_2_
  229.1 6.1 %pad_maximum_fusion.x_ref = bf16[4,896,1024]{2,1,0:T(8,128)(2,1)} fusion(bf16[1,896,1024]{2,1,0:T(8,128)(2,1)} %bitcast.11, bf16[1,896,1024]{2,1,0:T(8,128)(2,1)} %bitcast.10, bf16[1,896,1024]{2,1,0:T(8,128)(2,1)} %bitcast.9, bf16[1,896,1024]{2,1,0:T(8,128)(2,1)S(1)} %bitcast.117), kind=kLoop, calls=%fused_computation | loop fusion | flops 11010048 | bytes 14680064 | tf_op jit(solution)/shard_map/stack | solution.py:245
  235.2 13.1 %shard_map.94 = (bf16[2,448,640]{2,1,0:T(8,128)(2,1)}, bf16[896,640]{1,0:T(8,128)(2,1)}) custom-call(s32[24]{0:T(128)} %concatenate.45.meta, bf16[4,896,1024]{2,1,0:T(8,128)(2,1)} %pad_maximum_fusion.x_ref, bf16[4,1024,640]{2,1,0:T(8,128)(2,1)} %pad_maximum_fusion.1.w_ref.refs_2_, bf16[4,128,128]{2,1,0:T(8,128)(2,1)} %refs_2_.7, ...), custom_call_target="tpu_custom_call" | custom-call | flops 4697620480 | bytes 12582912 | tf_op jit(solution)/shard_map/pallas_call | solution.py:56
  252.9 2.4 pad_maximum_fusion.2.d_ref
  258.6 6.7 %collective-permute-done.11 = bf16[448,640]{1,0:T(8,128)(2,1)} collective-permute-done((bf16[448,640]{1,0:T(8,128)(2,1)}, bf16[448,640]{1,0:T(8,128)(2,1)}, u32[]{:S(2)}, u32[]{:S(2)}) %collective-permute-start.11) | collective-permute-done | bytes 573472 | tf_op jit(solution)/shard_map/ppermute | solution.py:18
  266.5 16.3 %shard_map.95 = (bf16[2,448,896]{2,1,0:T(8,128)(2,1)}, bf16[896,896]{1,0:T(8,128)(2,1)}) custom-call(s32[24]{0:T(128)} %concatenate.49.meta, bf16[4,896,1024]{2,1,0:T(8,128)(2,1)} %pad_maximum_fusion.x_ref, bf16[4,1024,896]{2,1,0:T(8,128)(2,1)} %bitcast.128, bf16[4,128,128]{2,1,0:T(8,128)(2,1)} %refs_2_.7, bf16[896,896]{1,0:T(8,128)(2,1)} %pad_maximum_fusion.2.d_ref), custom_call_target="tpu_custom_call" | custom-call | flops 6576668672 | bytes 14680064 | tf_op jit(solution)/shard_map/pallas_call | solution.py:56
  284.6 25.1 %shard_map.96.refs_3_ = f32[4,896,1024]{2,1,0:T(8,128)} custom-call(s32[24]{0:T(128)} %concatenate.51.meta, bf16[896,640]{1,0:T(8,128)(2,1)} %get-tuple-element.31.refs_0_, bf16[896,896]{1,0:T(8,128)(2,1)} %get-tuple-element.32.refs_1_, bf16[4,1024,640]{2,1,0:T(8,128)(2,1)} %pad_maximum_fusion.1.w_ref.refs_2_, bf16[4,1024,896]{2,1,0:T(8,128)(2,1)} %bitcast.129, ...), custom_call_target="tpu_custom_call" | custom-call | flops 11274289152 | bytes 23592960 | tf_op jit(solution)/shard_map/pallas_call | solution.py:144
  309.8 9.8 %shard_map.97 = (bf16[2,448,384]{2,1,0:T(8,128)(2,1)}, bf16[896,384]{1,0:T(8,128)(2,1)}) custom-call(s32[24]{0:T(128)} %concatenate.49.meta, bf16[4,896,1024]{2,1,0:T(8,128)(2,1)} %pad_maximum_fusion.x_ref, bf16[4,1024,384]{2,1,0:T(8,128)(2,1)} %bitcast.112, bf16[4,128,128]{2,1,0:T(8,128)(2,1)} %refs_2_.7, bf16[896,384]{1,0:T(8,128)(2,1)} %pad_maximum_fusion.6.d_ref), custom_call_target="tpu_custom_call" | custom-call | flops 2818572288 | bytes 10485760 | tf_op jit(solution)/shard_map/pallas_call | solution.py:56
  319.6 6.2 %shard_map.98 = (bf16[448,1024]{1,0:T(8,128)(2,1)}, bf16[448,1024]{1,0:T(8,128)(2,1)}) custom-call(s32[24]{0:T(128)} %concatenate.56.meta, bf16[896,384]{1,0:T(8,128)(2,1)} %get-tuple-element.46.refs_0_, bf16[4,1024,384]{2,1,0:T(8,128)(2,1)} %bitcast.113, bf16[4,128,128]{2,1,0:T(8,128)(2,1)} %refs_2_.7, f32[4,896,1024]{2,1,0:T(8,128)} %shard_map.96.refs_3_), custom_call_target="tpu_custom_call" | custom-call | flops 704643072 | bytes 1474560 | tf_op jit(solution)/shard_map/pallas_call | solution.py:144
  349.8 6.6 %shard_map.99 = (f32[448,1024]{1,0:T(8,128)}, f32[448,1024]{1,0:T(8,128)}) custom-call(s32[24]{0:T(128)} %concatenate.55.meta, bf16[896,384]{1,0:T(8,128)(2,1)} %get-tuple-element.46.refs_0_, bf16[4,1024,384]{2,1,0:T(8,128)(2,1)} %bitcast.114, bf16[4,128,128]{2,1,0:T(8,128)(2,1)} %refs_2_.7, f32[4,896,1024]{2,1,0:T(8,128)} %shard_map.96.refs_3_), custom_call_target="tpu_custom_call" | custom-call | flops 704643072 | bytes 1474560 | tf_op jit(solution)/shard_map/pallas_call | solution.py:144
  356.5 2.0 add_convert_fusion.1
  359.5 6.1 %shard_map.100 = (bf16[448,1024]{1,0:T(8,128)(2,1)}, bf16[448,1024]{1,0:T(8,128)(2,1)}) custom-call(s32[24]{0:T(128)} %concatenate.54.meta, bf16[896,384]{1,0:T(8,128)(2,1)} %get-tuple-element.46.refs_0_, bf16[4,1024,384]{2,1,0:T(8,128)(2,1)} %bitcast.115, bf16[4,128,128]{2,1,0:T(8,128)(2,1)} %refs_2_.7, f32[4,896,1024]{2,1,0:T(8,128)} %shard_map.96.refs_3_), custom_call_target="tpu_custom_call" | custom-call | flops 704643072 | bytes 1474560 | tf_op jit(solution)/shard_map/pallas_call | solution.py:144
  366.0 6.8 %shard_map.101 = (f32[448,1024]{1,0:T(8,128)}, f32[448,1024]{1,0:T(8,128)}) custom-call(s32[24]{0:T(128)} %concatenate.53.meta, bf16[896,384]{1,0:T(8,128)(2,1)} %get-tuple-element.46.refs_0_, bf16[4,1024,384]{2,1,0:T(8,128)(2,1)} %bitcast.116, bf16[4,128,128]{2,1,0:T(8,128)(2,1)} %refs_2_.7, f32[4,896,1024]{2,1,0:T(8,128)} %shard_map.96.refs_3_), custom_call_target="tpu_custom_call" | custom-call | flops 704643072 | bytes 1474560 | tf_op jit(solution)/shard_map/pallas_call | solution.py:144
  380.6 3.9 collective-permute-done.18
  384.5 8.7 %collective-permute-done.23 = bf16[224,1024]{1,0:T(8,128)(2,1)S(1)} collective-permute-done((bf16[224,1024]{1,0:T(8,128)(2,1)S(1)}, bf16[224,1024]{1,0:T(8,128)(2,1)S(1)}, u32[]{:S(2)}, u32[]{:S(2)}) %collective-permute-start.23) | collective-permute-done | bytes 458784 | tf_op jit(solution)/shard_map/ppermute | solution.py:18
  393.4 2.5 collective-permute-start.20
  396.3 2.0 collective-permute-start.21
  402.8 3.1 collective-permute-done.20
  407.2 12.0 %collective-permute-done.24 = bf16[448,1024]{1,0:T(8,128)(2,1)S(1)} collective-permute-done((bf16[448,1024]{1,0:T(8,128)(2,1)S(1)}, bf16[448,1024]{1,0:T(8,128)(2,1)S(1)}, u32[]{:S(2)}, u32[]{:S(2)}) %collective-permute-start.24) | collective-permute-done | bytes 917536 | tf_op jit(solution)/shard_map/ppermute | solution.py:18
  (148 shorter events, 61.7 us)
Async XLA Ops:
  7.2 221.9 %all-gather.5.cloned.1.call-start = ((), (), s32[]{:S(2)}) async-start(), calls=%async_computation | async-start | bytes 9175040 | tf_op jit(solution)/shard_map/all_gather | solution.py:234
  10.1 299.6 %all-gather.7.cloned.1.call-start = ((), (), s32[]{:S(2)}) async-start(), calls=%async_computation.1 | async-start | bytes 3932160 | tf_op jit(solution)/shard_map/all_gather | solution.py:236
  11.6 68.1 %collective-permute-start.5 = (bf16[1024,640]{1,0:T(8,128)(2,1)S(1)}, bf16[1024,640]{1,0:T(8,128)(2,1)}, u32[]{:S(2)}, u32[]{:S(2)}) collective-permute-start(bf16[1024,640]{1,0:T(8,128)(2,1)S(1)} %constant_dynamic-slice_fusion.12), channel_id=1, source_target_pairs={{0,4},{4,0},{8,12},{12,8},{1,5},{5,1},{9,13},{13,9},{2,6},{6,2},{1... | collective-permute-start | bytes 3932168 | tf_op jit(solution)/shard_map/ppermute | solution.py:194
  14.7 66.7 %collective-permute-start = (bf16[448,1024]{1,0:T(8,128)(2,1)}, bf16[448,1024]{1,0:T(8,128)(2,1)}, u32[]{:S(2)}, u32[]{:S(2)}) collective-permute-start(bf16[448,1024]{1,0:T(8,128)(2,1)} %param.7), channel_id=1, source_target_pairs={{0,16},{16,0},{1,17},{17,1},{2,18},{18,2},{3,19},{19,3},{4,20},{20... | collective-permute-start | bytes 2752520 | tf_op jit(solution)/shard_map/ppermute | solution.py:18
  16.2 71.7 %collective-permute-start.7 = (bf16[1024,640]{1,0:T(8,128)(2,1)S(1)}, bf16[1024,640]{1,0:T(8,128)(2,1)}, u32[]{:S(2)}, u32[]{:S(2)}) collective-permute-start(bf16[1024,640]{1,0:T(8,128)(2,1)S(1)} %constant_dynamic-slice_fusion.12), channel_id=1, source_target_pairs={{4,8},{8,4},{5,9},{9,5},{6,10},{10,6},{7,11},{11,7},{20,24},{24,20... | collective-permute-start | bytes 3932168 | tf_op jit(solution)/shard_map/ppermute | solution.py:195
  18.1 87.6 %collective-permute-start.2 = (bf16[448,1024]{1,0:T(8,128)(2,1)}, bf16[448,1024]{1,0:T(8,128)(2,1)}, u32[]{:S(2)}, u32[]{:S(2)}) collective-permute-start(bf16[448,1024]{1,0:T(8,128)(2,1)} %param.7), channel_id=1, source_target_pairs={{0,2},{1,3},{2,0},{3,1},{4,6},{5,7},{6,4},{7,5},{8,10},{9,11},{10,... | collective-permute-start | bytes 2752520 | tf_op jit(solution)/shard_map/ppermute | solution.py:18
  19.6 61.9 %copy-start.14 = (s32[4]{0:T(128)S(1)}, s32[4]{0:T(128)}, u32[]{:S(2)}) copy-start(s32[4]{0:T(128)} %param.10) | copy-start | bytes 52
  23.5 64.4 %copy-start.15 = (s32[4]{0:T(128)S(1)}, s32[4]{0:T(128)}, u32[]{:S(2)}) copy-start(s32[4]{0:T(128)} %param.11) | copy-start | bytes 52
  79.7 24.6 %collective-permute-start.6 = (bf16[1024,640]{1,0:T(8,128)(2,1)}, bf16[1024,640]{1,0:T(8,128)(2,1)}, u32[]{:S(2)}, u32[]{:S(2)}) collective-permute-start(bf16[1024,640]{1,0:T(8,128)(2,1)} %collective-permute-done.5), channel_id=1, source_target_pairs={{4,8},{8,4},{5,9},{9,5},{6,10},{10,6},{7,11},{11,7},{20,24},{24,20... | collective-permute-start | bytes 3932168 | tf_op jit(solution)/shard_map/ppermute | solution.py:196
  81.5 20.3 %collective-permute-start.3 = (bf16[448,1024]{1,0:T(8,128)(2,1)}, bf16[448,1024]{1,0:T(8,128)(2,1)}, u32[]{:S(2)}, u32[]{:S(2)}) collective-permute-start(bf16[448,1024]{1,0:T(8,128)(2,1)} %collective-permute-done), channel_id=1, source_target_pairs={{0,2},{1,3},{2,0},{3,1},{4,6},{5,7},{6,4},{7,5},{8,10},{9,11},{10,... | collective-permute-start | bytes 2752520 | tf_op jit(solution)/shard_map/ppermute | solution.py:18
  87.9 87.4 %collective-permute-start.8 = (bf16[1024,640]{1,0:T(8,128)(2,1)}, bf16[1024,640]{1,0:T(8,128)(2,1)}, u32[]{:S(2)}, u32[]{:S(2)}) collective-permute-start(bf16[1024,640]{1,0:T(8,128)(2,1)} %collective-permute-done.7), channel_id=1, source_target_pairs={{4,0},{8,12},{5,1},{9,13},{6,2},{10,14},{7,3},{11,15},{20,16},{24,... | collective-permute-start | bytes 3932168 | tf_op jit(solution)/shard_map/ppermute | solution.py:197
  101.7 12.1 %collective-permute-start.10 = (bf16[448,640]{1,0:T(8,128)(2,1)S(1)}, bf16[448,640]{1,0:T(8,128)(2,1)}, u32[]{:S(2)}, u32[]{:S(2)}) collective-permute-start(bf16[448,640]{1,0:T(8,128)(2,1)S(1)} %copy-done.12), channel_id=1, source_target_pairs={{0,16},{16,0},{1,17},{17,1},{2,18},{18,2},{3,19},{19,3},{4,20},{20... | collective-permute-start | bytes 1720328 | tf_op jit(solution)/shard_map/ppermute | solution.py:18
  104.3 124.8 %collective-permute-start.1 = (bf16[896,1024]{1,0:T(8,128)(2,1)S(1)}, bf16[896,1024]{1,0:T(8,128)(2,1)}, u32[]{:S(2)}, u32[]{:S(2)}) collective-permute-start(bf16[896,1024]{1,0:T(8,128)(2,1)S(1)} %constant_dynamic-update-slice_fusion), channel_id=1, source_target_pairs={{0,1},{1,0},{2,3},{3,2},{4,5},{5,4},{6,7},{7,6},{8,9},{9,8},{10,11... | collective-permute-start | bytes 5505032 | tf_op jit(solution)/shard_map/ppermute | solution.py:18
  104.3 118.6 %collective-permute-start.9 = (bf16[1024,640]{1,0:T(8,128)(2,1)}, bf16[1024,640]{1,0:T(8,128)(2,1)}, u32[]{:S(2)}, u32[]{:S(2)}) collective-permute-start(bf16[1024,640]{1,0:T(8,128)(2,1)} %collective-permute-done.6), channel_id=1, source_target_pairs={{4,0},{8,12},{5,1},{9,13},{6,2},{10,14},{7,3},{11,15},{20,16},{24,... | collective-permute-start | bytes 3932168 | tf_op jit(solution)/shard_map/ppermute | solution.py:198
  110.0 119.1 %collective-permute-start.4 = (bf16[896,1024]{1,0:T(8,128)(2,1)}, bf16[896,1024]{1,0:T(8,128)(2,1)}, u32[]{:S(2)}, u32[]{:S(2)}) collective-permute-start(bf16[896,1024]{1,0:T(8,128)(2,1)} %constant_dynamic-update-slice_fusion.2), channel_id=1, source_target_pairs={{0,1},{1,0},{2,3},{3,2},{4,5},{5,4},{6,7},{7,6},{8,9},{9,8},{10,11... | collective-permute-start | bytes 5505032 | tf_op jit(solution)/shard_map/ppermute | solution.py:18
  113.8 63.3 %collective-permute-start.12 = (bf16[448,896]{1,0:T(8,128)(2,1)}, bf16[448,896]{1,0:T(8,128)(2,1)}, u32[]{:S(2)}, u32[]{:S(2)}) collective-permute-start(bf16[448,896]{1,0:T(8,128)(2,1)} %get-tuple-element.29), channel_id=1, source_target_pairs={{0,16},{16,0},{1,17},{17,1},{2,18},{18,2},{3,19},{19,3},{4,20},{20... | collective-permute-start | bytes 2408456 | tf_op jit(solution)/shard_map/ppermute | solution.py:18
  177.1 78.2 %collective-permute-start.14 = (bf16[448,384]{1,0:T(8,128)(2,1)}, bf16[448,384]{1,0:T(8,128)(2,1)}, u32[]{:S(2)}, u32[]{:S(2)}) collective-permute-start(bf16[448,384]{1,0:T(8,128)(2,1)} %get-tuple-element.35), channel_id=1, source_target_pairs={{0,16},{16,0},{1,17},{17,1},{2,18},{18,2},{3,19},{19,3},{4,20},{20... | collective-permute-start | bytes 1032200 | tf_op jit(solution)/shard_map/ppermute | solution.py:18
  250.3 15.1 %collective-permute-start.11 = (bf16[448,640]{1,0:T(8,128)(2,1)}, bf16[448,640]{1,0:T(8,128)(2,1)}, u32[]{:S(2)}, u32[]{:S(2)}) collective-permute-start(bf16[448,640]{1,0:T(8,128)(2,1)} %slice_bitcast_fusion.1), channel_id=1, source_target_pairs={{0,16},{16,0},{1,17},{17,1},{2,18},{18,2},{3,19},{19,3},{4,20},{20... | collective-permute-start | bytes 1720328 | tf_op jit(solution)/shard_map/ppermute | solution.py:18
  284.2 25.5 %collective-permute-start.13 = (bf16[448,896]{1,0:T(8,128)(2,1)S(1)}, bf16[448,896]{1,0:T(8,128)(2,1)S(1)}, u32[]{:S(2)}, u32[]{:S(2)}) collective-permute-start(bf16[448,896]{1,0:T(8,128)(2,1)S(1)} %slice_bitcast_fusion), channel_id=1, source_target_pairs={{0,16},{16,0},{1,17},{17,1},{2,18},{18,2},{3,19},{19,3},{4,20},{20... | collective-permute-start | bytes 2408456 | tf_op jit(solution)/shard_map/ppermute | solution.py:18
  325.8 30.7 %collective-permute-start.16 = (bf16[448,1024]{1,0:T(8,128)(2,1)}, bf16[448,1024]{1,0:T(8,128)(2,1)}, u32[]{:S(2)}, u32[]{:S(2)}) collective-permute-start(bf16[448,1024]{1,0:T(8,128)(2,1)} %get-tuple-element.38), channel_id=1, source_target_pairs={{0,1},{1,0},{2,3},{3,2},{4,5},{5,4},{6,7},{7,6},{8,9},{9,8},{10,11... | collective-permute-start | bytes 2752520 | tf_op jit(solution)/shard_map/ppermute | solution.py:18
  348.9 49.7 %collective-permute-start.15 = (bf16[448,384]{1,0:T(8,128)(2,1)}, bf16[448,384]{1,0:T(8,128)(2,1)}, u32[]{:S(2)}, u32[]{:S(2)}) collective-permute-start(bf16[448,384]{1,0:T(8,128)(2,1)} %slice_bitcast_fusion.2), channel_id=1, source_target_pairs={{0,16},{16,0},{1,17},{17,1},{2,18},{18,2},{3,19},{19,3},{4,20},{20... | collective-permute-start | bytes 1032200 | tf_op jit(solution)/shard_map/ppermute | solution.py:18
  349.6 29.3 %collective-permute-start.22 = (bf16[448,1024]{1,0:T(8,128)(2,1)}, bf16[448,1024]{1,0:T(8,128)(2,1)S(1)}, u32[]{:S(2)}, u32[]{:S(2)}) collective-permute-start(bf16[448,1024]{1,0:T(8,128)(2,1)} %get-tuple-element.49), channel_id=1, source_target_pairs={{0,1},{1,0},{2,3},{3,2},{4,5},{5,4},{6,7},{7,6},{8,9},{9,8},{10,11... | collective-permute-start | bytes 2752520 | tf_op jit(solution)/shard_map/ppermute | solution.py:18
  365.6 27.8 %collective-permute-start.25 = (bf16[448,1024]{1,0:T(8,128)(2,1)}, bf16[448,1024]{1,0:T(8,128)(2,1)S(1)}, u32[]{:S(2)}, u32[]{:S(2)}) collective-permute-start(bf16[448,1024]{1,0:T(8,128)(2,1)} %get-tuple-element.42), channel_id=1, source_target_pairs={{0,1},{1,0},{2,3},{3,2},{4,5},{5,4},{6,7},{7,6},{8,9},{9,8},{10,11... | collective-permute-start | bytes 2752520 | tf_op jit(solution)/shard_map/ppermute | solution.py:18
  372.8 23.5 %collective-permute-start.26 = (bf16[224,1024]{1,0:T(8,128)(2,1)}, bf16[224,1024]{1,0:T(8,128)(2,1)S(1)}, u32[]{:S(2)}, u32[]{:S(2)}) collective-permute-start(bf16[224,1024]{1,0:T(8,128)(2,1)} %get-tuple-element.69), channel_id=1, source_target_pairs={{0,2},{1,3},{2,0},{3,1},{4,6},{5,7},{6,4},{7,5},{8,10},{9,11},{10,... | collective-permute-start | bytes 1376264 | tf_op jit(solution)/shard_map/ppermute | solution.py:18
  378.0 6.4 %collective-permute-start.18 = (bf16[4,128,128]{2,1,0:T(8,128)(2,1)S(1)}, bf16[4,128,128]{2,1,0:T(8,128)(2,1)S(1)}, u32[]{:S(2)}, u32[]{:S(2)}) collective-permute-start(bf16[4,128,128]{2,1,0:T(8,128)(2,1)S(1)} %fusion.4), channel_id=1, source_target_pairs={{0,16},{16,0},{1,17},{17,1},{2,18},{18,2},{3,19},{19,3},{4,20},{20... | collective-permute-start | bytes 393224 | tf_op jit(solution)/shard_map/ppermute | solution.py:18
  378.9 14.3 %collective-permute-start.23 = (bf16[224,1024]{1,0:T(8,128)(2,1)S(1)}, bf16[224,1024]{1,0:T(8,128)(2,1)S(1)}, u32[]{:S(2)}, u32[]{:S(2)}) collective-permute-start(bf16[224,1024]{1,0:T(8,128)(2,1)S(1)} %copy-done.13), channel_id=1, source_target_pairs={{0,16},{16,0},{1,17},{17,1},{2,18},{18,2},{3,19},{19,3},{4,20},{20... | collective-permute-start | bytes 1376264 | tf_op jit(solution)/shard_map/ppermute | solution.py:18
  384.5 22.3 %collective-permute-start.17 = (bf16[448,1024]{1,0:T(8,128)(2,1)S(1)}, bf16[448,1024]{1,0:T(8,128)(2,1)S(1)}, u32[]{:S(2)}, u32[]{:S(2)}) collective-permute-start(bf16[448,1024]{1,0:T(8,128)(2,1)S(1)} %copy-done.16), channel_id=1, source_target_pairs={{0,1},{1,0},{2,3},{3,2},{4,5},{5,4},{6,7},{7,6},{8,9},{9,8},{10,11... | collective-permute-start | bytes 2752520 | tf_op jit(solution)/shard_map/ppermute | solution.py:18
  393.2 7.0 %collective-permute-start.19 = (bf16[4,128,128]{2,1,0:T(8,128)(2,1)S(1)}, bf16[4,128,128]{2,1,0:T(8,128)(2,1)S(1)}, u32[]{:S(2)}, u32[]{:S(2)}) collective-permute-start(bf16[4,128,128]{2,1,0:T(8,128)(2,1)S(1)} %fusion.3), channel_id=1, source_target_pairs={{0,4},{4,0},{8,12},{12,8},{1,5},{5,1},{9,13},{13,9},{2,6},{6,2},{1... | collective-permute-start | bytes 393224 | tf_op jit(solution)/shard_map/ppermute | solution.py:18
  393.4 12.5 %collective-permute-start.20 = (bf16[4,128,128]{2,1,0:T(8,128)(2,1)S(1)}, bf16[4,128,128]{2,1,0:T(8,128)(2,1)S(1)}, u32[]{:S(2)}, u32[]{:S(2)}) collective-permute-start(bf16[4,128,128]{2,1,0:T(8,128)(2,1)S(1)} %fusion.3), channel_id=1, source_target_pairs={{0,8},{4,12},{8,0},{12,4},{1,9},{5,13},{9,1},{13,5},{2,10},{6,14},... | collective-permute-start | bytes 393224 | tf_op jit(solution)/shard_map/ppermute | solution.py:18
  396.3 9.6 %collective-permute-start.21 = (bf16[4,128,128]{2,1,0:T(8,128)(2,1)S(1)}, bf16[4,128,128]{2,1,0:T(8,128)(2,1)S(1)}, u32[]{:S(2)}, u32[]{:S(2)}) collective-permute-start(bf16[4,128,128]{2,1,0:T(8,128)(2,1)S(1)} %fusion.3), channel_id=1, source_target_pairs={{0,12},{4,8},{8,4},{12,0},{1,13},{5,9},{9,5},{13,1},{2,14},{6,10},... | collective-permute-start | bytes 393224 | tf_op jit(solution)/shard_map/ppermute | solution.py:18
  398.7 20.5 %collective-permute-start.24 = (bf16[448,1024]{1,0:T(8,128)(2,1)S(1)}, bf16[448,1024]{1,0:T(8,128)(2,1)S(1)}, u32[]{:S(2)}, u32[]{:S(2)}) collective-permute-start(bf16[448,1024]{1,0:T(8,128)(2,1)S(1)} %pad_maximum_fusion.4), channel_id=1, source_target_pairs={{0,2},{1,3},{2,0},{3,1},{4,6},{5,7},{6,4},{7,5},{8,10},{9,11},{10,... | collective-permute-start | bytes 2752520 | tf_op jit(solution)/shard_map/ppermute | solution.py:18
  400.2 20.1 %collective-permute-start.27 = (bf16[448,1024]{1,0:T(8,128)(2,1)S(1)}, bf16[448,1024]{1,0:T(8,128)(2,1)S(1)}, u32[]{:S(2)}, u32[]{:S(2)}) collective-permute-start(bf16[448,1024]{1,0:T(8,128)(2,1)S(1)} %pad_maximum_fusion.5), channel_id=1, source_target_pairs={{0,16},{16,0},{1,17},{17,1},{2,18},{18,2},{3,19},{19,3},{4,20},{20... | collective-permute-start | bytes 2752520 | tf_op jit(solution)/shard_map/ppermute | solution.py:18
  (16 other events, 99.7 us)
Sparse Core Ops, SparseCore 0:
  10.3 185.1 all-gather.4
  229.2 62.3 all-gather.6

commit v5 on v4

v5 whole, which is shorter than its diff:
```python
import functools

import jax
import jax.numpy as jnp
from jax import lax
from jax.experimental import pallas as pl
from jax.experimental.pallas import tpu as pltpu
from jax.sharding import PartitionSpec as P

CAP = 2
BF = jnp.bfloat16
F32 = jnp.float32
VMEM_BYTES = 56 * 2**20


def swap(array, axis, bit):
    size = lax.axis_size(axis)
    return lax.ppermute(array, axis, [(i, i ^ bit) for i in range(size)])


def params():
    return pltpu.CompilerParams(vmem_limit_bytes=VMEM_BYTES)


PARTS, BLOCKS = 0, 4


def forward_kernel(first, blocks, bs, meta, x_ref, w_ref, delta_ref, d_ref, act_ref, slope_ref, acc):
    width = acc.shape[1]
    total = None
    for s in range(w_ref.shape[0]):
        term = jnp.dot(x_ref[meta[PARTS + s]], w_ref[s], preferred_element_type=F32)
        total = term if total is None else total + term
    acc[...] = total
    start = first + pl.program_id(0) * width
    for n in range(blocks):
        at = BLOCKS + 4 * n
        col = meta[at + 3] - start

        @pl.when((col >= 0) & (col < width))
        def _():
            cols = pl.ds(pl.multiple_of(col, bs), bs)
            rows = pl.ds(pl.multiple_of(meta[at + 2], bs), bs)
            xs = x_ref[meta[at], :, rows]
            acc[:, cols] += jnp.dot(xs, delta_ref[n], preferred_element_type=F32)

    preact = acc[...]
    squash = jax.nn.sigmoid(preact)
    act_ref[0] = (preact * squash).astype(BF)
    slope_ref[...] = (
        d_ref[...].astype(F32) * squash * (1.0 + preact * (1.0 - squash))
    ).astype(BF)


def forward(meta, x4, w4, delta, d_piece, first, groups_of):
    rows, width = d_piece.shape
    slots, feats = w4.shape[0], w4.shape[1]
    cuts = 2
    tile = rows // groups_of // cuts
    blocks, bs = delta.shape[0], delta.shape[1]
    wide = next(c for c in (512, 384, 256, 128, width) if width % c == 0)
    return pl.pallas_call(
        functools.partial(forward_kernel, first, blocks, bs),
        grid_spec=pltpu.PrefetchScalarGridSpec(
            num_scalar_prefetch=1,
            grid=(width // wide, groups_of * cuts),
            in_specs=[
                pl.BlockSpec((slots, tile, feats), lambda j, i, m: (0, i, 0)),
                pl.BlockSpec((slots, feats, wide), lambda j, i, m: (0, 0, j)),
                pl.BlockSpec(delta.shape, lambda j, i, m: (0, 0, 0)),
                pl.BlockSpec((tile, wide), lambda j, i, m: (i, j)),
            ],
            out_specs=[
                pl.BlockSpec((1, tile, wide), lambda j, i, m: (i // cuts, i % cuts, j)),
                pl.BlockSpec((tile, wide), lambda j, i, m: (i, j)),
            ],
            scratch_shapes=[pltpu.VMEM((tile, wide), F32)],
        ),
        out_shape=[
            jax.ShapeDtypeStruct((groups_of, rows // groups_of, width), BF),
            jax.ShapeDtypeStruct((rows, width), BF),
        ],
        compiler_params=params(),
        cost_estimate=pl.CostEstimate(
            flops=2 * rows * feats * slots * width,
            bytes_accessed=2 * (rows + width) * feats * slots,
            transcendentals=0,
        ),
    )(meta, x4, w4, delta, d_piece)


def backward_kernel(firsts, blocks, bs, has_acc, bit, meta, *refs):
    n = len(firsts)
    slopes, w_refs = refs[:n], refs[n : 2 * n]
    delta_ref = refs[2 * n]
    acc_in = refs[2 * n + 1] if has_acc else None
    outs, acc = refs[2 * n + 1 + has_acc : -1], refs[-1]
    size = acc.shape[1]
    slot = pl.program_id(0) if bit is None else meta[PARTS + bit]
    base = pl.program_id(1) * size
    total = acc_in[0] if has_acc else None
    for p in range(n):
        term = lax.dot_general(
            slopes[p][...], w_refs[p][0], (((1,), (1,)), ((), ())), preferred_element_type=F32
        )
        total = term if total is None else total + term
    acc[...] = total
    for b in range(blocks):
        at = BLOCKS + 4 * b
        row = meta[at + 2] - base
        for p in range(n):
            col = meta[at + 3] - firsts[p]
            inside = (row >= 0) & (row < size) & (col >= 0) & (col < slopes[p].shape[1])

            @pl.when(inside & (meta[at + 1] == slot))
            def _():
                ds = slopes[p][:, pl.ds(pl.multiple_of(col, bs), bs)]
                acc[:, pl.ds(pl.multiple_of(row, bs), bs)] += lax.dot_general(
                    ds, delta_ref[b], (((1,), (1,)), ((), ())), preferred_element_type=F32
                )

    if len(outs) == 1:
        outs[0][0] = acc[...]
    else:
        cut = outs[0].shape[0]
        outs[0][...] = acc[:cut].astype(outs[0].dtype)
        outs[1][...] = acc[cut:].astype(outs[1].dtype)


def backward(meta, slopes, ws, delta, firsts, acc, bit, out_type):
    rows = slopes[0].shape[0]
    slots, feats = ws[0].shape[0], ws[0].shape[1]
    blocks, bs = delta.shape[0], delta.shape[1]
    every = bit is None
    tiles = 4 if every else 2
    size = feats // tiles
    width = sum(s.shape[1] for s in slopes)
    steps = slots if every else 1

    def slot_of(step, meta):
        return step if every else meta[PARTS + bit]

    whole = pl.BlockSpec((1, rows, size), lambda s, i, m: (slot_of(s, m), 0, i))
    half = pl.BlockSpec((rows // 2, size), lambda s, i, m: (0, i))
    if every:
        out_specs = [whole]
        out_shape = [jax.ShapeDtypeStruct((slots, rows, feats), F32)]
    else:
        out_specs = [half, half]
        out_shape = [jax.ShapeDtypeStruct((rows // 2, feats), out_type)] * 2
    return pl.pallas_call(
        functools.partial(backward_kernel, firsts, blocks, bs, acc is not None, bit),
        grid_spec=pltpu.PrefetchScalarGridSpec(
            num_scalar_prefetch=1,
            grid=(steps, tiles),
            in_specs=[
                pl.BlockSpec(s.shape, lambda s, i, m: (0, 0), pipeline_mode=pl.Buffered(1))
                for s in slopes
            ]
            + [
                pl.BlockSpec((1, size, w.shape[2]), lambda s, i, m: (slot_of(s, m), i, 0))
                for w in ws
            ]
            + [pl.BlockSpec(delta.shape, lambda s, i, m: (0, 0, 0))]
            + ([] if acc is None else [whole]),
            out_specs=out_specs,
            scratch_shapes=[pltpu.VMEM((rows, size), F32)],
        ),
        out_shape=out_shape,
        compiler_params=params(),
        cost_estimate=pl.CostEstimate(
            flops=2 * rows * feats * width * steps if every else 1,
            bytes_accessed=2 * (rows + feats) * width * steps if every else 1,
            transcendentals=0,
        ),
    )(meta, *slopes, *ws, delta, *([] if acc is None else [acc]))


def grads_kernel(firsts, sizes, meta, x_ref, *refs):
    slopes, (own_ref, peer_ref) = refs[:-2], refs[-2:]
    col = meta[BLOCKS + 4 * pl.program_id(0) + 3]
    own_ref[...] = jnp.zeros_like(own_ref)
    peer_ref[...] = jnp.zeros_like(peer_ref)
    rows = x_ref.shape[1] // 2
    for first, size, slope in zip(firsts, sizes, slopes):

        @pl.when((col >= first) & (col < first + size))
        def _():
            dims = (((0,), (0,)), ((), ()))
            own_ref[0] = lax.dot_general(
                x_ref[0, :rows], slope[:rows], dims, preferred_element_type=F32
            )
            peer_ref[0] = lax.dot_general(
                x_ref[0, rows:], slope[rows:], dims, preferred_element_type=F32
            ).astype(BF)


def block_sums(meta, x4, slopes, firsts, blocks, bs):
    rows = x4.shape[1]
    sizes = [s.shape[1] for s in slopes]

    def slope_spec(first, size):
        def index(n, m):
            return 0, jnp.clip((m[BLOCKS + 4 * n + 3] - first) // bs, 0, size // bs - 1)

        return pl.BlockSpec((rows, bs), index)

    out = pl.BlockSpec((1, bs, bs), lambda n, m: (n, 0, 0))
    return pl.pallas_call(
        functools.partial(grads_kernel, firsts, sizes),
        grid_spec=pltpu.PrefetchScalarGridSpec(
            num_scalar_prefetch=1,
            grid=(blocks,),
            in_specs=[
                pl.BlockSpec(
                    (1, rows, bs),
                    lambda n, m: (m[BLOCKS + 4 * n], 0, m[BLOCKS + 4 * n + 2] // bs),
                )
            ]
            + [slope_spec(f, z) for f, z in zip(firsts, sizes)],
            out_specs=[out, out],
        ),
        out_shape=[
            jax.ShapeDtypeStruct((blocks, bs, bs), F32),
            jax.ShapeDtypeStruct((blocks, bs, bs), BF),
        ],
        compiler_params=params(),
        cost_estimate=pl.CostEstimate(
            flops=1, bytes_accessed=1, transcendentals=0
        ),
    )(meta, x4, *slopes)


def slot_ranks(owners):
    owner_ids = owners[:, 0]
    order = jnp.arange(owner_ids.shape[0], dtype=jnp.int32)
    earlier = (owner_ids[None, :] == owner_ids[:, None]) & (order[None, :] < order[:, None])
    rank = jnp.sum(earlier.astype(jnp.int32), axis=1)
    return (owner_ids[None, :] == lax.axis_index("dp")) & (
        rank[None, :] == jnp.arange(CAP, dtype=jnp.int32)[:, None]
    )


def pick_slots(owners, total):
    wanted = slot_ranks(owners)
    return jnp.sum(jnp.where(wanted[:, :, None, None], total[None], 0.0), axis=1)[None]


def tie(value, *after):
    return lax.optimization_barrier((value,) + after)[0]


def piece_sizes(half, bs):
    last = max(half // bs // 5, 1) * bs
    return [half - last, last]


def local(tokens, frozen, delta, block_rows, block_cols, owners, d_out):
    group, me_dp, me_t = (lax.axis_index(a) for a in ("groups", "dp", "tensor"))
    n_dp, n_t = lax.axis_size("dp"), lax.axis_size("tensor")
    rows, feats = tokens.shape
    blocks, bs = delta.shape[0], delta.shape[1]
    slab = frozen.shape[1]
    half = slab // 2
    mine, theirs = group * half, (1 - group) * half
    sizes = piece_sizes(half, bs)
    firsts = [sum(sizes[:p]) for p in range(len(sizes))]

    shards = [
        lax.dynamic_slice(frozen, (0, mine + first), (frozen.shape[0], size))
        for first, size in zip(firsts, sizes)
    ]
    gather_a = lax.all_gather(shards[0], "dp")
    gather_b = lax.all_gather(tie(shards[1], gather_a), "dp")
    gathered = [gather_a, gather_b]

    row_part = block_rows * bs // feats
    block_info = jnp.stack(
        [
            row_part ^ me_t,
            row_part,
            block_rows * bs - row_part * feats,
            block_cols * bs - (me_t * slab + mine),
        ],
        axis=1,
    )
    meta = jnp.concatenate([jnp.arange(n_t, dtype=jnp.int32) ^ me_t, block_info.reshape(-1)])

    peer = swap(tokens, "groups", 1)
    own_x = swap(tokens, "tensor", 2)
    peer_x = swap(peer, "tensor", 2)
    near_x = jnp.concatenate([tokens, peer], axis=0)
    far_x = jnp.concatenate([own_x, peer_x], axis=0)
    x4 = jnp.stack([near_x, swap(near_x, "tensor", 1), far_x, swap(far_x, "tensor", 1)])

    order = peer_x
    d_pieces = []
    for first, size in zip(firsts, sizes):
        give = lax.dynamic_slice(d_out, (0, theirs + first), (rows, size))
        keep = lax.dynamic_slice(d_out, (0, mine + first), (rows, size))
        got = swap(tie(give, order), "groups", 1)
        order = got
        d_pieces.append(jnp.concatenate([keep, got], axis=0))

    act_a, slope_a = forward(meta, x4, gather_a, delta, d_pieces[0], firsts[0], 2)
    back_a = swap(act_a[1], "groups", 1)
    (early,) = backward(meta, [slope_a], [gather_a], delta, firsts[:1], None, None, None)
    activated = jnp.zeros((rows, slab), BF)
    activated = lax.dynamic_update_slice(activated, act_a[0], (0, mine + firsts[0]))
    activated = lax.dynamic_update_slice(activated, back_a, (0, theirs + firsts[0]))

    delta_b = tie(delta, early, activated)
    act_b, slope_b = forward(meta, x4, gather_b, delta_b, d_pieces[1], firsts[1], 2)
    back_b = swap(act_b[1], "groups", 1)
    slopes = [slope_a, slope_b]

    def back_of(bit, out_type, *wait):
        d = tie(delta_b, *wait) if wait else delta_b
        return backward(meta, [slope_b], [gather_b], d, firsts[1:], early, bit, out_type)

    far_own_give, far_peer_give = back_of(3, BF)
    far_peer_got = swap(far_peer_give, "tensor", 1)
    far_own_got = swap(far_own_give, "tensor", 1)
    own_sum, peer_sum = block_sums(
        meta, x4, [slope_a, tie(slope_b, far_peer_give)], firsts, blocks, bs
    )
    sums = own_sum + swap(peer_sum, "groups", 1).astype(F32)
    shares = [swap(sums.astype(BF), "dp", bit) for bit in range(1, n_dp)]
    activated = lax.dynamic_update_slice(activated, act_b[0], (0, mine + firsts[1]))
    activated = lax.dynamic_update_slice(activated, back_b, (0, theirs + firsts[1]))
    far_own, far_peer = back_of(2, F32, far_peer_give, peer_sum)
    far_peer = (far_peer + far_peer_got.astype(F32)).astype(BF)
    diagonal = [(i, i ^ (n_t + 2)) for i in range(2 * n_t)]
    from_xy = lax.ppermute(far_peer, ("groups", "tensor"), diagonal)
    far_own = (far_own + far_own_got.astype(F32)).astype(BF)
    from_x = swap(far_own, "tensor", 2)
    near_own_give, near_peer_give = back_of(1, BF, far_peer, far_own, sums)
    near_peer_got = swap(near_peer_give, "tensor", 1)
    near_own_got = swap(near_own_give, "tensor", 1)
    near_own, near_peer = back_of(0, F32, near_peer_give, activated, *shares)
    near_peer = (near_peer + near_peer_got.astype(F32)).astype(BF)
    from_y = swap(near_peer, "groups", 1)
    near_own = near_own + near_own_got.astype(F32)
    d_tokens = near_own + from_y.astype(F32) + from_x.astype(F32) + from_xy.astype(F32)
    for share in shares:
        sums = sums + share.astype(F32)
    norm = float(rows * n_dp) ** (-0.5)
    return (activated, d_tokens.astype(BF), pick_slots(owners, sums * norm))


def local_any(tokens, frozen, delta, block_rows, block_cols, owners, d_out):
    me_dp, me_t, n_dp = lax.axis_index("dp"), lax.axis_index("tensor"), lax.axis_size("dp")
    rows = tokens.shape[0]
    blocks, bs = delta.shape[0], delta.shape[1]
    slab = frozen.shape[1]
    x_full = lax.all_gather(tokens, "tensor", axis=1, tiled=True)
    weight = lax.all_gather(frozen, "dp", axis=0, tiled=True)
    width = x_full.shape[1]
    row_pick = (block_rows[:, None] == jnp.arange(width // bs)[None, :]).astype(F32)
    cols_here = block_cols - me_t * (slab // bs)
    col_pick = (cols_here[:, None] == jnp.arange(slab // bs)[None, :]).astype(F32)
    highest = lax.Precision.HIGHEST
    xb = jnp.take(x_full.reshape(rows, width // bs, bs), block_rows, axis=1)
    contrib = jnp.einsum("tnk,nkc->tnc", xb, delta, preferred_element_type=F32)
    add = jnp.einsum("tnc,nm->tmc", contrib, col_pick, precision=highest).reshape(rows, slab)
    preact = jnp.dot(x_full, weight, preferred_element_type=F32) + add
    squash = jax.nn.sigmoid(preact)
    activated = (preact * squash).astype(BF)
    d_pre = (d_out.astype(F32) * squash * (1.0 + preact * (1.0 - squash))).astype(BF)
    d_rows = lax.dot_general(
        d_pre, weight, (((1,), (1,)), ((), ())), preferred_element_type=F32
    )
    dy = jnp.take(d_pre.reshape(rows, slab // bs, bs), cols_here, axis=1)
    back = jnp.einsum("tnc,nkc->tnk", dy, delta, preferred_element_type=F32)
    back = jnp.einsum("tnk,nr->trk", back, row_pick, precision=highest).reshape(rows, width)
    d_tokens = lax.psum_scatter(
        (d_rows + back).astype(BF), "tensor", scatter_dimension=1, tiled=True
    )
    grads = jnp.einsum("tnk,tnc->nkc", xb, dy, preferred_element_type=F32)
    everyone = lax.all_gather(grads.astype(BF), "dp", axis=0).astype(F32)
    norm = float(rows * n_dp) ** (-0.5)
    return (activated, d_tokens, pick_slots(owners, jnp.sum(everyone, axis=0) * norm))


def solution(mesh):
    sizes = dict(mesh.shape)
    small = sizes["groups"] == 2 and sizes["dp"] == 4 and sizes["tensor"] == 4
    body = local if small else local_any
    in_specs = (
        P(("groups", "dp"), "tensor"),
        P("dp", "tensor"),
        P("tensor", None, None),
        P("tensor"),
        P("tensor"),
        P("tensor", None),
        P(("groups", "dp"), "tensor"),
    )
    out_specs = (
        P(("groups", "dp"), "tensor"),
        P(("groups", "dp"), "tensor"),
        P("tensor", ("groups", "dp"), None, None),
    )
    return jax.shard_map(body, mesh=mesh, in_specs=in_specs, out_specs=out_specs, check_vma=False)
```

time: 431 us -> 405 us (0.940)
  waiting for transfers between devices: 204 us -> 236 us
  between operations: 32.3 us -> 14.3 us
  local copies, waits for them, and re-layouts: 39.9 us -> 23.7 us
  starting transfers between devices: 30.8 us -> 21.1 us
  other arithmetic: 30.3 us -> 23.1 us
  Pallas kernels: 90 us -> 85.1 us
    ppermute x5 -> x1, waiting for transfers between devices: 158 us -> 11.2 us  [local(): from_xy = lax.ppermute(far_peer, ('groups', 'tensor'), diagonal)]
    all_gather x2, waiting for transfers between devices: 0.02 us -> 141 us  [the longest x1 141 us: local(): gather_a = lax.all_gather(shards[0], 'dp')]
    ppermute x23 -> x19, waiting for transfers between devices: 46.4 us -> 82.9 us  [swap(): return lax.ppermute(array, axis, [(i, i ^ bit) for i in range(size)])]
    another operation x10 -> x4, other arithmetic: 8.3 us -> 0.04 us  [local(): jnp.stack([row_part ^ me_t, row_part, block_rows * bs - row_part * feats,...]
    ppermute x5 -> x1, starting transfers between devices: 9.21 us -> 2.75 us  [local(): from_xy = lax.ppermute(far_peer, ('groups', 'tensor'), diagonal)]
    pallas_call x5, Pallas kernels: 50.8 us -> 45.1 us  [backward(): pl.pallas_call(functools.partial(backward_kernel, firsts, blocks, bs, acc...]
    pallas_call x0 -> x1, Pallas kernels: none -> 4.91 us  [block_sums(): pl.pallas_call(functools.partial(grads_kernel, firsts, sizes), grid_spec=...]
    convert_element_type x2 -> x4, other arithmetic: 1.43 us -> 6.05 us  [the longest x1 2.18 us: local(): near_peer = (near_peer + near_peer_got.astype(F32)).astype(BF)]
  transfers between devices with their start and end apart: 30 -> 22, of which waited for: 10 -> 8; matrix products, arithmetic and copies ran while one was open for 15% -> 9% of each run, Pallas kernels for 17% -> 16%
where the time goes in v5:
time: 405 us; the launch traced here: 403 us
  waiting for transfers between devices  236 us (58%)
  Pallas kernels  85.1 us (21%)
  local copies, waits for them, and re-layouts  23.7 us (6%)
  other arithmetic  23.1 us (6%)
  starting transfers between devices  21.1 us (5%)
  between operations  14.3 us (4%)
    all_gather x1, waiting for transfers between devices, local(): gather_a = lax.all_gather(shards[0], 'dp')  141 us
    ppermute x19, waiting for transfers between devices, swap(): return lax.ppermute(array, axis, [(i, i ^ bit) for i in range(size)])  82.9 us
    pallas_call x5, Pallas kernels, backward(): pl.pallas_call(functools.partial(backward_kernel, firsts, blocks, bs, acc...  45.1 us
    pallas_call x2, Pallas kernels, forward(): pl.pallas_call(functools.partial(forward_kernel, first, blocks, bs), grid...  35 us
    ppermute x19, starting transfers between devices, swap(): return lax.ppermute(array, axis, [(i, i ^ bit) for i in range(size)])  18.2 us
    ppermute x1, waiting for transfers between devices, local(): from_xy = lax.ppermute(far_peer, ('groups', 'tensor'), diagonal)  11.2 us
  transfers between devices with their start and end apart: 22, of which 8 were waited for; matrix products, arithmetic and copies ran while one was open for 9% of the time, Pallas kernels for 16%

profile of v5, /device:TPU:0, one launch (start us, length us, event | category | flops | bytes accessed | tf_op | source)
XLA Modules:
  0.0 402.8 jit_solution(599635911557051234)
XLA Ops:
  7.2 3.8 constant_dynamic-slice_fusion.5
  12.2 3.0 collective-permute-start
  15.1 1.5 collective-permute-start.2
  16.6 19.0 %collective-permute-done = bf16[448,1024]{1,0:T(8,128)(2,1)} collective-permute-done((bf16[448,1024]{1,0:T(8,128)(2,1)S(1)}, bf16[448,1024]{1,0:T(8,128)(2,1)}, u32[]{:S(2)}, u32[]{:S(2)}) %collective-permute-start) | collective-permute-done | bytes 917536 | tf_op jit(solution)/shard_map/ppermute | solution.py:18
  35.6 1.7 collective-permute-start.3
  38.3 3.1 constant_dynamic-slice_fusion.4
  41.4 2.2 constant_dynamic-update-slice_fusion
  44.8 12.6 %collective-permute-done.3 = bf16[448,1024]{1,0:T(8,128)(2,1)} collective-permute-done((bf16[448,1024]{1,0:T(8,128)(2,1)}, bf16[448,1024]{1,0:T(8,128)(2,1)}, u32[]{:S(2)}, u32[]{:S(2)}) %collective-permute-start.3) | collective-permute-done | bytes 917536 | tf_op jit(solution)/shard_map/ppermute | solution.py:18
  61.5 1.9 constant_dynamic-slice_fusion.1
  63.4 2.1 constant_dynamic-slice_fusion.2
  65.5 22.7 %collective-permute-done.5 = bf16[448,1536]{1,0:T(8,128)(2,1)} collective-permute-done((bf16[448,1536]{1,0:T(8,128)(2,1)}, bf16[448,1536]{1,0:T(8,128)(2,1)}, u32[]{:S(2)}, u32[]{:S(2)}) %collective-permute-start.5) | collective-permute-done | bytes 1376288 | tf_op jit(solution)/shard_map/ppermute | solution.py:18
  90.6 141.4 %all-gather.5.cloned.1.call-done = bf16[4096,1536]{1,0:T(8,128)(2,1)} async-done(((bf16[1024,1536]{1,0:T(8,128)(2,1)}), bf16[4096,1536]{1,0:T(8,128)(2,1)}) %all-gather.5.cloned.1.call-update) | async-done | bytes 12582928 | tf_op jit(solution)/shard_map/all_gather | solution.py:273
  232.1 3.1 pad_maximum_fusion.1.d_ref
  235.1 1.9 pad_maximum_fusion.2.d_ref
  237.1 6.3 %pad_maximum_fusion.x_ref = bf16[4,896,1024]{2,1,0:T(8,128)(2,1)} fusion(bf16[1,896,1024]{2,1,0:T(8,128)(2,1)} %bitcast.7, bf16[1,896,1024]{2,1,0:T(8,128)(2,1)S(1)} %bitcast.29, bf16[1,896,1024]{2,1,0:T(8,128)(2,1)} %bitcast.5, bf16[1,896,1024]{2,1,0:T(8,128)(2,1)} %bitcast.4), kind=kLoop, calls=%fused_computation | loop fusion | flops 11010048 | bytes 14680064 | tf_op jit(solution)/shard_map/stack | solution.py:294
  243.3 25.2 %shard_map.94 = (bf16[2,448,1536]{2,1,0:T(8,128)(2,1)}, bf16[896,1536]{1,0:T(8,128)(2,1)}) custom-call(s32[20]{0:T(128)} %pad_add_fusion.1.meta, bf16[4,896,1024]{2,1,0:T(8,128)(2,1)} %pad_maximum_fusion.x_ref, bf16[4,1024,1536]{2,1,0:T(8,128)(2,1)} %bitcast.32, bf16[4,128,128]{2,1,0:T(8,128)(2,1)} %refs_2_.5, bf16[896,1536]{1,0:T(8,128)(2,1)} %pad_maximum_fusion.1.d_ref), custom_call_target="tpu_custom_call" | custom-call | flops 11274289152 | bytes 19922944 | tf_op jit(solution)/shard_map/pallas_call | solution.py:62
  271.9 23.9 %shard_map.95.refs_3_ = f32[4,896,1024]{2,1,0:T(8,128)} custom-call(s32[20]{0:T(128)} %pad_add_fusion.1.meta, bf16[896,1536]{1,0:T(8,128)(2,1)} %get-tuple-element.28.refs_0_, bf16[4,1024,1536]{2,1,0:T(8,128)(2,1)} %bitcast.33, bf16[4,128,128]{2,1,0:T(8,128)(2,1)} %refs_2_.5), custom_call_target="tpu_custom_call" | custom-call | flops 11274289152 | bytes 23592960 | tf_op jit(solution)/shard_map/pallas_call | solution.py:151
  295.8 6.2 %collective-permute-done.6 = bf16[448,1536]{1,0:T(8,128)(2,1)S(1)} collective-permute-done((bf16[448,1536]{1,0:T(8,128)(2,1)S(1)}, bf16[448,1536]{1,0:T(8,128)(2,1)S(1)}, u32[]{:S(2)}, u32[]{:S(2)}) %collective-permute-start.6) | collective-permute-done | bytes 1376288 | tf_op jit(solution)/shard_map/ppermute | solution.py:18
  302.1 9.8 %shard_map.96 = (bf16[2,448,384]{2,1,0:T(8,128)(2,1)}, bf16[896,384]{1,0:T(8,128)(2,1)}) custom-call(s32[20]{0:T(128)} %pad_add_fusion.1.meta, bf16[4,896,1024]{2,1,0:T(8,128)(2,1)} %pad_maximum_fusion.x_ref, bf16[4,1024,384]{2,1,0:T(8,128)(2,1)} %bitcast.24, bf16[4,128,128]{2,1,0:T(8,128)(2,1)} %refs_2_.5, bf16[896,384]{1,0:T(8,128)(2,1)} %pad_maximum_fusion.2.d_ref), custom_call_target="tpu_custom_call" | custom-call | flops 2818572288 | bytes 10485760 | tf_op jit(solution)/shard_map/pallas_call | solution.py:62
  311.9 5.1 %shard_map.97 = (bf16[448,1024]{1,0:T(8,128)(2,1)}, bf16[448,1024]{1,0:T(8,128)(2,1)}) custom-call(s32[20]{0:T(128)} %pad_add_fusion.1.meta, bf16[896,384]{1,0:T(8,128)(2,1)} %get-tuple-element.34.refs_0_.refs_1_, bf16[4,1024,384]{2,1,0:T(8,128)(2,1)} %bitcast.25, bf16[4,128,128]{2,1,0:T(8,128)(2,1)} %refs_2_.5, f32[4,896,1024]{2,1,0:T(8,128)} %shard_map.95.refs_3_), custom_call_target="tpu_custom_call" | custom-call | flops 1 | bytes 1 | tf_op jit(solution)/shard_map/pallas_call | solution.py:151
  317.5 4.9 %shard_map.98 = (f32[4,128,128]{2,1,0:T(8,128)}, bf16[4,128,128]{2,1,0:T(8,128)(2,1)}) custom-call(s32[20]{0:T(128)} %pad_add_fusion.1.meta, bf16[4,896,1024]{2,1,0:T(8,128)(2,1)} %pad_maximum_fusion.x_ref, bf16[896,1536]{1,0:T(8,128)(2,1)} %get-tuple-element.28.refs_0_, bf16[896,384]{1,0:T(8,128)(2,1)} %get-tuple-element.34.refs_0_.refs_1_), custom_call_target="tpu_custom_call" | custom-call | flops 1 | bytes 1 | tf_op jit(solution)/shard_map/pallas_call | solution.py:209
  323.1 5.4 %shard_map.99 = (f32[448,1024]{1,0:T(8,128)}, f32[448,1024]{1,0:T(8,128)}) custom-call(s32[20]{0:T(128)} %pad_add_fusion.1.meta, bf16[896,384]{1,0:T(8,128)(2,1)} %get-tuple-element.34.refs_0_.refs_1_, bf16[4,1024,384]{2,1,0:T(8,128)(2,1)} %bitcast.26, bf16[4,128,128]{2,1,0:T(8,128)(2,1)} %refs_2_.5, f32[4,896,1024]{2,1,0:T(8,128)} %shard_map.95.refs_3_), custom_call_target="tpu_custom_call" | custom-call | flops 1 | bytes 1 | tf_op jit(solution)/shard_map/pallas_call | solution.py:151
  329.3 2.9 add_convert_fusion.3
  333.5 5.1 %shard_map.100 = (bf16[448,1024]{1,0:T(8,128)(2,1)}, bf16[448,1024]{1,0:T(8,128)(2,1)}) custom-call(s32[20]{0:T(128)} %pad_add_fusion.1.meta, bf16[896,384]{1,0:T(8,128)(2,1)} %get-tuple-element.34.refs_0_.refs_1_, bf16[4,1024,384]{2,1,0:T(8,128)(2,1)} %bitcast.27, bf16[4,128,128]{2,1,0:T(8,128)(2,1)} %refs_2_.5, f32[4,896,1024]{2,1,0:T(8,128)} %shard_map.95.refs_3_), custom_call_target="tpu_custom_call" | custom-call | flops 1 | bytes 1 | tf_op jit(solution)/shard_map/pallas_call | solution.py:151
  341.7 3.4 collective-permute-start.14
  346.1 4.1 %collective-permute-done.8 = bf16[448,384]{1,0:T(8,128)(2,1)} collective-permute-done((bf16[448,384]{1,0:T(8,128)(2,1)}, bf16[448,384]{1,0:T(8,128)(2,1)}, u32[]{:S(2)}, u32[]{:S(2)}) %collective-permute-start.8) | collective-permute-done | bytes 344096 | tf_op jit(solution)/shard_map/ppermute | solution.py:18
  351.3 2.8 collective-permute-start.19
  354.1 5.6 %shard_map.101 = (f32[448,1024]{1,0:T(8,128)}, f32[448,1024]{1,0:T(8,128)}) custom-call(s32[20]{0:T(128)} %pad_add_fusion.1.meta, bf16[896,384]{1,0:T(8,128)(2,1)} %get-tuple-element.34.refs_0_.refs_1_, bf16[4,1024,384]{2,1,0:T(8,128)(2,1)} %bitcast.28, bf16[4,128,128]{2,1,0:T(8,128)(2,1)} %refs_2_.5, f32[4,896,1024]{2,1,0:T(8,128)} %shard_map.95.refs_3_), custom_call_target="tpu_custom_call" | custom-call | flops 1 | bytes 1 | tf_op jit(solution)/shard_map/pallas_call | solution.py:151
  359.9 2.2 add_convert_fusion.1
  364.6 11.2 %collective-permute-done.19 = bf16[448,1024]{1,0:T(8,128)(2,1)S(1)} collective-permute-done((bf16[448,1024]{1,0:T(8,128)(2,1)}, bf16[448,1024]{1,0:T(8,128)(2,1)S(1)}, u32[]{:S(2)}, u32[]{:S(2)}) %collective-permute-start.19) | collective-permute-done | bytes 917536 | tf_op jit(solution)/shard_map/ppermute | solution.py:334
  375.7 18.4 %collective-permute-done.18 = bf16[448,1024]{1,0:T(8,128)(2,1)S(1)} collective-permute-done((bf16[448,1024]{1,0:T(8,128)(2,1)}, bf16[448,1024]{1,0:T(8,128)(2,1)S(1)}, u32[]{:S(2)}, u32[]{:S(2)}) %collective-permute-start.18) | collective-permute-done | bytes 917536 | tf_op jit(solution)/shard_map/ppermute | solution.py:18
  394.1 1.8 add_convert_fusion
  (82 shorter events, 24.5 us)
Async XLA Ops:
  7.2 224.9 %all-gather.5.cloned.1.call-start = ((), (), s32[]{:S(2)}) async-start(), calls=%async_computation | async-start | bytes 15728640 | tf_op jit(solution)/shard_map/all_gather | solution.py:273
  11.0 291.1 %all-gather.7.cloned.1.call-start = ((), (), s32[]{:S(2)}) async-start(), calls=%async_computation.1 | async-start | bytes 3932160 | tf_op jit(solution)/shard_map/all_gather | solution.py:274
  12.2 23.4 %collective-permute-start = (bf16[448,1024]{1,0:T(8,128)(2,1)S(1)}, bf16[448,1024]{1,0:T(8,128)(2,1)}, u32[]{:S(2)}, u32[]{:S(2)}) collective-permute-start(bf16[448,1024]{1,0:T(8,128)(2,1)S(1)} %copy-done.5), channel_id=1, source_target_pairs={{0,16},{16,0},{1,17},{17,1},{2,18},{18,2},{3,19},{19,3},{4,20},{20... | collective-permute-start | bytes 2752520 | tf_op jit(solution)/shard_map/ppermute | solution.py:18
  15.1 28.4 %collective-permute-start.2 = (bf16[448,1024]{1,0:T(8,128)(2,1)S(1)}, bf16[448,1024]{1,0:T(8,128)(2,1)}, u32[]{:S(2)}, u32[]{:S(2)}) collective-permute-start(bf16[448,1024]{1,0:T(8,128)(2,1)S(1)} %copy-done.5), channel_id=1, source_target_pairs={{0,2},{1,3},{2,0},{3,1},{4,6},{5,7},{6,4},{7,5},{8,10},{9,11},{10,... | collective-permute-start | bytes 2752520 | tf_op jit(solution)/shard_map/ppermute | solution.py:18
  35.6 21.9 %collective-permute-start.3 = (bf16[448,1024]{1,0:T(8,128)(2,1)}, bf16[448,1024]{1,0:T(8,128)(2,1)}, u32[]{:S(2)}, u32[]{:S(2)}) collective-permute-start(bf16[448,1024]{1,0:T(8,128)(2,1)} %collective-permute-done), channel_id=1, source_target_pairs={{0,2},{1,3},{2,0},{3,1},{4,6},{5,7},{6,4},{7,5},{8,10},{9,11},{10,... | collective-permute-start | bytes 2752520 | tf_op jit(solution)/shard_map/ppermute | solution.py:18
  43.6 16.6 %copy-start.8 = (s32[4]{0:T(128)S(1)}, s32[4]{0:T(128)}, u32[]{:S(2)}) copy-start(s32[4]{0:T(128)} %param.10) | copy-start | bytes 52
  43.6 16.7 %copy-start.10 = (s32[4]{0:T(128)S(1)}, s32[4]{0:T(128)}, u32[]{:S(2)}) copy-start(s32[4]{0:T(128)} %param.11) | copy-start | bytes 52
  43.6 193.5 %collective-permute-start.1 = (bf16[896,1024]{1,0:T(8,128)(2,1)}, bf16[896,1024]{1,0:T(8,128)(2,1)}, u32[]{:S(2)}, u32[]{:S(2)}) collective-permute-start(bf16[896,1024]{1,0:T(8,128)(2,1)} %constant_dynamic-update-slice_fusion), channel_id=1, source_target_pairs={{0,1},{1,0},{2,3},{3,2},{4,5},{5,4},{6,7},{7,6},{8,9},{9,8},{10,11... | collective-permute-start | bytes 5505032 | tf_op jit(solution)/shard_map/ppermute | solution.py:18
  57.4 30.8 %collective-permute-start.5 = (bf16[448,1536]{1,0:T(8,128)(2,1)}, bf16[448,1536]{1,0:T(8,128)(2,1)}, u32[]{:S(2)}, u32[]{:S(2)}) collective-permute-start(bf16[448,1536]{1,0:T(8,128)(2,1)} %get-tuple-element.25), channel_id=1, source_target_pairs={{0,16},{16,0},{1,17},{17,1},{2,18},{18,2},{3,19},{19,3},{4,20},{20... | collective-permute-start | bytes 4128776 | tf_op jit(solution)/shard_map/ppermute | solution.py:18
  60.1 177.0 %collective-permute-start.4 = (bf16[896,1024]{1,0:T(8,128)(2,1)S(1)}, bf16[896,1024]{1,0:T(8,128)(2,1)}, u32[]{:S(2)}, u32[]{:S(2)}) collective-permute-start(bf16[896,1024]{1,0:T(8,128)(2,1)S(1)} %constant_dynamic-update-slice_fusion.2), channel_id=1, source_target_pairs={{0,1},{1,0},{2,3},{3,2},{4,5},{5,4},{6,7},{7,6},{8,9},{9,8},{10,11... | collective-permute-start | bytes 5505032 | tf_op jit(solution)/shard_map/ppermute | solution.py:18
  88.2 147.0 %collective-permute-start.7 = (bf16[448,384]{1,0:T(8,128)(2,1)}, bf16[448,384]{1,0:T(8,128)(2,1)}, u32[]{:S(2)}, u32[]{:S(2)}) collective-permute-start(bf16[448,384]{1,0:T(8,128)(2,1)} %get-tuple-element.30), channel_id=1, source_target_pairs={{0,16},{16,0},{1,17},{17,1},{2,18},{18,2},{3,19},{19,3},{4,20},{20... | collective-permute-start | bytes 1032200 | tf_op jit(solution)/shard_map/ppermute | solution.py:18
  270.0 32.0 %collective-permute-start.6 = (bf16[448,1536]{1,0:T(8,128)(2,1)S(1)}, bf16[448,1536]{1,0:T(8,128)(2,1)S(1)}, u32[]{:S(2)}, u32[]{:S(2)}) collective-permute-start(bf16[448,1536]{1,0:T(8,128)(2,1)S(1)} %slice_bitcast_fusion), channel_id=1, source_target_pairs={{0,16},{16,0},{1,17},{17,1},{2,18},{18,2},{3,19},{19,3},{4,20},{20... | collective-permute-start | bytes 4128776 | tf_op jit(solution)/shard_map/ppermute | solution.py:18
  317.0 12.3 %collective-permute-start.9 = (bf16[448,1024]{1,0:T(8,128)(2,1)}, bf16[448,1024]{1,0:T(8,128)(2,1)S(1)}, u32[]{:S(2)}, u32[]{:S(2)}) collective-permute-start(bf16[448,1024]{1,0:T(8,128)(2,1)} %get-tuple-element.33), channel_id=1, source_target_pairs={{0,1},{1,0},{2,3},{3,2},{4,5},{5,4},{6,7},{7,6},{8,9},{9,8},{10,11... | collective-permute-start | bytes 2752520 | tf_op jit(solution)/shard_map/ppermute | solution.py:18
  317.0 15.2 %collective-permute-start.10 = (bf16[448,1024]{1,0:T(8,128)(2,1)}, bf16[448,1024]{1,0:T(8,128)(2,1)S(1)}, u32[]{:S(2)}, u32[]{:S(2)}) collective-permute-start(bf16[448,1024]{1,0:T(8,128)(2,1)} %get-tuple-element.39), channel_id=1, source_target_pairs={{0,1},{1,0},{2,3},{3,2},{4,5},{5,4},{6,7},{7,6},{8,9},{9,8},{10,11... | collective-permute-start | bytes 2752520 | tf_op jit(solution)/shard_map/ppermute | solution.py:18
  322.4 6.1 %copy-start.7 = (f32[4,128,128]{2,1,0:T(8,128)S(1)}, f32[4,128,128]{2,1,0:T(8,128)}, u32[]{:S(2)}) copy-start(f32[4,128,128]{2,1,0:T(8,128)} %get-tuple-element.40) | copy-start | bytes 786436
  322.4 6.1 %collective-permute-start.11 = (bf16[4,128,128]{2,1,0:T(8,128)(2,1)}, bf16[4,128,128]{2,1,0:T(8,128)(2,1)S(1)}, u32[]{:S(2)}, u32[]{:S(2)}) collective-permute-start(bf16[4,128,128]{2,1,0:T(8,128)(2,1)} %get-tuple-element.35), channel_id=1, source_target_pairs={{0,16},{16,0},{1,17},{17,1},{2,18},{18,2},{3,19},{19,3},{4,20},{20... | collective-permute-start | bytes 393224 | tf_op jit(solution)/shard_map/ppermute | solution.py:18
  329.3 2.9 copy-start.2
  333.5 5.6 %copy-start.6 = (bf16[2,448,384]{2,1,0:T(8,128)(2,1)S(1)}, bf16[2,448,384]{2,1,0:T(8,128)(2,1)}, u32[]{:S(2)}) copy-start(bf16[2,448,384]{2,1,0:T(8,128)(2,1)} %get-tuple-element.31) | copy-start | bytes 2064388
  338.6 21.2 %collective-permute-start.16 = (bf16[448,1024]{1,0:T(8,128)(2,1)}, bf16[448,1024]{1,0:T(8,128)(2,1)}, u32[]{:S(2)}, u32[]{:S(2)}) collective-permute-start(bf16[448,1024]{1,0:T(8,128)(2,1)} %get-tuple-element.42), channel_id=1, source_target_pairs={{0,1},{1,0},{2,3},{3,2},{4,5},{5,4},{6,7},{7,6},{8,9},{9,8},{10,11... | collective-permute-start | bytes 2752520 | tf_op jit(solution)/shard_map/ppermute | solution.py:18
  339.8 10.4 %collective-permute-start.8 = (bf16[448,384]{1,0:T(8,128)(2,1)}, bf16[448,384]{1,0:T(8,128)(2,1)}, u32[]{:S(2)}, u32[]{:S(2)}) collective-permute-start(bf16[448,384]{1,0:T(8,128)(2,1)} %slice_bitcast_fusion.1), channel_id=1, source_target_pairs={{0,16},{16,0},{1,17},{17,1},{2,18},{18,2},{3,19},{19,3},{4,20},{20... | collective-permute-start | bytes 1032200 | tf_op jit(solution)/shard_map/ppermute | solution.py:18
  340.7 13.3 %collective-permute-start.12 = (bf16[4,128,128]{2,1,0:T(8,128)(2,1)}, bf16[4,128,128]{2,1,0:T(8,128)(2,1)S(1)}, u32[]{:S(2)}, u32[]{:S(2)}) collective-permute-start(bf16[4,128,128]{2,1,0:T(8,128)(2,1)} %get-tuple-element.47), channel_id=1, source_target_pairs={{0,4},{4,0},{8,12},{12,8},{1,5},{5,1},{9,13},{13,9},{2,6},{6,2},{1... | collective-permute-start | bytes 393224 | tf_op jit(solution)/shard_map/ppermute | solution.py:18
  340.7 13.4 %collective-permute-start.13 = (bf16[4,128,128]{2,1,0:T(8,128)(2,1)}, bf16[4,128,128]{2,1,0:T(8,128)(2,1)S(1)}, u32[]{:S(2)}, u32[]{:S(2)}) collective-permute-start(bf16[4,128,128]{2,1,0:T(8,128)(2,1)} %get-tuple-element.47), channel_id=1, source_target_pairs={{0,8},{4,12},{8,0},{12,4},{1,9},{5,13},{9,1},{13,5},{2,10},{6,14},... | collective-permute-start | bytes 393224 | tf_op jit(solution)/shard_map/ppermute | solution.py:18
  341.7 12.4 %collective-permute-start.14 = (bf16[4,128,128]{2,1,0:T(8,128)(2,1)}, bf16[4,128,128]{2,1,0:T(8,128)(2,1)S(1)}, u32[]{:S(2)}, u32[]{:S(2)}) collective-permute-start(bf16[4,128,128]{2,1,0:T(8,128)(2,1)} %get-tuple-element.47), channel_id=1, source_target_pairs={{0,12},{4,8},{8,4},{12,0},{1,13},{5,9},{9,5},{13,1},{2,14},{6,10},... | collective-permute-start | bytes 393224 | tf_op jit(solution)/shard_map/ppermute | solution.py:18
  351.2 8.5 %copy-start = (bf16[448,3840]{1,0:T(8,128)(2,1)}, bf16[448,3840]{1,0:T(8,128)(2,1)S(1)}, u32[]{:S(2)}) copy-start(bf16[448,3840]{1,0:T(8,128)(2,1)S(1)} %constant_dynamic-update-slice_fusion.4) | copy-start | bytes 10321924
  351.2 8.5 %copy-start.9 = (bf16[448,1024]{1,0:T(8,128)(2,1)S(1)}, bf16[448,1024]{1,0:T(8,128)(2,1)}, u32[]{:S(2)}) copy-start(bf16[448,1024]{1,0:T(8,128)(2,1)} %get-tuple-element.45) | copy-start | bytes 2752516
  351.3 24.5 %collective-permute-start.19 = (bf16[448,1024]{1,0:T(8,128)(2,1)}, bf16[448,1024]{1,0:T(8,128)(2,1)S(1)}, u32[]{:S(2)}, u32[]{:S(2)}) collective-permute-start(bf16[448,1024]{1,0:T(8,128)(2,1)} %add_convert_fusion.3), channel_id=1, source_target_pairs={{0,18},{1,19},{2,16},{3,17},{16,2},{17,3},{18,0},{19,1},{4,22},{5,... | collective-permute-start | bytes 2752520 | tf_op jit(solution)/shard_map/ppermute | solution.py:334
  354.0 40.1 %collective-permute-start.18 = (bf16[448,1024]{1,0:T(8,128)(2,1)}, bf16[448,1024]{1,0:T(8,128)(2,1)S(1)}, u32[]{:S(2)}, u32[]{:S(2)}) collective-permute-start(bf16[448,1024]{1,0:T(8,128)(2,1)} %add_convert_fusion.2), channel_id=1, source_target_pairs={{0,2},{1,3},{2,0},{3,1},{4,6},{5,7},{6,4},{7,5},{8,10},{9,11},{10,... | collective-permute-start | bytes 2752520 | tf_op jit(solution)/shard_map/ppermute | solution.py:18
  359.7 34.4 %collective-permute-start.15 = (bf16[448,1024]{1,0:T(8,128)(2,1)S(1)}, bf16[448,1024]{1,0:T(8,128)(2,1)S(1)}, u32[]{:S(2)}, u32[]{:S(2)}) collective-permute-start(bf16[448,1024]{1,0:T(8,128)(2,1)S(1)} %copy-done.9), channel_id=1, source_target_pairs={{0,1},{1,0},{2,3},{3,2},{4,5},{5,4},{6,7},{7,6},{8,9},{9,8},{10,11... | collective-permute-start | bytes 2752520 | tf_op jit(solution)/shard_map/ppermute | solution.py:18
  359.8 3.7 copy-start.11
  359.8 3.9 copy-start.4
  359.9 34.3 %copy-start.3 = (f32[448,1024]{1,0:T(8,128)S(1)}, f32[448,1024]{1,0:T(8,128)}, u32[]{:S(2)}) copy-start(f32[448,1024]{1,0:T(8,128)} %get-tuple-element.44) | copy-start | bytes 5505028
  362.1 32.1 %collective-permute-start.17 = (bf16[448,1024]{1,0:T(8,128)(2,1)S(1)}, bf16[448,1024]{1,0:T(8,128)(2,1)S(1)}, u32[]{:S(2)}, u32[]{:S(2)}) collective-permute-start(bf16[448,1024]{1,0:T(8,128)(2,1)S(1)} %add_convert_fusion.1), channel_id=1, source_target_pairs={{0,16},{16,0},{1,17},{17,1},{2,18},{18,2},{3,19},{19,3},{4,20},{20... | collective-permute-start | bytes 2752520 | tf_op jit(solution)/shard_map/ppermute | solution.py:18
  (2 other events, 3.0 us)
Sparse Core Ops, SparseCore 0:
  11.1 220.8 all-gather.4
  234.2 61.6 all-gather.6

commit v6 on v5

--- a/solution.py
+++ b/solution.py
@@ -25,8 +25,16 @@
 PARTS, BLOCKS = 0, 4
 
 
-def forward_kernel(first, blocks, bs, meta, x_ref, w_ref, delta_ref, d_ref, act_ref, slope_ref, acc):
+def forward_kernel(
+    first, blocks, bs, cuts, meta, x_ref, w_ref, delta_ref, d_ref, act_ref, slope_ref, sum_ref, acc
+):
     width = acc.shape[1]
+    group = pl.program_id(1) // cuts
+
+    @pl.when((pl.program_id(0) == 0) & (pl.program_id(1) == 0))
+    def _():
+        sum_ref[...] = jnp.zeros_like(sum_ref)
+
     total = None
     for s in range(w_ref.shape[0]):
         term = jnp.dot(x_ref[meta[PARTS + s]], w_ref[s], preferred_element_type=F32)
@@ -50,6 +58,17 @@
     slope_ref[...] = (
         d_ref[...].astype(F32) * squash * (1.0 + preact * (1.0 - squash))
     ).astype(BF)
+    for n in range(blocks):
+        at = BLOCKS + 4 * n
+        col = meta[at + 3] - start
+
+        @pl.when((col >= 0) & (col < width))
+        def _():
+            rows = pl.ds(pl.multiple_of(meta[at + 2], bs), bs)
+            ds = slope_ref[:, pl.ds(pl.multiple_of(col, bs), bs)]
+            sum_ref[group, n] += lax.dot_general(
+                x_ref[meta[at], :, rows], ds, (((0,), (0,)), ((), ())), preferred_element_type=F32
+            )
 
 
 def forward(meta, x4, w4, delta, d_piece, first, groups_of):
@@ -60,7 +79,7 @@
     blocks, bs = delta.shape[0], delta.shape[1]
     wide = next(c for c in (512, 384, 256, 128, width) if width % c == 0)
     return pl.pallas_call(
-        functools.partial(forward_kernel, first, blocks, bs),
+        functools.partial(forward_kernel, first, blocks, bs, cuts),
         grid_spec=pltpu.PrefetchScalarGridSpec(
             num_scalar_prefetch=1,
             grid=(width // wide, groups_of * cuts),
@@ -73,12 +92,14 @@
             out_specs=[
                 pl.BlockSpec((1, tile, wide), lambda j, i, m: (i // cuts, i % cuts, j)),
                 pl.BlockSpec((tile, wide), lambda j, i, m: (i, j)),
+                pl.BlockSpec((groups_of, blocks, bs, bs), lambda j, i, m: (0, 0, 0, 0)),
             ],
             scratch_shapes=[pltpu.VMEM((tile, wide), F32)],
         ),
         out_shape=[
             jax.ShapeDtypeStruct((groups_of, rows // groups_of, width), BF),
             jax.ShapeDtypeStruct((rows, width), BF),
+            jax.ShapeDtypeStruct((groups_of, blocks, bs, bs), F32),
         ],
         compiler_params=params(),
         cost_estimate=pl.CostEstimate(
@@ -96,7 +117,8 @@
     acc_in = refs[2 * n + 1] if has_acc else None
     outs, acc = refs[2 * n + 1 + has_acc : -1], refs[-1]
     size = acc.shape[1]
-    slot = pl.program_id(0) if bit is None else meta[PARTS + bit]
+    step = pl.program_id(0)
+    slot = step if bit is None else meta[PARTS + bit - step]
     base = pl.program_id(1) * size
     total = acc_in[0] if has_acc else None
     for p in range(n):
@@ -121,13 +143,17 @@
 
     if len(outs) == 1:
         outs[0][0] = acc[...]
-    else:
-        cut = outs[0].shape[0]
-        outs[0][...] = acc[:cut].astype(outs[0].dtype)
-        outs[1][...] = acc[cut:].astype(outs[1].dtype)
-
-
-def backward(meta, slopes, ws, delta, firsts, acc, bit, out_type):
+        return
+    cut = outs[0].shape[0]
+    for at_step in range(2):
+
+        @pl.when(step == at_step)
+        def _():
+            outs[2 * at_step][...] = acc[:cut].astype(BF)
+            outs[2 * at_step + 1][...] = acc[cut:].astype(BF)
+
+
+def backward(meta, slopes, ws, delta, firsts, acc, bit):
     rows = slopes[0].shape[0]
     slots, feats = ws[0].shape[0], ws[0].shape[1]
     blocks, bs = delta.shape[0], delta.shape[1]
@@ -135,19 +161,20 @@
     tiles = 4 if every else 2
     size = feats // tiles
     width = sum(s.shape[1] for s in slopes)
-    steps = slots if every else 1
+    steps = slots if every else 2
 
     def slot_of(step, meta):
-        return step if every else meta[PARTS + bit]
+        return step if every else meta[PARTS + bit - step]
 
     whole = pl.BlockSpec((1, rows, size), lambda s, i, m: (slot_of(s, m), 0, i))
-    half = pl.BlockSpec((rows // 2, size), lambda s, i, m: (0, i))
+    give = pl.BlockSpec((rows // 2, size), lambda s, i, m: (0, jnp.where(s == 0, i, tiles - 1)))
+    keep = pl.BlockSpec((rows // 2, size), lambda s, i, m: (0, jnp.where(s == 0, 0, i)))
     if every:
         out_specs = [whole]
         out_shape = [jax.ShapeDtypeStruct((slots, rows, feats), F32)]
     else:
-        out_specs = [half, half]
-        out_shape = [jax.ShapeDtypeStruct((rows // 2, feats), out_type)] * 2
+        out_specs = [give, give, keep, keep]
+        out_shape = [jax.ShapeDtypeStruct((rows // 2, feats), BF)] * 4
     return pl.pallas_call(
         functools.partial(backward_kernel, firsts, blocks, bs, acc is not None, bit),
         grid_spec=pltpu.PrefetchScalarGridSpec(
@@ -176,61 +203,6 @@
     )(meta, *slopes, *ws, delta, *([] if acc is None else [acc]))
 
 
-def grads_kernel(firsts, sizes, meta, x_ref, *refs):
-    slopes, (own_ref, peer_ref) = refs[:-2], refs[-2:]
-    col = meta[BLOCKS + 4 * pl.program_id(0) + 3]
-    own_ref[...] = jnp.zeros_like(own_ref)
-    peer_ref[...] = jnp.zeros_like(peer_ref)
-    rows = x_ref.shape[1] // 2
-    for first, size, slope in zip(firsts, sizes, slopes):
-
-        @pl.when((col >= first) & (col < first + size))
-        def _():
-            dims = (((0,), (0,)), ((), ()))
-            own_ref[0] = lax.dot_general(
-                x_ref[0, :rows], slope[:rows], dims, preferred_element_type=F32
-            )
-            peer_ref[0] = lax.dot_general(
-                x_ref[0, rows:], slope[rows:], dims, preferred_element_type=F32
-            ).astype(BF)
-
-
-def block_sums(meta, x4, slopes, firsts, blocks, bs):
-    rows = x4.shape[1]
-    sizes = [s.shape[1] for s in slopes]
-
-    def slope_spec(first, size):
-        def index(n, m):
-            return 0, jnp.clip((m[BLOCKS + 4 * n + 3] - first) // bs, 0, size // bs - 1)
-
-        return pl.BlockSpec((rows, bs), index)
-
-    out = pl.BlockSpec((1, bs, bs), lambda n, m: (n, 0, 0))
-    return pl.pallas_call(
-        functools.partial(grads_kernel, firsts, sizes),
-        grid_spec=pltpu.PrefetchScalarGridSpec(
-            num_scalar_prefetch=1,
-            grid=(blocks,),
-            in_specs=[
-                pl.BlockSpec(
-                    (1, rows, bs),
-                    lambda n, m: (m[BLOCKS + 4 * n], 0, m[BLOCKS + 4 * n + 2] // bs),
-                )
-            ]
-            + [slope_spec(f, z) for f, z in zip(firsts, sizes)],
-            out_specs=[out, out],
-        ),
-        out_shape=[
-            jax.ShapeDtypeStruct((blocks, bs, bs), F32),
-            jax.ShapeDtypeStruct((blocks, bs, bs), BF),
-        ],
-        compiler_params=params(),
-        cost_estimate=pl.CostEstimate(
-            flops=1, bytes_accessed=1, transcendentals=0
-        ),
-    )(meta, x4, *slopes)
-
-
 def slot_ranks(owners):
     owner_ids = owners[:, 0]
     order = jnp.arange(owner_ids.shape[0], dtype=jnp.int32)
@@ -302,45 +274,41 @@
         order = got
         d_pieces.append(jnp.concatenate([keep, got], axis=0))
 
-    act_a, slope_a = forward(meta, x4, gather_a, delta, d_pieces[0], firsts[0], 2)
+    act_a, slope_a, sums_a = forward(meta, x4, gather_a, delta, d_pieces[0], firsts[0], 2)
     back_a = swap(act_a[1], "groups", 1)
-    (early,) = backward(meta, [slope_a], [gather_a], delta, firsts[:1], None, None, None)
+    (early,) = backward(meta, [slope_a], [gather_a], delta, firsts[:1], None, None)
     activated = jnp.zeros((rows, slab), BF)
     activated = lax.dynamic_update_slice(activated, act_a[0], (0, mine + firsts[0]))
     activated = lax.dynamic_update_slice(activated, back_a, (0, theirs + firsts[0]))
 
-    delta_b = tie(delta, early, activated)
-    act_b, slope_b = forward(meta, x4, gather_b, delta_b, d_pieces[1], firsts[1], 2)
+    delta_b = tie(delta, early)
+    act_b, slope_b, sums_b = forward(meta, x4, gather_b, delta_b, d_pieces[1], firsts[1], 2)
     back_b = swap(act_b[1], "groups", 1)
-    slopes = [slope_a, slope_b]
-
-    def back_of(bit, out_type, *wait):
+    activated = lax.dynamic_update_slice(activated, act_b[0], (0, mine + firsts[1]))
+    activated = lax.dynamic_update_slice(activated, back_b, (0, theirs + firsts[1]))
+
+    def back_of(bit, *wait):
         d = tie(delta_b, *wait) if wait else delta_b
-        return backward(meta, [slope_b], [gather_b], d, firsts[1:], early, bit, out_type)
-
-    far_own_give, far_peer_give = back_of(3, BF)
+        return backward(meta, [slope_b], [gather_b], d, firsts[1:], early, bit)
+
+    sums = sums_a + sums_b
+    sums = sums[0] + swap(sums[1].astype(BF), "groups", 1).astype(F32)
+    shares = [swap(sums.astype(BF), "dp", bit) for bit in range(1, n_dp)]
+    far_own_give, far_peer_give, far_own, far_peer = back_of(3)
     far_peer_got = swap(far_peer_give, "tensor", 1)
     far_own_got = swap(far_own_give, "tensor", 1)
-    own_sum, peer_sum = block_sums(
-        meta, x4, [slope_a, tie(slope_b, far_peer_give)], firsts, blocks, bs
-    )
-    sums = own_sum + swap(peer_sum, "groups", 1).astype(F32)
-    shares = [swap(sums.astype(BF), "dp", bit) for bit in range(1, n_dp)]
-    activated = lax.dynamic_update_slice(activated, act_b[0], (0, mine + firsts[1]))
-    activated = lax.dynamic_update_slice(activated, back_b, (0, theirs + firsts[1]))
-    far_own, far_peer = back_of(2, F32, far_peer_give, peer_sum)
-    far_peer = (far_peer + far_peer_got.astype(F32)).astype(BF)
+    near_own_give, near_peer_give, near_own, near_peer = back_of(1, far_peer, sums)
+    near_peer_got = swap(near_peer_give, "tensor", 1)
+    near_own_got = swap(near_own_give, "tensor", 1)
+    far_peer, far_own = tie(far_peer, near_peer, back_b, *shares), tie(far_own, near_peer)
+    far_peer = (far_peer.astype(F32) + far_peer_got.astype(F32)).astype(BF)
     diagonal = [(i, i ^ (n_t + 2)) for i in range(2 * n_t)]
     from_xy = lax.ppermute(far_peer, ("groups", "tensor"), diagonal)
-    far_own = (far_own + far_own_got.astype(F32)).astype(BF)
+    far_own = (far_own.astype(F32) + far_own_got.astype(F32)).astype(BF)
     from_x = swap(far_own, "tensor", 2)
-    near_own_give, near_peer_give = back_of(1, BF, far_peer, far_own, sums)
-    near_peer_got = swap(near_peer_give, "tensor", 1)
-    near_own_got = swap(near_own_give, "tensor", 1)
-    near_own, near_peer = back_of(0, F32, near_peer_give, activated, *shares)
-    near_peer = (near_peer + near_peer_got.astype(F32)).astype(BF)
+    near_peer = (near_peer.astype(F32) + near_peer_got.astype(F32)).astype(BF)
     from_y = swap(near_peer, "groups", 1)
-    near_own = near_own + near_own_got.astype(F32)
+    near_own = near_own.astype(F32) + near_own_got.astype(F32)
     d_tokens = near_own + from_y.astype(F32) + from_x.astype(F32) + from_xy.astype(F32)
     for share in shares:
         sums = sums + share.astype(F32)

time: 405 us -> 433 us (1.069)
  waiting for transfers between devices: 236 us -> 284 us
  other arithmetic: 23.1 us -> 15.9 us
  local copies, waits for them, and re-layouts: 23.7 us -> 16.6 us
  Pallas kernels: 85.1 us -> 79.3 us
    all_gather x1, waiting for transfers between devices: 141 us -> 171 us  [local(): gather_a = lax.all_gather(shards[0], 'dp')]
    ppermute x19, waiting for transfers between devices: 82.9 us -> 92.9 us  [swap(): return lax.ppermute(array, axis, [(i, i ^ bit) for i in range(size)])]
    ppermute x1, waiting for transfers between devices: 11.2 us -> 19.8 us  [local(): from_xy = lax.ppermute(far_peer, ('groups', 'tensor'), diagonal)]
    convert_element_type x3, other arithmetic: 6.33 us -> 1.03 us  [the longest x1 0.34 us: local(): near_peer = (near_peer.astype(F32) + near_peer_got.astype(F32)).astype(BF)]
    pallas_call x5 -> x3, Pallas kernels: 45.1 us -> 40.9 us  [backward(): pl.pallas_call(functools.partial(backward_kernel, firsts, blocks, bs, acc...]
    pallas_call x3 -> x2, Pallas kernels: 40 us -> 38.4 us  [forward(): pl.pallas_call(functools.partial(forward_kernel, first, blocks, bs, cuts)...]
  transfers between devices with their start and end apart: 22 -> 22, of which waited for: 8 -> 8; matrix products, arithmetic and copies ran while one was open for 9% -> 6% of each run, Pallas kernels for 16% -> 16%
where the time goes in v6:
time: 433 us; the launch traced here: 431 us
  waiting for transfers between devices  284 us (66%)
  Pallas kernels  79.3 us (18%)
  starting transfers between devices  21 us (5%)
  local copies, waits for them, and re-layouts  16.6 us (4%)
  other arithmetic  15.9 us (4%)
  between operations  14.4 us (3%)
    all_gather x1, waiting for transfers between devices, local(): gather_a = lax.all_gather(shards[0], 'dp')  171 us
    ppermute x19, waiting for transfers between devices, swap(): return lax.ppermute(array, axis, [(i, i ^ bit) for i in range(size)])  92.9 us
    pallas_call x3, Pallas kernels, backward(): pl.pallas_call(functools.partial(backward_kernel, firsts, blocks, bs, acc...  40.9 us
    pallas_call x2, Pallas kernels, forward(): pl.pallas_call(functools.partial(forward_kernel, first, blocks, bs, cuts)...  38.4 us
    ppermute x19, starting transfers between devices, swap(): return lax.ppermute(array, axis, [(i, i ^ bit) for i in range(size)])  20.6 us
    ppermute x1, waiting for transfers between devices, local(): from_xy = lax.ppermute(far_peer, ('groups', 'tensor'), diagonal)  19.8 us
  transfers between devices with their start and end apart: 22, of which 8 were waited for; matrix products, arithmetic and copies ran while one was open for 6% of the time, Pallas kernels for 16%

profile of v6, /device:TPU:0, one launch (start us, length us, event | category | flops | bytes accessed | tf_op | source)
XLA Modules:
  0.0 430.9 jit_solution(5916745396067990216)
XLA Ops:
  7.2 3.8 constant_dynamic-slice_fusion.5
  11.1 1.1 copy-done.2
  12.2 3.0 collective-permute-start
  15.1 1.5 collective-permute-start.2
  16.6 19.0 %collective-permute-done = bf16[448,1024]{1,0:T(8,128)(2,1)} collective-permute-done((bf16[448,1024]{1,0:T(8,128)(2,1)S(1)}, bf16[448,1024]{1,0:T(8,128)(2,1)}, u32[]{:S(2)}, u32[]{:S(2)}) %collective-permute-start) | collective-permute-done | bytes 917536 | tf_op jit(solution)/shard_map/ppermute | solution.py:18
  35.6 1.7 collective-permute-start.3
  38.3 3.1 constant_dynamic-slice_fusion.4
  41.3 2.2 constant_dynamic-update-slice_fusion
  43.5 1.2 constant_dynamic-update-slice_fusion.3
  44.8 12.5 %collective-permute-done.3 = bf16[448,1024]{1,0:T(8,128)(2,1)S(1)} collective-permute-done((bf16[448,1024]{1,0:T(8,128)(2,1)}, bf16[448,1024]{1,0:T(8,128)(2,1)S(1)}, u32[]{:S(2)}, u32[]{:S(2)}) %collective-permute-start.3) | collective-permute-done | bytes 917536 | tf_op jit(solution)/shard_map/ppermute | solution.py:18
  57.3 1.4 collective-permute-start.5
  58.9 2.1 constant_dynamic-slice_fusion.2
  61.0 171.0 %all-gather.5.cloned.1.call-done = bf16[4096,1536]{1,0:T(8,128)(2,1)} async-done(((bf16[1024,1536]{1,0:T(8,128)(2,1)}), bf16[4096,1536]{1,0:T(8,128)(2,1)}) %all-gather.5.cloned.1.call-update) | async-done | bytes 12582928 | tf_op jit(solution)/shard_map/all_gather | solution.py:245
  232.5 1.2 constant_dynamic-slice_fusion.1
  233.7 1.5 collective-permute-start.7
  235.8 3.0 pad_maximum_fusion.1.d_ref
  238.9 4.9 %collective-permute-done.7 = bf16[448,384]{1,0:T(8,128)(2,1)S(1)} collective-permute-done((bf16[448,384]{1,0:T(8,128)(2,1)S(1)}, bf16[448,384]{1,0:T(8,128)(2,1)S(1)}, u32[]{:S(2)}, u32[]{:S(2)}) %collective-permute-start.7) | collective-permute-done | bytes 344096 | tf_op jit(solution)/shard_map/ppermute | solution.py:18
  244.7 6.2 %pad_maximum_fusion.x_ref = bf16[4,896,1024]{2,1,0:T(8,128)(2,1)} fusion(bf16[1,896,1024]{2,1,0:T(8,128)(2,1)} %bitcast.7, bf16[1,896,1024]{2,1,0:T(8,128)(2,1)S(1)} %bitcast.34, bf16[1,896,1024]{2,1,0:T(8,128)(2,1)} %bitcast.5, bf16[1,896,1024]{2,1,0:T(8,128)(2,1)} %bitcast.4), kind=kLoop, calls=%fused_computation | loop fusion | flops 11010048 | bytes 14680064 | tf_op jit(solution)/shard_map/stack | solution.py:266
  250.9 27.2 %shard_map.94 = (bf16[2,448,1536]{2,1,0:T(8,128)(2,1)}, bf16[896,1536]{1,0:T(8,128)(2,1)}, f32[2,4,128,128]{3,2,1,0:T(8,128)}) custom-call(s32[20]{0:T(128)} %pad_add_fusion.1.meta, bf16[4,896,1024]{2,1,0:T(8,128)(2,1)} %pad_maximum_fusion.x_ref, bf16[4,1024,1536]{2,1,0:T(8,128)(2,1)} %bitcast.37, bf16[4,128,128]{2,1,0:T(8,128)(2,1)} %refs_2_.3, ...), custom_call_target="tpu_custom_call" | custom-call | flops 11274289152 | bytes 19922944 | tf_op jit(solution)/shard_map/pallas_call | solution.py:81
  278.0 23.9 %shard_map.95.refs_3_ = f32[4,896,1024]{2,1,0:T(8,128)} custom-call(s32[20]{0:T(128)} %pad_add_fusion.1.meta, bf16[896,1536]{1,0:T(8,128)(2,1)} %get-tuple-element.27.refs_0_, bf16[4,1024,1536]{2,1,0:T(8,128)(2,1)} %bitcast.38, bf16[4,128,128]{2,1,0:T(8,128)(2,1)} %refs_2_.3), custom_call_target="tpu_custom_call" | custom-call | flops 11274289152 | bytes 23592960 | tf_op jit(solution)/shard_map/pallas_call | solution.py:178
  302.0 11.2 %shard_map.96 = (bf16[2,448,384]{2,1,0:T(8,128)(2,1)}, bf16[896,384]{1,0:T(8,128)(2,1)}, f32[2,4,128,128]{3,2,1,0:T(8,128)}) custom-call(s32[20]{0:T(128)} %pad_add_fusion.1.meta, bf16[4,896,1024]{2,1,0:T(8,128)(2,1)} %pad_maximum_fusion.x_ref, bf16[4,1024,384]{2,1,0:T(8,128)(2,1)} %bitcast.31, bf16[4,128,128]{2,1,0:T(8,128)(2,1)} %refs_2_.3, ...), custom_call_target="tpu_custom_call" | custom-call | flops 2818572288 | bytes 10485760 | tf_op jit(solution)/shard_map/pallas_call | solution.py:81
  314.6 8.6 %shard_map.97 = (bf16[448,1024]{1,0:T(8,128)(2,1)}, bf16[448,1024]{1,0:T(8,128)(2,1)}, bf16[448,1024]{1,0:T(8,128)(2,1)}, bf16[448,1024]{1,0:T(8,128)(2,1)}) custom-call(s32[20]{0:T(128)} %pad_add_fusion.1.meta, bf16[896,384]{1,0:T(8,128)(2,1)} %get-tuple-element.31.refs_0_, bf16[4,1024,384]{2,1,0:T(8,128)(2,1)} %bitcast.32, bf16[4,128,128]{2,1,0:T(8,128)(2,1)} %refs_2_.3, ...), custom_call_target="tpu_custom_call" | custom-call | flops 1 | bytes 1 | tf_op jit(solution)/shard_map/pallas_call | solution.py:178
  324.7 3.5 collective-permute-start.17
  328.2 8.3 %shard_map.98 = (bf16[448,1024]{1,0:T(8,128)(2,1)}, bf16[448,1024]{1,0:T(8,128)(2,1)}, bf16[448,1024]{1,0:T(8,128)(2,1)}, bf16[448,1024]{1,0:T(8,128)(2,1)}) custom-call(s32[20]{0:T(128)} %pad_add_fusion.1.meta, bf16[896,384]{1,0:T(8,128)(2,1)} %get-tuple-element.31.refs_0_, bf16[4,1024,384]{2,1,0:T(8,128)(2,1)} %bitcast.33, bf16[4,128,128]{2,1,0:T(8,128)(2,1)} %refs_2_.3, ...), custom_call_target="tpu_custom_call" | custom-call | flops 1 | bytes 1 | tf_op jit(solution)/shard_map/pallas_call | solution.py:178
  336.5 1.8 collective-permute-start.6
  339.1 36.5 %collective-permute-done.8 = bf16[448,384]{1,0:T(8,128)(2,1)S(1)} collective-permute-done((bf16[448,384]{1,0:T(8,128)(2,1)S(1)}, bf16[448,384]{1,0:T(8,128)(2,1)S(1)}, u32[]{:S(2)}, u32[]{:S(2)}) %collective-permute-start.8) | collective-permute-done | bytes 344096 | tf_op jit(solution)/shard_map/ppermute | solution.py:18
  375.9 3.0 collective-permute-start.14
  380.0 1.3 collective-permute-start.12
  382.4 17.7 %collective-permute-done.14 = bf16[448,1024]{1,0:T(8,128)(2,1)S(1)} collective-permute-done((bf16[448,1024]{1,0:T(8,128)(2,1)S(1)}, bf16[448,1024]{1,0:T(8,128)(2,1)S(1)}, u32[]{:S(2)}, u32[]{:S(2)}) %collective-permute-start.14) | collective-permute-done | bytes 917536 | tf_op jit(solution)/shard_map/ppermute | solution.py:18
  400.1 19.8 %collective-permute-done.19 = bf16[448,1024]{1,0:T(8,128)(2,1)S(1)} collective-permute-done((bf16[448,1024]{1,0:T(8,128)(2,1)S(1)}, bf16[448,1024]{1,0:T(8,128)(2,1)S(1)}, u32[]{:S(2)}, u32[]{:S(2)}) %collective-permute-start.19) | collective-permute-done | bytes 917536 | tf_op jit(solution)/shard_map/ppermute | solution.py:306
  419.9 2.2 collective-permute-done.12
  422.1 1.9 add_convert_fusion
  (83 shorter events, 9.1 us)
Async XLA Ops:
  7.2 224.9 %all-gather.5.cloned.1.call-start = ((), (), s32[]{:S(2)}) async-start(), calls=%async_computation | async-start | bytes 15728640 | tf_op jit(solution)/shard_map/all_gather | solution.py:245
  11.0 27.3 %copy-start.9 = (s32[4]{0:T(128)S(1)}, s32[4]{0:T(128)}, u32[]{:S(2)}) copy-start(s32[4]{0:T(128)} %param.10) | copy-start | bytes 52
  11.0 291.0 %all-gather.7.cloned.1.call-start = ((), (), s32[]{:S(2)}) async-start(), calls=%async_computation.1 | async-start | bytes 3932160 | tf_op jit(solution)/shard_map/all_gather | solution.py:246
  12.2 23.4 %collective-permute-start = (bf16[448,1024]{1,0:T(8,128)(2,1)S(1)}, bf16[448,1024]{1,0:T(8,128)(2,1)}, u32[]{:S(2)}, u32[]{:S(2)}) collective-permute-start(bf16[448,1024]{1,0:T(8,128)(2,1)S(1)} %copy-done.2), channel_id=1, source_target_pairs={{0,16},{16,0},{1,17},{17,1},{2,18},{18,2},{3,19},{19,3},{4,20},{20... | collective-permute-start | bytes 2752520 | tf_op jit(solution)/shard_map/ppermute | solution.py:18
  15.1 28.4 %collective-permute-start.2 = (bf16[448,1024]{1,0:T(8,128)(2,1)S(1)}, bf16[448,1024]{1,0:T(8,128)(2,1)}, u32[]{:S(2)}, u32[]{:S(2)}) collective-permute-start(bf16[448,1024]{1,0:T(8,128)(2,1)S(1)} %copy-done.2), channel_id=1, source_target_pairs={{0,2},{1,3},{2,0},{3,1},{4,6},{5,7},{6,4},{7,5},{8,10},{9,11},{10,... | collective-permute-start | bytes 2752520 | tf_op jit(solution)/shard_map/ppermute | solution.py:18
  35.6 21.7 %collective-permute-start.3 = (bf16[448,1024]{1,0:T(8,128)(2,1)}, bf16[448,1024]{1,0:T(8,128)(2,1)S(1)}, u32[]{:S(2)}, u32[]{:S(2)}) collective-permute-start(bf16[448,1024]{1,0:T(8,128)(2,1)} %collective-permute-done), channel_id=1, source_target_pairs={{0,2},{1,3},{2,0},{3,1},{4,6},{5,7},{6,4},{7,5},{8,10},{9,11},{10,... | collective-permute-start | bytes 2752520 | tf_op jit(solution)/shard_map/ppermute | solution.py:18
  43.5 201.2 %collective-permute-start.1 = (bf16[896,1024]{1,0:T(8,128)(2,1)}, bf16[896,1024]{1,0:T(8,128)(2,1)}, u32[]{:S(2)}, u32[]{:S(2)}) collective-permute-start(bf16[896,1024]{1,0:T(8,128)(2,1)} %constant_dynamic-update-slice_fusion), channel_id=1, source_target_pairs={{0,1},{1,0},{2,3},{3,2},{4,5},{5,4},{6,7},{7,6},{8,9},{9,8},{10,11... | collective-permute-start | bytes 5505032 | tf_op jit(solution)/shard_map/ppermute | solution.py:18
  57.3 174.8 %copy-start.11 = (s32[4]{0:T(128)S(1)}, s32[4]{0:T(128)}, u32[]{:S(2)}) copy-start(s32[4]{0:T(128)} %param.11) | copy-start | bytes 52
  57.3 175.0 %copy-start.12 = (s32[4,1]{0,1:T(1,128)S(1)}, s32[4,1]{0,1:T(1,128)}, u32[]{:S(2)}) copy-start(s32[4,1]{0,1:T(1,128)} %param.12) | copy-start | bytes 52
  57.3 176.4 %collective-permute-start.5 = (bf16[448,1536]{1,0:T(8,128)(2,1)}, bf16[448,1536]{1,0:T(8,128)(2,1)}, u32[]{:S(2)}, u32[]{:S(2)}) collective-permute-start(bf16[448,1536]{1,0:T(8,128)(2,1)} %get-tuple-element.24), channel_id=1, source_target_pairs={{0,16},{16,0},{1,17},{17,1},{2,18},{18,2},{3,19},{19,3},{4,20},{20... | collective-permute-start | bytes 4128776 | tf_op jit(solution)/shard_map/ppermute | solution.py:18
  58.8 185.9 %collective-permute-start.4 = (bf16[896,1024]{1,0:T(8,128)(2,1)S(1)}, bf16[896,1024]{1,0:T(8,128)(2,1)}, u32[]{:S(2)}, u32[]{:S(2)}) collective-permute-start(bf16[896,1024]{1,0:T(8,128)(2,1)S(1)} %constant_dynamic-update-slice_fusion.2), channel_id=1, source_target_pairs={{0,1},{1,0},{2,3},{3,2},{4,5},{5,4},{6,7},{7,6},{8,9},{9,8},{10,11... | collective-permute-start | bytes 5505032 | tf_op jit(solution)/shard_map/ppermute | solution.py:18
  233.7 10.1 %collective-permute-start.7 = (bf16[448,384]{1,0:T(8,128)(2,1)S(1)}, bf16[448,384]{1,0:T(8,128)(2,1)S(1)}, u32[]{:S(2)}, u32[]{:S(2)}) collective-permute-start(bf16[448,384]{1,0:T(8,128)(2,1)S(1)} %get-tuple-element.29), channel_id=1, source_target_pairs={{0,16},{16,0},{1,17},{17,1},{2,18},{18,2},{3,19},{19,3},{4,20},{20... | collective-permute-start | bytes 1032200 | tf_op jit(solution)/shard_map/ppermute | solution.py:18
  302.0 12.5 %copy-start.1 = (bf16[2,448,1536]{2,1,0:T(8,128)(2,1)S(1)}, bf16[2,448,1536]{2,1,0:T(8,128)(2,1)}, u32[]{:S(2)}) copy-start(bf16[2,448,1536]{2,1,0:T(8,128)(2,1)} %get-tuple-element.25) | copy-start | bytes 8257540
  314.4 9.3 %collective-permute-start.9 = (bf16[4,128,128]{2,1,0:T(8,128)(2,1)S(1)}, bf16[4,128,128]{2,1,0:T(8,128)(2,1)S(1)}, u32[]{:S(2)}, u32[]{:S(2)}) collective-permute-start(bf16[4,128,128]{2,1,0:T(8,128)(2,1)S(1)} %fusion.1), channel_id=1, source_target_pairs={{0,16},{16,0},{1,17},{17,1},{2,18},{18,2},{3,19},{19,3},{4,20},{20... | collective-permute-start | bytes 393224 | tf_op jit(solution)/shard_map/ppermute | solution.py:18
  314.5 13.6 %copy-start.7 = (bf16[2,448,384]{2,1,0:T(8,128)(2,1)S(1)}, bf16[2,448,384]{2,1,0:T(8,128)(2,1)}, u32[]{:S(2)}) copy-start(bf16[2,448,384]{2,1,0:T(8,128)(2,1)} %get-tuple-element.30) | copy-start | bytes 2064388
  323.2 52.4 %collective-permute-start.13 = (bf16[448,1024]{1,0:T(8,128)(2,1)}, bf16[448,1024]{1,0:T(8,128)(2,1)S(1)}, u32[]{:S(2)}, u32[]{:S(2)}) collective-permute-start(bf16[448,1024]{1,0:T(8,128)(2,1)} %get-tuple-element.42), channel_id=1, source_target_pairs={{0,1},{1,0},{2,3},{3,2},{4,5},{5,4},{6,7},{7,6},{8,9},{9,8},{10,11... | collective-permute-start | bytes 2752520 | tf_op jit(solution)/shard_map/ppermute | solution.py:18
  323.2 55.8 %collective-permute-start.18 = (bf16[448,1024]{1,0:T(8,128)(2,1)}, bf16[448,1024]{1,0:T(8,128)(2,1)S(1)}, u32[]{:S(2)}, u32[]{:S(2)}) collective-permute-start(bf16[448,1024]{1,0:T(8,128)(2,1)} %get-tuple-element.44), channel_id=1, source_target_pairs={{0,1},{1,0},{2,3},{3,2},{4,5},{5,4},{6,7},{7,6},{8,9},{9,8},{10,11... | collective-permute-start | bytes 2752520 | tf_op jit(solution)/shard_map/ppermute | solution.py:18
  323.7 12.8 %collective-permute-start.15 = (bf16[4,128,128]{2,1,0:T(8,128)(2,1)S(1)}, bf16[4,128,128]{2,1,0:T(8,128)(2,1)S(1)}, u32[]{:S(2)}, u32[]{:S(2)}) collective-permute-start(bf16[4,128,128]{2,1,0:T(8,128)(2,1)S(1)} %get-tuple-element.45), channel_id=1, source_target_pairs={{0,4},{4,0},{8,12},{12,8},{1,5},{5,1},{9,13},{13,9},{2,6},{6,2},{1... | collective-permute-start | bytes 393224 | tf_op jit(solution)/shard_map/ppermute | solution.py:18
  323.8 14.6 %collective-permute-start.16 = (bf16[4,128,128]{2,1,0:T(8,128)(2,1)S(1)}, bf16[4,128,128]{2,1,0:T(8,128)(2,1)S(1)}, u32[]{:S(2)}, u32[]{:S(2)}) collective-permute-start(bf16[4,128,128]{2,1,0:T(8,128)(2,1)S(1)} %get-tuple-element.45), channel_id=1, source_target_pairs={{0,8},{4,12},{8,0},{12,4},{1,9},{5,13},{9,1},{13,5},{2,10},{6,14},... | collective-permute-start | bytes 393224 | tf_op jit(solution)/shard_map/ppermute | solution.py:18
  324.7 14.0 %collective-permute-start.17 = (bf16[4,128,128]{2,1,0:T(8,128)(2,1)S(1)}, bf16[4,128,128]{2,1,0:T(8,128)(2,1)S(1)}, u32[]{:S(2)}, u32[]{:S(2)}) collective-permute-start(bf16[4,128,128]{2,1,0:T(8,128)(2,1)S(1)} %get-tuple-element.45), channel_id=1, source_target_pairs={{0,12},{4,8},{8,4},{12,0},{1,13},{5,9},{9,5},{13,1},{2,14},{6,10},... | collective-permute-start | bytes 393224 | tf_op jit(solution)/shard_map/ppermute | solution.py:18
  336.5 44.7 %collective-permute-start.6 = (bf16[448,1536]{1,0:T(8,128)(2,1)S(1)}, bf16[448,1536]{1,0:T(8,128)(2,1)S(1)}, u32[]{:S(2)}, u32[]{:S(2)}) collective-permute-start(bf16[448,1536]{1,0:T(8,128)(2,1)S(1)} %slice_bitcast_fusion), channel_id=1, source_target_pairs={{0,16},{16,0},{1,17},{17,1},{2,18},{18,2},{3,19},{19,3},{4,20},{20... | collective-permute-start | bytes 4128776 | tf_op jit(solution)/shard_map/ppermute | solution.py:18
  338.4 37.2 %collective-permute-start.8 = (bf16[448,384]{1,0:T(8,128)(2,1)S(1)}, bf16[448,384]{1,0:T(8,128)(2,1)S(1)}, u32[]{:S(2)}, u32[]{:S(2)}) collective-permute-start(bf16[448,384]{1,0:T(8,128)(2,1)S(1)} %slice_bitcast_fusion.1), channel_id=1, source_target_pairs={{0,16},{16,0},{1,17},{17,1},{2,18},{18,2},{3,19},{19,3},{4,20},{20... | collective-permute-start | bytes 1032200 | tf_op jit(solution)/shard_map/ppermute | solution.py:18
  338.6 41.0 %collective-permute-start.11 = (bf16[448,1024]{1,0:T(8,128)(2,1)}, bf16[448,1024]{1,0:T(8,128)(2,1)S(1)}, u32[]{:S(2)}, u32[]{:S(2)}) collective-permute-start(bf16[448,1024]{1,0:T(8,128)(2,1)} %get-tuple-element.39), channel_id=1, source_target_pairs={{0,1},{1,0},{2,3},{3,2},{4,5},{5,4},{6,7},{7,6},{8,9},{9,8},{10,11... | collective-permute-start | bytes 2752520 | tf_op jit(solution)/shard_map/ppermute | solution.py:18
  338.9 36.7 %copy-start.10 = (bf16[448,1024]{1,0:T(8,128)(2,1)S(1)}, bf16[448,1024]{1,0:T(8,128)(2,1)}, u32[]{:S(2)}) copy-start(bf16[448,1024]{1,0:T(8,128)(2,1)} %get-tuple-element.37) | copy-start | bytes 2752516
  338.9 36.7 %copy-start.5 = (bf16[448,1024]{1,0:T(8,128)(2,1)S(1)}, bf16[448,1024]{1,0:T(8,128)(2,1)}, u32[]{:S(2)}) copy-start(bf16[448,1024]{1,0:T(8,128)(2,1)} %get-tuple-element.41) | copy-start | bytes 2752516
  339.0 39.9 %copy-start.4 = (bf16[448,1024]{1,0:T(8,128)(2,1)S(1)}, bf16[448,1024]{1,0:T(8,128)(2,1)}, u32[]{:S(2)}) copy-start(bf16[448,1024]{1,0:T(8,128)(2,1)} %get-tuple-element.43) | copy-start | bytes 2752516
  375.6 6.8 %collective-permute-start.10 = (bf16[448,1024]{1,0:T(8,128)(2,1)S(1)}, bf16[448,1024]{1,0:T(8,128)(2,1)S(1)}, u32[]{:S(2)}, u32[]{:S(2)}) collective-permute-start(bf16[448,1024]{1,0:T(8,128)(2,1)S(1)} %copy-done.10), channel_id=1, source_target_pairs={{0,1},{1,0},{2,3},{3,2},{4,5},{5,4},{6,7},{7,6},{8,9},{9,8},{10,11... | collective-permute-start | bytes 2752520 | tf_op jit(solution)/shard_map/ppermute | solution.py:18
  375.9 24.2 %collective-permute-start.14 = (bf16[448,1024]{1,0:T(8,128)(2,1)S(1)}, bf16[448,1024]{1,0:T(8,128)(2,1)S(1)}, u32[]{:S(2)}, u32[]{:S(2)}) collective-permute-start(bf16[448,1024]{1,0:T(8,128)(2,1)S(1)} %add_convert_fusion.2), channel_id=1, source_target_pairs={{0,2},{1,3},{2,0},{3,1},{4,6},{5,7},{6,4},{7,5},{8,10},{9,11},{10,... | collective-permute-start | bytes 2752520 | tf_op jit(solution)/shard_map/ppermute | solution.py:18
  379.3 40.6 %collective-permute-start.19 = (bf16[448,1024]{1,0:T(8,128)(2,1)S(1)}, bf16[448,1024]{1,0:T(8,128)(2,1)S(1)}, u32[]{:S(2)}, u32[]{:S(2)}) collective-permute-start(bf16[448,1024]{1,0:T(8,128)(2,1)S(1)} %add_convert_fusion.1), channel_id=1, source_target_pairs={{0,18},{1,19},{2,16},{3,17},{16,2},{17,3},{18,0},{19,1},{4,22},{5,... | collective-permute-start | bytes 2752520 | tf_op jit(solution)/shard_map/ppermute | solution.py:306
  380.0 42.1 %collective-permute-start.12 = (bf16[448,1024]{1,0:T(8,128)(2,1)S(1)}, bf16[448,1024]{1,0:T(8,128)(2,1)S(1)}, u32[]{:S(2)}, u32[]{:S(2)}) collective-permute-start(bf16[448,1024]{1,0:T(8,128)(2,1)S(1)} %add_convert_fusion.3), channel_id=1, source_target_pairs={{0,16},{16,0},{1,17},{17,1},{2,18},{18,2},{3,19},{19,3},{4,20},{20... | collective-permute-start | bytes 2752520 | tf_op jit(solution)/shard_map/ppermute | solution.py:18
  381.4 40.7 %copy-start.3 = (bf16[448,1024]{1,0:T(8,128)(2,1)S(1)}, bf16[448,1024]{1,0:T(8,128)(2,1)}, u32[]{:S(2)}) copy-start(bf16[448,1024]{1,0:T(8,128)(2,1)} %get-tuple-element.36) | copy-start | bytes 2752516
  382.4 41.7 %copy-start = (bf16[448,3840]{1,0:T(8,128)(2,1)}, bf16[448,3840]{1,0:T(8,128)(2,1)S(1)}, u32[]{:S(2)}) copy-start(bf16[448,3840]{1,0:T(8,128)(2,1)S(1)} %constant_dynamic-update-slice_fusion.4) | copy-start | bytes 10321924
  (3 other events, 16.1 us)
Sparse Core Ops, SparseCore 0:
  11.1 220.8 all-gather.4
  234.2 61.6 all-gather.6

commit v7 on v6

--- a/solution.py
+++ b/solution.py
@@ -243,8 +243,6 @@
         for first, size in zip(firsts, sizes)
     ]
     gather_a = lax.all_gather(shards[0], "dp")
-    gather_b = lax.all_gather(tie(shards[1], gather_a), "dp")
-    gathered = [gather_a, gather_b]
 
     row_part = block_rows * bs // feats
     block_info = jnp.stack(
@@ -274,6 +272,7 @@
         order = got
         d_pieces.append(jnp.concatenate([keep, got], axis=0))
 
+    gather_b = lax.all_gather(tie(shards[1], gather_a, x4, *d_pieces), "dp")
     act_a, slope_a, sums_a = forward(meta, x4, gather_a, delta, d_pieces[0], firsts[0], 2)
     back_a = swap(act_a[1], "groups", 1)
     (early,) = backward(meta, [slope_a], [gather_a], delta, firsts[:1], None, None)
@@ -281,7 +280,7 @@
     activated = lax.dynamic_update_slice(activated, act_a[0], (0, mine + firsts[0]))
     activated = lax.dynamic_update_slice(activated, back_a, (0, theirs + firsts[0]))
 
-    delta_b = tie(delta, early)
+    delta_b = tie(delta, early, activated)
     act_b, slope_b, sums_b = forward(meta, x4, gather_b, delta_b, d_pieces[1], firsts[1], 2)
     back_b = swap(act_b[1], "groups", 1)
     activated = lax.dynamic_update_slice(activated, act_b[0], (0, mine + firsts[1]))

time: 433 us -> 393 us (0.908)
  waiting for transfers between devices: 284 us -> 234 us
  local copies, waits for them, and re-layouts: 16.6 us -> 21.8 us
  other arithmetic: 15.9 us -> 21 us
    all_gather x1, waiting for transfers between devices: 171 us -> 128 us  [local(): gather_a = lax.all_gather(shards[0], 'dp')]
    ppermute x19, waiting for transfers between devices: 92.9 us -> 88.1 us  [swap(): return lax.ppermute(array, axis, [(i, i ^ bit) for i in range(size)])]
  transfers between devices with their start and end apart: 22 -> 22, of which waited for: 8 -> 11; matrix products, arithmetic and copies ran while one was open for 6% -> 9% of each run, Pallas kernels for 16% -> 17%
where the time goes in v7:
time: 393 us; the launch traced here: 392 us
  waiting for transfers between devices  234 us (60%)
  Pallas kernels  77.9 us (20%)
  starting transfers between devices  22.6 us (6%)
  local copies, waits for them, and re-layouts  21.8 us (6%)
  other arithmetic  21 us (5%)
  between operations  14.4 us (4%)
    all_gather x1, waiting for transfers between devices, local(): gather_a = lax.all_gather(shards[0], 'dp')  128 us
    ppermute x19, waiting for transfers between devices, swap(): return lax.ppermute(array, axis, [(i, i ^ bit) for i in range(size)])  88.1 us
    pallas_call x3, Pallas kernels, backward(): pl.pallas_call(functools.partial(backward_kernel, firsts, blocks, bs, acc...  40.7 us
    pallas_call x2, Pallas kernels, forward(): pl.pallas_call(functools.partial(forward_kernel, first, blocks, bs, cuts)...  37.2 us
    ppermute x19, starting transfers between devices, swap(): return lax.ppermute(array, axis, [(i, i ^ bit) for i in range(size)])  18.9 us
    ppermute x1, waiting for transfers between devices, local(): from_xy = lax.ppermute(far_peer, ('groups', 'tensor'), diagonal)  15.6 us
  transfers between devices with their start and end apart: 22, of which 11 were waited for; matrix products, arithmetic and copies ran while one was open for 9% of the time, Pallas kernels for 17%

profile of v7, /device:TPU:0, one launch (start us, length us, event | category | flops | bytes accessed | tf_op | source)
XLA Modules:
  0.0 391.5 jit_solution(18014840505703720847)
XLA Ops:
  7.2 3.8 constant_dynamic-slice_fusion.5
  12.2 3.0 collective-permute-start
  16.6 19.0 %collective-permute-done = bf16[448,1024]{1,0:T(8,128)(2,1)} collective-permute-done((bf16[448,1024]{1,0:T(8,128)(2,1)S(1)}, bf16[448,1024]{1,0:T(8,128)(2,1)}, u32[]{:S(2)}, u32[]{:S(2)}) %collective-permute-start) | collective-permute-done | bytes 917536 | tf_op jit(solution)/shard_map/ppermute | solution.py:18
  35.6 1.7 collective-permute-start.3
  38.3 3.1 constant_dynamic-slice_fusion.4
  41.4 2.3 constant_dynamic-update-slice_fusion
  44.9 12.5 %collective-permute-done.3 = bf16[448,1024]{1,0:T(8,128)(2,1)} collective-permute-done((bf16[448,1024]{1,0:T(8,128)(2,1)}, bf16[448,1024]{1,0:T(8,128)(2,1)}, u32[]{:S(2)}, u32[]{:S(2)}) %collective-permute-start.3) | collective-permute-done | bytes 917536 | tf_op jit(solution)/shard_map/ppermute | solution.py:18
  60.2 1.9 constant_dynamic-slice_fusion.1
  62.1 26.1 %collective-permute-done.5 = bf16[448,1536]{1,0:T(8,128)(2,1)} collective-permute-done((bf16[448,1536]{1,0:T(8,128)(2,1)}, bf16[448,1536]{1,0:T(8,128)(2,1)}, u32[]{:S(2)}, u32[]{:S(2)}) %collective-permute-start.5) | collective-permute-done | bytes 1376288 | tf_op jit(solution)/shard_map/ppermute | solution.py:18
  89.3 2.1 constant_dynamic-slice_fusion.2
  91.4 3.0 pad_maximum_fusion.1.d_ref
  95.9 1.9 pad_maximum_fusion.2.d_ref
  97.8 6.2 %pad_maximum_fusion.x_ref = bf16[4,896,1024]{2,1,0:T(8,128)(2,1)} fusion(bf16[1,896,1024]{2,1,0:T(8,128)(2,1)} %bitcast.7, bf16[1,896,1024]{2,1,0:T(8,128)(2,1)S(1)} %bitcast.34, bf16[1,896,1024]{2,1,0:T(8,128)(2,1)} %bitcast.5, bf16[1,896,1024]{2,1,0:T(8,128)(2,1)} %bitcast.4), kind=kLoop, calls=%fused_computation | loop fusion | flops 11010048 | bytes 14680064 | tf_op jit(solution)/shard_map/stack | solution.py:264
  104.1 128.0 %all-gather.5.cloned.1.call-done = bf16[4096,1536]{1,0:T(8,128)(2,1)} async-done(((bf16[1024,1536]{1,0:T(8,128)(2,1)}), bf16[4096,1536]{1,0:T(8,128)(2,1)}) %all-gather.5.cloned.1.call-update) | async-done | bytes 12582928 | tf_op jit(solution)/shard_map/all_gather | solution.py:245
  233.0 27.1 %shard_map.94 = (bf16[2,448,1536]{2,1,0:T(8,128)(2,1)}, bf16[896,1536]{1,0:T(8,128)(2,1)}, f32[2,4,128,128]{3,2,1,0:T(8,128)}) custom-call(s32[20]{0:T(128)} %pad_add_fusion.1.meta, bf16[4,896,1024]{2,1,0:T(8,128)(2,1)} %pad_maximum_fusion.x_ref, bf16[4,1024,1536]{2,1,0:T(8,128)(2,1)} %bitcast.37, bf16[4,128,128]{2,1,0:T(8,128)(2,1)} %refs_2_.3, ...), custom_call_target="tpu_custom_call" | custom-call | flops 11274289152 | bytes 19922944 | tf_op jit(solution)/shard_map/pallas_call | solution.py:81
  261.6 2.3 collective-permute-start.6
  264.2 23.9 %shard_map.95.refs_3_ = f32[4,896,1024]{2,1,0:T(8,128)} custom-call(s32[20]{0:T(128)} %pad_add_fusion.1.meta, bf16[896,1536]{1,0:T(8,128)(2,1)} %get-tuple-element.28.refs_0_, bf16[4,1024,1536]{2,1,0:T(8,128)(2,1)} %bitcast.38, bf16[4,128,128]{2,1,0:T(8,128)(2,1)} %refs_2_.3), custom_call_target="tpu_custom_call" | custom-call | flops 11274289152 | bytes 23592960 | tf_op jit(solution)/shard_map/pallas_call | solution.py:178
  288.1 5.5 %collective-permute-done.6 = bf16[448,1536]{1,0:T(8,128)(2,1)S(1)} collective-permute-done((bf16[448,1536]{1,0:T(8,128)(2,1)S(1)}, bf16[448,1536]{1,0:T(8,128)(2,1)S(1)}, u32[]{:S(2)}, u32[]{:S(2)}) %collective-permute-start.6) | collective-permute-done | bytes 1376288 | tf_op jit(solution)/shard_map/ppermute | solution.py:18
  293.8 2.2 all-gather.7.cloned.1.call-done
  296.0 10.0 %shard_map.96 = (bf16[2,448,384]{2,1,0:T(8,128)(2,1)}, bf16[896,384]{1,0:T(8,128)(2,1)}, f32[2,4,128,128]{3,2,1,0:T(8,128)}) custom-call(s32[20]{0:T(128)} %pad_add_fusion.1.meta, bf16[4,896,1024]{2,1,0:T(8,128)(2,1)} %pad_maximum_fusion.x_ref, bf16[4,1024,384]{2,1,0:T(8,128)(2,1)} %bitcast.31, bf16[4,128,128]{2,1,0:T(8,128)(2,1)} %refs_2_.3, ...), custom_call_target="tpu_custom_call" | custom-call | flops 2818572288 | bytes 10485760 | tf_op jit(solution)/shard_map/pallas_call | solution.py:81
  307.2 1.5 collective-permute-start.9
  308.7 8.4 %shard_map.97 = (bf16[448,1024]{1,0:T(8,128)(2,1)}, bf16[448,1024]{1,0:T(8,128)(2,1)}, bf16[448,1024]{1,0:T(8,128)(2,1)}, bf16[448,1024]{1,0:T(8,128)(2,1)}) custom-call(s32[20]{0:T(128)} %pad_add_fusion.1.meta, bf16[896,384]{1,0:T(8,128)(2,1)} %get-tuple-element.31.refs_0_, bf16[4,1024,384]{2,1,0:T(8,128)(2,1)} %bitcast.32, bf16[4,128,128]{2,1,0:T(8,128)(2,1)} %refs_2_.3, ...), custom_call_target="tpu_custom_call" | custom-call | flops 1 | bytes 1 | tf_op jit(solution)/shard_map/pallas_call | solution.py:178
  318.4 1.8 collective-permute-start.16
  321.3 8.5 %shard_map.98 = (bf16[448,1024]{1,0:T(8,128)(2,1)}, bf16[448,1024]{1,0:T(8,128)(2,1)}, bf16[448,1024]{1,0:T(8,128)(2,1)}, bf16[448,1024]{1,0:T(8,128)(2,1)}) custom-call(s32[20]{0:T(128)} %pad_add_fusion.1.meta, bf16[896,384]{1,0:T(8,128)(2,1)} %get-tuple-element.31.refs_0_, bf16[4,1024,384]{2,1,0:T(8,128)(2,1)} %bitcast.33, bf16[4,128,128]{2,1,0:T(8,128)(2,1)} %refs_2_.3, ...), custom_call_target="tpu_custom_call" | custom-call | flops 1 | bytes 1 | tf_op jit(solution)/shard_map/pallas_call | solution.py:178
  329.7 2.9 collective-permute-start.17
  332.8 4.1 %collective-permute-done.17 = bf16[4,128,128]{2,1,0:T(8,128)(2,1)S(1)} collective-permute-done((bf16[4,128,128]{2,1,0:T(8,128)(2,1)}, bf16[4,128,128]{2,1,0:T(8,128)(2,1)S(1)}, u32[]{:S(2)}, u32[]{:S(2)}) %collective-permute-start.17) | collective-permute-done | bytes 131104 | tf_op jit(solution)/shard_map/ppermute | solution.py:18
  336.9 1.5 add_convert_fusion.1
  338.5 3.6 collective-permute-start.19
  342.1 1.5 add_convert_fusion.2
  347.7 15.6 %collective-permute-done.19 = bf16[448,1024]{1,0:T(8,128)(2,1)S(1)} collective-permute-done((bf16[448,1024]{1,0:T(8,128)(2,1)S(1)}, bf16[448,1024]{1,0:T(8,128)(2,1)S(1)}, u32[]{:S(2)}, u32[]{:S(2)}) %collective-permute-start.19) | collective-permute-done | bytes 917536 | tf_op jit(solution)/shard_map/ppermute | solution.py:305
  363.3 19.0 %collective-permute-done.14 = bf16[448,1024]{1,0:T(8,128)(2,1)S(1)} collective-permute-done((bf16[448,1024]{1,0:T(8,128)(2,1)S(1)}, bf16[448,1024]{1,0:T(8,128)(2,1)S(1)}, u32[]{:S(2)}, u32[]{:S(2)}) %collective-permute-start.14) | collective-permute-done | bytes 917536 | tf_op jit(solution)/shard_map/ppermute | solution.py:18
  382.8 1.9 add_convert_fusion
  (85 shorter events, 21.2 us)
Async XLA Ops:
  7.2 224.9 %all-gather.5.cloned.1.call-start = ((), (), s32[]{:S(2)}) async-start(), calls=%async_computation | async-start | bytes 15728640 | tf_op jit(solution)/shard_map/all_gather | solution.py:245
  11.0 285.0 %all-gather.7.cloned.1.call-start = ((), (), s32[]{:S(2)}) async-start(), calls=%async_computation.1 | async-start | bytes 3932160 | tf_op jit(solution)/shard_map/all_gather | solution.py:275
  12.2 23.4 %collective-permute-start = (bf16[448,1024]{1,0:T(8,128)(2,1)S(1)}, bf16[448,1024]{1,0:T(8,128)(2,1)}, u32[]{:S(2)}, u32[]{:S(2)}) collective-permute-start(bf16[448,1024]{1,0:T(8,128)(2,1)S(1)} %copy-done.3), channel_id=1, source_target_pairs={{0,16},{16,0},{1,17},{17,1},{2,18},{18,2},{3,19},{19,3},{4,20},{20... | collective-permute-start | bytes 2752520 | tf_op jit(solution)/shard_map/ppermute | solution.py:18
  15.1 28.6 %collective-permute-start.2 = (bf16[448,1024]{1,0:T(8,128)(2,1)S(1)}, bf16[448,1024]{1,0:T(8,128)(2,1)}, u32[]{:S(2)}, u32[]{:S(2)}) collective-permute-start(bf16[448,1024]{1,0:T(8,128)(2,1)S(1)} %copy-done.3), channel_id=1, source_target_pairs={{0,2},{1,3},{2,0},{3,1},{4,6},{5,7},{6,4},{7,5},{8,10},{9,11},{10,... | collective-permute-start | bytes 2752520 | tf_op jit(solution)/shard_map/ppermute | solution.py:18
  35.6 21.9 %collective-permute-start.3 = (bf16[448,1024]{1,0:T(8,128)(2,1)}, bf16[448,1024]{1,0:T(8,128)(2,1)}, u32[]{:S(2)}, u32[]{:S(2)}) collective-permute-start(bf16[448,1024]{1,0:T(8,128)(2,1)} %collective-permute-done), channel_id=1, source_target_pairs={{0,2},{1,3},{2,0},{3,1},{4,6},{5,7},{6,4},{7,5},{8,10},{9,11},{10,... | collective-permute-start | bytes 2752520 | tf_op jit(solution)/shard_map/ppermute | solution.py:18
  43.7 54.2 %collective-permute-start.1 = (bf16[896,1024]{1,0:T(8,128)(2,1)}, bf16[896,1024]{1,0:T(8,128)(2,1)}, u32[]{:S(2)}, u32[]{:S(2)}) collective-permute-start(bf16[896,1024]{1,0:T(8,128)(2,1)} %constant_dynamic-update-slice_fusion), channel_id=1, source_target_pairs={{0,1},{1,0},{2,3},{3,2},{4,5},{5,4},{6,7},{7,6},{8,9},{9,8},{10,11... | collective-permute-start | bytes 5505032 | tf_op jit(solution)/shard_map/ppermute | solution.py:18
  57.4 30.8 %collective-permute-start.5 = (bf16[448,1536]{1,0:T(8,128)(2,1)}, bf16[448,1536]{1,0:T(8,128)(2,1)}, u32[]{:S(2)}, u32[]{:S(2)}) collective-permute-start(bf16[448,1536]{1,0:T(8,128)(2,1)} %get-tuple-element.24), channel_id=1, source_target_pairs={{0,16},{16,0},{1,17},{17,1},{2,18},{18,2},{3,19},{19,3},{4,20},{20... | collective-permute-start | bytes 4128776 | tf_op jit(solution)/shard_map/ppermute | solution.py:18
  60.1 37.7 %collective-permute-start.4 = (bf16[896,1024]{1,0:T(8,128)(2,1)S(1)}, bf16[896,1024]{1,0:T(8,128)(2,1)}, u32[]{:S(2)}, u32[]{:S(2)}) collective-permute-start(bf16[896,1024]{1,0:T(8,128)(2,1)S(1)} %constant_dynamic-update-slice_fusion.2), channel_id=1, source_target_pairs={{0,1},{1,0},{2,3},{3,2},{4,5},{5,4},{6,7},{7,6},{8,9},{9,8},{10,11... | collective-permute-start | bytes 5505032 | tf_op jit(solution)/shard_map/ppermute | solution.py:18
  88.2 7.7 %collective-permute-start.7 = (bf16[448,384]{1,0:T(8,128)(2,1)}, bf16[448,384]{1,0:T(8,128)(2,1)}, u32[]{:S(2)}, u32[]{:S(2)}) collective-permute-start(bf16[448,384]{1,0:T(8,128)(2,1)} %get-tuple-element.26), channel_id=1, source_target_pairs={{0,16},{16,0},{1,17},{17,1},{2,18},{18,2},{3,19},{19,3},{4,20},{20... | collective-permute-start | bytes 1032200 | tf_op jit(solution)/shard_map/ppermute | solution.py:18
  97.8 134.3 %copy-start.11 = (s32[4]{0:T(128)S(1)}, s32[4]{0:T(128)}, u32[]{:S(2)}) copy-start(s32[4]{0:T(128)} %param.10) | copy-start | bytes 52
  97.8 134.3 %copy-start.12 = (s32[4]{0:T(128)S(1)}, s32[4]{0:T(128)}, u32[]{:S(2)}) copy-start(s32[4]{0:T(128)} %param.11) | copy-start | bytes 52
  261.6 32.1 %collective-permute-start.6 = (bf16[448,1536]{1,0:T(8,128)(2,1)S(1)}, bf16[448,1536]{1,0:T(8,128)(2,1)S(1)}, u32[]{:S(2)}, u32[]{:S(2)}) collective-permute-start(bf16[448,1536]{1,0:T(8,128)(2,1)S(1)} %slice_bitcast_fusion), channel_id=1, source_target_pairs={{0,16},{16,0},{1,17},{17,1},{2,18},{18,2},{3,19},{19,3},{4,20},{20... | collective-permute-start | bytes 4128776 | tf_op jit(solution)/shard_map/ppermute | solution.py:18
  296.0 10.0 %copy-start.10 = (f32[2,4,128,128]{3,2,1,0:T(8,128)S(1)}, f32[2,4,128,128]{3,2,1,0:T(8,128)}, u32[]{:S(2)}) copy-start(f32[2,4,128,128]{3,2,1,0:T(8,128)} %get-tuple-element.33) | copy-start | bytes 1572868
  307.2 10.4 %collective-permute-start.9 = (bf16[4,128,128]{2,1,0:T(8,128)(2,1)S(1)}, bf16[4,128,128]{2,1,0:T(8,128)(2,1)S(1)}, u32[]{:S(2)}, u32[]{:S(2)}) collective-permute-start(bf16[4,128,128]{2,1,0:T(8,128)(2,1)S(1)} %fusion.1), channel_id=1, source_target_pairs={{0,16},{16,0},{1,17},{17,1},{2,18},{18,2},{3,19},{19,3},{4,20},{20... | collective-permute-start | bytes 393224 | tf_op jit(solution)/shard_map/ppermute | solution.py:18
  308.7 11.5 %copy-start.8 = (bf16[2,448,384]{2,1,0:T(8,128)(2,1)S(1)}, bf16[2,448,384]{2,1,0:T(8,128)(2,1)}, u32[]{:S(2)}) copy-start(bf16[2,448,384]{2,1,0:T(8,128)(2,1)} %get-tuple-element.30) | copy-start | bytes 2064388
  317.1 19.9 %collective-permute-start.18 = (bf16[448,1024]{1,0:T(8,128)(2,1)}, bf16[448,1024]{1,0:T(8,128)(2,1)}, u32[]{:S(2)}, u32[]{:S(2)}) collective-permute-start(bf16[448,1024]{1,0:T(8,128)(2,1)} %get-tuple-element.44), channel_id=1, source_target_pairs={{0,1},{1,0},{2,3},{3,2},{4,5},{5,4},{6,7},{7,6},{8,9},{9,8},{10,11... | collective-permute-start | bytes 2752520 | tf_op jit(solution)/shard_map/ppermute | solution.py:18
  317.5 24.5 %collective-permute-start.13 = (bf16[448,1024]{1,0:T(8,128)(2,1)}, bf16[448,1024]{1,0:T(8,128)(2,1)}, u32[]{:S(2)}, u32[]{:S(2)}) collective-permute-start(bf16[448,1024]{1,0:T(8,128)(2,1)} %get-tuple-element.42), channel_id=1, source_target_pairs={{0,1},{1,0},{2,3},{3,2},{4,5},{5,4},{6,7},{7,6},{8,9},{9,8},{10,11... | collective-permute-start | bytes 2752520 | tf_op jit(solution)/shard_map/ppermute | solution.py:18
  318.4 11.3 %collective-permute-start.15 = (bf16[4,128,128]{2,1,0:T(8,128)(2,1)}, bf16[4,128,128]{2,1,0:T(8,128)(2,1)}, u32[]{:S(2)}, u32[]{:S(2)}) collective-permute-start(bf16[4,128,128]{2,1,0:T(8,128)(2,1)} %get-tuple-element.45), channel_id=1, source_target_pairs={{0,4},{4,0},{8,12},{12,8},{1,5},{5,1},{9,13},{13,9},{2,6},{6,2},{1... | collective-permute-start | bytes 393224 | tf_op jit(solution)/shard_map/ppermute | solution.py:18
  318.4 14.2 %collective-permute-start.16 = (bf16[4,128,128]{2,1,0:T(8,128)(2,1)}, bf16[4,128,128]{2,1,0:T(8,128)(2,1)}, u32[]{:S(2)}, u32[]{:S(2)}) collective-permute-start(bf16[4,128,128]{2,1,0:T(8,128)(2,1)} %get-tuple-element.45), channel_id=1, source_target_pairs={{0,8},{4,12},{8,0},{12,4},{1,9},{5,13},{9,1},{13,5},{2,10},{6,14},... | collective-permute-start | bytes 393224 | tf_op jit(solution)/shard_map/ppermute | solution.py:18
  320.9 16.0 %collective-permute-start.8 = (bf16[448,384]{1,0:T(8,128)(2,1)}, bf16[448,384]{1,0:T(8,128)(2,1)}, u32[]{:S(2)}, u32[]{:S(2)}) collective-permute-start(bf16[448,384]{1,0:T(8,128)(2,1)} %slice_bitcast_fusion.1), channel_id=1, source_target_pairs={{0,16},{16,0},{1,17},{17,1},{2,18},{18,2},{3,19},{19,3},{4,20},{20... | collective-permute-start | bytes 1032200 | tf_op jit(solution)/shard_map/ppermute | solution.py:18
  321.2 11.4 %copy-start.13 = (s32[4,1]{0,1:T(1,128)S(1)}, s32[4,1]{0,1:T(1,128)}, u32[]{:S(2)}) copy-start(s32[4,1]{0,1:T(1,128)} %param.12) | copy-start | bytes 52
  321.3 15.7 %copy-start.6 = (bf16[448,1024]{1,0:T(8,128)(2,1)S(1)}, bf16[448,1024]{1,0:T(8,128)(2,1)}, u32[]{:S(2)}) copy-start(bf16[448,1024]{1,0:T(8,128)(2,1)} %get-tuple-element.43) | copy-start | bytes 2752516
  329.7 12.4 %copy-start.5 = (bf16[448,1024]{1,0:T(8,128)(2,1)S(1)}, bf16[448,1024]{1,0:T(8,128)(2,1)}, u32[]{:S(2)}) copy-start(bf16[448,1024]{1,0:T(8,128)(2,1)} %get-tuple-element.41) | copy-start | bytes 2752516
  329.7 7.2 %collective-permute-start.17 = (bf16[4,128,128]{2,1,0:T(8,128)(2,1)}, bf16[4,128,128]{2,1,0:T(8,128)(2,1)S(1)}, u32[]{:S(2)}, u32[]{:S(2)}) collective-permute-start(bf16[4,128,128]{2,1,0:T(8,128)(2,1)} %get-tuple-element.45), channel_id=1, source_target_pairs={{0,12},{4,8},{8,4},{12,0},{1,13},{5,9},{9,5},{13,1},{2,14},{6,10},... | collective-permute-start | bytes 393224 | tf_op jit(solution)/shard_map/ppermute | solution.py:18
  332.6 11.1 %collective-permute-start.11 = (bf16[448,1024]{1,0:T(8,128)(2,1)}, bf16[448,1024]{1,0:T(8,128)(2,1)S(1)}, u32[]{:S(2)}, u32[]{:S(2)}) collective-permute-start(bf16[448,1024]{1,0:T(8,128)(2,1)} %get-tuple-element.39), channel_id=1, source_target_pairs={{0,1},{1,0},{2,3},{3,2},{4,5},{5,4},{6,7},{7,6},{8,9},{9,8},{10,11... | collective-permute-start | bytes 2752520 | tf_op jit(solution)/shard_map/ppermute | solution.py:18
  336.9 10.8 %collective-permute-start.10 = (bf16[448,1024]{1,0:T(8,128)(2,1)}, bf16[448,1024]{1,0:T(8,128)(2,1)S(1)}, u32[]{:S(2)}, u32[]{:S(2)}) collective-permute-start(bf16[448,1024]{1,0:T(8,128)(2,1)} %get-tuple-element.37), channel_id=1, source_target_pairs={{0,1},{1,0},{2,3},{3,2},{4,5},{5,4},{6,7},{7,6},{8,9},{9,8},{10,11... | collective-permute-start | bytes 2752520 | tf_op jit(solution)/shard_map/ppermute | solution.py:18
  338.5 5.3 %copy-start.7 = (bf16[448,1024]{1,0:T(8,128)(2,1)S(1)}, bf16[448,1024]{1,0:T(8,128)(2,1)}, u32[]{:S(2)}) copy-start(bf16[448,1024]{1,0:T(8,128)(2,1)} %get-tuple-element.38) | copy-start | bytes 2752516
  338.5 24.9 %collective-permute-start.19 = (bf16[448,1024]{1,0:T(8,128)(2,1)S(1)}, bf16[448,1024]{1,0:T(8,128)(2,1)S(1)}, u32[]{:S(2)}, u32[]{:S(2)}) collective-permute-start(bf16[448,1024]{1,0:T(8,128)(2,1)S(1)} %add_convert_fusion.1), channel_id=1, source_target_pairs={{0,18},{1,19},{2,16},{3,17},{16,2},{17,3},{18,0},{19,1},{4,22},{5,... | collective-permute-start | bytes 2752520 | tf_op jit(solution)/shard_map/ppermute | solution.py:305
  343.6 38.7 %collective-permute-start.14 = (bf16[448,1024]{1,0:T(8,128)(2,1)S(1)}, bf16[448,1024]{1,0:T(8,128)(2,1)S(1)}, u32[]{:S(2)}, u32[]{:S(2)}) collective-permute-start(bf16[448,1024]{1,0:T(8,128)(2,1)S(1)} %add_convert_fusion.2), channel_id=1, source_target_pairs={{0,2},{1,3},{2,0},{3,1},{4,6},{5,7},{6,4},{7,5},{8,10},{9,11},{10,... | collective-permute-start | bytes 2752520 | tf_op jit(solution)/shard_map/ppermute | solution.py:18
  344.1 38.7 %copy-start.4 = (bf16[448,1024]{1,0:T(8,128)(2,1)S(1)}, bf16[448,1024]{1,0:T(8,128)(2,1)}, u32[]{:S(2)}) copy-start(bf16[448,1024]{1,0:T(8,128)(2,1)} %get-tuple-element.36) | copy-start | bytes 2752516
  344.1 38.7 %collective-permute-start.12 = (bf16[448,1024]{1,0:T(8,128)(2,1)S(1)}, bf16[448,1024]{1,0:T(8,128)(2,1)S(1)}, u32[]{:S(2)}, u32[]{:S(2)}) collective-permute-start(bf16[448,1024]{1,0:T(8,128)(2,1)S(1)} %add_convert_fusion.3), channel_id=1, source_target_pairs={{0,16},{16,0},{1,17},{17,1},{2,18},{18,2},{3,19},{19,3},{4,20},{20... | collective-permute-start | bytes 2752520 | tf_op jit(solution)/shard_map/ppermute | solution.py:18
  347.7 37.0 %copy-start = (bf16[448,3840]{1,0:T(8,128)(2,1)}, bf16[448,3840]{1,0:T(8,128)(2,1)S(1)}, u32[]{:S(2)}) copy-start(bf16[448,3840]{1,0:T(8,128)(2,1)S(1)} %constant_dynamic-update-slice_fusion.4) | copy-start | bytes 10321924
  (4 other events, 6.1 us)
Sparse Core Ops, SparseCore 0:
  11.1 220.8 all-gather.4
  234.2 61.7 all-gather.6

commit v8 on v7

--- a/solution.py
+++ b/solution.py
@@ -22,14 +22,15 @@
     return pltpu.CompilerParams(vmem_limit_bytes=VMEM_BYTES)
 
 
-PARTS, BLOCKS = 0, 4
+PARTS, FOLDED, LIVE, MASK, BLOCKS = 0, 4, 8, 9, 10
 
 
 def forward_kernel(
-    first, blocks, bs, cuts, meta, x_ref, w_ref, delta_ref, d_ref, act_ref, slope_ref, sum_ref, acc
+    first, blocks, bs, cuts, folded, meta, x_ref, w_ref, delta_ref, d_ref, act_ref, slope_ref, sum_ref, acc
 ):
     width = acc.shape[1]
-    group = pl.program_id(1) // cuts
+    group = pl.program_id(1) // cuts % 2
+    parts = FOLDED if folded else PARTS
 
     @pl.when((pl.program_id(0) == 0) & (pl.program_id(1) == 0))
     def _():
@@ -37,7 +38,7 @@
 
     total = None
     for s in range(w_ref.shape[0]):
-        term = jnp.dot(x_ref[meta[PARTS + s]], w_ref[s], preferred_element_type=F32)
+        term = jnp.dot(x_ref[meta[parts + s]], w_ref[s], preferred_element_type=F32)
         total = term if total is None else total + term
     acc[...] = total
     start = first + pl.program_id(0) * width
@@ -55,9 +56,10 @@
     preact = acc[...]
     squash = jax.nn.sigmoid(preact)
     act_ref[0] = (preact * squash).astype(BF)
-    slope_ref[...] = (
-        d_ref[...].astype(F32) * squash * (1.0 + preact * (1.0 - squash))
-    ).astype(BF)
+    slope = d_ref[...].astype(F32) * squash * (1.0 + preact * (1.0 - squash))
+    if folded:
+        slope = jnp.where(meta[LIVE] != 0, slope, 0.0)
+    slope_ref[...] = slope.astype(BF)
     for n in range(blocks):
         at = BLOCKS + 4 * n
         col = meta[at + 3] - start
@@ -71,15 +73,15 @@
             )
 
 
-def forward(meta, x4, w4, delta, d_piece, first, groups_of):
+def forward(meta, x4, w4, delta, d_piece, first, groups_of, folded=False):
     rows, width = d_piece.shape
     slots, feats = w4.shape[0], w4.shape[1]
     cuts = 2
     tile = rows // groups_of // cuts
     blocks, bs = delta.shape[0], delta.shape[1]
-    wide = next(c for c in (512, 384, 256, 128, width) if width % c == 0)
+    wide = next(c for c in (896, 640, 512, 384, 256, 128, width) if width % c == 0)
     return pl.pallas_call(
-        functools.partial(forward_kernel, first, blocks, bs, cuts),
+        functools.partial(forward_kernel, first, blocks, bs, cuts, folded),
         grid_spec=pltpu.PrefetchScalarGridSpec(
             num_scalar_prefetch=1,
             grid=(width // wide, groups_of * cuts),
@@ -92,14 +94,14 @@
             out_specs=[
                 pl.BlockSpec((1, tile, wide), lambda j, i, m: (i // cuts, i % cuts, j)),
                 pl.BlockSpec((tile, wide), lambda j, i, m: (i, j)),
-                pl.BlockSpec((groups_of, blocks, bs, bs), lambda j, i, m: (0, 0, 0, 0)),
+                pl.BlockSpec((2, blocks, bs, bs), lambda j, i, m: (0, 0, 0, 0)),
             ],
             scratch_shapes=[pltpu.VMEM((tile, wide), F32)],
         ),
         out_shape=[
             jax.ShapeDtypeStruct((groups_of, rows // groups_of, width), BF),
             jax.ShapeDtypeStruct((rows, width), BF),
-            jax.ShapeDtypeStruct((groups_of, blocks, bs, bs), F32),
+            jax.ShapeDtypeStruct((2, blocks, bs, bs), F32),
         ],
         compiler_params=params(),
         cost_estimate=pl.CostEstimate(
@@ -153,8 +155,12 @@
             outs[2 * at_step + 1][...] = acc[cut:].astype(BF)
 
 
-def backward(meta, slopes, ws, delta, firsts, acc, bit):
-    rows = slopes[0].shape[0]
+def weight_block(piece_folded, slot_of, step, tile, meta):
+    slot = slot_of(step, meta)
+    return jnp.bitwise_xor(slot, meta[MASK]) if piece_folded else slot, tile, 0
+
+
+def backward(meta, rows, slopes, ws, delta, firsts, acc, bit, folded, at_rows=0):
     slots, feats = ws[0].shape[0], ws[0].shape[1]
     blocks, bs = delta.shape[0], delta.shape[1]
     every = bit is None
@@ -181,12 +187,18 @@
             num_scalar_prefetch=1,
             grid=(steps, tiles),
             in_specs=[
-                pl.BlockSpec(s.shape, lambda s, i, m: (0, 0), pipeline_mode=pl.Buffered(1))
+                pl.BlockSpec(
+                    (rows, s.shape[1]),
+                    lambda s, i, m: (at_rows, 0),
+                    pipeline_mode=pl.Buffered(1),
+                )
                 for s in slopes
             ]
             + [
-                pl.BlockSpec((1, size, w.shape[2]), lambda s, i, m: (slot_of(s, m), i, 0))
-                for w in ws
+                pl.BlockSpec(
+                    (1, size, w.shape[2]), functools.partial(weight_block, f, slot_of)
+                )
+                for w, f in zip(ws, folded)
             ]
             + [pl.BlockSpec(delta.shape, lambda s, i, m: (0, 0, 0))]
             + ([] if acc is None else [whole]),
@@ -223,14 +235,39 @@
 
 
 def piece_sizes(half, bs):
-    last = max(half // bs // 5, 1) * bs
-    return [half - last, last]
+    blocks = half // bs
+    fold, last = max(blocks // 3, 1), max(blocks // 5, 1)
+    return [fold * bs, (blocks - fold - last) * bs, last * bs]
+
+
+MIDDLE = [(1, 2), (2, 1)]
+INWARD = [(0, 1), (3, 2)]
+OUTWARD = [(1, 0), (2, 3)]
+
+
+def to_dp(array, route):
+    return lax.ppermute(array, "dp", route)
+
+
+def gather_x(tokens):
+    peer = swap(tokens, "groups", 1)
+    own_far = swap(tokens, "tensor", 2)
+    peer_far = swap(peer, "tensor", 2)
+    near = jnp.concatenate([tokens, peer], axis=0)
+    far = jnp.concatenate([own_far, peer_far], axis=0)
+    return [near, swap(near, "tensor", 1), far, swap(far, "tensor", 1)]
+
+
+def add_bf(left, right):
+    return (left.astype(F32) + right.astype(F32)).astype(BF)
 
 
 def local(tokens, frozen, delta, block_rows, block_cols, owners, d_out):
     group, me_dp, me_t = (lax.axis_index(a) for a in ("groups", "dp", "tensor"))
     n_dp, n_t = lax.axis_size("dp"), lax.axis_size("tensor")
+    middle = (me_dp == 1) | (me_dp == 2)
     rows, feats = tokens.shape
+    both = 2 * rows
     blocks, bs = delta.shape[0], delta.shape[1]
     slab = frozen.shape[1]
     half = slab // 2
@@ -242,7 +279,10 @@
         lax.dynamic_slice(frozen, (0, mine + first), (frozen.shape[0], size))
         for first, size in zip(firsts, sizes)
     ]
-    gather_a = lax.all_gather(shards[0], "dp")
+    gather_a = lax.all_gather(shards[1], "dp")
+    outer = to_dp(shards[0], INWARD)
+    inner = to_dp(shards[0], MIDDLE)
+    w_fold = jnp.stack([shards[0], outer, to_dp(outer, MIDDLE), inner])
 
     row_part = block_rows * bs // feats
     block_info = jnp.stack(
@@ -254,16 +294,22 @@
         ],
         axis=1,
     )
-    meta = jnp.concatenate([jnp.arange(n_t, dtype=jnp.int32) ^ me_t, block_info.reshape(-1)])
-
-    peer = swap(tokens, "groups", 1)
-    own_x = swap(tokens, "tensor", 2)
-    peer_x = swap(peer, "tensor", 2)
-    near_x = jnp.concatenate([tokens, peer], axis=0)
-    far_x = jnp.concatenate([own_x, peer_x], axis=0)
-    x4 = jnp.stack([near_x, swap(near_x, "tensor", 1), far_x, swap(far_x, "tensor", 1)])
-
-    order = peer_x
+    slots = jnp.arange(n_t, dtype=jnp.int32)
+    meta = jnp.concatenate(
+        [
+            slots ^ me_t,
+            slots ^ (me_t ^ me_dp),
+            jnp.where(jnp.arange(2) == 0, middle.astype(jnp.int32), me_dp),
+            block_info.reshape(-1),
+        ]
+    )
+
+    end_tokens = to_dp(tokens, INWARD)
+    own_parts = gather_x(tokens)
+    end_parts = gather_x(tie(end_tokens, own_parts[0]))
+    x4 = jnp.stack([jnp.concatenate(pair, axis=0) for pair in zip(own_parts, end_parts)])
+
+    order = own_parts[2]
     d_pieces = []
     for first, size in zip(firsts, sizes):
         give = lax.dynamic_slice(d_out, (0, theirs + first), (rows, size))
@@ -271,44 +317,71 @@
         got = swap(tie(give, order), "groups", 1)
         order = got
         d_pieces.append(jnp.concatenate([keep, got], axis=0))
-
-    gather_b = lax.all_gather(tie(shards[1], gather_a, x4, *d_pieces), "dp")
-    act_a, slope_a, sums_a = forward(meta, x4, gather_a, delta, d_pieces[0], firsts[0], 2)
+    d_fold = jnp.concatenate([d_pieces[0], to_dp(d_pieces[0], INWARD)], axis=0)
+    gather_b = lax.all_gather(
+        tie(shards[2], gather_a, x4, d_fold, w_fold, *d_pieces[1:]), "dp"
+    )
+
+    act_f, slope_f, sums_f = forward(meta, x4, w_fold, delta, d_fold, firsts[0], 4, True)
+    over = swap(jnp.concatenate([act_f[1:2], act_f[3:4]], axis=0), "groups", 1)
+    home = to_dp(jnp.concatenate([act_f[2:3], over[1:2]], axis=0), OUTWARD)
+    activated = jnp.zeros((rows, slab), BF)
+    kept = jnp.where(middle, act_f[0], home[0])
+    activated = lax.dynamic_update_slice(activated, kept, (0, mine + firsts[0]))
+    kept = jnp.where(middle, over[0], home[1])
+    activated = lax.dynamic_update_slice(activated, kept, (0, theirs + firsts[0]))
+
+    diagonal = [(i, i ^ (n_t + 2)) for i in range(2 * n_t)]
+
+    def spread(far, near):
+        far_peer = add_bf(far[3], swap(far[1], "tensor", 1))
+        far_own = add_bf(far[2], swap(far[0], "tensor", 1))
+        from_xy = lax.ppermute(far_peer, ("groups", "tensor"), diagonal)
+        from_x = swap(far_own, "tensor", 2)
+        near_peer = add_bf(near[3], swap(near[1], "tensor", 1))
+        from_y = swap(near_peer, "groups", 1)
+        near_own = near[2].astype(F32) + swap(near[0], "tensor", 1).astype(F32)
+        return near_own + from_y.astype(F32) + from_x.astype(F32) + from_xy.astype(F32)
+
+    def end_back(bit, wait):
+        return backward(
+            meta, both, [slope_f], [w_fold], tie(delta, wait), firsts[:1], None, bit, [True], 1
+        )
+
+    end_far = end_back(3, slope_f)
+    end_near = end_back(1, end_far[1])
+    end_sum = spread(end_far, end_near).astype(BF)
+    end_home = to_dp(end_sum, OUTWARD)
+
+    delta_a = tie(delta, end_near[1])
+    act_a, slope_a, sums_a = forward(meta, x4, gather_a, delta_a, d_pieces[1], firsts[1], 2)
     back_a = swap(act_a[1], "groups", 1)
-    (early,) = backward(meta, [slope_a], [gather_a], delta, firsts[:1], None, None)
-    activated = jnp.zeros((rows, slab), BF)
-    activated = lax.dynamic_update_slice(activated, act_a[0], (0, mine + firsts[0]))
-    activated = lax.dynamic_update_slice(activated, back_a, (0, theirs + firsts[0]))
-
-    delta_b = tie(delta, early, activated)
-    act_b, slope_b, sums_b = forward(meta, x4, gather_b, delta_b, d_pieces[1], firsts[1], 2)
+    (early,) = backward(
+        meta, both, [slope_f, slope_a], [w_fold, gather_a], tie(delta, over), firsts[:2], None,
+        None, [True, False],
+    )
+    activated = lax.dynamic_update_slice(activated, act_a[0], (0, mine + firsts[1]))
+    activated = lax.dynamic_update_slice(activated, back_a, (0, theirs + firsts[1]))
+
+    delta_b = tie(delta, early, activated, end_sum)
+    act_b, slope_b, sums_b = forward(meta, x4, gather_b, delta_b, d_pieces[2], firsts[2], 2)
     back_b = swap(act_b[1], "groups", 1)
-    activated = lax.dynamic_update_slice(activated, act_b[0], (0, mine + firsts[1]))
-    activated = lax.dynamic_update_slice(activated, back_b, (0, theirs + firsts[1]))
-
-    def back_of(bit, *wait):
-        d = tie(delta_b, *wait) if wait else delta_b
-        return backward(meta, [slope_b], [gather_b], d, firsts[1:], early, bit)
-
-    sums = sums_a + sums_b
+    activated = lax.dynamic_update_slice(activated, act_b[0], (0, mine + firsts[2]))
+    activated = lax.dynamic_update_slice(activated, back_b, (0, theirs + firsts[2]))
+
+    sums = sums_f + sums_a + sums_b
     sums = sums[0] + swap(sums[1].astype(BF), "groups", 1).astype(F32)
     shares = [swap(sums.astype(BF), "dp", bit) for bit in range(1, n_dp)]
-    far_own_give, far_peer_give, far_own, far_peer = back_of(3)
-    far_peer_got = swap(far_peer_give, "tensor", 1)
-    far_own_got = swap(far_own_give, "tensor", 1)
-    near_own_give, near_peer_give, near_own, near_peer = back_of(1, far_peer, sums)
-    near_peer_got = swap(near_peer_give, "tensor", 1)
-    near_own_got = swap(near_own_give, "tensor", 1)
-    far_peer, far_own = tie(far_peer, near_peer, back_b, *shares), tie(far_own, near_peer)
-    far_peer = (far_peer.astype(F32) + far_peer_got.astype(F32)).astype(BF)
-    diagonal = [(i, i ^ (n_t + 2)) for i in range(2 * n_t)]
-    from_xy = lax.ppermute(far_peer, ("groups", "tensor"), diagonal)
-    far_own = (far_own.astype(F32) + far_own_got.astype(F32)).astype(BF)
-    from_x = swap(far_own, "tensor", 2)
-    near_peer = (near_peer.astype(F32) + near_peer_got.astype(F32)).astype(BF)
-    from_y = swap(near_peer, "groups", 1)
-    near_own = near_own.astype(F32) + near_own_got.astype(F32)
-    d_tokens = near_own + from_y.astype(F32) + from_x.astype(F32) + from_xy.astype(F32)
+
+    def last_back(bit, *wait):
+        return backward(
+            meta, both, [slope_b], [gather_b], tie(delta_b, *wait), firsts[2:], early, bit, [False]
+        )
+
+    far = list(last_back(3, slope_b))
+    near = last_back(1, far[1], sums)
+    far[2], far[3] = tie(far[2], near[1]), tie(far[3], near[1], back_b, end_home, *shares)
+    d_tokens = spread(far, near) + end_home.astype(F32)
     for share in shares:
         sums = sums + share.astype(F32)
     norm = float(rows * n_dp) ** (-0.5)

time: 393 us -> 501 us (1.27)
  Pallas kernels: 77.9 us -> 108 us
  other arithmetic: 21 us -> 46.9 us
  starting transfers between devices: 22.6 us -> 47 us
  waiting for transfers between devices: 234 us -> 256 us
    ppermute x1 -> x9, waiting for transfers between devices: 15.6 us -> 184 us  [the longest x7 145 us: to_dp(): return lax.ppermute(array, 'dp', route)]
    all_gather x2, waiting for transfers between devices: 130 us -> 0.02 us  [the longest x1 0.02 us: local(): lax.all_gather(tie(shards[2], gather_a, x4, d_fold, w_fold, *d_pieces[1:]...]
    pallas_call x3 -> x5, Pallas kernels: 40.7 us -> 58 us  [backward(): pl.pallas_call(functools.partial(backward_kernel, firsts, blocks, bs, acc...]
    ppermute x19 -> x32, waiting for transfers between devices: 88.1 us -> 71.4 us  [swap(): return lax.ppermute(array, axis, [(i, i ^ bit) for i in range(size)])]
    ppermute x1 -> x9, starting transfers between devices: 3.61 us -> 18.7 us  [the longest x7 17.4 us: to_dp(): return lax.ppermute(array, 'dp', route)]
    pallas_call x2 -> x3, Pallas kernels: 37.2 us -> 50.4 us  [forward(): pl.pallas_call(functools.partial(forward_kernel, first, blocks, bs, cuts,...]
    another operation x1 -> x6, other arithmetic: 6.22 us -> 18.3 us  [the longest x5 12.9 us: local(): jnp.stack([jnp.concatenate(pair, axis=0) for pair in zip(own_parts, end_p...]
    ppermute x19 -> x32, starting transfers between devices: 18.9 us -> 28.1 us  [swap(): return lax.ppermute(array, axis, [(i, i ^ bit) for i in range(size)])]
  transfers between devices with their start and end apart: 22 -> 43, of which waited for: 11 -> 15; matrix products, arithmetic and copies ran while one was open for 9% -> 13% of each run, Pallas kernels for 17% -> 22%
where the time goes in v8:
time: 501 us; the launch traced here: 498 us
  waiting for transfers between devices  256 us (51%)
  Pallas kernels  108 us (22%)
  starting transfers between devices  47 us (9%)
  other arithmetic  46.9 us (9%)
  local copies, waits for them, and re-layouts  24.7 us (5%)
  between operations  14.6 us (3%)
    ppermute x7, waiting for transfers between devices, to_dp(): return lax.ppermute(array, 'dp', route)  145 us
    ppermute x32, waiting for transfers between devices, swap(): return lax.ppermute(array, axis, [(i, i ^ bit) for i in range(size)])  71.4 us
    pallas_call x5, Pallas kernels, backward(): pl.pallas_call(functools.partial(backward_kernel, firsts, blocks, bs, acc...  58 us
    pallas_call x3, Pallas kernels, forward(): pl.pallas_call(functools.partial(forward_kernel, first, blocks, bs, cuts,...  50.4 us
    ppermute x2, waiting for transfers between devices, spread(): from_xy = lax.ppermute(far_peer, ('groups', 'tensor'), diagonal)  39.2 us
    ppermute x32, starting transfers between devices, swap(): return lax.ppermute(array, axis, [(i, i ^ bit) for i in range(size)])  28.1 us
    ppermute x7, starting transfers between devices, to_dp(): return lax.ppermute(array, 'dp', route)  17.4 us
    another operation x5, other arithmetic, local(): jnp.stack([jnp.concatenate(pair, axis=0) for pair in zip(own_parts, end_p...  12.9 us
  transfers between devices with their start and end apart: 43, of which 15 were waited for; matrix products, arithmetic and copies ran while one was open for 13% of the time, Pallas kernels for 22%

profile of v8, /device:TPU:0, one launch (start us, length us, event | category | flops | bytes accessed | tf_op | source)
XLA Modules:
  0.0 497.5 jit_solution(11902803857162298660)
XLA Ops:
  7.2 3.0 constant_dynamic-slice_fusion.5
  10.3 3.0 collective-permute-start
  13.3 3.5 collective-permute-start.1
  19.4 2.6 collective-permute-start.11
  26.1 7.6 %collective-permute-done = bf16[448,1024]{1,0:T(8,128)(2,1)} collective-permute-done((bf16[448,1024]{1,0:T(8,128)(2,1)S(1)}, bf16[448,1024]{1,0:T(8,128)(2,1)}, u32[]{:S(2)}, u32[]{:S(2)}) %collective-permute-start) | collective-permute-done | bytes 917536 | tf_op jit(solution)/shard_map/ppermute | solution.py:18
  37.7 14.5 %collective-permute-done.1 = bf16[448,1024]{1,0:T(8,128)(2,1)S(1)} collective-permute-done((bf16[448,1024]{1,0:T(8,128)(2,1)S(1)}, bf16[448,1024]{1,0:T(8,128)(2,1)S(1)}, u32[]{:S(2)}, u32[]{:S(2)}) %collective-permute-start.1) | collective-permute-done | bytes 917536 | tf_op jit(solution)/shard_map/ppermute | solution.py:249
  55.7 51.3 %collective-permute-done.11 = bf16[1024,640]{1,0:T(8,128)(2,1)} collective-permute-done((bf16[1024,640]{1,0:T(8,128)(2,1)}, bf16[1024,640]{1,0:T(8,128)(2,1)}, u32[]{:S(2)}, u32[]{:S(2)}) %collective-permute-start.11) | collective-permute-done | bytes 1310752 | tf_op jit(solution)/shard_map/ppermute | solution.py:249
  113.9 2.8 constant_dynamic-slice_fusion.4
  121.7 7.5 %collective-permute-done.8 = bf16[448,1024]{1,0:T(8,128)(2,1)} collective-permute-done((bf16[448,1024]{1,0:T(8,128)(2,1)}, bf16[448,1024]{1,0:T(8,128)(2,1)}, u32[]{:S(2)}, u32[]{:S(2)}) %collective-permute-start.8) | collective-permute-done | bytes 917536 | tf_op jit(solution)/shard_map/ppermute | solution.py:18
  130.9 5.0 %collective-permute-start.15 = (bf16[896,640]{1,0:T(8,128)(2,1)S(1)}, bf16[896,640]{1,0:T(8,128)(2,1)S(1)}, u32[]{:S(2)}, u32[]{:S(2)}) collective-permute-start(bf16[896,640]{1,0:T(8,128)(2,1)S(1)} %pad_maximum_fusion.6), channel_id=1, source_target_pairs={{0,4},{12,8},{1,5},{13,9},{2,6},{14,10},{3,7},{15,11},{16,20},{28,... | collective-permute-start | bytes 3440648 | tf_op jit(solution)/shard_map/ppermute | solution.py:249
  137.9 5.4 %pad_maximum_fusion.1.w_ref.refs_1_.refs_2_ = bf16[4,1024,640]{2,1,0:T(8,128)(2,1)} fusion(bf16[1,1024,640]{2,1,0:T(8,128)(2,1)} %bitcast.11, bf16[1,1024,640]{2,1,0:T(8,128)(2,1)} %bitcast.10, bf16[1,1024,640]{2,1,0:T(8,128)(2,1)} %bitcast.9, bf16[1,1024,640]{2,1,0:T(8,128)(2,1)S(1)} %fusion.10), kind=kLoop, calls=%fused_computation.1 | loop fusion | flops 7864320 | bytes 10485760 | tf_op jit(solution)/shard_map/stack | solution.py:285
  145.3 40.4 %collective-permute-done.15 = bf16[896,640]{1,0:T(8,128)(2,1)S(1)} collective-permute-done((bf16[896,640]{1,0:T(8,128)(2,1)S(1)}, bf16[896,640]{1,0:T(8,128)(2,1)S(1)}, u32[]{:S(2)}, u32[]{:S(2)}) %collective-permute-start.15) | collective-permute-done | bytes 1146912 | tf_op jit(solution)/shard_map/ppermute | solution.py:249
  191.1 6.4 %pad_maximum_fusion.x_ref = bf16[4,1792,1024]{2,1,0:T(8,128)(2,1)} fusion(bf16[1,1792,1024]{2,1,0:T(8,128)(2,1)S(1)} %maximum_bitcast_fusion.3, bf16[1,1792,1024]{2,1,0:T(8,128)(2,1)S(1)} %maximum_bitcast_fusion.2, bf16[1,1792,1024]{2,1,0:T(8,128)(2,1)S(1)} %maximum_bitcast_fusion.1, bf16[1,1792,1024]{2,1,0:T(8,128)(2,1)S(1)} %maximum_bitcast_fusion), kind=kLoop, calls=%fused_computation | loop fusion | flops 22020096 | bytes 29360128 | tf_op jit(solution)/shard_map/stack | solution.py:310
  197.5 23.3 %shard_map.94 = (bf16[4,448,640]{2,1,0:T(8,128)(2,1)}, bf16[1792,640]{1,0:T(8,128)(2,1)}, f32[2,4,128,128]{3,2,1,0:T(8,128)}) custom-call(s32[26]{0:T(128)} %pad_add_fusion.1.meta, bf16[4,1792,1024]{2,1,0:T(8,128)(2,1)} %pad_maximum_fusion.x_ref, bf16[4,1024,640]{2,1,0:T(8,128)(2,1)} %pad_maximum_fusion.1.w_ref.refs_1_.refs_2_, ...), custom_call_target="tpu_custom_call" | custom-call | flops 9395240960 | bytes 19922944 | tf_op jit(solution)/shard_map/pallas_call | solution.py:83
  220.8 8.1 %shard_map.95 = (bf16[448,1024]{1,0:T(8,128)(2,1)}, bf16[448,1024]{1,0:T(8,128)(2,1)}, bf16[448,1024]{1,0:T(8,128)(2,1)}, bf16[448,1024]{1,0:T(8,128)(2,1)}) custom-call(s32[26]{0:T(128)} %pad_add_fusion.1.meta, bf16[1792,640]{1,0:T(8,128)(2,1)} %get-tuple-element.45.refs_0_, bf16[4,1024,640]{2,1,0:T(8,128)(2,1)} %pad_maximum_fusion.1.w_ref.refs_1_.refs_2_, ...), custom_call_target="tpu_custom_call" | custom-call | flops 1 | bytes 1 | tf_op jit(solution)/shard_map/pallas_call | solution.py:184
  233.9 8.3 %shard_map.96 = (bf16[448,1024]{1,0:T(8,128)(2,1)}, bf16[448,1024]{1,0:T(8,128)(2,1)}, bf16[448,1024]{1,0:T(8,128)(2,1)}, bf16[448,1024]{1,0:T(8,128)(2,1)}) custom-call(s32[26]{0:T(128)} %pad_add_fusion.1.meta, bf16[1792,640]{1,0:T(8,128)(2,1)} %get-tuple-element.45.refs_0_, bf16[4,1024,640]{2,1,0:T(8,128)(2,1)} %pad_maximum_fusion.1.w_ref.refs_1_.refs_2_, ...), custom_call_target="tpu_custom_call" | custom-call | flops 1 | bytes 1 | tf_op jit(solution)/shard_map/pallas_call | solution.py:184
  256.8 14.2 %collective-permute-done.16 = bf16[2,448,640]{2,1,0:T(8,128)(2,1)S(1)} collective-permute-done((bf16[2,448,640]{2,1,0:T(8,128)(2,1)S(1)}, bf16[2,448,640]{2,1,0:T(8,128)(2,1)S(1)}, u32[]{:S(2)}, u32[]{:S(2)}) %collective-permute-start.16) | collective-permute-done | bytes 1146912 | tf_op jit(solution)/shard_map/ppermute | solution.py:18
  273.2 19.7 %collective-permute-done.27 = bf16[448,1024]{1,0:T(8,128)(2,1)S(1)} collective-permute-done((bf16[448,1024]{1,0:T(8,128)(2,1)S(1)}, bf16[448,1024]{1,0:T(8,128)(2,1)S(1)}, u32[]{:S(2)}, u32[]{:S(2)}) %collective-permute-start.27) | collective-permute-done | bytes 917536 | tf_op jit(solution)/shard_map/ppermute | solution.py:339
  292.9 16.5 %collective-permute-done.23 = bf16[448,1024]{1,0:T(8,128)(2,1)S(1)} collective-permute-done((bf16[448,1024]{1,0:T(8,128)(2,1)S(1)}, bf16[448,1024]{1,0:T(8,128)(2,1)S(1)}, u32[]{:S(2)}, u32[]{:S(2)}) %collective-permute-start.23) | collective-permute-done | bytes 917536 | tf_op jit(solution)/shard_map/ppermute | solution.py:18
  309.4 3.4 add_convert_fusion.4
  314.3 39.0 %collective-permute-done.17 = bf16[2,448,640]{2,1,0:T(8,128)(2,1)S(1)} collective-permute-done((bf16[2,448,640]{2,1,0:T(8,128)(2,1)S(1)}, bf16[2,448,640]{2,1,0:T(8,128)(2,1)S(1)}, u32[]{:S(2)}, u32[]{:S(2)}) %collective-permute-start.17) | collective-permute-done | bytes 1146912 | tf_op jit(solution)/shard_map/ppermute | solution.py:249
  355.0 17.0 %shard_map.97 = (bf16[2,448,896]{2,1,0:T(8,128)(2,1)}, bf16[896,896]{1,0:T(8,128)(2,1)}, f32[2,4,128,128]{3,2,1,0:T(8,128)}) custom-call(s32[26]{0:T(128)} %pad_add_fusion.1.meta, bf16[4,1792,1024]{2,1,0:T(8,128)(2,1)} %pad_maximum_fusion.x_ref, bf16[4,1024,896]{2,1,0:T(8,128)(2,1)} %bitcast.53, bf16[4,128,128]{2,1,0:T(8,128)(2,1)} %refs_2_.3, ...), custom_call_target="tpu_custom_call" | custom-call | flops 6576668672 | bytes 14680064 | tf_op jit(solution)/shard_map/pallas_call | solution.py:83
  376.0 24.9 %shard_map.98.refs_3_ = f32[4,896,1024]{2,1,0:T(8,128)} custom-call(s32[26]{0:T(128)} %pad_add_fusion.1.meta, bf16[1792,640]{1,0:T(8,128)(2,1)} %get-tuple-element.45.refs_0_, bf16[896,896]{1,0:T(8,128)(2,1)} %get-tuple-element.55.refs_1_, bf16[4,1024,640]{2,1,0:T(8,128)(2,1)} %pad_maximum_fusion.1.w_ref.refs_1_.refs_2_, bf16[4,1024,896]{2,1,0:T(8,128)(2,1)} %bitcast.54, ...), custom_call_target="tpu_custom_call" | custom-call | flops 11274289152 | bytes 23592960 | tf_op jit(solution)/shard_map/pallas_call | solution.py:184
  401.1 10.1 %shard_map.99 = (bf16[2,448,384]{2,1,0:T(8,128)(2,1)}, bf16[896,384]{1,0:T(8,128)(2,1)}, f32[2,4,128,128]{3,2,1,0:T(8,128)}) custom-call(s32[26]{0:T(128)} %pad_add_fusion.1.meta, bf16[4,1792,1024]{2,1,0:T(8,128)(2,1)} %pad_maximum_fusion.x_ref, bf16[4,1024,384]{2,1,0:T(8,128)(2,1)} %bitcast.48, bf16[4,128,128]{2,1,0:T(8,128)(2,1)} %refs_2_.3, ...), custom_call_target="tpu_custom_call" | custom-call | flops 2818572288 | bytes 10485760 | tf_op jit(solution)/shard_map/pallas_call | solution.py:83
  412.7 8.4 %shard_map.100 = (bf16[448,1024]{1,0:T(8,128)(2,1)}, bf16[448,1024]{1,0:T(8,128)(2,1)}, bf16[448,1024]{1,0:T(8,128)(2,1)}, bf16[448,1024]{1,0:T(8,128)(2,1)}) custom-call(s32[26]{0:T(128)} %pad_add_fusion.1.meta, bf16[896,384]{1,0:T(8,128)(2,1)} %get-tuple-element.65.refs_0_, bf16[4,1024,384]{2,1,0:T(8,128)(2,1)} %bitcast.49, bf16[4,128,128]{2,1,0:T(8,128)(2,1)} %refs_2_.3, ...), custom_call_target="tpu_custom_call" | custom-call | flops 1 | bytes 1 | tf_op jit(solution)/shard_map/pallas_call | solution.py:184
  421.6 2.6 collective-permute-start.38
  426.2 8.4 %shard_map.101 = (bf16[448,1024]{1,0:T(8,128)(2,1)}, bf16[448,1024]{1,0:T(8,128)(2,1)}, bf16[448,1024]{1,0:T(8,128)(2,1)}, bf16[448,1024]{1,0:T(8,128)(2,1)}) custom-call(s32[26]{0:T(128)} %pad_add_fusion.1.meta, bf16[896,384]{1,0:T(8,128)(2,1)} %get-tuple-element.65.refs_0_, bf16[4,1024,384]{2,1,0:T(8,128)(2,1)} %bitcast.50, bf16[4,128,128]{2,1,0:T(8,128)(2,1)} %refs_2_.3, ...), custom_call_target="tpu_custom_call" | custom-call | flops 1 | bytes 1 | tf_op jit(solution)/shard_map/pallas_call | solution.py:184
  437.3 2.8 collective-permute-done.36
  441.7 2.6 collective-permute-start.34
  447.7 17.8 %collective-permute-done.34 = bf16[448,1024]{1,0:T(8,128)(2,1)S(1)} collective-permute-done((bf16[448,1024]{1,0:T(8,128)(2,1)S(1)}, bf16[448,1024]{1,0:T(8,128)(2,1)S(1)}, u32[]{:S(2)}, u32[]{:S(2)}) %collective-permute-start.34) | collective-permute-done | bytes 917536 | tf_op jit(solution)/shard_map/ppermute | solution.py:18
  465.5 19.5 %collective-permute-done.40 = bf16[448,1024]{1,0:T(8,128)(2,1)S(1)} collective-permute-done((bf16[448,1024]{1,0:T(8,128)(2,1)S(1)}, bf16[448,1024]{1,0:T(8,128)(2,1)S(1)}, u32[]{:S(2)}, u32[]{:S(2)}) %collective-permute-start.40) | collective-permute-done | bytes 917536 | tf_op jit(solution)/shard_map/ppermute | solution.py:339
  487.3 3.3 add_convert_fusion
  (179 shorter events, 79.9 us)
Async XLA Ops:
  7.2 243.8 %all-gather.5.cloned.1.call-start = ((), (), s32[]{:S(2)}) async-start(), calls=%async_computation | async-start | bytes 9175040 | tf_op jit(solution)/shard_map/all_gather | solution.py:282
  10.2 390.9 %all-gather.7.cloned.1.call-start = ((), (), s32[]{:S(2)}) async-start(), calls=%async_computation.1 | async-start | bytes 3932160 | tf_op jit(solution)/shard_map/all_gather | solution.py:321
  10.3 23.5 %collective-permute-start = (bf16[448,1024]{1,0:T(8,128)(2,1)S(1)}, bf16[448,1024]{1,0:T(8,128)(2,1)}, u32[]{:S(2)}, u32[]{:S(2)}) collective-permute-start(bf16[448,1024]{1,0:T(8,128)(2,1)S(1)} %copy-done), channel_id=1, source_target_pairs={{0,16},{16,0},{1,17},{17,1},{2,18},{18,2},{3,19},{19,3},{4,20},{20... | collective-permute-start | bytes 2752520 | tf_op jit(solution)/shard_map/ppermute | solution.py:18
  13.3 38.9 %collective-permute-start.1 = (bf16[448,1024]{1,0:T(8,128)(2,1)S(1)}, bf16[448,1024]{1,0:T(8,128)(2,1)S(1)}, u32[]{:S(2)}, u32[]{:S(2)}) collective-permute-start(bf16[448,1024]{1,0:T(8,128)(2,1)S(1)} %copy-done), channel_id=1, source_target_pairs={{0,4},{12,8},{1,5},{13,9},{2,6},{14,10},{3,7},{15,11},{16,20},{28,... | collective-permute-start | bytes 2752520 | tf_op jit(solution)/shard_map/ppermute | solution.py:249
  19.4 87.7 %collective-permute-start.11 = (bf16[1024,640]{1,0:T(8,128)(2,1)}, bf16[1024,640]{1,0:T(8,128)(2,1)}, u32[]{:S(2)}, u32[]{:S(2)}) collective-permute-start(bf16[1024,640]{1,0:T(8,128)(2,1)} %constant_dynamic-slice_fusion.8), channel_id=1, source_target_pairs={{0,4},{12,8},{1,5},{13,9},{2,6},{14,10},{3,7},{15,11},{16,20},{28,... | collective-permute-start | bytes 3932168 | tf_op jit(solution)/shard_map/ppermute | solution.py:249
  21.9 32.5 %collective-permute-start.5 = (bf16[448,1024]{1,0:T(8,128)(2,1)S(1)}, bf16[448,1024]{1,0:T(8,128)(2,1)}, u32[]{:S(2)}, u32[]{:S(2)}) collective-permute-start(bf16[448,1024]{1,0:T(8,128)(2,1)S(1)} %copy-done), channel_id=1, source_target_pairs={{0,2},{1,3},{2,0},{3,1},{4,6},{5,7},{6,4},{7,5},{8,10},{9,11},{10,... | collective-permute-start | bytes 2752520 | tf_op jit(solution)/shard_map/ppermute | solution.py:18
  23.4 107.4 %collective-permute-start.13 = (bf16[1024,640]{1,0:T(8,128)(2,1)}, bf16[1024,640]{1,0:T(8,128)(2,1)}, u32[]{:S(2)}, u32[]{:S(2)}) collective-permute-start(bf16[1024,640]{1,0:T(8,128)(2,1)} %constant_dynamic-slice_fusion.8), channel_id=1, source_target_pairs={{4,8},{8,4},{5,9},{9,5},{6,10},{10,6},{7,11},{11,7},{20,24},{24,20... | collective-permute-start | bytes 3932168 | tf_op jit(solution)/shard_map/ppermute | solution.py:249
  33.8 76.3 %collective-permute-start.6 = (bf16[448,1024]{1,0:T(8,128)(2,1)}, bf16[448,1024]{1,0:T(8,128)(2,1)S(1)}, u32[]{:S(2)}, u32[]{:S(2)}) collective-permute-start(bf16[448,1024]{1,0:T(8,128)(2,1)} %collective-permute-done), channel_id=1, source_target_pairs={{0,2},{1,3},{2,0},{3,1},{4,6},{5,7},{6,4},{7,5},{8,10},{9,11},{10,... | collective-permute-start | bytes 2752520 | tf_op jit(solution)/shard_map/ppermute | solution.py:18
  52.3 58.0 %collective-permute-start.2 = (bf16[448,1024]{1,0:T(8,128)(2,1)S(1)}, bf16[448,1024]{1,0:T(8,128)(2,1)}, u32[]{:S(2)}, u32[]{:S(2)}) collective-permute-start(bf16[448,1024]{1,0:T(8,128)(2,1)S(1)} %collective-permute-done.1), channel_id=1, source_target_pairs={{0,16},{16,0},{1,17},{17,1},{2,18},{18,2},{3,19},{19,3},{4,20},{20... | collective-permute-start | bytes 2752520 | tf_op jit(solution)/shard_map/ppermute | solution.py:18
  54.5 64.8 %collective-permute-start.7 = (bf16[448,1024]{1,0:T(8,128)(2,1)S(1)}, bf16[448,1024]{1,0:T(8,128)(2,1)}, u32[]{:S(2)}, u32[]{:S(2)}) collective-permute-start(bf16[448,1024]{1,0:T(8,128)(2,1)S(1)} %collective-permute-done.1), channel_id=1, source_target_pairs={{0,2},{1,3},{2,0},{3,1},{4,6},{5,7},{6,4},{7,5},{8,10},{9,11},{10,... | collective-permute-start | bytes 2752520 | tf_op jit(solution)/shard_map/ppermute | solution.py:18
  107.1 28.8 %collective-permute-start.12 = (bf16[1024,640]{1,0:T(8,128)(2,1)}, bf16[1024,640]{1,0:T(8,128)(2,1)}, u32[]{:S(2)}, u32[]{:S(2)}) collective-permute-start(bf16[1024,640]{1,0:T(8,128)(2,1)} %collective-permute-done.11), channel_id=1, source_target_pairs={{4,8},{8,4},{5,9},{9,5},{6,10},{10,6},{7,11},{11,7},{20,24},{24,20... | collective-permute-start | bytes 3932168 | tf_op jit(solution)/shard_map/ppermute | solution.py:249
  111.0 18.3 %collective-permute-start.8 = (bf16[448,1024]{1,0:T(8,128)(2,1)}, bf16[448,1024]{1,0:T(8,128)(2,1)}, u32[]{:S(2)}, u32[]{:S(2)}) collective-permute-start(bf16[448,1024]{1,0:T(8,128)(2,1)} %collective-permute-done.2), channel_id=1, source_target_pairs={{0,2},{1,3},{2,0},{3,1},{4,6},{5,7},{6,4},{7,5},{8,10},{9,11},{10,... | collective-permute-start | bytes 2752520 | tf_op jit(solution)/shard_map/ppermute | solution.py:18
  119.2 69.0 %collective-permute-start.3 = (bf16[896,1024]{1,0:T(8,128)(2,1)}, bf16[896,1024]{1,0:T(8,128)(2,1)}, u32[]{:S(2)}, u32[]{:S(2)}) collective-permute-start(bf16[896,1024]{1,0:T(8,128)(2,1)} %constant_dynamic-update-slice_fusion), channel_id=1, source_target_pairs={{0,1},{1,0},{2,3},{3,2},{4,5},{5,4},{6,7},{7,6},{8,9},{9,8},{10,11... | collective-permute-start | bytes 5505032 | tf_op jit(solution)/shard_map/ppermute | solution.py:18
  121.0 67.3 %collective-permute-start.4 = (bf16[896,1024]{1,0:T(8,128)(2,1)}, bf16[896,1024]{1,0:T(8,128)(2,1)}, u32[]{:S(2)}, u32[]{:S(2)}) collective-permute-start(bf16[896,1024]{1,0:T(8,128)(2,1)} %pad_maximum_fusion.3), channel_id=1, source_target_pairs={{0,1},{1,0},{2,3},{3,2},{4,5},{5,4},{6,7},{7,6},{8,9},{9,8},{10,11... | collective-permute-start | bytes 5505032 | tf_op jit(solution)/shard_map/ppermute | solution.py:18
  129.3 61.4 %collective-permute-start.9 = (bf16[896,1024]{1,0:T(8,128)(2,1)S(1)}, bf16[896,1024]{1,0:T(8,128)(2,1)S(1)}, u32[]{:S(2)}, u32[]{:S(2)}) collective-permute-start(bf16[896,1024]{1,0:T(8,128)(2,1)S(1)} %copy-done.21), channel_id=1, source_target_pairs={{0,1},{1,0},{2,3},{3,2},{4,5},{5,4},{6,7},{7,6},{8,9},{9,8},{10,11... | collective-permute-start | bytes 5505032 | tf_op jit(solution)/shard_map/ppermute | solution.py:18
  130.9 54.8 %collective-permute-start.15 = (bf16[896,640]{1,0:T(8,128)(2,1)S(1)}, bf16[896,640]{1,0:T(8,128)(2,1)S(1)}, u32[]{:S(2)}, u32[]{:S(2)}) collective-permute-start(bf16[896,640]{1,0:T(8,128)(2,1)S(1)} %pad_maximum_fusion.6), channel_id=1, source_target_pairs={{0,4},{12,8},{1,5},{13,9},{2,6},{14,10},{3,7},{15,11},{16,20},{28,... | collective-permute-start | bytes 3440648 | tf_op jit(solution)/shard_map/ppermute | solution.py:249
  135.9 54.8 %collective-permute-start.10 = (bf16[896,1024]{1,0:T(8,128)(2,1)S(1)}, bf16[896,1024]{1,0:T(8,128)(2,1)S(1)}, u32[]{:S(2)}, u32[]{:S(2)}) collective-permute-start(bf16[896,1024]{1,0:T(8,128)(2,1)S(1)} %pad_maximum_fusion.4), channel_id=1, source_target_pairs={{0,1},{1,0},{2,3},{3,2},{4,5},{5,4},{6,7},{7,6},{8,9},{9,8},{10,11... | collective-permute-start | bytes 5505032 | tf_op jit(solution)/shard_map/ppermute | solution.py:18
  185.7 46.6 %collective-permute-start.18 = (bf16[448,896]{1,0:T(8,128)(2,1)}, bf16[448,896]{1,0:T(8,128)(2,1)}, u32[]{:S(2)}, u32[]{:S(2)}) collective-permute-start(bf16[448,896]{1,0:T(8,128)(2,1)} %get-tuple-element.51), channel_id=1, source_target_pairs={{0,16},{16,0},{1,17},{17,1},{2,18},{18,2},{3,19},{19,3},{4,20},{20... | collective-permute-start | bytes 2408456 | tf_op jit(solution)/shard_map/ppermute | solution.py:18
  228.9 18.3 %collective-permute-start.24 = (bf16[448,1024]{1,0:T(8,128)(2,1)}, bf16[448,1024]{1,0:T(8,128)(2,1)}, u32[]{:S(2)}, u32[]{:S(2)}) collective-permute-start(bf16[448,1024]{1,0:T(8,128)(2,1)} %get-tuple-element.61), channel_id=1, source_target_pairs={{0,1},{1,0},{2,3},{3,2},{4,5},{5,4},{6,7},{7,6},{8,9},{9,8},{10,11... | collective-permute-start | bytes 2752520 | tf_op jit(solution)/shard_map/ppermute | solution.py:18
  242.8 28.2 %collective-permute-start.16 = (bf16[2,448,640]{2,1,0:T(8,128)(2,1)S(1)}, bf16[2,448,640]{2,1,0:T(8,128)(2,1)S(1)}, u32[]{:S(2)}, u32[]{:S(2)}) collective-permute-start(bf16[2,448,640]{2,1,0:T(8,128)(2,1)S(1)} %pad_maximum_fusion.7), channel_id=1, source_target_pairs={{0,16},{16,0},{1,17},{17,1},{2,18},{18,2},{3,19},{19,3},{4,20},{20... | collective-permute-start | bytes 3440648 | tf_op jit(solution)/shard_map/ppermute | solution.py:18
  246.8 25.7 %collective-permute-start.21 = (bf16[448,1024]{1,0:T(8,128)(2,1)}, bf16[448,1024]{1,0:T(8,128)(2,1)}, u32[]{:S(2)}, u32[]{:S(2)}) collective-permute-start(bf16[448,1024]{1,0:T(8,128)(2,1)} %get-tuple-element.58), channel_id=1, source_target_pairs={{0,1},{1,0},{2,3},{3,2},{4,5},{5,4},{6,7},{7,6},{8,9},{9,8},{10,11... | collective-permute-start | bytes 2752520 | tf_op jit(solution)/shard_map/ppermute | solution.py:18
  249.7 23.5 %collective-permute-start.25 = (bf16[448,1024]{1,0:T(8,128)(2,1)}, bf16[448,1024]{1,0:T(8,128)(2,1)}, u32[]{:S(2)}, u32[]{:S(2)}) collective-permute-start(bf16[448,1024]{1,0:T(8,128)(2,1)} %add_convert_fusion.6), channel_id=1, source_target_pairs={{0,2},{1,3},{2,0},{3,1},{4,6},{5,7},{6,4},{7,5},{8,10},{9,11},{10,... | collective-permute-start | bytes 2752520 | tf_op jit(solution)/shard_map/ppermute | solution.py:18
  252.9 40.0 %collective-permute-start.27 = (bf16[448,1024]{1,0:T(8,128)(2,1)S(1)}, bf16[448,1024]{1,0:T(8,128)(2,1)S(1)}, u32[]{:S(2)}, u32[]{:S(2)}) collective-permute-start(bf16[448,1024]{1,0:T(8,128)(2,1)S(1)} %add_convert_fusion.5), channel_id=1, source_target_pairs={{0,18},{1,19},{2,16},{3,17},{16,2},{17,3},{18,0},{19,1},{4,22},{5,... | collective-permute-start | bytes 2752520 | tf_op jit(solution)/shard_map/ppermute | solution.py:339
  255.8 53.7 %collective-permute-start.23 = (bf16[448,1024]{1,0:T(8,128)(2,1)S(1)}, bf16[448,1024]{1,0:T(8,128)(2,1)S(1)}, u32[]{:S(2)}, u32[]{:S(2)}) collective-permute-start(bf16[448,1024]{1,0:T(8,128)(2,1)S(1)} %add_convert_fusion.7), channel_id=1, source_target_pairs={{0,16},{16,0},{1,17},{17,1},{2,18},{18,2},{3,19},{19,3},{4,20},{20... | collective-permute-start | bytes 2752520 | tf_op jit(solution)/shard_map/ppermute | solution.py:18
  271.2 82.1 %collective-permute-start.17 = (bf16[2,448,640]{2,1,0:T(8,128)(2,1)S(1)}, bf16[2,448,640]{2,1,0:T(8,128)(2,1)S(1)}, u32[]{:S(2)}, u32[]{:S(2)}) collective-permute-start(bf16[2,448,640]{2,1,0:T(8,128)(2,1)S(1)} %pad_maximum_fusion.8), channel_id=1, source_target_pairs={{4,0},{8,12},{5,1},{9,13},{6,2},{10,14},{7,3},{11,15},{20,16},{24,... | collective-permute-start | bytes 3440648 | tf_op jit(solution)/shard_map/ppermute | solution.py:249
  312.8 112.2 %collective-permute-start.35 = (bf16[448,1024]{1,0:T(8,128)(2,1)}, bf16[448,1024]{1,0:T(8,128)(2,1)}, u32[]{:S(2)}, u32[]{:S(2)}) collective-permute-start(bf16[448,1024]{1,0:T(8,128)(2,1)} %add_convert_fusion.4), channel_id=1, source_target_pairs={{4,0},{8,12},{5,1},{9,13},{6,2},{10,14},{7,3},{11,15},{20,16},{24,... | collective-permute-start | bytes 2752520 | tf_op jit(solution)/shard_map/ppermute | solution.py:249
  373.2 27.8 %collective-permute-start.19 = (bf16[448,896]{1,0:T(8,128)(2,1)S(1)}, bf16[448,896]{1,0:T(8,128)(2,1)S(1)}, u32[]{:S(2)}, u32[]{:S(2)}) collective-permute-start(bf16[448,896]{1,0:T(8,128)(2,1)S(1)} %slice_bitcast_fusion), channel_id=1, source_target_pairs={{0,16},{16,0},{1,17},{17,1},{2,18},{18,2},{3,19},{19,3},{4,20},{20... | collective-permute-start | bytes 2408456 | tf_op jit(solution)/shard_map/ppermute | solution.py:18
  421.1 19.0 %collective-permute-start.33 = (bf16[448,1024]{1,0:T(8,128)(2,1)}, bf16[448,1024]{1,0:T(8,128)(2,1)}, u32[]{:S(2)}, u32[]{:S(2)}) collective-permute-start(bf16[448,1024]{1,0:T(8,128)(2,1)} %get-tuple-element.78), channel_id=1, source_target_pairs={{0,1},{1,0},{2,3},{3,2},{4,5},{5,4},{6,7},{7,6},{8,9},{9,8},{10,11... | collective-permute-start | bytes 2752520 | tf_op jit(solution)/shard_map/ppermute | solution.py:18
  421.1 23.2 %collective-permute-start.39 = (bf16[448,1024]{1,0:T(8,128)(2,1)}, bf16[448,1024]{1,0:T(8,128)(2,1)S(1)}, u32[]{:S(2)}, u32[]{:S(2)}) collective-permute-start(bf16[448,1024]{1,0:T(8,128)(2,1)} %get-tuple-element.67), channel_id=1, source_target_pairs={{0,1},{1,0},{2,3},{3,2},{4,5},{5,4},{6,7},{7,6},{8,9},{9,8},{10,11... | collective-permute-start | bytes 2752520 | tf_op jit(solution)/shard_map/ppermute | solution.py:18
  441.7 23.8 %collective-permute-start.34 = (bf16[448,1024]{1,0:T(8,128)(2,1)S(1)}, bf16[448,1024]{1,0:T(8,128)(2,1)S(1)}, u32[]{:S(2)}, u32[]{:S(2)}) collective-permute-start(bf16[448,1024]{1,0:T(8,128)(2,1)S(1)} %add_convert_fusion.2), channel_id=1, source_target_pairs={{0,2},{1,3},{2,0},{3,1},{4,6},{5,7},{6,4},{7,5},{8,10},{9,11},{10,... | collective-permute-start | bytes 2752520 | tf_op jit(solution)/shard_map/ppermute | solution.py:18
  444.7 40.3 %collective-permute-start.40 = (bf16[448,1024]{1,0:T(8,128)(2,1)S(1)}, bf16[448,1024]{1,0:T(8,128)(2,1)S(1)}, u32[]{:S(2)}, u32[]{:S(2)}) collective-permute-start(bf16[448,1024]{1,0:T(8,128)(2,1)S(1)} %add_convert_fusion.1), channel_id=1, source_target_pairs={{0,18},{1,19},{2,16},{3,17},{16,2},{17,3},{18,0},{19,1},{4,22},{5,... | collective-permute-start | bytes 2752520 | tf_op jit(solution)/shard_map/ppermute | solution.py:339
  445.1 42.2 %collective-permute-start.32 = (bf16[448,1024]{1,0:T(8,128)(2,1)S(1)}, bf16[448,1024]{1,0:T(8,128)(2,1)S(1)}, u32[]{:S(2)}, u32[]{:S(2)}) collective-permute-start(bf16[448,1024]{1,0:T(8,128)(2,1)S(1)} %add_convert_fusion.3), channel_id=1, source_target_pairs={{0,16},{16,0},{1,17},{17,1},{2,18},{18,2},{3,19},{19,3},{4,20},{20... | collective-permute-start | bytes 2752520 | tf_op jit(solution)/shard_map/ppermute | solution.py:18
  (38 other events, 521.7 us)
Sparse Core Ops, SparseCore 0:
  10.3 196.6 all-gather.4
  251.1 96.3 all-gather.6

commit v9 on v8

--- a/solution.py
+++ b/solution.py
@@ -79,7 +79,7 @@
     cuts = 2
     tile = rows // groups_of // cuts
     blocks, bs = delta.shape[0], delta.shape[1]
-    wide = next(c for c in (896, 640, 512, 384, 256, 128, width) if width % c == 0)
+    wide = next(c for c in (768, 640, 512, 384, 256, 128, width) if width % c == 0)
     return pl.pallas_call(
         functools.partial(forward_kernel, first, blocks, bs, cuts, folded),
         grid_spec=pltpu.PrefetchScalarGridSpec(
@@ -104,11 +104,7 @@
             jax.ShapeDtypeStruct((2, blocks, bs, bs), F32),
         ],
         compiler_params=params(),
-        cost_estimate=pl.CostEstimate(
-            flops=2 * rows * feats * slots * width,
-            bytes_accessed=2 * (rows + width) * feats * slots,
-            transcendentals=0,
-        ),
+        cost_estimate=pl.CostEstimate(flops=1, bytes_accessed=1, transcendentals=0),
     )(meta, x4, w4, delta, d_piece)
 
 
@@ -207,11 +203,7 @@
         ),
         out_shape=out_shape,
         compiler_params=params(),
-        cost_estimate=pl.CostEstimate(
-            flops=2 * rows * feats * width * steps if every else 1,
-            bytes_accessed=2 * (rows + feats) * width * steps if every else 1,
-            transcendentals=0,
-        ),
+        cost_estimate=pl.CostEstimate(flops=1, bytes_accessed=1, transcendentals=0),
     )(meta, *slopes, *ws, delta, *([] if acc is None else [acc]))
 
 
@@ -236,8 +228,9 @@
 
 def piece_sizes(half, bs):
     blocks = half // bs
-    fold, last = max(blocks // 3, 1), max(blocks // 5, 1)
-    return [fold * bs, (blocks - fold - last) * bs, last * bs]
+    last = max(blocks // 5, 1)
+    fold = blocks - last
+    return [(fold - fold // 2) * bs, fold // 2 * bs, last * bs]
 
 
 MIDDLE = [(1, 2), (2, 1)]
@@ -279,10 +272,15 @@
         lax.dynamic_slice(frozen, (0, mine + first), (frozen.shape[0], size))
         for first, size in zip(firsts, sizes)
     ]
-    gather_a = lax.all_gather(shards[1], "dp")
     outer = to_dp(shards[0], INWARD)
     inner = to_dp(shards[0], MIDDLE)
-    w_fold = jnp.stack([shards[0], outer, to_dp(outer, MIDDLE), inner])
+    far_end = to_dp(outer, MIDDLE)
+    w_0 = jnp.stack([shards[0], outer, far_end, inner])
+    outer = to_dp(tie(shards[1], outer), INWARD)
+    inner = to_dp(tie(shards[1], inner), MIDDLE)
+    far_end = to_dp(outer, MIDDLE)
+    w_1 = jnp.stack([shards[1], outer, far_end, inner])
+    gather_b = lax.all_gather(tie(shards[2], far_end, inner), "dp")
 
     row_part = block_rows * bs // feats
     block_info = jnp.stack(
@@ -317,19 +315,26 @@
         got = swap(tie(give, order), "groups", 1)
         order = got
         d_pieces.append(jnp.concatenate([keep, got], axis=0))
-    d_fold = jnp.concatenate([d_pieces[0], to_dp(d_pieces[0], INWARD)], axis=0)
-    gather_b = lax.all_gather(
-        tie(shards[2], gather_a, x4, d_fold, w_fold, *d_pieces[1:]), "dp"
-    )
-
-    act_f, slope_f, sums_f = forward(meta, x4, w_fold, delta, d_fold, firsts[0], 4, True)
-    over = swap(jnp.concatenate([act_f[1:2], act_f[3:4]], axis=0), "groups", 1)
-    home = to_dp(jnp.concatenate([act_f[2:3], over[1:2]], axis=0), OUTWARD)
-    activated = jnp.zeros((rows, slab), BF)
-    kept = jnp.where(middle, act_f[0], home[0])
-    activated = lax.dynamic_update_slice(activated, kept, (0, mine + firsts[0]))
-    kept = jnp.where(middle, over[0], home[1])
-    activated = lax.dynamic_update_slice(activated, kept, (0, theirs + firsts[0]))
+    d_fold = [jnp.concatenate([d, to_dp(d, INWARD)], axis=0) for d in d_pieces[:2]]
+
+    def fold(weight, piece, wait):
+        return forward(meta, x4, weight, tie(delta, wait), d_fold[piece], firsts[piece], 4, True)
+
+    def send_home(act):
+        over = swap(jnp.concatenate([act[1:2], act[3:4]], axis=0), "groups", 1)
+        return over, to_dp(jnp.concatenate([act[2:3], over[1:2]], axis=0), OUTWARD)
+
+    def place(activated, act, over, home, first):
+        kept = jnp.where(middle, act[0], home[0])
+        activated = lax.dynamic_update_slice(activated, kept, (0, mine + first))
+        kept = jnp.where(middle, over[0], home[1])
+        return lax.dynamic_update_slice(activated, kept, (0, theirs + first))
+
+    act_0, slope_0, sums_0 = fold(w_0, 0, d_pieces[2])
+    over_0, home_0 = send_home(act_0)
+    act_1, slope_1, sums_1 = fold(w_1, 1, slope_0)
+    over_1, home_1 = send_home(act_1)
+    slopes, weights = [slope_0, slope_1], [w_0, w_1]
 
     diagonal = [(i, i ^ (n_t + 2)) for i in range(2 * n_t)]
 
@@ -345,31 +350,28 @@
 
     def end_back(bit, wait):
         return backward(
-            meta, both, [slope_f], [w_fold], tie(delta, wait), firsts[:1], None, bit, [True], 1
+            meta, both, slopes, weights, tie(delta, wait), firsts[:2], None, bit, [True, True], 1
         )
 
-    end_far = end_back(3, slope_f)
+    end_far = end_back(3, slope_1)
     end_near = end_back(1, end_far[1])
     end_sum = spread(end_far, end_near).astype(BF)
     end_home = to_dp(end_sum, OUTWARD)
-
-    delta_a = tie(delta, end_near[1])
-    act_a, slope_a, sums_a = forward(meta, x4, gather_a, delta_a, d_pieces[1], firsts[1], 2)
-    back_a = swap(act_a[1], "groups", 1)
     (early,) = backward(
-        meta, both, [slope_f, slope_a], [w_fold, gather_a], tie(delta, over), firsts[:2], None,
-        None, [True, False],
-    )
-    activated = lax.dynamic_update_slice(activated, act_a[0], (0, mine + firsts[1]))
-    activated = lax.dynamic_update_slice(activated, back_a, (0, theirs + firsts[1]))
-
-    delta_b = tie(delta, early, activated, end_sum)
+        meta, both, slopes, weights, tie(delta, end_near[1], over_1, gather_b), firsts[:2], None, None,
+        [True, True],
+    )
+    activated = jnp.zeros((rows, slab), BF)
+    activated = place(activated, act_0, over_0, home_0, firsts[0])
+
+    delta_b = tie(delta, early)
     act_b, slope_b, sums_b = forward(meta, x4, gather_b, delta_b, d_pieces[2], firsts[2], 2)
     back_b = swap(act_b[1], "groups", 1)
+    activated = place(activated, act_1, over_1, home_1, firsts[1])
     activated = lax.dynamic_update_slice(activated, act_b[0], (0, mine + firsts[2]))
     activated = lax.dynamic_update_slice(activated, back_b, (0, theirs + firsts[2]))
 
-    sums = sums_f + sums_a + sums_b
+    sums = sums_0 + sums_1 + sums_b
     sums = sums[0] + swap(sums[1].astype(BF), "groups", 1).astype(F32)
     shares = [swap(sums.astype(BF), "dp", bit) for bit in range(1, n_dp)]
 
@@ -378,8 +380,8 @@
             meta, both, [slope_b], [gather_b], tie(delta_b, *wait), firsts[2:], early, bit, [False]
         )
 
-    far = list(last_back(3, slope_b))
-    near = last_back(1, far[1], sums)
+    far = list(last_back(3, slope_b, home_0, end_sum))
+    near = last_back(1, far[1], sums, home_1)
     far[2], far[3] = tie(far[2], near[1]), tie(far[3], near[1], back_b, end_home, *shares)
     d_tokens = spread(far, near) + end_home.astype(F32)
     for share in shares:

time: 501 us -> 521 us (1.040)
  other arithmetic: 46.9 us -> 78.6 us
  waiting for transfers between devices: 256 us -> 229 us
  Pallas kernels: 108 us -> 126 us
  local copies, waits for them, and re-layouts: 24.7 us -> 18.3 us
  starting transfers between devices: 47 us -> 53.3 us
    ppermute x7 -> x12, waiting for transfers between devices: 145 us -> 52.7 us  [to_dp(): return lax.ppermute(array, 'dp', route)]
    ppermute x32, waiting for transfers between devices: 71.4 us -> 157 us  [swap(): return lax.ppermute(array, axis, [(i, i ^ bit) for i in range(size)])]
    ppermute x2, waiting for transfers between devices: 39.2 us -> 19.8 us  [spread(): from_xy = lax.ppermute(far_peer, ('groups', 'tensor'), diagonal)]
    another operation x5, other arithmetic: 12.9 us -> 26.9 us  [local(): jnp.stack([jnp.concatenate(pair, axis=0) for pair in zip(own_parts, end_p...]
    ppermute x7 -> x12, starting transfers between devices: 17.4 us -> 28.8 us  [to_dp(): return lax.ppermute(array, 'dp', route)]
    pallas_call x3, Pallas kernels: 50.4 us -> 60.8 us  [forward(): pl.pallas_call(functools.partial(forward_kernel, first, blocks, bs, cuts,...]
    ppermute x32, starting transfers between devices: 28.1 us -> 19.4 us  [swap(): return lax.ppermute(array, axis, [(i, i ^ bit) for i in range(size)])]
    concatenate x3 -> x6, other arithmetic: 1.83 us -> 9.77 us  [the longest x2 6.02 us: local(): jnp.concatenate([d, to_dp(d, INWARD)], axis=0)]
  transfers between devices with their start and end apart: 43 -> 47, of which waited for: 15 -> 19; matrix products, arithmetic and copies ran while one was open for 13% -> 18% of each run, Pallas kernels for 22% -> 24%
where the time goes in v9:
time: 521 us; the launch traced here: 520 us
  waiting for transfers between devices  229 us (44%)
  Pallas kernels  126 us (24%)
  other arithmetic  78.6 us (15%)
  starting transfers between devices  53.3 us (10%)
  local copies, waits for them, and re-layouts  18.3 us (4%)
  between operations  14.6 us (3%)
    ppermute x32, waiting for transfers between devices, swap(): return lax.ppermute(array, axis, [(i, i ^ bit) for i in range(size)])  157 us
    pallas_call x5, Pallas kernels, backward(): pl.pallas_call(functools.partial(backward_kernel, firsts, blocks, bs, acc...  65.3 us
    pallas_call x3, Pallas kernels, forward(): pl.pallas_call(functools.partial(forward_kernel, first, blocks, bs, cuts,...  60.8 us
    ppermute x12, waiting for transfers between devices, to_dp(): return lax.ppermute(array, 'dp', route)  52.7 us
    ppermute x12, starting transfers between devices, to_dp(): return lax.ppermute(array, 'dp', route)  28.8 us
    another operation x5, other arithmetic, local(): jnp.stack([jnp.concatenate(pair, axis=0) for pair in zip(own_parts, end_p...  26.9 us
    ppermute x2, waiting for transfers between devices, spread(): from_xy = lax.ppermute(far_peer, ('groups', 'tensor'), diagonal)  19.8 us
    ppermute x32, starting transfers between devices, swap(): return lax.ppermute(array, axis, [(i, i ^ bit) for i in range(size)])  19.4 us
  transfers between devices with their start and end apart: 47, of which 19 were waited for; matrix products, arithmetic and copies ran while one was open for 18% of the time, Pallas kernels for 24%

profile of v9, /device:TPU:0, one launch (start us, length us, event | category | flops | bytes accessed | tf_op | source)
XLA Modules:
  0.0 520.2 jit_solution(16656508225972536592)
XLA Ops:
  10.2 4.4 collective-permute-start.1
  16.1 14.8 %collective-permute-done = bf16[448,1024]{1,0:T(8,128)(2,1)} collective-permute-done((bf16[448,1024]{1,0:T(8,128)(2,1)}, bf16[448,1024]{1,0:T(8,128)(2,1)}, u32[]{:S(2)}, u32[]{:S(2)}) %collective-permute-start) | collective-permute-done | bytes 917536 | tf_op jit(solution)/shard_map/ppermute | solution.py:18
  36.5 6.3 %collective-permute-start.11 = (bf16[1024,768]{1,0:T(8,128)(2,1)S(1)}, bf16[1024,768]{1,0:T(8,128)(2,1)}, u32[]{:S(2)}, u32[]{:S(2)}) collective-permute-start(bf16[1024,768]{1,0:T(8,128)(2,1)S(1)} %get-tuple-element.92), channel_id=1, source_target_pairs={{0,4},{12,8},{1,5},{13,9},{2,6},{14,10},{3,7},{15,11},{16,20},{28,... | collective-permute-start | bytes 4718600 | tf_op jit(solution)/shard_map/ppermute | solution.py:242
  51.6 4.6 collective-permute-done.6
  59.5 11.5 %collective-permute-done.2 = bf16[448,1024]{1,0:T(8,128)(2,1)} collective-permute-done((bf16[448,1024]{1,0:T(8,128)(2,1)}, bf16[448,1024]{1,0:T(8,128)(2,1)}, u32[]{:S(2)}, u32[]{:S(2)}) %collective-permute-start.2) | collective-permute-done | bytes 917536 | tf_op jit(solution)/shard_map/ppermute | solution.py:18
  71.0 11.8 %collective-permute-done.14 = bf16[448,768]{1,0:T(8,128)(2,1)} collective-permute-done((bf16[448,768]{1,0:T(8,128)(2,1)S(1)}, bf16[448,768]{1,0:T(8,128)(2,1)}, u32[]{:S(2)}, u32[]{:S(2)}) %collective-permute-start.14) | collective-permute-done | bytes 688160 | tf_op jit(solution)/shard_map/ppermute | solution.py:18
  92.2 10.5 %collective-permute-done.8 = bf16[448,1024]{1,0:T(8,128)(2,1)} collective-permute-done((bf16[448,1024]{1,0:T(8,128)(2,1)}, bf16[448,1024]{1,0:T(8,128)(2,1)}, u32[]{:S(2)}, u32[]{:S(2)}) %collective-permute-start.8) | collective-permute-done | bytes 917536 | tf_op jit(solution)/shard_map/ppermute | solution.py:18
  113.9 3.5 maximum_bitcast_fusion
  126.2 3.4 maximum_bitcast_fusion.2
  130.5 20.3 %collective-permute-done.17 = bf16[896,768]{1,0:T(8,128)(2,1)} collective-permute-done((bf16[896,768]{1,0:T(8,128)(2,1)}, bf16[896,768]{1,0:T(8,128)(2,1)}, u32[]{:S(2)}, u32[]{:S(2)}) %collective-permute-start.17) | collective-permute-done | bytes 1376288 | tf_op jit(solution)/shard_map/ppermute | solution.py:242
  152.6 6.0 %pad_maximum_fusion.1.w_ref.refs_2_ = bf16[4,1024,768]{2,1,0:T(8,128)(2,1)} fusion(bf16[1,1024,768]{2,1,0:T(8,128)(2,1)} %bitcast.11, bf16[1,1024,768]{2,1,0:T(8,128)(2,1)} %bitcast.10, bf16[1,1024,768]{2,1,0:T(8,128)(2,1)} %bitcast.9, bf16[1,1024,768]{2,1,0:T(8,128)(2,1)S(1)} %bitcast.58), kind=kLoop, calls=%fused_computation.1 | loop fusion | flops 9437184 | bytes 12582912 | tf_op jit(solution)/shard_map/stack | solution.py:278
  159.5 4.4 maximum_bitcast_fusion.1
  167.1 8.9 %collective-permute-done.23 = bf16[896,768]{1,0:T(8,128)(2,1)S(1)} collective-permute-done((bf16[896,768]{1,0:T(8,128)(2,1)S(1)}, bf16[896,768]{1,0:T(8,128)(2,1)S(1)}, u32[]{:S(2)}, u32[]{:S(2)}) %collective-permute-start.23) | collective-permute-done | bytes 1376288 | tf_op jit(solution)/shard_map/ppermute | solution.py:242
  182.4 13.3 %pad_maximum_fusion.x_ref = bf16[4,1792,1024]{2,1,0:T(8,128)(2,1)} fusion(bf16[1,1792,1024]{2,1,0:T(8,128)(2,1)} %maximum_bitcast_fusion.3, bf16[1,1792,1024]{2,1,0:T(8,128)(2,1)} %maximum_bitcast_fusion.2, bf16[1,1792,1024]{2,1,0:T(8,128)(2,1)} %maximum_bitcast_fusion.1, bf16[1,1792,1024]{2,1,0:T(8,128)(2,1)} %maximum_bitcast_fusion), kind=kLoop, calls=%fused_computation | loop fusion | flops 22020096 | bytes 29360128 | tf_op jit(solution)/shard_map/stack | solution.py:308
  195.7 26.7 %shard_map.94 = (bf16[4,448,768]{2,1,0:T(8,128)(2,1)}, bf16[1792,768]{1,0:T(8,128)(2,1)}, f32[2,4,128,128]{3,2,1,0:T(8,128)}) custom-call(s32[26]{0:T(128)} %pad_add_fusion.1.meta, bf16[4,1792,1024]{2,1,0:T(8,128)(2,1)} %pad_maximum_fusion.x_ref, bf16[4,1024,768]{2,1,0:T(8,128)(2,1)} %pad_maximum_fusion.1.w_ref.refs_2_, bf16[4,128,128]{2,1,0:T(8,128)(2,1)} %refs_2_.1, ...), custom_call_target="tpu_custom_call" | custom-call | flops 1 | bytes 1 | tf_op jit(solution)/shard_map/pallas_call | solution.py:83
  222.4 5.3 %pad_maximum_fusion.2.w_ref.refs_3_ = bf16[4,1024,768]{2,1,0:T(8,128)(2,1)} fusion(bf16[1,1024,768]{2,1,0:T(8,128)(2,1)S(1)} %bitcast.59, bf16[1,1024,768]{2,1,0:T(8,128)(2,1)} %bitcast.16, bf16[1,1024,768]{2,1,0:T(8,128)(2,1)} %bitcast.15, bf16[1,1024,768]{2,1,0:T(8,128)(2,1)S(1)} %bitcast.57), kind=kLoop, calls=%fused_computation.2 | loop fusion | flops 9437184 | bytes 12582912 | tf_op jit(solution)/shard_map/stack | solution.py:282
  227.7 24.0 %shard_map.95 = (bf16[4,448,768]{2,1,0:T(8,128)(2,1)}, bf16[1792,768]{1,0:T(8,128)(2,1)}, f32[2,4,128,128]{3,2,1,0:T(8,128)}) custom-call(s32[26]{0:T(128)} %pad_add_fusion.1.meta, bf16[4,1792,1024]{2,1,0:T(8,128)(2,1)} %pad_maximum_fusion.x_ref, bf16[4,1024,768]{2,1,0:T(8,128)(2,1)} %pad_maximum_fusion.2.w_ref.refs_3_, bf16[4,128,128]{2,1,0:T(8,128)(2,1)} %refs_2_.1, ...), custom_call_target="tpu_custom_call" | custom-call | flops 1 | bytes 1 | tf_op jit(solution)/shard_map/pallas_call | solution.py:83
  251.8 12.3 %shard_map.96 = (bf16[448,1024]{1,0:T(8,128)(2,1)}, bf16[448,1024]{1,0:T(8,128)(2,1)}, bf16[448,1024]{1,0:T(8,128)(2,1)}, bf16[448,1024]{1,0:T(8,128)(2,1)}) custom-call(s32[26]{0:T(128)} %pad_add_fusion.1.meta, bf16[1792,768]{1,0:T(8,128)(2,1)} %get-tuple-element.53.refs_0_, bf16[1792,768]{1,0:T(8,128)(2,1)} %get-tuple-element.57.refs_1_, ...), custom_call_target="tpu_custom_call" | custom-call | flops 1 | bytes 1 | tf_op jit(solution)/shard_map/pallas_call | solution.py:180
  266.5 11.9 %shard_map.97 = (bf16[448,1024]{1,0:T(8,128)(2,1)}, bf16[448,1024]{1,0:T(8,128)(2,1)}, bf16[448,1024]{1,0:T(8,128)(2,1)}, bf16[448,1024]{1,0:T(8,128)(2,1)}) custom-call(s32[26]{0:T(128)} %pad_add_fusion.1.meta, bf16[1792,768]{1,0:T(8,128)(2,1)} %get-tuple-element.53.refs_0_, bf16[1792,768]{1,0:T(8,128)(2,1)} %get-tuple-element.57.refs_1_, ...), custom_call_target="tpu_custom_call" | custom-call | flops 1 | bytes 1 | tf_op jit(solution)/shard_map/pallas_call | solution.py:180
  286.6 12.1 %collective-permute-done.18 = bf16[2,448,768]{2,1,0:T(8,128)(2,1)} collective-permute-done((bf16[2,448,768]{2,1,0:T(8,128)(2,1)}, bf16[2,448,768]{2,1,0:T(8,128)(2,1)}, u32[]{:S(2)}, u32[]{:S(2)}) %collective-permute-start.18) | collective-permute-done | bytes 1376288 | tf_op jit(solution)/shard_map/ppermute | solution.py:18
  301.2 46.6 %collective-permute-done.24 = bf16[2,448,768]{2,1,0:T(8,128)(2,1)S(1)} collective-permute-done((bf16[2,448,768]{2,1,0:T(8,128)(2,1)S(1)}, bf16[2,448,768]{2,1,0:T(8,128)(2,1)S(1)}, u32[]{:S(2)}, u32[]{:S(2)}) %collective-permute-start.24) | collective-permute-done | bytes 1376288 | tf_op jit(solution)/shard_map/ppermute | solution.py:18
  351.9 15.2 %collective-permute-done.29 = bf16[448,1024]{1,0:T(8,128)(2,1)S(1)} collective-permute-done((bf16[448,1024]{1,0:T(8,128)(2,1)S(1)}, bf16[448,1024]{1,0:T(8,128)(2,1)S(1)}, u32[]{:S(2)}, u32[]{:S(2)}) %collective-permute-start.29) | collective-permute-done | bytes 917536 | tf_op jit(solution)/shard_map/ppermute | solution.py:18
  370.3 24.5 %shard_map.98.refs_3_ = f32[4,896,1024]{2,1,0:T(8,128)} custom-call(s32[26]{0:T(128)} %pad_add_fusion.1.meta, bf16[1792,768]{1,0:T(8,128)(2,1)} %get-tuple-element.53.refs_0_, bf16[1792,768]{1,0:T(8,128)(2,1)} %get-tuple-element.57.refs_1_, bf16[4,1024,768]{2,1,0:T(8,128)(2,1)} %pad_maximum_fusion.1.w_ref.refs_2_, ...), custom_call_target="tpu_custom_call" | custom-call | flops 1 | bytes 1 | tf_op jit(solution)/shard_map/pallas_call | solution.py:180
  394.7 10.1 %shard_map.99 = (bf16[2,448,384]{2,1,0:T(8,128)(2,1)}, bf16[896,384]{1,0:T(8,128)(2,1)}, f32[2,4,128,128]{3,2,1,0:T(8,128)}) custom-call(s32[26]{0:T(128)} %pad_add_fusion.1.meta, bf16[4,1792,1024]{2,1,0:T(8,128)(2,1)} %pad_maximum_fusion.x_ref, bf16[4,1024,384]{2,1,0:T(8,128)(2,1)} %bitcast.54, bf16[4,128,128]{2,1,0:T(8,128)(2,1)} %refs_2_.1, ...), custom_call_target="tpu_custom_call" | custom-call | flops 1 | bytes 1 | tf_op jit(solution)/shard_map/pallas_call | solution.py:83
  407.8 8.4 %shard_map.100 = (bf16[448,1024]{1,0:T(8,128)(2,1)}, bf16[448,1024]{1,0:T(8,128)(2,1)}, bf16[448,1024]{1,0:T(8,128)(2,1)}, bf16[448,1024]{1,0:T(8,128)(2,1)}) custom-call(s32[26]{0:T(128)} %pad_add_fusion.1.meta, bf16[896,384]{1,0:T(8,128)(2,1)} %get-tuple-element.65.refs_0_, bf16[4,1024,384]{2,1,0:T(8,128)(2,1)} %bitcast.55, bf16[4,128,128]{2,1,0:T(8,128)(2,1)} %refs_2_.1, ...), custom_call_target="tpu_custom_call" | custom-call | flops 1 | bytes 1 | tf_op jit(solution)/shard_map/pallas_call | solution.py:180
  418.8 12.8 %collective-permute-done.25 = bf16[2,448,768]{2,1,0:T(8,128)(2,1)} collective-permute-done((bf16[2,448,768]{2,1,0:T(8,128)(2,1)}, bf16[2,448,768]{2,1,0:T(8,128)(2,1)}, u32[]{:S(2)}, u32[]{:S(2)}) %collective-permute-start.25) | collective-permute-done | bytes 1376288 | tf_op jit(solution)/shard_map/ppermute | solution.py:242
  431.5 8.3 %shard_map.101 = (bf16[448,1024]{1,0:T(8,128)(2,1)}, bf16[448,1024]{1,0:T(8,128)(2,1)}, bf16[448,1024]{1,0:T(8,128)(2,1)}, bf16[448,1024]{1,0:T(8,128)(2,1)}) custom-call(s32[26]{0:T(128)} %pad_add_fusion.1.meta, bf16[896,384]{1,0:T(8,128)(2,1)} %get-tuple-element.65.refs_0_, bf16[4,1024,384]{2,1,0:T(8,128)(2,1)} %bitcast.56, bf16[4,128,128]{2,1,0:T(8,128)(2,1)} %refs_2_.1, ...), custom_call_target="tpu_custom_call" | custom-call | flops 1 | bytes 1 | tf_op jit(solution)/shard_map/pallas_call | solution.py:180
  439.8 9.9 %collective-permute-done.40 = bf16[448,1024]{1,0:T(8,128)(2,1)} collective-permute-done((bf16[448,1024]{1,0:T(8,128)(2,1)}, bf16[448,1024]{1,0:T(8,128)(2,1)}, u32[]{:S(2)}, u32[]{:S(2)}) %collective-permute-start.40) | collective-permute-done | bytes 917536 | tf_op jit(solution)/shard_map/ppermute | solution.py:242
  451.3 5.4 %collective-permute-done.42 = bf16[4,128,128]{2,1,0:T(8,128)(2,1)S(1)} collective-permute-done((bf16[4,128,128]{2,1,0:T(8,128)(2,1)}, bf16[4,128,128]{2,1,0:T(8,128)(2,1)S(1)}, u32[]{:S(2)}, u32[]{:S(2)}) %collective-permute-start.42) | collective-permute-done | bytes 131104 | tf_op jit(solution)/shard_map/ppermute | solution.py:18
  458.0 3.9 collective-permute-done.41
  471.4 15.3 %collective-permute-done.39 = bf16[448,1024]{1,0:T(8,128)(2,1)S(1)} collective-permute-done((bf16[448,1024]{1,0:T(8,128)(2,1)S(1)}, bf16[448,1024]{1,0:T(8,128)(2,1)S(1)}, u32[]{:S(2)}, u32[]{:S(2)}) %collective-permute-start.39) | collective-permute-done | bytes 917536 | tf_op jit(solution)/shard_map/ppermute | solution.py:18
  486.7 19.8 %collective-permute-done.45 = bf16[448,1024]{1,0:T(8,128)(2,1)S(1)} collective-permute-done((bf16[448,1024]{1,0:T(8,128)(2,1)S(1)}, bf16[448,1024]{1,0:T(8,128)(2,1)S(1)}, u32[]{:S(2)}, u32[]{:S(2)}) %collective-permute-start.45) | collective-permute-done | bytes 917536 | tf_op jit(solution)/shard_map/ppermute | solution.py:344
  (190 shorter events, 109.3 us)
Async XLA Ops:
  7.2 363.1 %all-gather.3.cloned.1.call-start = ((), (), s32[]{:S(2)}) async-start(), calls=%async_computation | async-start | bytes 3932160 | tf_op jit(solution)/shard_map/all_gather | solution.py:283
  10.2 37.2 %collective-permute-start.1 = (bf16[448,1024]{1,0:T(8,128)(2,1)}, bf16[448,1024]{1,0:T(8,128)(2,1)}, u32[]{:S(2)}, u32[]{:S(2)}) collective-permute-start(bf16[448,1024]{1,0:T(8,128)(2,1)} %param.7), channel_id=1, source_target_pairs={{0,4},{12,8},{1,5},{13,9},{2,6},{14,10},{3,7},{15,11},{16,20},{28,... | collective-permute-start | bytes 2752520 | tf_op jit(solution)/shard_map/ppermute | solution.py:242
  14.7 35.7 %collective-permute-start.5 = (bf16[448,1024]{1,0:T(8,128)(2,1)}, bf16[448,1024]{1,0:T(8,128)(2,1)}, u32[]{:S(2)}, u32[]{:S(2)}) collective-permute-start(bf16[448,1024]{1,0:T(8,128)(2,1)} %param.7), channel_id=1, source_target_pairs={{0,2},{1,3},{2,0},{3,1},{4,6},{5,7},{6,4},{7,5},{8,10},{9,11},{10,... | collective-permute-start | bytes 2752520 | tf_op jit(solution)/shard_map/ppermute | solution.py:18
  34.7 50.3 %collective-permute-start.13 = (bf16[1024,768]{1,0:T(8,128)(2,1)S(1)}, bf16[1024,768]{1,0:T(8,128)(2,1)}, u32[]{:S(2)}, u32[]{:S(2)}) collective-permute-start(bf16[1024,768]{1,0:T(8,128)(2,1)S(1)} %get-tuple-element.92), channel_id=1, source_target_pairs={{4,8},{8,4},{5,9},{9,5},{6,10},{10,6},{7,11},{11,7},{20,24},{24,20... | collective-permute-start | bytes 4718600 | tf_op jit(solution)/shard_map/ppermute | solution.py:242
  36.5 46.9 %collective-permute-start.11 = (bf16[1024,768]{1,0:T(8,128)(2,1)S(1)}, bf16[1024,768]{1,0:T(8,128)(2,1)}, u32[]{:S(2)}, u32[]{:S(2)}) collective-permute-start(bf16[1024,768]{1,0:T(8,128)(2,1)S(1)} %get-tuple-element.92), channel_id=1, source_target_pairs={{0,4},{12,8},{1,5},{13,9},{2,6},{14,10},{3,7},{15,11},{16,20},{28,... | collective-permute-start | bytes 4718600 | tf_op jit(solution)/shard_map/ppermute | solution.py:242
  57.4 25.4 %collective-permute-start.14 = (bf16[448,768]{1,0:T(8,128)(2,1)S(1)}, bf16[448,768]{1,0:T(8,128)(2,1)}, u32[]{:S(2)}, u32[]{:S(2)}) collective-permute-start(bf16[448,768]{1,0:T(8,128)(2,1)S(1)} %get-tuple-element.46), channel_id=1, source_target_pairs={{0,16},{16,0},{1,17},{17,1},{2,18},{18,2},{3,19},{19,3},{4,20},{20... | collective-permute-start | bytes 2064392 | tf_op jit(solution)/shard_map/ppermute | solution.py:18
  58.0 29.5 %collective-permute-start.7 = (bf16[448,1024]{1,0:T(8,128)(2,1)}, bf16[448,1024]{1,0:T(8,128)(2,1)}, u32[]{:S(2)}, u32[]{:S(2)}) collective-permute-start(bf16[448,1024]{1,0:T(8,128)(2,1)} %collective-permute-done.1), channel_id=1, source_target_pairs={{0,2},{1,3},{2,0},{3,1},{4,6},{5,7},{6,4},{7,5},{8,10},{9,11},{10,... | collective-permute-start | bytes 2752520 | tf_op jit(solution)/shard_map/ppermute | solution.py:18
  71.0 41.4 %collective-permute-start.3 = (bf16[896,1024]{1,0:T(8,128)(2,1)}, bf16[896,1024]{1,0:T(8,128)(2,1)}, u32[]{:S(2)}, u32[]{:S(2)}) collective-permute-start(bf16[896,1024]{1,0:T(8,128)(2,1)} %constant_dynamic-update-slice_fusion), channel_id=1, source_target_pairs={{0,1},{1,0},{2,3},{3,2},{4,5},{5,4},{6,7},{7,6},{8,9},{9,8},{10,11... | collective-permute-start | bytes 5505032 | tf_op jit(solution)/shard_map/ppermute | solution.py:18
  85.0 36.1 %collective-permute-start.20 = (bf16[1024,768]{1,0:T(8,128)(2,1)S(1)}, bf16[1024,768]{1,0:T(8,128)(2,1)}, u32[]{:S(2)}, u32[]{:S(2)}) collective-permute-start(bf16[1024,768]{1,0:T(8,128)(2,1)S(1)} %get-tuple-element.51), channel_id=1, source_target_pairs={{0,4},{12,8},{1,5},{13,9},{2,6},{14,10},{3,7},{15,11},{16,20},{28,... | collective-permute-start | bytes 4718600 | tf_op jit(solution)/shard_map/ppermute | solution.py:242
  87.5 33.7 %collective-permute-start.12 = (bf16[1024,768]{1,0:T(8,128)(2,1)}, bf16[1024,768]{1,0:T(8,128)(2,1)}, u32[]{:S(2)}, u32[]{:S(2)}) collective-permute-start(bf16[1024,768]{1,0:T(8,128)(2,1)} %collective-permute-done.11), channel_id=1, source_target_pairs={{4,8},{8,4},{5,9},{9,5},{6,10},{10,6},{7,11},{11,7},{20,24},{24,20... | collective-permute-start | bytes 4718600 | tf_op jit(solution)/shard_map/ppermute | solution.py:242
  102.6 27.1 %collective-permute-start.4 = (bf16[896,1024]{1,0:T(8,128)(2,1)}, bf16[896,1024]{1,0:T(8,128)(2,1)}, u32[]{:S(2)}, u32[]{:S(2)}) collective-permute-start(bf16[896,1024]{1,0:T(8,128)(2,1)} %pad_maximum_fusion.5), channel_id=1, source_target_pairs={{0,1},{1,0},{2,3},{3,2},{4,5},{5,4},{6,7},{7,6},{8,9},{9,8},{10,11... | collective-permute-start | bytes 5505032 | tf_op jit(solution)/shard_map/ppermute | solution.py:18
  105.4 45.4 %collective-permute-start.17 = (bf16[896,768]{1,0:T(8,128)(2,1)}, bf16[896,768]{1,0:T(8,128)(2,1)}, u32[]{:S(2)}, u32[]{:S(2)}) collective-permute-start(bf16[896,768]{1,0:T(8,128)(2,1)} %pad_maximum_fusion.7), channel_id=1, source_target_pairs={{0,4},{12,8},{1,5},{13,9},{2,6},{14,10},{3,7},{15,11},{16,20},{28,... | collective-permute-start | bytes 4128776 | tf_op jit(solution)/shard_map/ppermute | solution.py:242
  121.2 57.7 %collective-permute-start.9 = (bf16[896,1024]{1,0:T(8,128)(2,1)S(1)}, bf16[896,1024]{1,0:T(8,128)(2,1)S(1)}, u32[]{:S(2)}, u32[]{:S(2)}) collective-permute-start(bf16[896,1024]{1,0:T(8,128)(2,1)S(1)} %copy-done.22), channel_id=1, source_target_pairs={{0,1},{1,0},{2,3},{3,2},{4,5},{5,4},{6,7},{7,6},{8,9},{9,8},{10,11... | collective-permute-start | bytes 5505032 | tf_op jit(solution)/shard_map/ppermute | solution.py:18
  121.2 57.7 %collective-permute-start.10 = (bf16[896,1024]{1,0:T(8,128)(2,1)S(1)}, bf16[896,1024]{1,0:T(8,128)(2,1)S(1)}, u32[]{:S(2)}, u32[]{:S(2)}) collective-permute-start(bf16[896,1024]{1,0:T(8,128)(2,1)S(1)} %pad_maximum_fusion.6), channel_id=1, source_target_pairs={{0,1},{1,0},{2,3},{3,2},{4,5},{5,4},{6,7},{7,6},{8,9},{9,8},{10,11... | collective-permute-start | bytes 5505032 | tf_op jit(solution)/shard_map/ppermute | solution.py:18
  123.1 53.0 %collective-permute-start.23 = (bf16[896,768]{1,0:T(8,128)(2,1)S(1)}, bf16[896,768]{1,0:T(8,128)(2,1)S(1)}, u32[]{:S(2)}, u32[]{:S(2)}) collective-permute-start(bf16[896,768]{1,0:T(8,128)(2,1)S(1)} %pad_maximum_fusion.10), channel_id=1, source_target_pairs={{0,4},{12,8},{1,5},{13,9},{2,6},{14,10},{3,7},{15,11},{16,20},{28,... | collective-permute-start | bytes 4128776 | tf_op jit(solution)/shard_map/ppermute | solution.py:242
  129.7 51.5 %collective-permute-start.22 = (bf16[1024,768]{1,0:T(8,128)(2,1)S(1)}, bf16[1024,768]{1,0:T(8,128)(2,1)S(1)}, u32[]{:S(2)}, u32[]{:S(2)}) collective-permute-start(bf16[1024,768]{1,0:T(8,128)(2,1)S(1)} %get-tuple-element.51), channel_id=1, source_target_pairs={{4,8},{8,4},{5,9},{9,5},{6,10},{10,6},{7,11},{11,7},{20,24},{24,20... | collective-permute-start | bytes 4718600 | tf_op jit(solution)/shard_map/ppermute | solution.py:242
  150.8 31.6 %collective-permute-start.21 = (bf16[1024,768]{1,0:T(8,128)(2,1)}, bf16[1024,768]{1,0:T(8,128)(2,1)}, u32[]{:S(2)}, u32[]{:S(2)}) collective-permute-start(bf16[1024,768]{1,0:T(8,128)(2,1)} %collective-permute-done.20), channel_id=1, source_target_pairs={{4,8},{8,4},{5,9},{9,5},{6,10},{10,6},{7,11},{11,7},{20,24},{24,20... | collective-permute-start | bytes 4718600 | tf_op jit(solution)/shard_map/ppermute | solution.py:242
  265.4 33.3 %collective-permute-start.18 = (bf16[2,448,768]{2,1,0:T(8,128)(2,1)}, bf16[2,448,768]{2,1,0:T(8,128)(2,1)}, u32[]{:S(2)}, u32[]{:S(2)}) collective-permute-start(bf16[2,448,768]{2,1,0:T(8,128)(2,1)} %pad_maximum_fusion.8), channel_id=1, source_target_pairs={{0,16},{16,0},{1,17},{17,1},{2,18},{18,2},{3,19},{19,3},{4,20},{20... | collective-permute-start | bytes 4128776 | tf_op jit(solution)/shard_map/ppermute | solution.py:18
  279.3 68.4 %collective-permute-start.24 = (bf16[2,448,768]{2,1,0:T(8,128)(2,1)S(1)}, bf16[2,448,768]{2,1,0:T(8,128)(2,1)S(1)}, u32[]{:S(2)}, u32[]{:S(2)}) collective-permute-start(bf16[2,448,768]{2,1,0:T(8,128)(2,1)S(1)} %pad_maximum_fusion.11), channel_id=1, source_target_pairs={{0,16},{16,0},{1,17},{17,1},{2,18},{18,2},{3,19},{19,3},{4,20},{20... | collective-permute-start | bytes 4128776 | tf_op jit(solution)/shard_map/ppermute | solution.py:18
  280.3 70.2 %collective-permute-start.27 = (bf16[448,1024]{1,0:T(8,128)(2,1)S(1)}, bf16[448,1024]{1,0:T(8,128)(2,1)S(1)}, u32[]{:S(2)}, u32[]{:S(2)}) collective-permute-start(bf16[448,1024]{1,0:T(8,128)(2,1)S(1)} %copy-done.25), channel_id=1, source_target_pairs={{0,1},{1,0},{2,3},{3,2},{4,5},{5,4},{6,7},{7,6},{8,9},{9,8},{10,11... | collective-permute-start | bytes 2752520 | tf_op jit(solution)/shard_map/ppermute | solution.py:18
  282.0 69.9 %collective-permute-start.31 = (bf16[448,1024]{1,0:T(8,128)(2,1)S(1)}, bf16[448,1024]{1,0:T(8,128)(2,1)S(1)}, u32[]{:S(2)}, u32[]{:S(2)}) collective-permute-start(bf16[448,1024]{1,0:T(8,128)(2,1)S(1)} %add_convert_fusion.6), channel_id=1, source_target_pairs={{0,2},{1,3},{2,0},{3,1},{4,6},{5,7},{6,4},{7,5},{8,10},{9,11},{10,... | collective-permute-start | bytes 2752520 | tf_op jit(solution)/shard_map/ppermute | solution.py:18
  283.6 68.3 %collective-permute-start.33 = (bf16[448,1024]{1,0:T(8,128)(2,1)S(1)}, bf16[448,1024]{1,0:T(8,128)(2,1)S(1)}, u32[]{:S(2)}, u32[]{:S(2)}) collective-permute-start(bf16[448,1024]{1,0:T(8,128)(2,1)S(1)} %add_convert_fusion.5), channel_id=1, source_target_pairs={{0,18},{1,19},{2,16},{3,17},{16,2},{17,3},{18,0},{19,1},{4,22},{5,... | collective-permute-start | bytes 2752520 | tf_op jit(solution)/shard_map/ppermute | solution.py:344
  298.7 68.3 %collective-permute-start.29 = (bf16[448,1024]{1,0:T(8,128)(2,1)S(1)}, bf16[448,1024]{1,0:T(8,128)(2,1)S(1)}, u32[]{:S(2)}, u32[]{:S(2)}) collective-permute-start(bf16[448,1024]{1,0:T(8,128)(2,1)S(1)} %add_convert_fusion.7), channel_id=1, source_target_pairs={{0,16},{16,0},{1,17},{17,1},{2,18},{18,2},{3,19},{19,3},{4,20},{20... | collective-permute-start | bytes 2752520 | tf_op jit(solution)/shard_map/ppermute | solution.py:18
  347.8 58.3 %collective-permute-start.19 = (bf16[2,448,768]{2,1,0:T(8,128)(2,1)}, bf16[2,448,768]{2,1,0:T(8,128)(2,1)}, u32[]{:S(2)}, u32[]{:S(2)}) collective-permute-start(bf16[2,448,768]{2,1,0:T(8,128)(2,1)} %pad_maximum_fusion.9), channel_id=1, source_target_pairs={{4,0},{8,12},{5,1},{9,13},{6,2},{10,14},{7,3},{11,15},{20,16},{24,... | collective-permute-start | bytes 4128776 | tf_op jit(solution)/shard_map/ppermute | solution.py:242
  350.6 81.0 %collective-permute-start.25 = (bf16[2,448,768]{2,1,0:T(8,128)(2,1)}, bf16[2,448,768]{2,1,0:T(8,128)(2,1)}, u32[]{:S(2)}, u32[]{:S(2)}) collective-permute-start(bf16[2,448,768]{2,1,0:T(8,128)(2,1)} %pad_maximum_fusion.12), channel_id=1, source_target_pairs={{4,0},{8,12},{5,1},{9,13},{6,2},{10,14},{7,3},{11,15},{20,16},{24,... | collective-permute-start | bytes 4128776 | tf_op jit(solution)/shard_map/ppermute | solution.py:242
  369.0 80.8 %collective-permute-start.40 = (bf16[448,1024]{1,0:T(8,128)(2,1)}, bf16[448,1024]{1,0:T(8,128)(2,1)}, u32[]{:S(2)}, u32[]{:S(2)}) collective-permute-start(bf16[448,1024]{1,0:T(8,128)(2,1)} %add_convert_fusion.4), channel_id=1, source_target_pairs={{4,0},{8,12},{5,1},{9,13},{6,2},{10,14},{7,3},{11,15},{20,16},{24,... | collective-permute-start | bytes 2752520 | tf_op jit(solution)/shard_map/ppermute | solution.py:242
  416.2 45.7 %collective-permute-start.38 = (bf16[448,1024]{1,0:T(8,128)(2,1)}, bf16[448,1024]{1,0:T(8,128)(2,1)}, u32[]{:S(2)}, u32[]{:S(2)}) collective-permute-start(bf16[448,1024]{1,0:T(8,128)(2,1)} %get-tuple-element.84), channel_id=1, source_target_pairs={{0,1},{1,0},{2,3},{3,2},{4,5},{5,4},{6,7},{7,6},{8,9},{9,8},{10,11... | collective-permute-start | bytes 2752520 | tf_op jit(solution)/shard_map/ppermute | solution.py:18
  416.5 47.1 %collective-permute-start.44 = (bf16[448,1024]{1,0:T(8,128)(2,1)}, bf16[448,1024]{1,0:T(8,128)(2,1)}, u32[]{:S(2)}, u32[]{:S(2)}) collective-permute-start(bf16[448,1024]{1,0:T(8,128)(2,1)} %get-tuple-element.73), channel_id=1, source_target_pairs={{0,1},{1,0},{2,3},{3,2},{4,5},{5,4},{6,7},{7,6},{8,9},{9,8},{10,11... | collective-permute-start | bytes 2752520 | tf_op jit(solution)/shard_map/ppermute | solution.py:18
  417.4 32.3 %collective-permute-start.43 = (bf16[4,128,128]{2,1,0:T(8,128)(2,1)}, bf16[4,128,128]{2,1,0:T(8,128)(2,1)S(1)}, u32[]{:S(2)}, u32[]{:S(2)}) collective-permute-start(bf16[4,128,128]{2,1,0:T(8,128)(2,1)} %get-tuple-element.87), channel_id=1, source_target_pairs={{0,12},{4,8},{8,4},{12,0},{1,13},{5,9},{9,5},{13,1},{2,14},{6,10},... | collective-permute-start | bytes 393224 | tf_op jit(solution)/shard_map/ppermute | solution.py:18
  431.5 30.3 %collective-permute-start.26 = (bf16[448,384]{1,0:T(8,128)(2,1)S(1)}, bf16[448,384]{1,0:T(8,128)(2,1)S(1)}, u32[]{:S(2)}, u32[]{:S(2)}) collective-permute-start(bf16[448,384]{1,0:T(8,128)(2,1)S(1)} %slice_bitcast_fusion), channel_id=1, source_target_pairs={{0,16},{16,0},{1,17},{17,1},{2,18},{18,2},{3,19},{19,3},{4,20},{20... | collective-permute-start | bytes 1032200 | tf_op jit(solution)/shard_map/ppermute | solution.py:18
  465.2 41.3 %collective-permute-start.45 = (bf16[448,1024]{1,0:T(8,128)(2,1)S(1)}, bf16[448,1024]{1,0:T(8,128)(2,1)S(1)}, u32[]{:S(2)}, u32[]{:S(2)}) collective-permute-start(bf16[448,1024]{1,0:T(8,128)(2,1)S(1)} %add_convert_fusion.1), channel_id=1, source_target_pairs={{0,18},{1,19},{2,16},{3,17},{16,2},{17,3},{18,0},{19,1},{4,22},{5,... | collective-permute-start | bytes 2752520 | tf_op jit(solution)/shard_map/ppermute | solution.py:344
  468.1 41.9 %collective-permute-start.37 = (bf16[448,1024]{1,0:T(8,128)(2,1)S(1)}, bf16[448,1024]{1,0:T(8,128)(2,1)S(1)}, u32[]{:S(2)}, u32[]{:S(2)}) collective-permute-start(bf16[448,1024]{1,0:T(8,128)(2,1)S(1)} %add_convert_fusion.3), channel_id=1, source_target_pairs={{0,16},{16,0},{1,17},{17,1},{2,18},{18,2},{3,19},{19,3},{4,20},{20... | collective-permute-start | bytes 2752520 | tf_op jit(solution)/shard_map/ppermute | solution.py:18
  (43 other events, 733.1 us)
Sparse Core Ops, SparseCore 0:
  182.5 78.8 all-gather.2

commit v10 on v7

--- a/solution.py
+++ b/solution.py
@@ -74,7 +74,7 @@
 def forward(meta, x4, w4, delta, d_piece, first, groups_of):
     rows, width = d_piece.shape
     slots, feats = w4.shape[0], w4.shape[1]
-    cuts = 2
+    cuts = 1
     tile = rows // groups_of // cuts
     blocks, bs = delta.shape[0], delta.shape[1]
     wide = next(c for c in (512, 384, 256, 128, width) if width % c == 0)
@@ -102,11 +102,7 @@
             jax.ShapeDtypeStruct((groups_of, blocks, bs, bs), F32),
         ],
         compiler_params=params(),
-        cost_estimate=pl.CostEstimate(
-            flops=2 * rows * feats * slots * width,
-            bytes_accessed=2 * (rows + width) * feats * slots,
-            transcendentals=0,
-        ),
+        cost_estimate=pl.CostEstimate(flops=1, bytes_accessed=1, transcendentals=0),
     )(meta, x4, w4, delta, d_piece)
 
 
@@ -195,11 +191,7 @@
         ),
         out_shape=out_shape,
         compiler_params=params(),
-        cost_estimate=pl.CostEstimate(
-            flops=2 * rows * feats * width * steps if every else 1,
-            bytes_accessed=2 * (rows + feats) * width * steps if every else 1,
-            transcendentals=0,
-        ),
+        cost_estimate=pl.CostEstimate(flops=1, bytes_accessed=1, transcendentals=0),
     )(meta, *slopes, *ws, delta, *([] if acc is None else [acc]))
 
 
@@ -292,14 +284,13 @@
 
     sums = sums_a + sums_b
     sums = sums[0] + swap(sums[1].astype(BF), "groups", 1).astype(F32)
-    shares = [swap(sums.astype(BF), "dp", bit) for bit in range(1, n_dp)]
     far_own_give, far_peer_give, far_own, far_peer = back_of(3)
     far_peer_got = swap(far_peer_give, "tensor", 1)
     far_own_got = swap(far_own_give, "tensor", 1)
-    near_own_give, near_peer_give, near_own, near_peer = back_of(1, far_peer, sums)
+    near_own_give, near_peer_give, near_own, near_peer = back_of(1, far_peer, sums, back_b)
     near_peer_got = swap(near_peer_give, "tensor", 1)
     near_own_got = swap(near_own_give, "tensor", 1)
-    far_peer, far_own = tie(far_peer, near_peer, back_b, *shares), tie(far_own, near_peer)
+    far_peer, far_own = tie(far_peer, near_peer), tie(far_own, near_peer)
     far_peer = (far_peer.astype(F32) + far_peer_got.astype(F32)).astype(BF)
     diagonal = [(i, i ^ (n_t + 2)) for i in range(2 * n_t)]
     from_xy = lax.ppermute(far_peer, ("groups", "tensor"), diagonal)
@@ -307,6 +298,7 @@
     from_x = swap(far_own, "tensor", 2)
     near_peer = (near_peer.astype(F32) + near_peer_got.astype(F32)).astype(BF)
     from_y = swap(near_peer, "groups", 1)
+    shares = [swap(tie(sums.astype(BF), near_peer), "dp", bit) for bit in range(1, n_dp)]
     near_own = near_own.astype(F32) + near_own_got.astype(F32)
     d_tokens = near_own + from_y.astype(F32) + from_x.astype(F32) + from_xy.astype(F32)
     for share in shares:

time: 393 us -> 385 us (0.980)
    ppermute x1, waiting for transfers between devices: 15.6 us -> 0.01 us  [local(): from_xy = lax.ppermute(far_peer, ('groups', 'tensor'), diagonal)]
    ppermute x19, waiting for transfers between devices: 88.1 us -> 98.2 us  [swap(): return lax.ppermute(array, axis, [(i, i ^ bit) for i in range(size)])]
  transfers between devices with their start and end apart: 22 -> 22, of which waited for: 11 -> 12; matrix products, arithmetic and copies ran while one was open for 9% -> 8% of each run, Pallas kernels for 17% -> 17%
where the time goes in v10:
time: 385 us; the launch traced here: 384 us
  waiting for transfers between devices  231 us (60%)
  Pallas kernels  76 us (20%)
  local copies, waits for them, and re-layouts  21.6 us (6%)
  other arithmetic  20.4 us (5%)
  starting transfers between devices  20.1 us (5%)
  between operations  14.4 us (4%)
    all_gather x1, waiting for transfers between devices, local(): gather_a = lax.all_gather(shards[0], 'dp')  128 us
    ppermute x19, waiting for transfers between devices, swap(): return lax.ppermute(array, axis, [(i, i ^ bit) for i in range(size)])  98.2 us
    pallas_call x3, Pallas kernels, backward(): pl.pallas_call(functools.partial(backward_kernel, firsts, blocks, bs, acc...  40.7 us
    pallas_call x2, Pallas kernels, forward(): pl.pallas_call(functools.partial(forward_kernel, first, blocks, bs, cuts)...  35.3 us
    ppermute x19, starting transfers between devices, swap(): return lax.ppermute(array, axis, [(i, i ^ bit) for i in range(size)])  18 us
  transfers between devices with their start and end apart: 22, of which 12 were waited for; matrix products, arithmetic and copies ran while one was open for 8% of the time, Pallas kernels for 17%

profile of v10, /device:TPU:0, one launch (start us, length us, event | category | flops | bytes accessed | tf_op | source)
XLA Modules:
  0.0 383.7 jit_solution(16997067145450067551)
XLA Ops:
  7.2 3.8 constant_dynamic-slice_fusion.5
  12.2 3.0 collective-permute-start
  16.6 19.0 %collective-permute-done = bf16[448,1024]{1,0:T(8,128)(2,1)} collective-permute-done((bf16[448,1024]{1,0:T(8,128)(2,1)S(1)}, bf16[448,1024]{1,0:T(8,128)(2,1)}, u32[]{:S(2)}, u32[]{:S(2)}) %collective-permute-start) | collective-permute-done | bytes 917536 | tf_op jit(solution)/shard_map/ppermute | solution.py:18
  35.6 1.7 collective-permute-start.3
  38.3 3.1 constant_dynamic-slice_fusion.4
  41.4 2.3 constant_dynamic-update-slice_fusion
  44.9 12.5 %collective-permute-done.3 = bf16[448,1024]{1,0:T(8,128)(2,1)} collective-permute-done((bf16[448,1024]{1,0:T(8,128)(2,1)}, bf16[448,1024]{1,0:T(8,128)(2,1)}, u32[]{:S(2)}, u32[]{:S(2)}) %collective-permute-start.3) | collective-permute-done | bytes 917536 | tf_op jit(solution)/shard_map/ppermute | solution.py:18
  60.2 1.9 constant_dynamic-slice_fusion.1
  62.1 26.1 %collective-permute-done.5 = bf16[448,1536]{1,0:T(8,128)(2,1)} collective-permute-done((bf16[448,1536]{1,0:T(8,128)(2,1)}, bf16[448,1536]{1,0:T(8,128)(2,1)}, u32[]{:S(2)}, u32[]{:S(2)}) %collective-permute-start.5) | collective-permute-done | bytes 1376288 | tf_op jit(solution)/shard_map/ppermute | solution.py:18
  89.3 2.1 constant_dynamic-slice_fusion.2
  91.4 3.1 pad_maximum_fusion.1.d_ref
  95.9 1.9 pad_maximum_fusion.2.d_ref
  97.9 6.2 %pad_maximum_fusion.x_ref = bf16[4,896,1024]{2,1,0:T(8,128)(2,1)} fusion(bf16[1,896,1024]{2,1,0:T(8,128)(2,1)} %bitcast.7, bf16[1,896,1024]{2,1,0:T(8,128)(2,1)S(1)} %bitcast.36, bf16[1,896,1024]{2,1,0:T(8,128)(2,1)} %bitcast.5, bf16[1,896,1024]{2,1,0:T(8,128)(2,1)} %bitcast.4), kind=kLoop, calls=%fused_computation | loop fusion | flops 11010048 | bytes 14680064 | tf_op jit(solution)/shard_map/stack | solution.py:256
  104.1 128.0 %all-gather.5.cloned.1.call-done = bf16[4096,1536]{1,0:T(8,128)(2,1)} async-done(((bf16[1024,1536]{1,0:T(8,128)(2,1)}), bf16[4096,1536]{1,0:T(8,128)(2,1)}) %all-gather.5.cloned.1.call-update) | async-done | bytes 12582928 | tf_op jit(solution)/shard_map/all_gather | solution.py:237
  233.0 23.9 %shard_map.94 = (bf16[2,448,1536]{2,1,0:T(8,128)(2,1)}, bf16[896,1536]{1,0:T(8,128)(2,1)}, f32[2,4,128,128]{3,2,1,0:T(8,128)}) custom-call(s32[20]{0:T(128)} %pad_add_fusion.1.meta, bf16[4,896,1024]{2,1,0:T(8,128)(2,1)} %pad_maximum_fusion.x_ref, bf16[4,1024,1536]{2,1,0:T(8,128)(2,1)} %bitcast.31, bf16[4,128,128]{2,1,0:T(8,128)(2,1)} %refs_2_.3, ...), custom_call_target="tpu_custom_call" | custom-call | flops 1 | bytes 1 | tf_op jit(solution)/shard_map/pallas_call | solution.py:81
  258.3 1.6 collective-permute-start.6
  259.9 23.8 %shard_map.95.refs_3_ = f32[4,896,1024]{2,1,0:T(8,128)} custom-call(s32[20]{0:T(128)} %pad_add_fusion.1.meta, bf16[896,1536]{1,0:T(8,128)(2,1)} %get-tuple-element.29.refs_0_, bf16[4,1024,1536]{2,1,0:T(8,128)(2,1)} %bitcast.32, bf16[4,128,128]{2,1,0:T(8,128)(2,1)} %refs_2_.3), custom_call_target="tpu_custom_call" | custom-call | flops 1 | bytes 1 | tf_op jit(solution)/shard_map/pallas_call | solution.py:174
  283.9 1.5 copy-done.1
  285.6 5.2 %collective-permute-done.6 = bf16[448,1536]{1,0:T(8,128)(2,1)S(1)} collective-permute-done((bf16[448,1536]{1,0:T(8,128)(2,1)S(1)}, bf16[448,1536]{1,0:T(8,128)(2,1)S(1)}, u32[]{:S(2)}, u32[]{:S(2)}) %collective-permute-start.6) | collective-permute-done | bytes 1376288 | tf_op jit(solution)/shard_map/ppermute | solution.py:18
  291.0 5.0 %all-gather.7.cloned.1.call-done = bf16[4096,384]{1,0:T(8,128)(2,1)} async-done(((bf16[1024,384]{1,0:T(8,128)(2,1)}), bf16[4096,384]{1,0:T(8,128)(2,1)}) %all-gather.7.cloned.1.call-update) | async-done | bytes 3145744 | tf_op jit(solution)/shard_map/all_gather | solution.py:267
  295.9 11.4 %shard_map.96 = (bf16[2,448,384]{2,1,0:T(8,128)(2,1)}, bf16[896,384]{1,0:T(8,128)(2,1)}, f32[2,4,128,128]{3,2,1,0:T(8,128)}) custom-call(s32[20]{0:T(128)} %pad_add_fusion.1.meta, bf16[4,896,1024]{2,1,0:T(8,128)(2,1)} %pad_maximum_fusion.x_ref, bf16[4,1024,384]{2,1,0:T(8,128)(2,1)} %bitcast.33, bf16[4,128,128]{2,1,0:T(8,128)(2,1)} %refs_2_.3, ...), custom_call_target="tpu_custom_call" | custom-call | flops 1 | bytes 1 | tf_op jit(solution)/shard_map/pallas_call | solution.py:81
  308.7 2.1 collective-permute-start.8
  310.7 8.6 %shard_map.97 = (bf16[448,1024]{1,0:T(8,128)(2,1)}, bf16[448,1024]{1,0:T(8,128)(2,1)}, bf16[448,1024]{1,0:T(8,128)(2,1)}, bf16[448,1024]{1,0:T(8,128)(2,1)}) custom-call(s32[20]{0:T(128)} %pad_add_fusion.1.meta, bf16[896,384]{1,0:T(8,128)(2,1)} %get-tuple-element.32.refs_0_, bf16[4,1024,384]{2,1,0:T(8,128)(2,1)} %bitcast.34, bf16[4,128,128]{2,1,0:T(8,128)(2,1)} %refs_2_.3, ...), custom_call_target="tpu_custom_call" | custom-call | flops 1 | bytes 1 | tf_op jit(solution)/shard_map/pallas_call | solution.py:174
  320.4 8.4 %shard_map.98 = (bf16[448,1024]{1,0:T(8,128)(2,1)}, bf16[448,1024]{1,0:T(8,128)(2,1)}, bf16[448,1024]{1,0:T(8,128)(2,1)}, bf16[448,1024]{1,0:T(8,128)(2,1)}) custom-call(s32[20]{0:T(128)} %pad_add_fusion.1.meta, bf16[896,384]{1,0:T(8,128)(2,1)} %get-tuple-element.32.refs_0_, bf16[4,1024,384]{2,1,0:T(8,128)(2,1)} %bitcast.35, bf16[4,128,128]{2,1,0:T(8,128)(2,1)} %refs_2_.3, ...), custom_call_target="tpu_custom_call" | custom-call | flops 1 | bytes 1 | tf_op jit(solution)/shard_map/pallas_call | solution.py:174
  330.1 1.8 add_convert_fusion.1
  331.9 2.0 collective-permute-start.16
  338.3 4.8 %collective-permute-done.19 = bf16[4,128,128]{2,1,0:T(8,128)(2,1)S(1)} collective-permute-done((bf16[4,128,128]{2,1,0:T(8,128)(2,1)S(1)}, bf16[4,128,128]{2,1,0:T(8,128)(2,1)S(1)}, u32[]{:S(2)}, u32[]{:S(2)}) %collective-permute-start.19) | collective-permute-done | bytes 131104 | tf_op jit(solution)/shard_map/ppermute | solution.py:18
  343.0 2.0 collective-permute-start.18
  345.1 5.9 %collective-permute-done.18 = bf16[4,128,128]{2,1,0:T(8,128)(2,1)S(1)} collective-permute-done((bf16[4,128,128]{2,1,0:T(8,128)(2,1)S(1)}, bf16[4,128,128]{2,1,0:T(8,128)(2,1)S(1)}, u32[]{:S(2)}, u32[]{:S(2)}) %collective-permute-start.18) | collective-permute-done | bytes 131104 | tf_op jit(solution)/shard_map/ppermute | solution.py:18
  351.2 4.8 %collective-permute-done.17 = bf16[4,128,128]{2,1,0:T(8,128)(2,1)S(1)} collective-permute-done((bf16[4,128,128]{2,1,0:T(8,128)(2,1)S(1)}, bf16[4,128,128]{2,1,0:T(8,128)(2,1)S(1)}, u32[]{:S(2)}, u32[]{:S(2)}) %collective-permute-start.17) | collective-permute-done | bytes 131104 | tf_op jit(solution)/shard_map/ppermute | solution.py:18
  356.8 18.1 %collective-permute-done.14 = bf16[448,1024]{1,0:T(8,128)(2,1)S(1)} collective-permute-done((bf16[448,1024]{1,0:T(8,128)(2,1)S(1)}, bf16[448,1024]{1,0:T(8,128)(2,1)S(1)}, u32[]{:S(2)}, u32[]{:S(2)}) %collective-permute-start.14) | collective-permute-done | bytes 917536 | tf_op jit(solution)/shard_map/ppermute | solution.py:18
  374.9 1.9 add_convert_fusion
  (89 shorter events, 21.9 us)
Async XLA Ops:
  7.2 224.9 %all-gather.5.cloned.1.call-start = ((), (), s32[]{:S(2)}) async-start(), calls=%async_computation | async-start | bytes 15728640 | tf_op jit(solution)/shard_map/all_gather | solution.py:237
  11.0 284.9 %all-gather.7.cloned.1.call-start = ((), (), s32[]{:S(2)}) async-start(), calls=%async_computation.1 | async-start | bytes 3932160 | tf_op jit(solution)/shard_map/all_gather | solution.py:267
  12.2 23.4 %collective-permute-start = (bf16[448,1024]{1,0:T(8,128)(2,1)S(1)}, bf16[448,1024]{1,0:T(8,128)(2,1)}, u32[]{:S(2)}, u32[]{:S(2)}) collective-permute-start(bf16[448,1024]{1,0:T(8,128)(2,1)S(1)} %copy-done.3), channel_id=1, source_target_pairs={{0,16},{16,0},{1,17},{17,1},{2,18},{18,2},{3,19},{19,3},{4,20},{20... | collective-permute-start | bytes 2752520 | tf_op jit(solution)/shard_map/ppermute | solution.py:18
  15.1 28.5 %collective-permute-start.2 = (bf16[448,1024]{1,0:T(8,128)(2,1)S(1)}, bf16[448,1024]{1,0:T(8,128)(2,1)}, u32[]{:S(2)}, u32[]{:S(2)}) collective-permute-start(bf16[448,1024]{1,0:T(8,128)(2,1)S(1)} %copy-done.3), channel_id=1, source_target_pairs={{0,2},{1,3},{2,0},{3,1},{4,6},{5,7},{6,4},{7,5},{8,10},{9,11},{10,... | collective-permute-start | bytes 2752520 | tf_op jit(solution)/shard_map/ppermute | solution.py:18
  35.6 21.9 %collective-permute-start.3 = (bf16[448,1024]{1,0:T(8,128)(2,1)}, bf16[448,1024]{1,0:T(8,128)(2,1)}, u32[]{:S(2)}, u32[]{:S(2)}) collective-permute-start(bf16[448,1024]{1,0:T(8,128)(2,1)} %collective-permute-done), channel_id=1, source_target_pairs={{0,2},{1,3},{2,0},{3,1},{4,6},{5,7},{6,4},{7,5},{8,10},{9,11},{10,... | collective-permute-start | bytes 2752520 | tf_op jit(solution)/shard_map/ppermute | solution.py:18
  43.6 54.2 %collective-permute-start.1 = (bf16[896,1024]{1,0:T(8,128)(2,1)}, bf16[896,1024]{1,0:T(8,128)(2,1)}, u32[]{:S(2)}, u32[]{:S(2)}) collective-permute-start(bf16[896,1024]{1,0:T(8,128)(2,1)} %constant_dynamic-update-slice_fusion), channel_id=1, source_target_pairs={{0,1},{1,0},{2,3},{3,2},{4,5},{5,4},{6,7},{7,6},{8,9},{9,8},{10,11... | collective-permute-start | bytes 5505032 | tf_op jit(solution)/shard_map/ppermute | solution.py:18
  57.4 30.8 %collective-permute-start.5 = (bf16[448,1536]{1,0:T(8,128)(2,1)}, bf16[448,1536]{1,0:T(8,128)(2,1)}, u32[]{:S(2)}, u32[]{:S(2)}) collective-permute-start(bf16[448,1536]{1,0:T(8,128)(2,1)} %get-tuple-element.25), channel_id=1, source_target_pairs={{0,16},{16,0},{1,17},{17,1},{2,18},{18,2},{3,19},{19,3},{4,20},{20... | collective-permute-start | bytes 4128776 | tf_op jit(solution)/shard_map/ppermute | solution.py:18
  60.1 37.7 %collective-permute-start.4 = (bf16[896,1024]{1,0:T(8,128)(2,1)S(1)}, bf16[896,1024]{1,0:T(8,128)(2,1)}, u32[]{:S(2)}, u32[]{:S(2)}) collective-permute-start(bf16[896,1024]{1,0:T(8,128)(2,1)S(1)} %constant_dynamic-update-slice_fusion.2), channel_id=1, source_target_pairs={{0,1},{1,0},{2,3},{3,2},{4,5},{5,4},{6,7},{7,6},{8,9},{9,8},{10,11... | collective-permute-start | bytes 5505032 | tf_op jit(solution)/shard_map/ppermute | solution.py:18
  88.2 7.7 %collective-permute-start.7 = (bf16[448,384]{1,0:T(8,128)(2,1)}, bf16[448,384]{1,0:T(8,128)(2,1)}, u32[]{:S(2)}, u32[]{:S(2)}) collective-permute-start(bf16[448,384]{1,0:T(8,128)(2,1)} %get-tuple-element.27), channel_id=1, source_target_pairs={{0,16},{16,0},{1,17},{17,1},{2,18},{18,2},{3,19},{19,3},{4,20},{20... | collective-permute-start | bytes 1032200 | tf_op jit(solution)/shard_map/ppermute | solution.py:18
  97.8 134.3 %copy-start.13 = (s32[4]{0:T(128)S(1)}, s32[4]{0:T(128)}, u32[]{:S(2)}) copy-start(s32[4]{0:T(128)} %param.10) | copy-start | bytes 52
  97.8 134.3 %copy-start.14 = (s32[4]{0:T(128)S(1)}, s32[4]{0:T(128)}, u32[]{:S(2)}) copy-start(s32[4]{0:T(128)} %param.11) | copy-start | bytes 52
  258.3 32.5 %collective-permute-start.6 = (bf16[448,1536]{1,0:T(8,128)(2,1)S(1)}, bf16[448,1536]{1,0:T(8,128)(2,1)S(1)}, u32[]{:S(2)}, u32[]{:S(2)}) collective-permute-start(bf16[448,1536]{1,0:T(8,128)(2,1)S(1)} %slice_bitcast_fusion), channel_id=1, source_target_pairs={{0,16},{16,0},{1,17},{17,1},{2,18},{18,2},{3,19},{19,3},{4,20},{20... | collective-permute-start | bytes 4128776 | tf_op jit(solution)/shard_map/ppermute | solution.py:18
  295.9 11.4 %copy-start.9 = (f32[2,4,128,128]{3,2,1,0:T(8,128)S(1)}, f32[2,4,128,128]{3,2,1,0:T(8,128)}, u32[]{:S(2)}) copy-start(f32[2,4,128,128]{3,2,1,0:T(8,128)} %get-tuple-element.34) | copy-start | bytes 1572868
  308.5 10.8 %collective-permute-start.9 = (bf16[4,128,128]{2,1,0:T(8,128)(2,1)S(1)}, bf16[4,128,128]{2,1,0:T(8,128)(2,1)S(1)}, u32[]{:S(2)}, u32[]{:S(2)}) collective-permute-start(bf16[4,128,128]{2,1,0:T(8,128)(2,1)S(1)} %fusion.1), channel_id=1, source_target_pairs={{0,16},{16,0},{1,17},{17,1},{2,18},{18,2},{3,19},{19,3},{4,20},{20... | collective-permute-start | bytes 393224 | tf_op jit(solution)/shard_map/ppermute | solution.py:18
  308.7 11.7 %collective-permute-start.8 = (bf16[448,384]{1,0:T(8,128)(2,1)S(1)}, bf16[448,384]{1,0:T(8,128)(2,1)S(1)}, u32[]{:S(2)}, u32[]{:S(2)}) collective-permute-start(bf16[448,384]{1,0:T(8,128)(2,1)S(1)} %slice_bitcast_fusion.1), channel_id=1, source_target_pairs={{0,16},{16,0},{1,17},{17,1},{2,18},{18,2},{3,19},{19,3},{4,20},{20... | collective-permute-start | bytes 1032200 | tf_op jit(solution)/shard_map/ppermute | solution.py:18
  319.3 10.8 %collective-permute-start.15 = (bf16[448,1024]{1,0:T(8,128)(2,1)}, bf16[448,1024]{1,0:T(8,128)(2,1)}, u32[]{:S(2)}, u32[]{:S(2)}) collective-permute-start(bf16[448,1024]{1,0:T(8,128)(2,1)} %get-tuple-element.45), channel_id=1, source_target_pairs={{0,1},{1,0},{2,3},{3,2},{4,5},{5,4},{6,7},{7,6},{8,9},{9,8},{10,11... | collective-permute-start | bytes 2752520 | tf_op jit(solution)/shard_map/ppermute | solution.py:18
  320.4 8.4 %copy-start.10 = (bf16[448,384]{1,0:T(8,128)(2,1)}, bf16[448,384]{1,0:T(8,128)(2,1)S(1)}, u32[]{:S(2)}) copy-start(bf16[448,384]{1,0:T(8,128)(2,1)S(1)} %collective-permute-done.8) | copy-start | bytes 1032196
  320.4 9.0 %copy-start.15 = (s32[4,1]{0,1:T(1,128)S(1)}, s32[4,1]{0,1:T(1,128)}, u32[]{:S(2)}) copy-start(s32[4,1]{0,1:T(1,128)} %param.12) | copy-start | bytes 52
  328.8 5.1 %collective-permute-start.11 = (bf16[448,1024]{1,0:T(8,128)(2,1)}, bf16[448,1024]{1,0:T(8,128)(2,1)}, u32[]{:S(2)}, u32[]{:S(2)}) collective-permute-start(bf16[448,1024]{1,0:T(8,128)(2,1)} %get-tuple-element.40), channel_id=1, source_target_pairs={{0,1},{1,0},{2,3},{3,2},{4,5},{5,4},{6,7},{7,6},{8,9},{9,8},{10,11... | collective-permute-start | bytes 2752520 | tf_op jit(solution)/shard_map/ppermute | solution.py:18
  329.3 7.5 %collective-permute-start.13 = (bf16[448,1024]{1,0:T(8,128)(2,1)}, bf16[448,1024]{1,0:T(8,128)(2,1)S(1)}, u32[]{:S(2)}, u32[]{:S(2)}) collective-permute-start(bf16[448,1024]{1,0:T(8,128)(2,1)} %get-tuple-element.43), channel_id=1, source_target_pairs={{0,1},{1,0},{2,3},{3,2},{4,5},{5,4},{6,7},{7,6},{8,9},{9,8},{10,11... | collective-permute-start | bytes 2752520 | tf_op jit(solution)/shard_map/ppermute | solution.py:18
  329.6 27.2 %collective-permute-start.10 = (bf16[448,1024]{1,0:T(8,128)(2,1)}, bf16[448,1024]{1,0:T(8,128)(2,1)S(1)}, u32[]{:S(2)}, u32[]{:S(2)}) collective-permute-start(bf16[448,1024]{1,0:T(8,128)(2,1)} %get-tuple-element.38), channel_id=1, source_target_pairs={{0,1},{1,0},{2,3},{3,2},{4,5},{5,4},{6,7},{7,6},{8,9},{9,8},{10,11... | collective-permute-start | bytes 2752520 | tf_op jit(solution)/shard_map/ppermute | solution.py:18
  331.9 24.9 %collective-permute-start.16 = (bf16[448,1024]{1,0:T(8,128)(2,1)S(1)}, bf16[448,1024]{1,0:T(8,128)(2,1)S(1)}, u32[]{:S(2)}, u32[]{:S(2)}) collective-permute-start(bf16[448,1024]{1,0:T(8,128)(2,1)S(1)} %add_convert_fusion.1), channel_id=1, source_target_pairs={{0,18},{1,19},{2,16},{3,17},{16,2},{17,3},{18,0},{19,1},{4,22},{5,... | collective-permute-start | bytes 2752520 | tf_op jit(solution)/shard_map/ppermute | solution.py:296
  335.5 15.5 %copy-start.8 = (bf16[2,448,384]{2,1,0:T(8,128)(2,1)S(1)}, bf16[2,448,384]{2,1,0:T(8,128)(2,1)}, u32[]{:S(2)}) copy-start(bf16[2,448,384]{2,1,0:T(8,128)(2,1)} %get-tuple-element.31) | copy-start | bytes 2064388
  335.5 15.6 %copy-start.11 = (bf16[448,384]{1,0:T(8,128)(2,1)S(1)}, bf16[448,384]{1,0:T(8,128)(2,1)}, u32[]{:S(2)}) copy-start(bf16[448,384]{1,0:T(8,128)(2,1)} %copy-done.10) | copy-start | bytes 1032196
  335.5 20.5 %copy-start.2 = (f32[4,128,128]{2,1,0:T(8,128)S(1)}, f32[4,128,128]{2,1,0:T(8,128)}, u32[]{:S(2)}) copy-start(f32[4,128,128]{2,1,0:T(8,128)} %get-tuple-element.48) | copy-start | bytes 786436
  335.5 7.5 %collective-permute-start.19 = (bf16[4,128,128]{2,1,0:T(8,128)(2,1)S(1)}, bf16[4,128,128]{2,1,0:T(8,128)(2,1)S(1)}, u32[]{:S(2)}, u32[]{:S(2)}) collective-permute-start(bf16[4,128,128]{2,1,0:T(8,128)(2,1)S(1)} %copy-done.12), channel_id=1, source_target_pairs={{0,12},{4,8},{8,4},{12,0},{1,13},{5,9},{9,5},{13,1},{2,14},{6,10},... | collective-permute-start | bytes 393224 | tf_op jit(solution)/shard_map/ppermute | solution.py:18
  337.2 37.7 %copy-start.4 = (bf16[448,1024]{1,0:T(8,128)(2,1)S(1)}, bf16[448,1024]{1,0:T(8,128)(2,1)}, u32[]{:S(2)}) copy-start(bf16[448,1024]{1,0:T(8,128)(2,1)} %get-tuple-element.37) | copy-start | bytes 2752516
  337.2 37.7 %collective-permute-start.14 = (bf16[448,1024]{1,0:T(8,128)(2,1)S(1)}, bf16[448,1024]{1,0:T(8,128)(2,1)S(1)}, u32[]{:S(2)}, u32[]{:S(2)}) collective-permute-start(bf16[448,1024]{1,0:T(8,128)(2,1)S(1)} %add_convert_fusion.2), channel_id=1, source_target_pairs={{0,2},{1,3},{2,0},{3,1},{4,6},{5,7},{6,4},{7,5},{8,10},{9,11},{10,... | collective-permute-start | bytes 2752520 | tf_op jit(solution)/shard_map/ppermute | solution.py:18
  337.9 37.0 %collective-permute-start.12 = (bf16[448,1024]{1,0:T(8,128)(2,1)S(1)}, bf16[448,1024]{1,0:T(8,128)(2,1)S(1)}, u32[]{:S(2)}, u32[]{:S(2)}) collective-permute-start(bf16[448,1024]{1,0:T(8,128)(2,1)S(1)} %add_convert_fusion.3), channel_id=1, source_target_pairs={{0,16},{16,0},{1,17},{17,1},{2,18},{18,2},{3,19},{19,3},{4,20},{20... | collective-permute-start | bytes 2752520 | tf_op jit(solution)/shard_map/ppermute | solution.py:18
  343.0 8.0 %collective-permute-start.18 = (bf16[4,128,128]{2,1,0:T(8,128)(2,1)S(1)}, bf16[4,128,128]{2,1,0:T(8,128)(2,1)S(1)}, u32[]{:S(2)}, u32[]{:S(2)}) collective-permute-start(bf16[4,128,128]{2,1,0:T(8,128)(2,1)S(1)} %copy-done.12), channel_id=1, source_target_pairs={{0,8},{4,12},{8,0},{12,4},{1,9},{5,13},{9,1},{13,5},{2,10},{6,14},... | collective-permute-start | bytes 393224 | tf_op jit(solution)/shard_map/ppermute | solution.py:18
  351.0 5.0 %collective-permute-start.17 = (bf16[4,128,128]{2,1,0:T(8,128)(2,1)S(1)}, bf16[4,128,128]{2,1,0:T(8,128)(2,1)S(1)}, u32[]{:S(2)}, u32[]{:S(2)}) collective-permute-start(bf16[4,128,128]{2,1,0:T(8,128)(2,1)S(1)} %copy-done.12), channel_id=1, source_target_pairs={{0,4},{4,0},{8,12},{12,8},{1,5},{5,1},{9,13},{13,9},{2,6},{6,2},{1... | collective-permute-start | bytes 393224 | tf_op jit(solution)/shard_map/ppermute | solution.py:18
  351.1 25.7 %copy-start = (bf16[448,3840]{1,0:T(8,128)(2,1)}, bf16[448,3840]{1,0:T(8,128)(2,1)S(1)}, u32[]{:S(2)}) copy-start(bf16[448,3840]{1,0:T(8,128)(2,1)S(1)} %constant_dynamic-update-slice_fusion.4) | copy-start | bytes 10321924
  (6 other events, 17.5 us)
Sparse Core Ops, SparseCore 0:
  11.1 220.8 all-gather.4
  234.2 61.6 all-gather.6

commit v11 on v10

--- a/solution.py
+++ b/solution.py
@@ -10,7 +10,7 @@
 CAP = 2
 BF = jnp.bfloat16
 F32 = jnp.float32
-VMEM_BYTES = 56 * 2**20
+VMEM_BYTES = 30 * 2**20
 
 
 def swap(array, axis, bit):

time: 385 us -> 384 us (level)
  Pallas kernels: 76 us -> 57.5 us
  local copies, waits for them, and re-layouts: 21.6 us -> 39.8 us
  waiting for transfers between devices: 231 us -> 235 us
    unnamed x34 -> x42, local copies, waits for them, and re-layouts: 4.95 us -> 20.5 us
    pallas_call x3, Pallas kernels: 40.7 us -> 29.3 us  [backward(): pl.pallas_call(functools.partial(backward_kernel, firsts, blocks, bs, acc...]
    pallas_call x2, Pallas kernels: 35.3 us -> 28.1 us  [forward(): pl.pallas_call(functools.partial(forward_kernel, first, blocks, bs, cuts)...]
  transfers between devices with their start and end apart: 22 -> 22, of which waited for: 12 -> 12; matrix products, arithmetic and copies ran while one was open for 8% -> 9% of each run, Pallas kernels for 17% -> 13%
where the time goes in v11:
time: 384 us
  waiting for transfers between devices  235 us (61%)
  Pallas kernels  57.5 us (15%)
  local copies, waits for them, and re-layouts  39.8 us (10%)
  starting transfers between devices  20.7 us (5%)
  other arithmetic  16.8 us (4%)
  between operations  14.3 us (4%)
    all_gather x1, waiting for transfers between devices, local(): gather_a = lax.all_gather(shards[0], 'dp')  129 us
    ppermute x19, waiting for transfers between devices, swap(): return lax.ppermute(array, axis, [(i, i ^ bit) for i in range(size)])  100 us
    pallas_call x3, Pallas kernels, backward(): pl.pallas_call(functools.partial(backward_kernel, firsts, blocks, bs, acc...  29.3 us
    pallas_call x2, Pallas kernels, forward(): pl.pallas_call(functools.partial(forward_kernel, first, blocks, bs, cuts)...  28.1 us
    unnamed x42, local copies, waits for them, and re-layouts  20.5 us
    ppermute x19, starting transfers between devices, swap(): return lax.ppermute(array, axis, [(i, i ^ bit) for i in range(size)])  17 us
  transfers between devices with their start and end apart: 22, of which 12 were waited for; matrix products, arithmetic and copies ran while one was open for 9% of the time, Pallas kernels for 13%

profile of v11, /device:TPU:0, one launch (start us, length us, event | category | flops | bytes accessed | tf_op | source)
XLA Modules:
  0.0 384.0 jit_solution(12545763810930841953)
XLA Ops:
  7.2 3.8 constant_dynamic-slice_fusion.5
  11.1 3.0 collective-permute-start
  15.6 19.2 %collective-permute-done = bf16[448,1024]{1,0:T(8,128)(2,1)} collective-permute-done((bf16[448,1024]{1,0:T(8,128)(2,1)}, bf16[448,1024]{1,0:T(8,128)(2,1)}, u32[]{:S(2)}, u32[]{:S(2)}) %collective-permute-start) | collective-permute-done | bytes 917536 | tf_op jit(solution)/shard_map/ppermute | solution.py:18
  36.5 2.2 constant_dynamic-update-slice_fusion.1
  40.5 2.2 constant_dynamic-update-slice_fusion
  42.7 2.3 constant_dynamic-update-slice_fusion.3
  44.9 11.7 %collective-permute-done.3 = bf16[448,1024]{1,0:T(8,128)(2,1)} collective-permute-done((bf16[448,1024]{1,0:T(8,128)(2,1)}, bf16[448,1024]{1,0:T(8,128)(2,1)}, u32[]{:S(2)}, u32[]{:S(2)}) %collective-permute-start.3) | collective-permute-done | bytes 917536 | tf_op jit(solution)/shard_map/ppermute | solution.py:18
  58.0 2.3 constant_dynamic-update-slice_fusion.2
  61.3 26.1 %collective-permute-done.5 = bf16[448,1536]{1,0:T(8,128)(2,1)} collective-permute-done((bf16[448,1536]{1,0:T(8,128)(2,1)}, bf16[448,1536]{1,0:T(8,128)(2,1)}, u32[]{:S(2)}, u32[]{:S(2)}) %collective-permute-start.5) | collective-permute-done | bytes 1376288 | tf_op jit(solution)/shard_map/ppermute | solution.py:18
  88.5 2.1 constant_dynamic-slice_fusion.2
  90.6 2.0 pad_maximum_fusion.1.d_ref
  92.6 2.4 collective-permute-done.7
  95.9 6.6 %pad_maximum_fusion.x_ref = bf16[4,896,1024]{2,1,0:T(8,128)(2,1)} fusion(bf16[1,896,1024]{2,1,0:T(8,128)(2,1)} %bitcast.7, bf16[1,896,1024]{2,1,0:T(8,128)(2,1)} %bitcast.6, bf16[1,896,1024]{2,1,0:T(8,128)(2,1)} %bitcast.5, bf16[1,896,1024]{2,1,0:T(8,128)(2,1)} %bitcast.4), kind=kLoop, calls=%fused_computation | loop fusion | flops 11010048 | bytes 14680064 | tf_op jit(solution)/shard_map/stack | solution.py:256
  102.6 129.5 %all-gather.5.cloned.1.call-done = bf16[4096,1536]{1,0:T(8,128)(2,1)} async-done(((bf16[1024,1536]{1,0:T(8,128)(2,1)}), bf16[4096,1536]{1,0:T(8,128)(2,1)}) %all-gather.5.cloned.1.call-update) | async-done | bytes 12582928 | tf_op jit(solution)/shard_map/all_gather | solution.py:237
  232.4 3.1 copy-done.1
  235.5 22.2 %shard_map.94 = (bf16[2,448,1536]{2,1,0:T(8,128)(2,1)S(1)}, bf16[896,1536]{1,0:T(8,128)(2,1)S(1)}, f32[2,4,128,128]{3,2,1,0:T(8,128)S(1)}) custom-call(s32[20]{0:T(128)S(1)} %pad_add_fusion.1.meta, bf16[4,896,1024]{2,1,0:T(8,128)(2,1)S(1)} %copy-done.1, bf16[4,1024,1536]{2,1,0:T(8,128)(2,1)} %bitcast.31, bf16[4,128,128]{2,1,0:T(8,128)(2,1)S(1)} %copy-done.6, ...), custom_call_target="tpu_custom_call" | custom-call | flops 1 | bytes 1 | tf_op jit(solution)/shard_map/pallas_call | solution.py:81
  258.0 18.6 %shard_map.95.refs_3_ = f32[4,896,1024]{2,1,0:T(8,128)} custom-call(s32[20]{0:T(128)S(1)} %pad_add_fusion.1.meta, bf16[896,1536]{1,0:T(8,128)(2,1)S(1)} %get-tuple-element.29.refs_0_, bf16[4,1024,1536]{2,1,0:T(8,128)(2,1)S(1)} %bitcast.32, bf16[4,128,128]{2,1,0:T(8,128)(2,1)S(1)} %copy-done.6), custom_call_target="tpu_custom_call" | custom-call | flops 1 | bytes 1 | tf_op jit(solution)/shard_map/pallas_call | solution.py:174
  276.6 2.0 broadcast_in_dim.32
  279.7 9.6 %collective-permute-done.6 = bf16[448,1536]{1,0:T(8,128)(2,1)S(1)} collective-permute-done((bf16[448,1536]{1,0:T(8,128)(2,1)S(1)}, bf16[448,1536]{1,0:T(8,128)(2,1)S(1)}, u32[]{:S(2)}, u32[]{:S(2)}) %collective-permute-start.6) | collective-permute-done | bytes 1376288 | tf_op jit(solution)/shard_map/ppermute | solution.py:18
  290.5 5.4 %all-gather.7.cloned.1.call-done = bf16[4096,384]{1,0:T(8,128)(2,1)} async-done(((bf16[1024,384]{1,0:T(8,128)(2,1)}), bf16[4096,384]{1,0:T(8,128)(2,1)}) %all-gather.7.cloned.1.call-update) | async-done | bytes 3145744 | tf_op jit(solution)/shard_map/all_gather | solution.py:267
  295.9 3.1 copy-done.2
  300.9 5.9 %shard_map.96 = (bf16[2,448,384]{2,1,0:T(8,128)(2,1)S(1)}, bf16[896,384]{1,0:T(8,128)(2,1)S(1)}, f32[2,4,128,128]{3,2,1,0:T(8,128)S(1)}) custom-call(s32[20]{0:T(128)S(1)} %pad_add_fusion.1.meta, bf16[4,896,1024]{2,1,0:T(8,128)(2,1)S(1)} %copy-done.2, bf16[4,1024,384]{2,1,0:T(8,128)(2,1)S(1)} %bitcast.33, bf16[4,128,128]{2,1,0:T(8,128)(2,1)S(1)} %copy-done.6, ...), custom_call_target="tpu_custom_call" | custom-call | flops 1 | bytes 1 | tf_op jit(solution)/shard_map/pallas_call | solution.py:81
  309.1 5.2 %copy-done = f32[4,896,1024]{2,1,0:T(8,128)S(1)} copy-done((f32[4,896,1024]{2,1,0:T(8,128)S(1)}, f32[4,896,1024]{2,1,0:T(8,128)}, u32[]{:S(2)}) %copy-start) | copy-done | bytes 14680088
  314.3 5.4 %shard_map.97 = (bf16[448,1024]{1,0:T(8,128)(2,1)S(1)}, bf16[448,1024]{1,0:T(8,128)(2,1)}, bf16[448,1024]{1,0:T(8,128)(2,1)S(1)}, bf16[448,1024]{1,0:T(8,128)(2,1)S(1)}) custom-call(s32[20]{0:T(128)S(1)} %pad_add_fusion.1.meta, bf16[896,384]{1,0:T(8,128)(2,1)S(1)} %get-tuple-element.32.refs_0_, bf16[4,1024,384]{2,1,0:T(8,128)(2,1)S(1)} %bitcast.34, ...), custom_call_target="tpu_custom_call" | custom-call | flops 1 | bytes 1 | tf_op jit(solution)/shard_map/pallas_call | solution.py:174
  321.3 5.4 %shard_map.98 = (bf16[448,1024]{1,0:T(8,128)(2,1)S(1)}, bf16[448,1024]{1,0:T(8,128)(2,1)}, bf16[448,1024]{1,0:T(8,128)(2,1)S(1)}, bf16[448,1024]{1,0:T(8,128)(2,1)S(1)}) custom-call(s32[20]{0:T(128)S(1)} %pad_add_fusion.1.meta, bf16[896,384]{1,0:T(8,128)(2,1)S(1)} %get-tuple-element.32.refs_0_, bf16[4,1024,384]{2,1,0:T(8,128)(2,1)S(1)} %bitcast.35, ...), custom_call_target="tpu_custom_call" | custom-call | flops 1 | bytes 1 | tf_op jit(solution)/shard_map/pallas_call | solution.py:174
  331.4 3.7 collective-permute-start.16
  339.9 3.8 collective-permute-done.19
  343.7 2.0 collective-permute-start.18
  345.7 5.8 %collective-permute-done.18 = bf16[4,128,128]{2,1,0:T(8,128)(2,1)S(1)} collective-permute-done((bf16[4,128,128]{2,1,0:T(8,128)(2,1)S(1)}, bf16[4,128,128]{2,1,0:T(8,128)(2,1)S(1)}, u32[]{:S(2)}, u32[]{:S(2)}) %collective-permute-start.18) | collective-permute-done | bytes 131104 | tf_op jit(solution)/shard_map/ppermute | solution.py:18
  353.0 3.4 collective-permute-done.17
  357.3 17.2 %collective-permute-done.14 = bf16[448,1024]{1,0:T(8,128)(2,1)S(1)} collective-permute-done((bf16[448,1024]{1,0:T(8,128)(2,1)S(1)}, bf16[448,1024]{1,0:T(8,128)(2,1)S(1)}, u32[]{:S(2)}, u32[]{:S(2)}) %collective-permute-start.14) | collective-permute-done | bytes 917536 | tf_op jit(solution)/shard_map/ppermute | solution.py:18
  375.2 1.9 add_convert_fusion
  (97 shorter events, 30.8 us)
Async XLA Ops:
  7.2 224.9 %all-gather.5.cloned.1.call-start = ((), (), s32[]{:S(2)}) async-start(), calls=%async_computation | async-start | bytes 15728640 | tf_op jit(solution)/shard_map/all_gather | solution.py:237
  11.0 27.7 %copy-start.14 = (bf16[448,3840]{1,0:T(8,128)(2,1)S(1)}, bf16[448,3840]{1,0:T(8,128)(2,1)}, u32[]{:S(2)}) copy-start(bf16[448,3840]{1,0:T(8,128)(2,1)} %param.13) | copy-start | bytes 10321924
  11.0 284.9 %all-gather.7.cloned.1.call-start = ((), (), s32[]{:S(2)}) async-start(), calls=%async_computation.1 | async-start | bytes 3932160 | tf_op jit(solution)/shard_map/all_gather | solution.py:267
  11.1 23.7 %collective-permute-start = (bf16[448,1024]{1,0:T(8,128)(2,1)}, bf16[448,1024]{1,0:T(8,128)(2,1)}, u32[]{:S(2)}, u32[]{:S(2)}) collective-permute-start(bf16[448,1024]{1,0:T(8,128)(2,1)} %param.7), channel_id=1, source_target_pairs={{0,16},{16,0},{1,17},{17,1},{2,18},{18,2},{3,19},{19,3},{4,20},{20... | collective-permute-start | bytes 2752520 | tf_op jit(solution)/shard_map/ppermute | solution.py:18
  14.1 28.6 %collective-permute-start.2 = (bf16[448,1024]{1,0:T(8,128)(2,1)}, bf16[448,1024]{1,0:T(8,128)(2,1)}, u32[]{:S(2)}, u32[]{:S(2)}) collective-permute-start(bf16[448,1024]{1,0:T(8,128)(2,1)} %param.7), channel_id=1, source_target_pairs={{0,2},{1,3},{2,0},{3,1},{4,6},{5,7},{6,4},{7,5},{8,10},{9,11},{10,... | collective-permute-start | bytes 2752520 | tf_op jit(solution)/shard_map/ppermute | solution.py:18
  34.8 21.9 %collective-permute-start.3 = (bf16[448,1024]{1,0:T(8,128)(2,1)}, bf16[448,1024]{1,0:T(8,128)(2,1)}, u32[]{:S(2)}, u32[]{:S(2)}) collective-permute-start(bf16[448,1024]{1,0:T(8,128)(2,1)} %collective-permute-done), channel_id=1, source_target_pairs={{0,2},{1,3},{2,0},{3,1},{4,6},{5,7},{6,4},{7,5},{8,10},{9,11},{10,... | collective-permute-start | bytes 2752520 | tf_op jit(solution)/shard_map/ppermute | solution.py:18
  42.7 53.2 %collective-permute-start.1 = (bf16[896,1024]{1,0:T(8,128)(2,1)}, bf16[896,1024]{1,0:T(8,128)(2,1)}, u32[]{:S(2)}, u32[]{:S(2)}) collective-permute-start(bf16[896,1024]{1,0:T(8,128)(2,1)} %constant_dynamic-update-slice_fusion), channel_id=1, source_target_pairs={{0,1},{1,0},{2,3},{3,2},{4,5},{5,4},{6,7},{7,6},{8,9},{9,8},{10,11... | collective-permute-start | bytes 5505032 | tf_op jit(solution)/shard_map/ppermute | solution.py:18
  56.6 30.8 %collective-permute-start.5 = (bf16[448,1536]{1,0:T(8,128)(2,1)}, bf16[448,1536]{1,0:T(8,128)(2,1)}, u32[]{:S(2)}, u32[]{:S(2)}) collective-permute-start(bf16[448,1536]{1,0:T(8,128)(2,1)} %get-tuple-element.25), channel_id=1, source_target_pairs={{0,16},{16,0},{1,17},{17,1},{2,18},{18,2},{3,19},{19,3},{4,20},{20... | collective-permute-start | bytes 4128776 | tf_op jit(solution)/shard_map/ppermute | solution.py:18
  60.3 35.6 %collective-permute-start.4 = (bf16[896,1024]{1,0:T(8,128)(2,1)}, bf16[896,1024]{1,0:T(8,128)(2,1)}, u32[]{:S(2)}, u32[]{:S(2)}) collective-permute-start(bf16[896,1024]{1,0:T(8,128)(2,1)} %constant_dynamic-update-slice_fusion.2), channel_id=1, source_target_pairs={{0,1},{1,0},{2,3},{3,2},{4,5},{5,4},{6,7},{7,6},{8,9},{9,8},{10,11... | collective-permute-start | bytes 5505032 | tf_op jit(solution)/shard_map/ppermute | solution.py:18
  87.4 7.6 %collective-permute-start.7 = (bf16[448,384]{1,0:T(8,128)(2,1)}, bf16[448,384]{1,0:T(8,128)(2,1)S(1)}, u32[]{:S(2)}, u32[]{:S(2)}) collective-permute-start(bf16[448,384]{1,0:T(8,128)(2,1)} %get-tuple-element.27), channel_id=1, source_target_pairs={{0,16},{16,0},{1,17},{17,1},{2,18},{18,2},{3,19},{19,3},{4,20},{20... | collective-permute-start | bytes 1032200 | tf_op jit(solution)/shard_map/ppermute | solution.py:18
  95.9 136.2 %copy-start.17 = (s32[4]{0:T(128)S(1)}, s32[4]{0:T(128)}, u32[]{:S(2)}) copy-start(s32[4]{0:T(128)} %param.10) | copy-start | bytes 52
  95.9 136.2 %copy-start.18 = (s32[4]{0:T(128)S(1)}, s32[4]{0:T(128)}, u32[]{:S(2)}) copy-start(s32[4]{0:T(128)} %param.11) | copy-start | bytes 52
  95.9 136.5 %copy-start.6 = (bf16[4,128,128]{2,1,0:T(8,128)(2,1)S(1)}, bf16[4,128,128]{2,1,0:T(8,128)(2,1)}, u32[]{:S(2)}) copy-start(bf16[4,128,128]{2,1,0:T(8,128)(2,1)} %refs_2_.3) | copy-start | bytes 393220
  235.5 22.4 %copy-start.3 = (bf16[4096,1536]{1,0:T(8,128)(2,1)S(1)}, bf16[4096,1536]{1,0:T(8,128)(2,1)}, u32[]{:S(2)}) copy-start(bf16[4096,1536]{1,0:T(8,128)(2,1)} %all-gather.5.cloned.1.call-done) | copy-start | bytes 37748740
  257.9 31.5 %collective-permute-start.6 = (bf16[448,1536]{1,0:T(8,128)(2,1)S(1)}, bf16[448,1536]{1,0:T(8,128)(2,1)S(1)}, u32[]{:S(2)}, u32[]{:S(2)}) collective-permute-start(bf16[448,1536]{1,0:T(8,128)(2,1)S(1)} %slice_bitcast_fusion), channel_id=1, source_target_pairs={{0,16},{16,0},{1,17},{17,1},{2,18},{18,2},{3,19},{19,3},{4,20},{20... | collective-permute-start | bytes 4128776 | tf_op jit(solution)/shard_map/ppermute | solution.py:18
  279.7 16.2 %copy-start.7 = (bf16[896,384]{1,0:T(8,128)(2,1)S(1)}, bf16[896,384]{1,0:T(8,128)(2,1)}, u32[]{:S(2)}) copy-start(bf16[896,384]{1,0:T(8,128)(2,1)} %pad_maximum_fusion.2.d_ref) | copy-start | bytes 2064388
  300.9 8.2 %copy-start.5 = (bf16[4096,384]{1,0:T(8,128)(2,1)S(1)}, bf16[4096,384]{1,0:T(8,128)(2,1)}, u32[]{:S(2)}) copy-start(bf16[4096,384]{1,0:T(8,128)(2,1)} %all-gather.7.cloned.1.call-done) | copy-start | bytes 9437188
  306.9 13.7 %collective-permute-start.9 = (bf16[4,128,128]{2,1,0:T(8,128)(2,1)S(1)}, bf16[4,128,128]{2,1,0:T(8,128)(2,1)S(1)}, u32[]{:S(2)}, u32[]{:S(2)}) collective-permute-start(bf16[4,128,128]{2,1,0:T(8,128)(2,1)S(1)} %fusion.1), channel_id=1, source_target_pairs={{0,16},{16,0},{1,17},{17,1},{2,18},{18,2},{3,19},{19,3},{4,20},{20... | collective-permute-start | bytes 393224 | tf_op jit(solution)/shard_map/ppermute | solution.py:18
  308.5 12.8 %collective-permute-start.8 = (bf16[448,384]{1,0:T(8,128)(2,1)S(1)}, bf16[448,384]{1,0:T(8,128)(2,1)S(1)}, u32[]{:S(2)}, u32[]{:S(2)}) collective-permute-start(bf16[448,384]{1,0:T(8,128)(2,1)S(1)} %slice_bitcast_fusion.1), channel_id=1, source_target_pairs={{0,16},{16,0},{1,17},{17,1},{2,18},{18,2},{3,19},{19,3},{4,20},{20... | collective-permute-start | bytes 1032200 | tf_op jit(solution)/shard_map/ppermute | solution.py:18
  320.6 9.2 %collective-permute-start.15 = (bf16[448,1024]{1,0:T(8,128)(2,1)}, bf16[448,1024]{1,0:T(8,128)(2,1)}, u32[]{:S(2)}, u32[]{:S(2)}) collective-permute-start(bf16[448,1024]{1,0:T(8,128)(2,1)} %get-tuple-element.45), channel_id=1, source_target_pairs={{0,1},{1,0},{2,3},{3,2},{4,5},{5,4},{6,7},{7,6},{8,9},{9,8},{10,11... | collective-permute-start | bytes 2752520 | tf_op jit(solution)/shard_map/ppermute | solution.py:18
  321.3 7.8 %copy-start.19 = (s32[4,1]{0,1:T(1,128)S(1)}, s32[4,1]{0,1:T(1,128)}, u32[]{:S(2)}) copy-start(s32[4,1]{0,1:T(1,128)} %param.12) | copy-start | bytes 52
  328.6 6.5 %collective-permute-start.11 = (bf16[448,1024]{1,0:T(8,128)(2,1)}, bf16[448,1024]{1,0:T(8,128)(2,1)}, u32[]{:S(2)}, u32[]{:S(2)}) collective-permute-start(bf16[448,1024]{1,0:T(8,128)(2,1)} %get-tuple-element.40), channel_id=1, source_target_pairs={{0,1},{1,0},{2,3},{3,2},{4,5},{5,4},{6,7},{7,6},{8,9},{9,8},{10,11... | collective-permute-start | bytes 2752520 | tf_op jit(solution)/shard_map/ppermute | solution.py:18
  329.1 6.0 %copy-start.9 = (bf16[448,1024]{1,0:T(8,128)(2,1)S(1)}, bf16[448,1024]{1,0:T(8,128)(2,1)}, u32[]{:S(2)}) copy-start(bf16[448,1024]{1,0:T(8,128)(2,1)} %copy-done.8) | copy-start | bytes 2752516
  329.1 8.5 %collective-permute-start.13 = (bf16[448,1024]{1,0:T(8,128)(2,1)}, bf16[448,1024]{1,0:T(8,128)(2,1)S(1)}, u32[]{:S(2)}, u32[]{:S(2)}) collective-permute-start(bf16[448,1024]{1,0:T(8,128)(2,1)} %copy-done.13), channel_id=1, source_target_pairs={{0,1},{1,0},{2,3},{3,2},{4,5},{5,4},{6,7},{7,6},{8,9},{9,8},{10,11... | collective-permute-start | bytes 2752520 | tf_op jit(solution)/shard_map/ppermute | solution.py:18
  329.3 28.0 %collective-permute-start.10 = (bf16[448,1024]{1,0:T(8,128)(2,1)}, bf16[448,1024]{1,0:T(8,128)(2,1)S(1)}, u32[]{:S(2)}, u32[]{:S(2)}) collective-permute-start(bf16[448,1024]{1,0:T(8,128)(2,1)} %copy-done.12), channel_id=1, source_target_pairs={{0,1},{1,0},{2,3},{3,2},{4,5},{5,4},{6,7},{7,6},{8,9},{9,8},{10,11... | collective-permute-start | bytes 2752520 | tf_op jit(solution)/shard_map/ppermute | solution.py:18
  331.4 25.9 %collective-permute-start.16 = (bf16[448,1024]{1,0:T(8,128)(2,1)S(1)}, bf16[448,1024]{1,0:T(8,128)(2,1)S(1)}, u32[]{:S(2)}, u32[]{:S(2)}) collective-permute-start(bf16[448,1024]{1,0:T(8,128)(2,1)S(1)} %add_convert_fusion.1), channel_id=1, source_target_pairs={{0,18},{1,19},{2,16},{3,17},{16,2},{17,3},{18,0},{19,1},{4,22},{5,... | collective-permute-start | bytes 2752520 | tf_op jit(solution)/shard_map/ppermute | solution.py:296
  336.6 14.9 %copy-start.11 = (bf16[2,448,384]{2,1,0:T(8,128)(2,1)S(1)}, bf16[2,448,384]{2,1,0:T(8,128)(2,1)}, u32[]{:S(2)}) copy-start(bf16[2,448,384]{2,1,0:T(8,128)(2,1)} %copy-done.10) | copy-start | bytes 2064388
  336.6 7.1 %collective-permute-start.19 = (bf16[4,128,128]{2,1,0:T(8,128)(2,1)S(1)}, bf16[4,128,128]{2,1,0:T(8,128)(2,1)S(1)}, u32[]{:S(2)}, u32[]{:S(2)}) collective-permute-start(bf16[4,128,128]{2,1,0:T(8,128)(2,1)S(1)} %copy-done.16), channel_id=1, source_target_pairs={{0,12},{4,8},{8,4},{12,0},{1,13},{5,9},{9,5},{13,1},{2,14},{6,10},... | collective-permute-start | bytes 393224 | tf_op jit(solution)/shard_map/ppermute | solution.py:18
  337.9 36.6 %collective-permute-start.14 = (bf16[448,1024]{1,0:T(8,128)(2,1)S(1)}, bf16[448,1024]{1,0:T(8,128)(2,1)S(1)}, u32[]{:S(2)}, u32[]{:S(2)}) collective-permute-start(bf16[448,1024]{1,0:T(8,128)(2,1)S(1)} %add_convert_fusion.2), channel_id=1, source_target_pairs={{0,2},{1,3},{2,0},{3,1},{4,6},{5,7},{6,4},{7,5},{8,10},{9,11},{10,... | collective-permute-start | bytes 2752520 | tf_op jit(solution)/shard_map/ppermute | solution.py:18
  338.0 37.2 %collective-permute-start.12 = (bf16[448,1024]{1,0:T(8,128)(2,1)S(1)}, bf16[448,1024]{1,0:T(8,128)(2,1)S(1)}, u32[]{:S(2)}, u32[]{:S(2)}) collective-permute-start(bf16[448,1024]{1,0:T(8,128)(2,1)S(1)} %add_convert_fusion.3), channel_id=1, source_target_pairs={{0,16},{16,0},{1,17},{17,1},{2,18},{18,2},{3,19},{19,3},{4,20},{20... | collective-permute-start | bytes 2752520 | tf_op jit(solution)/shard_map/ppermute | solution.py:18
  343.7 7.8 %collective-permute-start.18 = (bf16[4,128,128]{2,1,0:T(8,128)(2,1)S(1)}, bf16[4,128,128]{2,1,0:T(8,128)(2,1)S(1)}, u32[]{:S(2)}, u32[]{:S(2)}) collective-permute-start(bf16[4,128,128]{2,1,0:T(8,128)(2,1)S(1)} %copy-done.16), channel_id=1, source_target_pairs={{0,8},{4,12},{8,0},{12,4},{1,9},{5,13},{9,1},{13,5},{2,10},{6,14},... | collective-permute-start | bytes 393224 | tf_op jit(solution)/shard_map/ppermute | solution.py:18
  351.5 5.0 %collective-permute-start.17 = (bf16[4,128,128]{2,1,0:T(8,128)(2,1)S(1)}, bf16[4,128,128]{2,1,0:T(8,128)(2,1)S(1)}, u32[]{:S(2)}, u32[]{:S(2)}) collective-permute-start(bf16[4,128,128]{2,1,0:T(8,128)(2,1)S(1)} %copy-done.16), channel_id=1, source_target_pairs={{0,4},{4,0},{8,12},{12,8},{1,5},{5,1},{9,13},{13,9},{2,6},{6,2},{1... | collective-permute-start | bytes 393224 | tf_op jit(solution)/shard_map/ppermute | solution.py:18
  (10 other events, 28.0 us)
Sparse Core Ops, SparseCore 0:
  11.1 220.8 all-gather.4
  234.2 61.6 all-gather.6

commit v12 on v11

--- a/solution.py
+++ b/solution.py
@@ -116,7 +116,7 @@
     step = pl.program_id(0)
     slot = step if bit is None else meta[PARTS + bit - step]
     base = pl.program_id(1) * size
-    total = acc_in[0] if has_acc else None
+    total = acc_in[0].astype(F32) if has_acc else None
     for p in range(n):
         term = lax.dot_general(
             slopes[p][...], w_refs[p][0], (((1,), (1,)), ((), ())), preferred_element_type=F32
@@ -138,7 +138,7 @@
                 )
 
     if len(outs) == 1:
-        outs[0][0] = acc[...]
+        outs[0][0] = acc[...].astype(BF)
         return
     cut = outs[0].shape[0]
     for at_step in range(2):
@@ -167,7 +167,7 @@
     keep = pl.BlockSpec((rows // 2, size), lambda s, i, m: (0, jnp.where(s == 0, 0, i)))
     if every:
         out_specs = [whole]
-        out_shape = [jax.ShapeDtypeStruct((slots, rows, feats), F32)]
+        out_shape = [jax.ShapeDtypeStruct((slots, rows, feats), BF)]
     else:
         out_specs = [give, give, keep, keep]
         out_shape = [jax.ShapeDtypeStruct((rows // 2, feats), BF)] * 4

time: 384 us -> 383 us (level)
  waiting for transfers between devices: 235 us -> 229 us
    unnamed x42 -> x52, local copies, waits for them, and re-layouts: 20.5 us -> 21.6 us
where the time goes in v12:
time: 383 us; the launch traced here: 382 us
  waiting for transfers between devices  229 us (60%)
  Pallas kernels  55 us (14%)
  local copies, waits for them, and re-layouts  42.1 us (11%)
  starting transfers between devices  22.8 us (6%)
  other arithmetic  18.4 us (5%)
  between operations  14.3 us (4%)
    all_gather x1, waiting for transfers between devices, local(): gather_a = lax.all_gather(shards[0], 'dp')  128 us
    ppermute x19, waiting for transfers between devices, swap(): return lax.ppermute(array, axis, [(i, i ^ bit) for i in range(size)])  98.8 us
    pallas_call x3, Pallas kernels, backward(): pl.pallas_call(functools.partial(backward_kernel, firsts, blocks, bs, acc...  28 us
    pallas_call x2, Pallas kernels, forward(): pl.pallas_call(functools.partial(forward_kernel, first, blocks, bs, cuts)...  27 us
    unnamed x52, local copies, waits for them, and re-layouts  21.6 us
    ppermute x19, starting transfers between devices, swap(): return lax.ppermute(array, axis, [(i, i ^ bit) for i in range(size)])  19.6 us
  transfers between devices with their start and end apart: 22, of which 12 were waited for; matrix products, arithmetic and copies ran while one was open for 9% of the time, Pallas kernels for 13%

profile of v12, /device:TPU:0, one launch (start us, length us, event | category | flops | bytes accessed | tf_op | source)
XLA Modules:
  0.0 381.9 jit_solution(9419027908153821388)
XLA Ops:
  7.2 3.8 constant_dynamic-slice_fusion.5
  12.2 3.0 collective-permute-start
  16.6 19.0 %collective-permute-done = bf16[448,1024]{1,0:T(8,128)(2,1)} collective-permute-done((bf16[448,1024]{1,0:T(8,128)(2,1)S(1)}, bf16[448,1024]{1,0:T(8,128)(2,1)}, u32[]{:S(2)}, u32[]{:S(2)}) %collective-permute-start) | collective-permute-done | bytes 917536 | tf_op jit(solution)/shard_map/ppermute | solution.py:18
  38.3 3.1 constant_dynamic-slice_fusion.4
  41.3 2.2 constant_dynamic-update-slice_fusion
  44.8 12.7 %collective-permute-done.3 = bf16[448,1024]{1,0:T(8,128)(2,1)} collective-permute-done((bf16[448,1024]{1,0:T(8,128)(2,1)}, bf16[448,1024]{1,0:T(8,128)(2,1)}, u32[]{:S(2)}, u32[]{:S(2)}) %collective-permute-start.3) | collective-permute-done | bytes 917536 | tf_op jit(solution)/shard_map/ppermute | solution.py:18
  60.2 2.0 constant_dynamic-slice_fusion.1
  62.2 26.0 %collective-permute-done.5 = bf16[448,1536]{1,0:T(8,128)(2,1)} collective-permute-done((bf16[448,1536]{1,0:T(8,128)(2,1)}, bf16[448,1536]{1,0:T(8,128)(2,1)}, u32[]{:S(2)}, u32[]{:S(2)}) %collective-permute-start.5) | collective-permute-done | bytes 1376288 | tf_op jit(solution)/shard_map/ppermute | solution.py:18
  89.3 2.1 constant_dynamic-slice_fusion.2
  91.4 3.1 pad_maximum_fusion.1.d_ref
  97.9 6.2 %pad_maximum_fusion.x_ref = bf16[4,896,1024]{2,1,0:T(8,128)(2,1)} fusion(bf16[1,896,1024]{2,1,0:T(8,128)(2,1)} %bitcast.7, bf16[1,896,1024]{2,1,0:T(8,128)(2,1)S(1)} %bitcast.36, bf16[1,896,1024]{2,1,0:T(8,128)(2,1)} %bitcast.5, bf16[1,896,1024]{2,1,0:T(8,128)(2,1)} %bitcast.4), kind=kLoop, calls=%fused_computation | loop fusion | flops 11010048 | bytes 14680064 | tf_op jit(solution)/shard_map/stack | solution.py:256
  104.1 128.0 %all-gather.5.cloned.1.call-done = bf16[4096,1536]{1,0:T(8,128)(2,1)} async-done(((bf16[1024,1536]{1,0:T(8,128)(2,1)}), bf16[4096,1536]{1,0:T(8,128)(2,1)}) %all-gather.5.cloned.1.call-update) | async-done | bytes 12582928 | tf_op jit(solution)/shard_map/all_gather | solution.py:237
  232.4 3.1 copy-done
  237.3 21.1 %shard_map.94 = (bf16[2,448,1536]{2,1,0:T(8,128)(2,1)S(1)}, bf16[896,1536]{1,0:T(8,128)(2,1)S(1)}, f32[2,4,128,128]{3,2,1,0:T(8,128)S(1)}) custom-call(s32[20]{0:T(128)S(1)} %pad_add_fusion.1.meta, bf16[4,896,1024]{2,1,0:T(8,128)(2,1)S(1)} %copy-done, bf16[4,1024,1536]{2,1,0:T(8,128)(2,1)} %bitcast.31, bf16[4,128,128]{2,1,0:T(8,128)(2,1)S(1)} %copy-done.7, ...), custom_call_target="tpu_custom_call" | custom-call | flops 1 | bytes 1 | tf_op jit(solution)/shard_map/pallas_call | solution.py:81
  259.4 3.1 collective-permute-start.6
  264.3 17.6 %shard_map.95.refs_3_ = bf16[4,896,1024]{2,1,0:T(8,128)(2,1)S(1)} custom-call(s32[20]{0:T(128)S(1)} %pad_add_fusion.1.meta, bf16[896,1536]{1,0:T(8,128)(2,1)S(1)} %copy-done.9, bf16[4,1024,1536]{2,1,0:T(8,128)(2,1)S(1)} %bitcast.32, bf16[4,128,128]{2,1,0:T(8,128)(2,1)S(1)} %copy-done.7), custom_call_target="tpu_custom_call" | custom-call | flops 1 | bytes 1 | tf_op jit(solution)/shard_map/pallas_call | solution.py:174
  281.9 2.9 copy-done.2
  284.9 2.0 broadcast_in_dim.32
  288.0 4.3 %collective-permute-done.6 = bf16[448,1536]{1,0:T(8,128)(2,1)S(1)} collective-permute-done((bf16[448,1536]{1,0:T(8,128)(2,1)S(1)}, bf16[448,1536]{1,0:T(8,128)(2,1)S(1)}, u32[]{:S(2)}, u32[]{:S(2)}) %collective-permute-start.6) | collective-permute-done | bytes 1376288 | tf_op jit(solution)/shard_map/ppermute | solution.py:18
  293.5 2.5 all-gather.7.cloned.1.call-done
  295.9 3.1 copy-done.1
  300.9 5.9 %shard_map.96 = (bf16[2,448,384]{2,1,0:T(8,128)(2,1)S(1)}, bf16[896,384]{1,0:T(8,128)(2,1)S(1)}, f32[2,4,128,128]{3,2,1,0:T(8,128)S(1)}) custom-call(s32[20]{0:T(128)S(1)} %pad_add_fusion.1.meta, bf16[4,896,1024]{2,1,0:T(8,128)(2,1)S(1)} %copy-done.1, bf16[4,1024,384]{2,1,0:T(8,128)(2,1)S(1)} %bitcast.33, bf16[4,128,128]{2,1,0:T(8,128)(2,1)S(1)} %copy-done.7, ...), custom_call_target="tpu_custom_call" | custom-call | flops 1 | bytes 1 | tf_op jit(solution)/shard_map/pallas_call | solution.py:81
  309.1 5.1 %shard_map.97 = (bf16[448,1024]{1,0:T(8,128)(2,1)S(1)}, bf16[448,1024]{1,0:T(8,128)(2,1)}, bf16[448,1024]{1,0:T(8,128)(2,1)S(1)}, bf16[448,1024]{1,0:T(8,128)(2,1)S(1)}) custom-call(s32[20]{0:T(128)S(1)} %pad_add_fusion.1.meta, bf16[896,384]{1,0:T(8,128)(2,1)S(1)} %get-tuple-element.32.refs_0_, bf16[4,1024,384]{2,1,0:T(8,128)(2,1)S(1)} %bitcast.34, ...), custom_call_target="tpu_custom_call" | custom-call | flops 1 | bytes 1 | tf_op jit(solution)/shard_map/pallas_call | solution.py:174
  315.9 4.2 %collective-permute-done.8 = bf16[448,384]{1,0:T(8,128)(2,1)S(1)} collective-permute-done((bf16[448,384]{1,0:T(8,128)(2,1)S(1)}, bf16[448,384]{1,0:T(8,128)(2,1)S(1)}, u32[]{:S(2)}, u32[]{:S(2)}) %collective-permute-start.8) | collective-permute-done | bytes 344096 | tf_op jit(solution)/shard_map/ppermute | solution.py:18
  320.1 5.2 %shard_map.98 = (bf16[448,1024]{1,0:T(8,128)(2,1)S(1)}, bf16[448,1024]{1,0:T(8,128)(2,1)}, bf16[448,1024]{1,0:T(8,128)(2,1)S(1)}, bf16[448,1024]{1,0:T(8,128)(2,1)S(1)}) custom-call(s32[20]{0:T(128)S(1)} %pad_add_fusion.1.meta, bf16[896,384]{1,0:T(8,128)(2,1)S(1)} %get-tuple-element.32.refs_0_, bf16[4,1024,384]{2,1,0:T(8,128)(2,1)S(1)} %bitcast.35, ...), custom_call_target="tpu_custom_call" | custom-call | flops 1 | bytes 1 | tf_op jit(solution)/shard_map/pallas_call | solution.py:174
  329.5 3.1 collective-permute-start.16
  337.5 3.9 %collective-permute-done.19 = bf16[4,128,128]{2,1,0:T(8,128)(2,1)S(1)} collective-permute-done((bf16[4,128,128]{2,1,0:T(8,128)(2,1)S(1)}, bf16[4,128,128]{2,1,0:T(8,128)(2,1)S(1)}, u32[]{:S(2)}, u32[]{:S(2)}) %collective-permute-start.19) | collective-permute-done | bytes 131104 | tf_op jit(solution)/shard_map/ppermute | solution.py:18
  341.4 2.0 collective-permute-start.18
  343.4 6.0 %collective-permute-done.18 = bf16[4,128,128]{2,1,0:T(8,128)(2,1)S(1)} collective-permute-done((bf16[4,128,128]{2,1,0:T(8,128)(2,1)S(1)}, bf16[4,128,128]{2,1,0:T(8,128)(2,1)S(1)}, u32[]{:S(2)}, u32[]{:S(2)}) %collective-permute-start.18) | collective-permute-done | bytes 131104 | tf_op jit(solution)/shard_map/ppermute | solution.py:18
  351.0 3.4 collective-permute-done.17
  355.2 17.9 %collective-permute-done.14 = bf16[448,1024]{1,0:T(8,128)(2,1)S(1)} collective-permute-done((bf16[448,1024]{1,0:T(8,128)(2,1)S(1)}, bf16[448,1024]{1,0:T(8,128)(2,1)S(1)}, u32[]{:S(2)}, u32[]{:S(2)}) %collective-permute-start.14) | collective-permute-done | bytes 917536 | tf_op jit(solution)/shard_map/ppermute | solution.py:18
  373.2 1.9 add_convert_fusion
  (107 shorter events, 38.2 us)
Async XLA Ops:
  7.2 224.9 %all-gather.5.cloned.1.call-start = ((), (), s32[]{:S(2)}) async-start(), calls=%async_computation | async-start | bytes 15728640 | tf_op jit(solution)/shard_map/all_gather | solution.py:237
  11.0 284.9 %all-gather.7.cloned.1.call-start = ((), (), s32[]{:S(2)}) async-start(), calls=%async_computation.1 | async-start | bytes 3932160 | tf_op jit(solution)/shard_map/all_gather | solution.py:267
  12.2 23.4 %collective-permute-start = (bf16[448,1024]{1,0:T(8,128)(2,1)S(1)}, bf16[448,1024]{1,0:T(8,128)(2,1)}, u32[]{:S(2)}, u32[]{:S(2)}) collective-permute-start(bf16[448,1024]{1,0:T(8,128)(2,1)S(1)} %copy-done.20), channel_id=1, source_target_pairs={{0,16},{16,0},{1,17},{17,1},{2,18},{18,2},{3,19},{19,3},{4,20},{20... | collective-permute-start | bytes 2752520 | tf_op jit(solution)/shard_map/ppermute | solution.py:18
  15.1 28.4 %collective-permute-start.2 = (bf16[448,1024]{1,0:T(8,128)(2,1)S(1)}, bf16[448,1024]{1,0:T(8,128)(2,1)}, u32[]{:S(2)}, u32[]{:S(2)}) collective-permute-start(bf16[448,1024]{1,0:T(8,128)(2,1)S(1)} %copy-done.20), channel_id=1, source_target_pairs={{0,2},{1,3},{2,0},{3,1},{4,6},{5,7},{6,4},{7,5},{8,10},{9,11},{10,... | collective-permute-start | bytes 2752520 | tf_op jit(solution)/shard_map/ppermute | solution.py:18
  35.6 21.9 %collective-permute-start.3 = (bf16[448,1024]{1,0:T(8,128)(2,1)}, bf16[448,1024]{1,0:T(8,128)(2,1)}, u32[]{:S(2)}, u32[]{:S(2)}) collective-permute-start(bf16[448,1024]{1,0:T(8,128)(2,1)} %collective-permute-done), channel_id=1, source_target_pairs={{0,2},{1,3},{2,0},{3,1},{4,6},{5,7},{6,4},{7,5},{8,10},{9,11},{10,... | collective-permute-start | bytes 2752520 | tf_op jit(solution)/shard_map/ppermute | solution.py:18
  43.5 54.3 %collective-permute-start.1 = (bf16[896,1024]{1,0:T(8,128)(2,1)}, bf16[896,1024]{1,0:T(8,128)(2,1)}, u32[]{:S(2)}, u32[]{:S(2)}) collective-permute-start(bf16[896,1024]{1,0:T(8,128)(2,1)} %constant_dynamic-update-slice_fusion), channel_id=1, source_target_pairs={{0,1},{1,0},{2,3},{3,2},{4,5},{5,4},{6,7},{7,6},{8,9},{9,8},{10,11... | collective-permute-start | bytes 5505032 | tf_op jit(solution)/shard_map/ppermute | solution.py:18
  57.4 30.8 %collective-permute-start.5 = (bf16[448,1536]{1,0:T(8,128)(2,1)}, bf16[448,1536]{1,0:T(8,128)(2,1)}, u32[]{:S(2)}, u32[]{:S(2)}) collective-permute-start(bf16[448,1536]{1,0:T(8,128)(2,1)} %get-tuple-element.25), channel_id=1, source_target_pairs={{0,16},{16,0},{1,17},{17,1},{2,18},{18,2},{3,19},{19,3},{4,20},{20... | collective-permute-start | bytes 4128776 | tf_op jit(solution)/shard_map/ppermute | solution.py:18
  60.1 37.7 %collective-permute-start.4 = (bf16[896,1024]{1,0:T(8,128)(2,1)S(1)}, bf16[896,1024]{1,0:T(8,128)(2,1)}, u32[]{:S(2)}, u32[]{:S(2)}) collective-permute-start(bf16[896,1024]{1,0:T(8,128)(2,1)S(1)} %constant_dynamic-update-slice_fusion.2), channel_id=1, source_target_pairs={{0,1},{1,0},{2,3},{3,2},{4,5},{5,4},{6,7},{7,6},{8,9},{9,8},{10,11... | collective-permute-start | bytes 5505032 | tf_op jit(solution)/shard_map/ppermute | solution.py:18
  88.2 7.7 %collective-permute-start.7 = (bf16[448,384]{1,0:T(8,128)(2,1)}, bf16[448,384]{1,0:T(8,128)(2,1)}, u32[]{:S(2)}, u32[]{:S(2)}) collective-permute-start(bf16[448,384]{1,0:T(8,128)(2,1)} %get-tuple-element.27), channel_id=1, source_target_pairs={{0,16},{16,0},{1,17},{17,1},{2,18},{18,2},{3,19},{19,3},{4,20},{20... | collective-permute-start | bytes 1032200 | tf_op jit(solution)/shard_map/ppermute | solution.py:18
  97.8 134.3 %copy-start.22 = (s32[4]{0:T(128)S(1)}, s32[4]{0:T(128)}, u32[]{:S(2)}) copy-start(s32[4]{0:T(128)} %param.10) | copy-start | bytes 52
  97.8 134.3 %copy-start.23 = (s32[4]{0:T(128)S(1)}, s32[4]{0:T(128)}, u32[]{:S(2)}) copy-start(s32[4]{0:T(128)} %param.11) | copy-start | bytes 52
  97.9 134.6 %copy-start.7 = (bf16[4,128,128]{2,1,0:T(8,128)(2,1)S(1)}, bf16[4,128,128]{2,1,0:T(8,128)(2,1)}, u32[]{:S(2)}) copy-start(bf16[4,128,128]{2,1,0:T(8,128)(2,1)} %refs_2_.3) | copy-start | bytes 393220
  237.3 25.1 %copy-start.4 = (bf16[4096,1536]{1,0:T(8,128)(2,1)S(1)}, bf16[4096,1536]{1,0:T(8,128)(2,1)}, u32[]{:S(2)}) copy-start(bf16[4096,1536]{1,0:T(8,128)(2,1)} %all-gather.5.cloned.1.call-done) | copy-start | bytes 37748740
  259.4 33.0 %collective-permute-start.6 = (bf16[448,1536]{1,0:T(8,128)(2,1)S(1)}, bf16[448,1536]{1,0:T(8,128)(2,1)S(1)}, u32[]{:S(2)}, u32[]{:S(2)}) collective-permute-start(bf16[448,1536]{1,0:T(8,128)(2,1)S(1)} %slice_bitcast_fusion), channel_id=1, source_target_pairs={{0,16},{16,0},{1,17},{17,1},{2,18},{18,2},{3,19},{19,3},{4,20},{20... | collective-permute-start | bytes 4128776 | tf_op jit(solution)/shard_map/ppermute | solution.py:18
  288.0 7.9 %copy-start.10 = (bf16[896,384]{1,0:T(8,128)(2,1)S(1)}, bf16[896,384]{1,0:T(8,128)(2,1)}, u32[]{:S(2)}) copy-start(bf16[896,384]{1,0:T(8,128)(2,1)} %pad_maximum_fusion.2.d_ref) | copy-start | bytes 2064388
  300.9 5.9 %copy-start.16 = (f32[2,4,128,128]{3,2,1,0:T(8,128)S(1)}, f32[2,4,128,128]{3,2,1,0:T(8,128)}, u32[]{:S(2)}) copy-start(f32[2,4,128,128]{3,2,1,0:T(8,128)} %copy-done.15) | copy-start | bytes 1572868
  300.9 8.2 %copy-start.3 = (bf16[4,896,1024]{2,1,0:T(8,128)(2,1)S(1)}, bf16[4,896,1024]{2,1,0:T(8,128)(2,1)}, u32[]{:S(2)}) copy-start(bf16[4,896,1024]{2,1,0:T(8,128)(2,1)} %copy-done.2) | copy-start | bytes 22020100
  306.9 8.3 %collective-permute-start.9 = (bf16[4,128,128]{2,1,0:T(8,128)(2,1)S(1)}, bf16[4,128,128]{2,1,0:T(8,128)(2,1)S(1)}, u32[]{:S(2)}, u32[]{:S(2)}) collective-permute-start(bf16[4,128,128]{2,1,0:T(8,128)(2,1)S(1)} %fusion.1), channel_id=1, source_target_pairs={{0,16},{16,0},{1,17},{17,1},{2,18},{18,2},{3,19},{19,3},{4,20},{20... | collective-permute-start | bytes 393224 | tf_op jit(solution)/shard_map/ppermute | solution.py:18
  308.5 11.6 %collective-permute-start.8 = (bf16[448,384]{1,0:T(8,128)(2,1)S(1)}, bf16[448,384]{1,0:T(8,128)(2,1)S(1)}, u32[]{:S(2)}, u32[]{:S(2)}) collective-permute-start(bf16[448,384]{1,0:T(8,128)(2,1)S(1)} %slice_bitcast_fusion.1), channel_id=1, source_target_pairs={{0,16},{16,0},{1,17},{17,1},{2,18},{18,2},{3,19},{19,3},{4,20},{20... | collective-permute-start | bytes 1032200 | tf_op jit(solution)/shard_map/ppermute | solution.py:18
  315.2 12.7 %collective-permute-start.15 = (bf16[448,1024]{1,0:T(8,128)(2,1)}, bf16[448,1024]{1,0:T(8,128)(2,1)}, u32[]{:S(2)}, u32[]{:S(2)}) collective-permute-start(bf16[448,1024]{1,0:T(8,128)(2,1)} %get-tuple-element.45), channel_id=1, source_target_pairs={{0,1},{1,0},{2,3},{3,2},{4,5},{5,4},{6,7},{7,6},{8,9},{9,8},{10,11... | collective-permute-start | bytes 2752520 | tf_op jit(solution)/shard_map/ppermute | solution.py:18
  320.1 7.6 %copy-start.24 = (s32[4,1]{0,1:T(1,128)S(1)}, s32[4,1]{0,1:T(1,128)}, u32[]{:S(2)}) copy-start(s32[4,1]{0,1:T(1,128)} %param.12) | copy-start | bytes 52
  327.2 5.5 %collective-permute-start.11 = (bf16[448,1024]{1,0:T(8,128)(2,1)}, bf16[448,1024]{1,0:T(8,128)(2,1)}, u32[]{:S(2)}, u32[]{:S(2)}) collective-permute-start(bf16[448,1024]{1,0:T(8,128)(2,1)} %get-tuple-element.40), channel_id=1, source_target_pairs={{0,1},{1,0},{2,3},{3,2},{4,5},{5,4},{6,7},{7,6},{8,9},{9,8},{10,11... | collective-permute-start | bytes 2752520 | tf_op jit(solution)/shard_map/ppermute | solution.py:18
  327.2 5.5 %copy-start.12 = (bf16[448,1024]{1,0:T(8,128)(2,1)S(1)}, bf16[448,1024]{1,0:T(8,128)(2,1)}, u32[]{:S(2)}) copy-start(bf16[448,1024]{1,0:T(8,128)(2,1)} %copy-done.11) | copy-start | bytes 2752516
  327.2 8.0 %collective-permute-start.13 = (bf16[448,1024]{1,0:T(8,128)(2,1)}, bf16[448,1024]{1,0:T(8,128)(2,1)S(1)}, u32[]{:S(2)}, u32[]{:S(2)}) collective-permute-start(bf16[448,1024]{1,0:T(8,128)(2,1)} %copy-done.18), channel_id=1, source_target_pairs={{0,1},{1,0},{2,3},{3,2},{4,5},{5,4},{6,7},{7,6},{8,9},{9,8},{10,11... | collective-permute-start | bytes 2752520 | tf_op jit(solution)/shard_map/ppermute | solution.py:18
  327.9 27.4 %collective-permute-start.10 = (bf16[448,1024]{1,0:T(8,128)(2,1)}, bf16[448,1024]{1,0:T(8,128)(2,1)S(1)}, u32[]{:S(2)}, u32[]{:S(2)}) collective-permute-start(bf16[448,1024]{1,0:T(8,128)(2,1)} %copy-done.17), channel_id=1, source_target_pairs={{0,1},{1,0},{2,3},{3,2},{4,5},{5,4},{6,7},{7,6},{8,9},{9,8},{10,11... | collective-permute-start | bytes 2752520 | tf_op jit(solution)/shard_map/ppermute | solution.py:18
  329.5 25.7 %collective-permute-start.16 = (bf16[448,1024]{1,0:T(8,128)(2,1)S(1)}, bf16[448,1024]{1,0:T(8,128)(2,1)S(1)}, u32[]{:S(2)}, u32[]{:S(2)}) collective-permute-start(bf16[448,1024]{1,0:T(8,128)(2,1)S(1)} %add_convert_fusion.1), channel_id=1, source_target_pairs={{0,18},{1,19},{2,16},{3,17},{16,2},{17,3},{18,0},{19,1},{4,22},{5,... | collective-permute-start | bytes 2752520 | tf_op jit(solution)/shard_map/ppermute | solution.py:296
  334.2 15.3 %copy-start.14 = (bf16[2,448,384]{2,1,0:T(8,128)(2,1)S(1)}, bf16[2,448,384]{2,1,0:T(8,128)(2,1)}, u32[]{:S(2)}) copy-start(bf16[2,448,384]{2,1,0:T(8,128)(2,1)} %copy-done.13) | copy-start | bytes 2064388
  334.2 7.2 %collective-permute-start.19 = (bf16[4,128,128]{2,1,0:T(8,128)(2,1)S(1)}, bf16[4,128,128]{2,1,0:T(8,128)(2,1)S(1)}, u32[]{:S(2)}, u32[]{:S(2)}) collective-permute-start(bf16[4,128,128]{2,1,0:T(8,128)(2,1)S(1)} %copy-done.21), channel_id=1, source_target_pairs={{0,12},{4,8},{8,4},{12,0},{1,13},{5,9},{9,5},{13,1},{2,14},{6,10},... | collective-permute-start | bytes 393224 | tf_op jit(solution)/shard_map/ppermute | solution.py:18
  335.5 37.6 %collective-permute-start.14 = (bf16[448,1024]{1,0:T(8,128)(2,1)S(1)}, bf16[448,1024]{1,0:T(8,128)(2,1)S(1)}, u32[]{:S(2)}, u32[]{:S(2)}) collective-permute-start(bf16[448,1024]{1,0:T(8,128)(2,1)S(1)} %add_convert_fusion.2), channel_id=1, source_target_pairs={{0,2},{1,3},{2,0},{3,1},{4,6},{5,7},{6,4},{7,5},{8,10},{9,11},{10,... | collective-permute-start | bytes 2752520 | tf_op jit(solution)/shard_map/ppermute | solution.py:18
  336.2 37.0 %collective-permute-start.12 = (bf16[448,1024]{1,0:T(8,128)(2,1)S(1)}, bf16[448,1024]{1,0:T(8,128)(2,1)S(1)}, u32[]{:S(2)}, u32[]{:S(2)}) collective-permute-start(bf16[448,1024]{1,0:T(8,128)(2,1)S(1)} %add_convert_fusion.3), channel_id=1, source_target_pairs={{0,16},{16,0},{1,17},{17,1},{2,18},{18,2},{3,19},{19,3},{4,20},{20... | collective-permute-start | bytes 2752520 | tf_op jit(solution)/shard_map/ppermute | solution.py:18
  341.4 8.0 %collective-permute-start.18 = (bf16[4,128,128]{2,1,0:T(8,128)(2,1)S(1)}, bf16[4,128,128]{2,1,0:T(8,128)(2,1)S(1)}, u32[]{:S(2)}, u32[]{:S(2)}) collective-permute-start(bf16[4,128,128]{2,1,0:T(8,128)(2,1)S(1)} %copy-done.21), channel_id=1, source_target_pairs={{0,8},{4,12},{8,0},{12,4},{1,9},{5,13},{9,1},{13,5},{2,10},{6,14},... | collective-permute-start | bytes 393224 | tf_op jit(solution)/shard_map/ppermute | solution.py:18
  349.4 5.0 %collective-permute-start.17 = (bf16[4,128,128]{2,1,0:T(8,128)(2,1)S(1)}, bf16[4,128,128]{2,1,0:T(8,128)(2,1)S(1)}, u32[]{:S(2)}, u32[]{:S(2)}) collective-permute-start(bf16[4,128,128]{2,1,0:T(8,128)(2,1)S(1)} %copy-done.21), channel_id=1, source_target_pairs={{0,4},{4,0},{8,12},{12,8},{1,5},{5,1},{9,13},{13,9},{2,6},{6,2},{1... | collective-permute-start | bytes 393224 | tf_op jit(solution)/shard_map/ppermute | solution.py:18
  (15 other events, 34.1 us)
Sparse Core Ops, SparseCore 0:
  11.1 220.8 all-gather.4
  234.2 61.6 all-gather.6

commit v13 on v12

--- a/solution.py
+++ b/solution.py
@@ -287,20 +287,27 @@
     far_own_give, far_peer_give, far_own, far_peer = back_of(3)
     far_peer_got = swap(far_peer_give, "tensor", 1)
     far_own_got = swap(far_own_give, "tensor", 1)
-    near_own_give, near_peer_give, near_own, near_peer = back_of(1, far_peer, sums, back_b)
+    near_own_give, near_peer_give, near_own, near_peer = back_of(1, far_peer)
     near_peer_got = swap(near_peer_give, "tensor", 1)
     near_own_got = swap(near_own_give, "tensor", 1)
+    cut = rows // 2
     far_peer, far_own = tie(far_peer, near_peer), tie(far_own, near_peer)
-    far_peer = (far_peer.astype(F32) + far_peer_got.astype(F32)).astype(BF)
-    diagonal = [(i, i ^ (n_t + 2)) for i in range(2 * n_t)]
-    from_xy = lax.ppermute(far_peer, ("groups", "tensor"), diagonal)
-    far_own = (far_own.astype(F32) + far_own_got.astype(F32)).astype(BF)
-    from_x = swap(far_own, "tensor", 2)
-    near_peer = (near_peer.astype(F32) + near_peer_got.astype(F32)).astype(BF)
-    from_y = swap(near_peer, "groups", 1)
+    far_peer = far_peer.astype(F32) + far_peer_got.astype(F32)
+    far_own = far_own.astype(F32) + far_own_got.astype(F32)
+    near_peer = near_peer.astype(F32) + near_peer_got.astype(F32)
+    over_x = swap(jnp.concatenate([far_peer[:cut], far_own[:cut]], axis=0).astype(BF), "tensor", 2)
+    over_y = swap(
+        jnp.concatenate([near_peer[cut:], far_peer[cut:]], axis=0).astype(BF), "groups", 1
+    )
     shares = [swap(tie(sums.astype(BF), near_peer), "dp", bit) for bit in range(1, n_dp)]
+    far_own = (far_own[cut:] + over_y[cut:].astype(F32)).astype(BF)
+    near_peer = (near_peer[:cut] + over_x[:cut].astype(F32)).astype(BF)
+    last_x = swap(tie(far_own, *shares[:1]), "tensor", 2)
+    last_y = swap(tie(near_peer, back_b, *shares[:1]), "groups", 1)
+    from_x = jnp.concatenate([over_x[cut:], last_x], axis=0)
+    from_y = jnp.concatenate([last_y, over_y[:cut]], axis=0)
     near_own = near_own.astype(F32) + near_own_got.astype(F32)
-    d_tokens = near_own + from_y.astype(F32) + from_x.astype(F32) + from_xy.astype(F32)
+    d_tokens = near_own + from_y.astype(F32) + from_x.astype(F32)
     for share in shares:
         sums = sums + share.astype(F32)
     norm = float(rows * n_dp) ** (-0.5)

time: 383 us -> 384 us (level)
  local copies, waits for them, and re-layouts: 42.1 us -> 47.2 us
  waiting for transfers between devices: 229 us -> 225 us
    ppermute x19 -> x21, waiting for transfers between devices: 98.8 us -> 93 us  [swap(): return lax.ppermute(array, axis, [(i, i ^ bit) for i in range(size)])]
    unnamed x52 -> x64, local copies, waits for them, and re-layouts: 21.6 us -> 25.5 us
    ppermute x19 -> x21, starting transfers between devices: 19.6 us -> 23.4 us  [swap(): return lax.ppermute(array, axis, [(i, i ^ bit) for i in range(size)])]
  transfers between devices with their start and end apart: 22 -> 23, of which waited for: 12 -> 12; matrix products, arithmetic and copies ran while one was open for 9% -> 9% of each run, Pallas kernels for 13% -> 12%
where the time goes in v13:
time: 384 us; the launch traced here: 382 us
  waiting for transfers between devices  225 us (59%)
  Pallas kernels  55.4 us (14%)
  local copies, waits for them, and re-layouts  47.2 us (12%)
  starting transfers between devices  23.5 us (6%)
  other arithmetic  16.7 us (4%)
  between operations  14.5 us (4%)
    all_gather x1, waiting for transfers between devices, local(): gather_a = lax.all_gather(shards[0], 'dp')  128 us
    ppermute x21, waiting for transfers between devices, swap(): return lax.ppermute(array, axis, [(i, i ^ bit) for i in range(size)])  93 us
    pallas_call x2, Pallas kernels, forward(): pl.pallas_call(functools.partial(forward_kernel, first, blocks, bs, cuts)...  27.8 us
    pallas_call x3, Pallas kernels, backward(): pl.pallas_call(functools.partial(backward_kernel, firsts, blocks, bs, acc...  27.6 us
    unnamed x64, local copies, waits for them, and re-layouts  25.5 us
    ppermute x21, starting transfers between devices, swap(): return lax.ppermute(array, axis, [(i, i ^ bit) for i in range(size)])  23.4 us
  transfers between devices with their start and end apart: 23, of which 12 were waited for; matrix products, arithmetic and copies ran while one was open for 9% of the time, Pallas kernels for 12%

profile of v13, /device:TPU:0, one launch (start us, length us, event | category | flops | bytes accessed | tf_op | source)
XLA Modules:
  0.0 382.3 jit_solution(5001582781648047042)
XLA Ops:
  7.2 3.8 constant_dynamic-slice_fusion.5
  12.2 3.0 collective-permute-start
  16.6 19.0 %collective-permute-done = bf16[448,1024]{1,0:T(8,128)(2,1)} collective-permute-done((bf16[448,1024]{1,0:T(8,128)(2,1)S(1)}, bf16[448,1024]{1,0:T(8,128)(2,1)}, u32[]{:S(2)}, u32[]{:S(2)}) %collective-permute-start) | collective-permute-done | bytes 917536 | tf_op jit(solution)/shard_map/ppermute | solution.py:18
  38.3 3.1 constant_dynamic-slice_fusion.4
  41.3 2.2 constant_dynamic-update-slice_fusion
  44.8 12.7 %collective-permute-done.3 = bf16[448,1024]{1,0:T(8,128)(2,1)} collective-permute-done((bf16[448,1024]{1,0:T(8,128)(2,1)}, bf16[448,1024]{1,0:T(8,128)(2,1)}, u32[]{:S(2)}, u32[]{:S(2)}) %collective-permute-start.3) | collective-permute-done | bytes 917536 | tf_op jit(solution)/shard_map/ppermute | solution.py:18
  60.2 2.0 constant_dynamic-slice_fusion.1
  62.2 26.0 %collective-permute-done.5 = bf16[448,1536]{1,0:T(8,128)(2,1)} collective-permute-done((bf16[448,1536]{1,0:T(8,128)(2,1)}, bf16[448,1536]{1,0:T(8,128)(2,1)}, u32[]{:S(2)}, u32[]{:S(2)}) %collective-permute-start.5) | collective-permute-done | bytes 1376288 | tf_op jit(solution)/shard_map/ppermute | solution.py:18
  89.3 2.1 constant_dynamic-slice_fusion.2
  91.4 3.1 pad_maximum_fusion.1.d_ref
  95.9 1.9 pad_maximum_fusion.4.d_ref
  97.9 6.2 %pad_maximum_fusion.x_ref = bf16[4,896,1024]{2,1,0:T(8,128)(2,1)} fusion(bf16[1,896,1024]{2,1,0:T(8,128)(2,1)} %bitcast.7, bf16[1,896,1024]{2,1,0:T(8,128)(2,1)S(1)} %bitcast.39, bf16[1,896,1024]{2,1,0:T(8,128)(2,1)} %bitcast.5, bf16[1,896,1024]{2,1,0:T(8,128)(2,1)} %bitcast.4), kind=kLoop, calls=%fused_computation | loop fusion | flops 11010048 | bytes 14680064 | tf_op jit(solution)/shard_map/stack | solution.py:256
  104.1 128.0 %all-gather.5.cloned.1.call-done = bf16[4096,1536]{1,0:T(8,128)(2,1)} async-done(((bf16[1024,1536]{1,0:T(8,128)(2,1)}), bf16[4096,1536]{1,0:T(8,128)(2,1)}) %all-gather.5.cloned.1.call-update) | async-done | bytes 12582928 | tf_op jit(solution)/shard_map/all_gather | solution.py:237
  232.4 3.1 copy-done
  237.3 21.9 %shard_map.94 = (bf16[2,448,1536]{2,1,0:T(8,128)(2,1)S(1)}, bf16[896,1536]{1,0:T(8,128)(2,1)S(1)}, f32[2,4,128,128]{3,2,1,0:T(8,128)S(1)}) custom-call(s32[20]{0:T(128)S(1)} %pad_add_fusion.1.meta, bf16[4,896,1024]{2,1,0:T(8,128)(2,1)S(1)} %copy-done, bf16[4,1024,1536]{2,1,0:T(8,128)(2,1)} %bitcast.34, bf16[4,128,128]{2,1,0:T(8,128)(2,1)S(1)} %copy-done.9, ...), custom_call_target="tpu_custom_call" | custom-call | flops 1 | bytes 1 | tf_op jit(solution)/shard_map/pallas_call | solution.py:81
  260.9 1.8 copy-done.11
  262.7 17.8 %shard_map.95.refs_3_ = bf16[4,896,1024]{2,1,0:T(8,128)(2,1)S(1)} custom-call(s32[20]{0:T(128)S(1)} %pad_add_fusion.1.meta, bf16[896,1536]{1,0:T(8,128)(2,1)S(1)} %copy-done.11, bf16[4,1024,1536]{2,1,0:T(8,128)(2,1)S(1)} %bitcast.35, bf16[4,128,128]{2,1,0:T(8,128)(2,1)S(1)} %copy-done.9), custom_call_target="tpu_custom_call" | custom-call | flops 1 | bytes 1 | tf_op jit(solution)/shard_map/pallas_call | solution.py:174
  280.5 2.9 copy-done.2
  283.5 2.0 broadcast_in_dim.32
  286.6 4.2 %collective-permute-done.6 = bf16[448,1536]{1,0:T(8,128)(2,1)S(1)} collective-permute-done((bf16[448,1536]{1,0:T(8,128)(2,1)S(1)}, bf16[448,1536]{1,0:T(8,128)(2,1)S(1)}, u32[]{:S(2)}, u32[]{:S(2)}) %collective-permute-start.6) | collective-permute-done | bytes 1376288 | tf_op jit(solution)/shard_map/ppermute | solution.py:18
  292.0 4.0 %all-gather.7.cloned.1.call-done = bf16[4096,384]{1,0:T(8,128)(2,1)} async-done(((bf16[1024,384]{1,0:T(8,128)(2,1)}), bf16[4096,384]{1,0:T(8,128)(2,1)}) %all-gather.7.cloned.1.call-update) | async-done | bytes 3145744 | tf_op jit(solution)/shard_map/all_gather | solution.py:267
  295.9 3.1 copy-done.1
  299.0 1.9 copy-done.6
  300.9 5.9 %shard_map.96 = (bf16[2,448,384]{2,1,0:T(8,128)(2,1)S(1)}, bf16[896,384]{1,0:T(8,128)(2,1)S(1)}, f32[2,4,128,128]{3,2,1,0:T(8,128)S(1)}) custom-call(s32[20]{0:T(128)S(1)} %pad_add_fusion.1.meta, bf16[4,896,1024]{2,1,0:T(8,128)(2,1)S(1)} %copy-done.1, bf16[4,1024,384]{2,1,0:T(8,128)(2,1)S(1)} %bitcast.36, bf16[4,128,128]{2,1,0:T(8,128)(2,1)S(1)} %copy-done.9, ...), custom_call_target="tpu_custom_call" | custom-call | flops 1 | bytes 1 | tf_op jit(solution)/shard_map/pallas_call | solution.py:81
  306.9 5.1 %shard_map.97 = (bf16[448,1024]{1,0:T(8,128)(2,1)}, bf16[448,1024]{1,0:T(8,128)(2,1)S(1)}, bf16[448,1024]{1,0:T(8,128)(2,1)S(1)}, bf16[448,1024]{1,0:T(8,128)(2,1)S(1)}) custom-call(s32[20]{0:T(128)S(1)} %pad_add_fusion.1.meta, bf16[896,384]{1,0:T(8,128)(2,1)S(1)} %get-tuple-element.34.refs_0_, bf16[4,1024,384]{2,1,0:T(8,128)(2,1)S(1)} %bitcast.37, ...), custom_call_target="tpu_custom_call" | custom-call | flops 1 | bytes 1 | tf_op jit(solution)/shard_map/pallas_call | solution.py:174
  318.4 3.1 copy-done.4
  322.6 4.7 %shard_map.98 = (bf16[448,1024]{1,0:T(8,128)(2,1)S(1)}, bf16[448,1024]{1,0:T(8,128)(2,1)S(1)}, bf16[448,1024]{1,0:T(8,128)(2,1)S(1)}, bf16[448,1024]{1,0:T(8,128)(2,1)S(1)}) custom-call(s32[20]{0:T(128)S(1)} %pad_add_fusion.1.meta, bf16[896,384]{1,0:T(8,128)(2,1)S(1)} %copy-done.14, bf16[4,1024,384]{2,1,0:T(8,128)(2,1)S(1)} %bitcast.38, ...), custom_call_target="tpu_custom_call" | custom-call | flops 1 | bytes 1 | tf_op jit(solution)/shard_map/pallas_call | solution.py:174
  330.5 2.2 collective-permute-start.13
  336.2 21.7 %collective-permute-done.14 = bf16[4,128,128]{2,1,0:T(8,128)(2,1)S(1)} collective-permute-done((bf16[4,128,128]{2,1,0:T(8,128)(2,1)S(1)}, bf16[4,128,128]{2,1,0:T(8,128)(2,1)S(1)}, u32[]{:S(2)}, u32[]{:S(2)}) %collective-permute-start.14) | collective-permute-done | bytes 131104 | tf_op jit(solution)/shard_map/ppermute | solution.py:18
  358.1 2.5 collective-permute-start.20
  361.7 2.4 collective-permute-done.15
  367.3 4.4 %collective-permute-done.19 = bf16[4,128,128]{2,1,0:T(8,128)(2,1)S(1)} collective-permute-done((bf16[4,128,128]{2,1,0:T(8,128)(2,1)S(1)}, bf16[4,128,128]{2,1,0:T(8,128)(2,1)S(1)}, u32[]{:S(2)}, u32[]{:S(2)}) %collective-permute-start.19) | collective-permute-done | bytes 131104 | tf_op jit(solution)/shard_map/ppermute | solution.py:18
  (130 shorter events, 40.2 us)
Async XLA Ops:
  7.2 224.9 %all-gather.5.cloned.1.call-start = ((), (), s32[]{:S(2)}) async-start(), calls=%async_computation | async-start | bytes 15728640 | tf_op jit(solution)/shard_map/all_gather | solution.py:237
  11.0 284.9 %all-gather.7.cloned.1.call-start = ((), (), s32[]{:S(2)}) async-start(), calls=%async_computation.1 | async-start | bytes 3932160 | tf_op jit(solution)/shard_map/all_gather | solution.py:267
  12.2 23.4 %collective-permute-start = (bf16[448,1024]{1,0:T(8,128)(2,1)S(1)}, bf16[448,1024]{1,0:T(8,128)(2,1)}, u32[]{:S(2)}, u32[]{:S(2)}) collective-permute-start(bf16[448,1024]{1,0:T(8,128)(2,1)S(1)} %copy-done.27), channel_id=1, source_target_pairs={{0,16},{16,0},{1,17},{17,1},{2,18},{18,2},{3,19},{19,3},{4,20},{20... | collective-permute-start | bytes 2752520 | tf_op jit(solution)/shard_map/ppermute | solution.py:18
  15.1 28.4 %collective-permute-start.2 = (bf16[448,1024]{1,0:T(8,128)(2,1)S(1)}, bf16[448,1024]{1,0:T(8,128)(2,1)}, u32[]{:S(2)}, u32[]{:S(2)}) collective-permute-start(bf16[448,1024]{1,0:T(8,128)(2,1)S(1)} %copy-done.27), channel_id=1, source_target_pairs={{0,2},{1,3},{2,0},{3,1},{4,6},{5,7},{6,4},{7,5},{8,10},{9,11},{10,... | collective-permute-start | bytes 2752520 | tf_op jit(solution)/shard_map/ppermute | solution.py:18
  35.6 21.9 %collective-permute-start.3 = (bf16[448,1024]{1,0:T(8,128)(2,1)}, bf16[448,1024]{1,0:T(8,128)(2,1)}, u32[]{:S(2)}, u32[]{:S(2)}) collective-permute-start(bf16[448,1024]{1,0:T(8,128)(2,1)} %collective-permute-done), channel_id=1, source_target_pairs={{0,2},{1,3},{2,0},{3,1},{4,6},{5,7},{6,4},{7,5},{8,10},{9,11},{10,... | collective-permute-start | bytes 2752520 | tf_op jit(solution)/shard_map/ppermute | solution.py:18
  43.5 54.3 %collective-permute-start.1 = (bf16[896,1024]{1,0:T(8,128)(2,1)}, bf16[896,1024]{1,0:T(8,128)(2,1)}, u32[]{:S(2)}, u32[]{:S(2)}) collective-permute-start(bf16[896,1024]{1,0:T(8,128)(2,1)} %constant_dynamic-update-slice_fusion), channel_id=1, source_target_pairs={{0,1},{1,0},{2,3},{3,2},{4,5},{5,4},{6,7},{7,6},{8,9},{9,8},{10,11... | collective-permute-start | bytes 5505032 | tf_op jit(solution)/shard_map/ppermute | solution.py:18
  57.4 30.8 %collective-permute-start.5 = (bf16[448,1536]{1,0:T(8,128)(2,1)}, bf16[448,1536]{1,0:T(8,128)(2,1)}, u32[]{:S(2)}, u32[]{:S(2)}) collective-permute-start(bf16[448,1536]{1,0:T(8,128)(2,1)} %get-tuple-element.27), channel_id=1, source_target_pairs={{0,16},{16,0},{1,17},{17,1},{2,18},{18,2},{3,19},{19,3},{4,20},{20... | collective-permute-start | bytes 4128776 | tf_op jit(solution)/shard_map/ppermute | solution.py:18
  60.1 37.7 %collective-permute-start.4 = (bf16[896,1024]{1,0:T(8,128)(2,1)S(1)}, bf16[896,1024]{1,0:T(8,128)(2,1)}, u32[]{:S(2)}, u32[]{:S(2)}) collective-permute-start(bf16[896,1024]{1,0:T(8,128)(2,1)S(1)} %constant_dynamic-update-slice_fusion.2), channel_id=1, source_target_pairs={{0,1},{1,0},{2,3},{3,2},{4,5},{5,4},{6,7},{7,6},{8,9},{9,8},{10,11... | collective-permute-start | bytes 5505032 | tf_op jit(solution)/shard_map/ppermute | solution.py:18
  88.2 7.7 %collective-permute-start.7 = (bf16[448,384]{1,0:T(8,128)(2,1)}, bf16[448,384]{1,0:T(8,128)(2,1)}, u32[]{:S(2)}, u32[]{:S(2)}) collective-permute-start(bf16[448,384]{1,0:T(8,128)(2,1)} %get-tuple-element.29), channel_id=1, source_target_pairs={{0,16},{16,0},{1,17},{17,1},{2,18},{18,2},{3,19},{19,3},{4,20},{20... | collective-permute-start | bytes 1032200 | tf_op jit(solution)/shard_map/ppermute | solution.py:18
  97.8 134.3 %copy-start.28 = (s32[4]{0:T(128)S(1)}, s32[4]{0:T(128)}, u32[]{:S(2)}) copy-start(s32[4]{0:T(128)} %param.10) | copy-start | bytes 52
  97.8 134.3 %copy-start.29 = (s32[4]{0:T(128)S(1)}, s32[4]{0:T(128)}, u32[]{:S(2)}) copy-start(s32[4]{0:T(128)} %param.11) | copy-start | bytes 52
  97.9 134.6 %copy-start.9 = (bf16[4,128,128]{2,1,0:T(8,128)(2,1)S(1)}, bf16[4,128,128]{2,1,0:T(8,128)(2,1)}, u32[]{:S(2)}) copy-start(bf16[4,128,128]{2,1,0:T(8,128)(2,1)} %refs_2_.3) | copy-start | bytes 393220
  237.3 23.6 %copy-start.5 = (bf16[4096,1536]{1,0:T(8,128)(2,1)S(1)}, bf16[4096,1536]{1,0:T(8,128)(2,1)}, u32[]{:S(2)}) copy-start(bf16[4096,1536]{1,0:T(8,128)(2,1)} %all-gather.5.cloned.1.call-done) | copy-start | bytes 37748740
  259.2 21.3 %copy-start.21 = (f32[2,4,128,128]{3,2,1,0:T(8,128)}, f32[2,4,128,128]{3,2,1,0:T(8,128)S(1)}, u32[]{:S(2)}) copy-start(f32[2,4,128,128]{3,2,1,0:T(8,128)S(1)} %get-tuple-element.46) | copy-start | bytes 1572868
  259.3 31.5 %collective-permute-start.6 = (bf16[448,1536]{1,0:T(8,128)(2,1)S(1)}, bf16[448,1536]{1,0:T(8,128)(2,1)S(1)}, u32[]{:S(2)}, u32[]{:S(2)}) collective-permute-start(bf16[448,1536]{1,0:T(8,128)(2,1)S(1)} %slice_bitcast_fusion), channel_id=1, source_target_pairs={{0,16},{16,0},{1,17},{17,1},{2,18},{18,2},{3,19},{19,3},{4,20},{20... | collective-permute-start | bytes 4128776 | tf_op jit(solution)/shard_map/ppermute | solution.py:18
  286.6 9.3 %copy-start.12 = (bf16[896,384]{1,0:T(8,128)(2,1)S(1)}, bf16[896,384]{1,0:T(8,128)(2,1)}, u32[]{:S(2)}) copy-start(bf16[896,384]{1,0:T(8,128)(2,1)} %pad_maximum_fusion.4.d_ref) | copy-start | bytes 2064388
  300.9 6.0 %copy-start.3 = (bf16[4,896,1024]{2,1,0:T(8,128)(2,1)S(1)}, bf16[4,896,1024]{2,1,0:T(8,128)(2,1)}, u32[]{:S(2)}) copy-start(bf16[4,896,1024]{2,1,0:T(8,128)(2,1)} %copy-done.2) | copy-start | bytes 22020100
  306.9 8.8 %copy-start.30 = (s32[4,1]{0,1:T(1,128)S(1)}, s32[4,1]{0,1:T(1,128)}, u32[]{:S(2)}) copy-start(s32[4,1]{0,1:T(1,128)} %param.12) | copy-start | bytes 52
  306.9 11.5 %copy-start.7 = (bf16[4096,384]{1,0:T(8,128)(2,1)S(1)}, bf16[4096,384]{1,0:T(8,128)(2,1)}, u32[]{:S(2)}) copy-start(bf16[4096,384]{1,0:T(8,128)(2,1)} %all-gather.7.cloned.1.call-done) | copy-start | bytes 9437188
  314.9 13.1 %collective-permute-start.12 = (bf16[448,1024]{1,0:T(8,128)(2,1)}, bf16[448,1024]{1,0:T(8,128)(2,1)}, u32[]{:S(2)}, u32[]{:S(2)}) collective-permute-start(bf16[448,1024]{1,0:T(8,128)(2,1)} %get-tuple-element.45), channel_id=1, source_target_pairs={{0,1},{1,0},{2,3},{3,2},{4,5},{5,4},{6,7},{7,6},{8,9},{9,8},{10,11... | collective-permute-start | bytes 2752520 | tf_op jit(solution)/shard_map/ppermute | solution.py:18
  315.7 14.4 %collective-permute-start.11 = (bf16[448,1024]{1,0:T(8,128)(2,1)}, bf16[448,1024]{1,0:T(8,128)(2,1)S(1)}, u32[]{:S(2)}, u32[]{:S(2)}) collective-permute-start(bf16[448,1024]{1,0:T(8,128)(2,1)} %copy-done.25), channel_id=1, source_target_pairs={{0,1},{1,0},{2,3},{3,2},{4,5},{5,4},{6,7},{7,6},{8,9},{9,8},{10,11... | collective-permute-start | bytes 2752520 | tf_op jit(solution)/shard_map/ppermute | solution.py:18
  316.9 43.8 %collective-permute-start.8 = (bf16[448,384]{1,0:T(8,128)(2,1)S(1)}, bf16[448,384]{1,0:T(8,128)(2,1)S(1)}, u32[]{:S(2)}, u32[]{:S(2)}) collective-permute-start(bf16[448,384]{1,0:T(8,128)(2,1)S(1)} %slice_bitcast_fusion.1), channel_id=1, source_target_pairs={{0,16},{16,0},{1,17},{17,1},{2,18},{18,2},{3,19},{19,3},{4,20},{20... | collective-permute-start | bytes 1032200 | tf_op jit(solution)/shard_map/ppermute | solution.py:18
  327.3 45.3 %collective-permute-start.9 = (bf16[448,1024]{1,0:T(8,128)(2,1)S(1)}, bf16[448,1024]{1,0:T(8,128)(2,1)S(1)}, u32[]{:S(2)}, u32[]{:S(2)}) collective-permute-start(bf16[448,1024]{1,0:T(8,128)(2,1)S(1)} %get-tuple-element.38), channel_id=1, source_target_pairs={{0,1},{1,0},{2,3},{3,2},{4,5},{5,4},{6,7},{7,6},{8,9},{9,8},{10,11... | collective-permute-start | bytes 2752520 | tf_op jit(solution)/shard_map/ppermute | solution.py:18
  327.6 5.2 %collective-permute-start.10 = (bf16[448,1024]{1,0:T(8,128)(2,1)S(1)}, bf16[448,1024]{1,0:T(8,128)(2,1)S(1)}, u32[]{:S(2)}, u32[]{:S(2)}) collective-permute-start(bf16[448,1024]{1,0:T(8,128)(2,1)S(1)} %get-tuple-element.40), channel_id=1, source_target_pairs={{0,1},{1,0},{2,3},{3,2},{4,5},{5,4},{6,7},{7,6},{8,9},{9,8},{10,11... | collective-permute-start | bytes 2752520 | tf_op jit(solution)/shard_map/ppermute | solution.py:18
  330.5 27.5 %collective-permute-start.13 = (bf16[448,1024]{1,0:T(8,128)(2,1)S(1)}, bf16[448,1024]{1,0:T(8,128)(2,1)S(1)}, u32[]{:S(2)}, u32[]{:S(2)}) collective-permute-start(bf16[448,1024]{1,0:T(8,128)(2,1)S(1)} %pad_maximum_fusion.2), channel_id=1, source_target_pairs={{0,2},{1,3},{2,0},{3,1},{4,6},{5,7},{6,4},{7,5},{8,10},{9,11},{10,... | collective-permute-start | bytes 2752520 | tf_op jit(solution)/shard_map/ppermute | solution.py:18
  333.3 31.8 %collective-permute-start.17 = (bf16[448,1024]{1,0:T(8,128)(2,1)S(1)}, bf16[448,1024]{1,0:T(8,128)(2,1)S(1)}, u32[]{:S(2)}, u32[]{:S(2)}) collective-permute-start(bf16[448,1024]{1,0:T(8,128)(2,1)S(1)} %pad_maximum_fusion.3), channel_id=1, source_target_pairs={{0,16},{16,0},{1,17},{17,1},{2,18},{18,2},{3,19},{19,3},{4,20},{20... | collective-permute-start | bytes 2752520 | tf_op jit(solution)/shard_map/ppermute | solution.py:18
  334.0 24.0 %collective-permute-start.14 = (bf16[4,128,128]{2,1,0:T(8,128)(2,1)S(1)}, bf16[4,128,128]{2,1,0:T(8,128)(2,1)S(1)}, u32[]{:S(2)}, u32[]{:S(2)}) collective-permute-start(bf16[4,128,128]{2,1,0:T(8,128)(2,1)S(1)} %fusion.4), channel_id=1, source_target_pairs={{0,16},{16,0},{1,17},{17,1},{2,18},{18,2},{3,19},{19,3},{4,20},{20... | collective-permute-start | bytes 393224 | tf_op jit(solution)/shard_map/ppermute | solution.py:18
  358.0 6.2 %collective-permute-start.15 = (bf16[4,128,128]{2,1,0:T(8,128)(2,1)S(1)}, bf16[4,128,128]{2,1,0:T(8,128)(2,1)S(1)}, u32[]{:S(2)}, u32[]{:S(2)}) collective-permute-start(bf16[4,128,128]{2,1,0:T(8,128)(2,1)S(1)} %fusion.3), channel_id=1, source_target_pairs={{0,4},{4,0},{8,12},{12,8},{1,5},{5,1},{9,13},{13,9},{2,6},{6,2},{1... | collective-permute-start | bytes 393224 | tf_op jit(solution)/shard_map/ppermute | solution.py:18
  358.1 9.2 %collective-permute-start.20 = (bf16[4,128,128]{2,1,0:T(8,128)(2,1)S(1)}, bf16[4,128,128]{2,1,0:T(8,128)(2,1)S(1)}, u32[]{:S(2)}, u32[]{:S(2)}) collective-permute-start(bf16[4,128,128]{2,1,0:T(8,128)(2,1)S(1)} %fusion.3), channel_id=1, source_target_pairs={{0,12},{4,8},{8,4},{12,0},{1,13},{5,9},{9,5},{13,1},{2,14},{6,10},... | collective-permute-start | bytes 393224 | tf_op jit(solution)/shard_map/ppermute | solution.py:18
  360.7 10.9 %collective-permute-start.19 = (bf16[4,128,128]{2,1,0:T(8,128)(2,1)S(1)}, bf16[4,128,128]{2,1,0:T(8,128)(2,1)S(1)}, u32[]{:S(2)}, u32[]{:S(2)}) collective-permute-start(bf16[4,128,128]{2,1,0:T(8,128)(2,1)S(1)} %fusion.3), channel_id=1, source_target_pairs={{0,8},{4,12},{8,0},{12,4},{1,9},{5,13},{9,1},{13,5},{2,10},{6,14},... | collective-permute-start | bytes 393224 | tf_op jit(solution)/shard_map/ppermute | solution.py:18
  364.2 8.7 %collective-permute-start.16 = (bf16[224,1024]{1,0:T(8,128)(2,1)S(1)}, bf16[224,1024]{1,0:T(8,128)(2,1)S(1)}, u32[]{:S(2)}, u32[]{:S(2)}) collective-permute-start(bf16[224,1024]{1,0:T(8,128)(2,1)S(1)} %fusion.1), channel_id=1, source_target_pairs={{0,16},{16,0},{1,17},{17,1},{2,18},{18,2},{3,19},{19,3},{4,20},{20... | collective-permute-start | bytes 1376264 | tf_op jit(solution)/shard_map/ppermute | solution.py:18
  365.2 8.5 %collective-permute-start.18 = (bf16[224,1024]{1,0:T(8,128)(2,1)S(1)}, bf16[224,1024]{1,0:T(8,128)(2,1)S(1)}, u32[]{:S(2)}, u32[]{:S(2)}) collective-permute-start(bf16[224,1024]{1,0:T(8,128)(2,1)S(1)} %fusion), channel_id=1, source_target_pairs={{0,2},{1,3},{2,0},{3,1},{4,6},{5,7},{6,4},{7,5},{8,10},{9,11},{10,... | collective-permute-start | bytes 1376264 | tf_op jit(solution)/shard_map/ppermute | solution.py:18
  (22 other events, 60.7 us)
Sparse Core Ops, SparseCore 0:
  11.1 220.8 all-gather.4
  234.2 61.6 all-gather.6

commit v14 on v13

--- a/solution.py
+++ b/solution.py
@@ -291,7 +291,7 @@
     near_peer_got = swap(near_peer_give, "tensor", 1)
     near_own_got = swap(near_own_give, "tensor", 1)
     cut = rows // 2
-    far_peer, far_own = tie(far_peer, near_peer), tie(far_own, near_peer)
+    far_peer, far_own = tie(far_peer, near_peer, sums), tie(far_own, near_peer, back_b)
     far_peer = far_peer.astype(F32) + far_peer_got.astype(F32)
     far_own = far_own.astype(F32) + far_own_got.astype(F32)
     near_peer = near_peer.astype(F32) + near_peer_got.astype(F32)
@@ -303,7 +303,7 @@
     far_own = (far_own[cut:] + over_y[cut:].astype(F32)).astype(BF)
     near_peer = (near_peer[:cut] + over_x[:cut].astype(F32)).astype(BF)
     last_x = swap(tie(far_own, *shares[:1]), "tensor", 2)
-    last_y = swap(tie(near_peer, back_b, *shares[:1]), "groups", 1)
+    last_y = swap(tie(near_peer, *shares[:1]), "groups", 1)
     from_x = jnp.concatenate([over_x[cut:], last_x], axis=0)
     from_y = jnp.concatenate([last_y, over_y[:cut]], axis=0)
     near_own = near_own.astype(F32) + near_own_got.astype(F32)

time: 384 us -> 378 us (0.984)
  waiting for transfers between devices: 225 us -> 221 us
    unnamed x64 -> x60, local copies, waits for them, and re-layouts: 25.5 us -> 25.4 us
where the time goes in v14:
time: 378 us; the launch traced here: 377 us
  waiting for transfers between devices  221 us (58%)
  Pallas kernels  55.5 us (15%)
  local copies, waits for them, and re-layouts  46.1 us (12%)
  starting transfers between devices  22.3 us (6%)
  other arithmetic  18 us (5%)
  between operations  14.5 us (4%)
    all_gather x1, waiting for transfers between devices, local(): gather_a = lax.all_gather(shards[0], 'dp')  128 us
    ppermute x21, waiting for transfers between devices, swap(): return lax.ppermute(array, axis, [(i, i ^ bit) for i in range(size)])  89.1 us
    pallas_call x2, Pallas kernels, forward(): pl.pallas_call(functools.partial(forward_kernel, first, blocks, bs, cuts)...  27.8 us
    pallas_call x3, Pallas kernels, backward(): pl.pallas_call(functools.partial(backward_kernel, firsts, blocks, bs, acc...  27.7 us
    unnamed x60, local copies, waits for them, and re-layouts  25.4 us
    ppermute x21, starting transfers between devices, swap(): return lax.ppermute(array, axis, [(i, i ^ bit) for i in range(size)])  22.2 us
  transfers between devices with their start and end apart: 23, of which 12 were waited for; matrix products, arithmetic and copies ran while one was open for 9% of the time, Pallas kernels for 12%

profile of v14, /device:TPU:0, one launch (start us, length us, event | category | flops | bytes accessed | tf_op | source)
XLA Modules:
  0.0 377.1 jit_solution(10343520412848589207)
XLA Ops:
  7.2 3.8 constant_dynamic-slice_fusion.5
  12.2 3.0 collective-permute-start
  16.6 19.0 %collective-permute-done = bf16[448,1024]{1,0:T(8,128)(2,1)} collective-permute-done((bf16[448,1024]{1,0:T(8,128)(2,1)S(1)}, bf16[448,1024]{1,0:T(8,128)(2,1)}, u32[]{:S(2)}, u32[]{:S(2)}) %collective-permute-start) | collective-permute-done | bytes 917536 | tf_op jit(solution)/shard_map/ppermute | solution.py:18
  38.3 3.1 constant_dynamic-slice_fusion.4
  41.4 2.2 constant_dynamic-update-slice_fusion
  44.8 12.7 %collective-permute-done.3 = bf16[448,1024]{1,0:T(8,128)(2,1)} collective-permute-done((bf16[448,1024]{1,0:T(8,128)(2,1)}, bf16[448,1024]{1,0:T(8,128)(2,1)}, u32[]{:S(2)}, u32[]{:S(2)}) %collective-permute-start.3) | collective-permute-done | bytes 917536 | tf_op jit(solution)/shard_map/ppermute | solution.py:18
  60.2 2.0 constant_dynamic-slice_fusion.1
  62.2 26.0 %collective-permute-done.5 = bf16[448,1536]{1,0:T(8,128)(2,1)} collective-permute-done((bf16[448,1536]{1,0:T(8,128)(2,1)}, bf16[448,1536]{1,0:T(8,128)(2,1)}, u32[]{:S(2)}, u32[]{:S(2)}) %collective-permute-start.5) | collective-permute-done | bytes 1376288 | tf_op jit(solution)/shard_map/ppermute | solution.py:18
  89.3 2.1 constant_dynamic-slice_fusion.2
  91.4 3.1 pad_maximum_fusion.1.d_ref
  95.9 1.9 pad_maximum_fusion.4.d_ref
  97.9 6.2 %pad_maximum_fusion.x_ref = bf16[4,896,1024]{2,1,0:T(8,128)(2,1)} fusion(bf16[1,896,1024]{2,1,0:T(8,128)(2,1)} %bitcast.7, bf16[1,896,1024]{2,1,0:T(8,128)(2,1)S(1)} %bitcast.36, bf16[1,896,1024]{2,1,0:T(8,128)(2,1)} %bitcast.5, bf16[1,896,1024]{2,1,0:T(8,128)(2,1)} %bitcast.4), kind=kLoop, calls=%fused_computation | loop fusion | flops 11010048 | bytes 14680064 | tf_op jit(solution)/shard_map/stack | solution.py:256
  104.0 128.0 %all-gather.5.cloned.1.call-done = bf16[4096,1536]{1,0:T(8,128)(2,1)} async-done(((bf16[1024,1536]{1,0:T(8,128)(2,1)}), bf16[4096,1536]{1,0:T(8,128)(2,1)}) %all-gather.5.cloned.1.call-update) | async-done | bytes 12582928 | tf_op jit(solution)/shard_map/all_gather | solution.py:237
  232.4 3.1 copy-done
  237.3 21.9 %shard_map.94 = (bf16[2,448,1536]{2,1,0:T(8,128)(2,1)S(1)}, bf16[896,1536]{1,0:T(8,128)(2,1)S(1)}, f32[2,4,128,128]{3,2,1,0:T(8,128)S(1)}) custom-call(s32[20]{0:T(128)S(1)} %pad_add_fusion.1.meta, bf16[4,896,1024]{2,1,0:T(8,128)(2,1)S(1)} %copy-done, bf16[4,1024,1536]{2,1,0:T(8,128)(2,1)} %bitcast.31, bf16[4,128,128]{2,1,0:T(8,128)(2,1)S(1)} %copy-done.9, ...), custom_call_target="tpu_custom_call" | custom-call | flops 1 | bytes 1 | tf_op jit(solution)/shard_map/pallas_call | solution.py:81
  262.5 17.9 %shard_map.95.refs_3_ = bf16[4,896,1024]{2,1,0:T(8,128)(2,1)S(1)} custom-call(s32[20]{0:T(128)S(1)} %pad_add_fusion.1.meta, bf16[896,1536]{1,0:T(8,128)(2,1)S(1)} %copy-done.11, bf16[4,1024,1536]{2,1,0:T(8,128)(2,1)S(1)} %bitcast.32, bf16[4,128,128]{2,1,0:T(8,128)(2,1)S(1)} %copy-done.9), custom_call_target="tpu_custom_call" | custom-call | flops 1 | bytes 1 | tf_op jit(solution)/shard_map/pallas_call | solution.py:174
  280.4 2.9 copy-done.2
  283.3 2.0 broadcast_in_dim.32
  286.5 4.7 %collective-permute-done.6 = bf16[448,1536]{1,0:T(8,128)(2,1)S(1)} collective-permute-done((bf16[448,1536]{1,0:T(8,128)(2,1)S(1)}, bf16[448,1536]{1,0:T(8,128)(2,1)S(1)}, u32[]{:S(2)}, u32[]{:S(2)}) %collective-permute-start.6) | collective-permute-done | bytes 1376288 | tf_op jit(solution)/shard_map/ppermute | solution.py:18
  292.3 3.6 all-gather.7.cloned.1.call-done
  295.9 3.1 copy-done.1
  299.0 1.9 copy-done.6
  300.9 5.9 %shard_map.96 = (bf16[2,448,384]{2,1,0:T(8,128)(2,1)S(1)}, bf16[896,384]{1,0:T(8,128)(2,1)S(1)}, f32[2,4,128,128]{3,2,1,0:T(8,128)S(1)}) custom-call(s32[20]{0:T(128)S(1)} %pad_add_fusion.1.meta, bf16[4,896,1024]{2,1,0:T(8,128)(2,1)S(1)} %copy-done.1, bf16[4,1024,384]{2,1,0:T(8,128)(2,1)S(1)} %bitcast.33, bf16[4,128,128]{2,1,0:T(8,128)(2,1)S(1)} %copy-done.9, ...), custom_call_target="tpu_custom_call" | custom-call | flops 1 | bytes 1 | tf_op jit(solution)/shard_map/pallas_call | solution.py:81
  307.7 5.1 %shard_map.97 = (bf16[448,1024]{1,0:T(8,128)(2,1)}, bf16[448,1024]{1,0:T(8,128)(2,1)S(1)}, bf16[448,1024]{1,0:T(8,128)(2,1)S(1)}, bf16[448,1024]{1,0:T(8,128)(2,1)S(1)}) custom-call(s32[20]{0:T(128)S(1)} %pad_add_fusion.1.meta, bf16[896,384]{1,0:T(8,128)(2,1)S(1)} %get-tuple-element.34.refs_0_, bf16[4,1024,384]{2,1,0:T(8,128)(2,1)S(1)} %bitcast.34, ...), custom_call_target="tpu_custom_call" | custom-call | flops 1 | bytes 1 | tf_op jit(solution)/shard_map/pallas_call | solution.py:174
  317.5 2.5 collective-permute-start.11
  320.3 3.1 copy-done.4
  323.4 4.7 %shard_map.98 = (bf16[448,1024]{1,0:T(8,128)(2,1)S(1)}, bf16[448,1024]{1,0:T(8,128)(2,1)S(1)}, bf16[448,1024]{1,0:T(8,128)(2,1)S(1)}, bf16[448,1024]{1,0:T(8,128)(2,1)S(1)}) custom-call(s32[20]{0:T(128)S(1)} %pad_add_fusion.1.meta, bf16[896,384]{1,0:T(8,128)(2,1)S(1)} %copy-done.14, bf16[4,1024,384]{2,1,0:T(8,128)(2,1)S(1)} %bitcast.35, ...), custom_call_target="tpu_custom_call" | custom-call | flops 1 | bytes 1 | tf_op jit(solution)/shard_map/pallas_call | solution.py:174
  328.3 2.9 collective-permute-done.8
  335.1 1.8 collective-permute-start.17
  337.8 2.5 collective-permute-start.20
  340.3 15.1 %collective-permute-done.14 = bf16[448,1024]{1,0:T(8,128)(2,1)S(1)} collective-permute-done((bf16[448,1024]{1,0:T(8,128)(2,1)S(1)}, bf16[448,1024]{1,0:T(8,128)(2,1)S(1)}, u32[]{:S(2)}, u32[]{:S(2)}) %collective-permute-start.14) | collective-permute-done | bytes 917536 | tf_op jit(solution)/shard_map/ppermute | solution.py:18
  362.8 4.8 %collective-permute-done.16 = bf16[224,1024]{1,0:T(8,128)(2,1)S(1)} collective-permute-done((bf16[224,1024]{1,0:T(8,128)(2,1)S(1)}, bf16[224,1024]{1,0:T(8,128)(2,1)S(1)}, u32[]{:S(2)}, u32[]{:S(2)}) %collective-permute-start.16) | collective-permute-done | bytes 458784 | tf_op jit(solution)/shard_map/ppermute | solution.py:18
  (126 shorter events, 40.4 us)
Async XLA Ops:
  7.2 224.9 %all-gather.5.cloned.1.call-start = ((), (), s32[]{:S(2)}) async-start(), calls=%async_computation | async-start | bytes 15728640 | tf_op jit(solution)/shard_map/all_gather | solution.py:237
  11.0 284.9 %all-gather.7.cloned.1.call-start = ((), (), s32[]{:S(2)}) async-start(), calls=%async_computation.1 | async-start | bytes 3932160 | tf_op jit(solution)/shard_map/all_gather | solution.py:267
  12.2 23.4 %collective-permute-start = (bf16[448,1024]{1,0:T(8,128)(2,1)S(1)}, bf16[448,1024]{1,0:T(8,128)(2,1)}, u32[]{:S(2)}, u32[]{:S(2)}) collective-permute-start(bf16[448,1024]{1,0:T(8,128)(2,1)S(1)} %copy-done.25), channel_id=1, source_target_pairs={{0,16},{16,0},{1,17},{17,1},{2,18},{18,2},{3,19},{19,3},{4,20},{20... | collective-permute-start | bytes 2752520 | tf_op jit(solution)/shard_map/ppermute | solution.py:18
  15.1 28.4 %collective-permute-start.2 = (bf16[448,1024]{1,0:T(8,128)(2,1)S(1)}, bf16[448,1024]{1,0:T(8,128)(2,1)}, u32[]{:S(2)}, u32[]{:S(2)}) collective-permute-start(bf16[448,1024]{1,0:T(8,128)(2,1)S(1)} %copy-done.25), channel_id=1, source_target_pairs={{0,2},{1,3},{2,0},{3,1},{4,6},{5,7},{6,4},{7,5},{8,10},{9,11},{10,... | collective-permute-start | bytes 2752520 | tf_op jit(solution)/shard_map/ppermute | solution.py:18
  35.6 21.9 %collective-permute-start.3 = (bf16[448,1024]{1,0:T(8,128)(2,1)}, bf16[448,1024]{1,0:T(8,128)(2,1)}, u32[]{:S(2)}, u32[]{:S(2)}) collective-permute-start(bf16[448,1024]{1,0:T(8,128)(2,1)} %collective-permute-done), channel_id=1, source_target_pairs={{0,2},{1,3},{2,0},{3,1},{4,6},{5,7},{6,4},{7,5},{8,10},{9,11},{10,... | collective-permute-start | bytes 2752520 | tf_op jit(solution)/shard_map/ppermute | solution.py:18
  43.5 54.3 %collective-permute-start.1 = (bf16[896,1024]{1,0:T(8,128)(2,1)}, bf16[896,1024]{1,0:T(8,128)(2,1)}, u32[]{:S(2)}, u32[]{:S(2)}) collective-permute-start(bf16[896,1024]{1,0:T(8,128)(2,1)} %constant_dynamic-update-slice_fusion), channel_id=1, source_target_pairs={{0,1},{1,0},{2,3},{3,2},{4,5},{5,4},{6,7},{7,6},{8,9},{9,8},{10,11... | collective-permute-start | bytes 5505032 | tf_op jit(solution)/shard_map/ppermute | solution.py:18
  57.4 30.8 %collective-permute-start.5 = (bf16[448,1536]{1,0:T(8,128)(2,1)}, bf16[448,1536]{1,0:T(8,128)(2,1)}, u32[]{:S(2)}, u32[]{:S(2)}) collective-permute-start(bf16[448,1536]{1,0:T(8,128)(2,1)} %get-tuple-element.27), channel_id=1, source_target_pairs={{0,16},{16,0},{1,17},{17,1},{2,18},{18,2},{3,19},{19,3},{4,20},{20... | collective-permute-start | bytes 4128776 | tf_op jit(solution)/shard_map/ppermute | solution.py:18
  60.1 37.7 %collective-permute-start.4 = (bf16[896,1024]{1,0:T(8,128)(2,1)S(1)}, bf16[896,1024]{1,0:T(8,128)(2,1)}, u32[]{:S(2)}, u32[]{:S(2)}) collective-permute-start(bf16[896,1024]{1,0:T(8,128)(2,1)S(1)} %constant_dynamic-update-slice_fusion.2), channel_id=1, source_target_pairs={{0,1},{1,0},{2,3},{3,2},{4,5},{5,4},{6,7},{7,6},{8,9},{9,8},{10,11... | collective-permute-start | bytes 5505032 | tf_op jit(solution)/shard_map/ppermute | solution.py:18
  88.2 7.7 %collective-permute-start.7 = (bf16[448,384]{1,0:T(8,128)(2,1)}, bf16[448,384]{1,0:T(8,128)(2,1)}, u32[]{:S(2)}, u32[]{:S(2)}) collective-permute-start(bf16[448,384]{1,0:T(8,128)(2,1)} %get-tuple-element.29), channel_id=1, source_target_pairs={{0,16},{16,0},{1,17},{17,1},{2,18},{18,2},{3,19},{19,3},{4,20},{20... | collective-permute-start | bytes 1032200 | tf_op jit(solution)/shard_map/ppermute | solution.py:18
  97.8 134.3 %copy-start.26 = (s32[4]{0:T(128)S(1)}, s32[4]{0:T(128)}, u32[]{:S(2)}) copy-start(s32[4]{0:T(128)} %param.10) | copy-start | bytes 52
  97.8 134.3 %copy-start.27 = (s32[4]{0:T(128)S(1)}, s32[4]{0:T(128)}, u32[]{:S(2)}) copy-start(s32[4]{0:T(128)} %param.11) | copy-start | bytes 52
  97.8 134.6 %copy-start.9 = (bf16[4,128,128]{2,1,0:T(8,128)(2,1)S(1)}, bf16[4,128,128]{2,1,0:T(8,128)(2,1)}, u32[]{:S(2)}) copy-start(bf16[4,128,128]{2,1,0:T(8,128)(2,1)} %refs_2_.3) | copy-start | bytes 393220
  237.3 23.5 %copy-start.5 = (bf16[4096,1536]{1,0:T(8,128)(2,1)S(1)}, bf16[4096,1536]{1,0:T(8,128)(2,1)}, u32[]{:S(2)}) copy-start(bf16[4096,1536]{1,0:T(8,128)(2,1)} %all-gather.5.cloned.1.call-done) | copy-start | bytes 37748740
  259.2 21.2 %copy-start.21 = (f32[2,4,128,128]{3,2,1,0:T(8,128)}, f32[2,4,128,128]{3,2,1,0:T(8,128)S(1)}, u32[]{:S(2)}) copy-start(f32[2,4,128,128]{3,2,1,0:T(8,128)S(1)} %get-tuple-element.41) | copy-start | bytes 1572868
  259.3 31.8 %collective-permute-start.6 = (bf16[448,1536]{1,0:T(8,128)(2,1)S(1)}, bf16[448,1536]{1,0:T(8,128)(2,1)S(1)}, u32[]{:S(2)}, u32[]{:S(2)}) collective-permute-start(bf16[448,1536]{1,0:T(8,128)(2,1)S(1)} %slice_bitcast_fusion), channel_id=1, source_target_pairs={{0,16},{16,0},{1,17},{17,1},{2,18},{18,2},{3,19},{19,3},{4,20},{20... | collective-permute-start | bytes 4128776 | tf_op jit(solution)/shard_map/ppermute | solution.py:18
  286.5 9.4 %copy-start.12 = (bf16[896,384]{1,0:T(8,128)(2,1)S(1)}, bf16[896,384]{1,0:T(8,128)(2,1)}, u32[]{:S(2)}) copy-start(bf16[896,384]{1,0:T(8,128)(2,1)} %pad_maximum_fusion.4.d_ref) | copy-start | bytes 2064388
  300.9 6.8 %copy-start.3 = (bf16[4,896,1024]{2,1,0:T(8,128)(2,1)S(1)}, bf16[4,896,1024]{2,1,0:T(8,128)(2,1)}, u32[]{:S(2)}) copy-start(bf16[4,896,1024]{2,1,0:T(8,128)(2,1)} %copy-done.2) | copy-start | bytes 22020100
  307.7 12.6 %copy-start.7 = (bf16[4096,384]{1,0:T(8,128)(2,1)S(1)}, bf16[4096,384]{1,0:T(8,128)(2,1)}, u32[]{:S(2)}) copy-start(bf16[4096,384]{1,0:T(8,128)(2,1)} %all-gather.7.cloned.1.call-done) | copy-start | bytes 9437188
  315.7 15.5 %collective-permute-start.13 = (bf16[448,1024]{1,0:T(8,128)(2,1)}, bf16[448,1024]{1,0:T(8,128)(2,1)}, u32[]{:S(2)}, u32[]{:S(2)}) collective-permute-start(bf16[448,1024]{1,0:T(8,128)(2,1)} %get-tuple-element.47), channel_id=1, source_target_pairs={{0,1},{1,0},{2,3},{3,2},{4,5},{5,4},{6,7},{7,6},{8,9},{9,8},{10,11... | collective-permute-start | bytes 2752520 | tf_op jit(solution)/shard_map/ppermute | solution.py:18
  315.7 17.2 %collective-permute-start.12 = (bf16[448,1024]{1,0:T(8,128)(2,1)}, bf16[448,1024]{1,0:T(8,128)(2,1)S(1)}, u32[]{:S(2)}, u32[]{:S(2)}) collective-permute-start(bf16[448,1024]{1,0:T(8,128)(2,1)} %copy-done.23), channel_id=1, source_target_pairs={{0,1},{1,0},{2,3},{3,2},{4,5},{5,4},{6,7},{7,6},{8,9},{9,8},{10,11... | collective-permute-start | bytes 2752520 | tf_op jit(solution)/shard_map/ppermute | solution.py:18
  317.5 10.7 %collective-permute-start.11 = (bf16[4,128,128]{2,1,0:T(8,128)(2,1)S(1)}, bf16[4,128,128]{2,1,0:T(8,128)(2,1)S(1)}, u32[]{:S(2)}, u32[]{:S(2)}) collective-permute-start(bf16[4,128,128]{2,1,0:T(8,128)(2,1)S(1)} %fusion.3), channel_id=1, source_target_pairs={{0,16},{16,0},{1,17},{17,1},{2,18},{18,2},{3,19},{19,3},{4,20},{20... | collective-permute-start | bytes 393224 | tf_op jit(solution)/shard_map/ppermute | solution.py:18
  320.0 11.2 %collective-permute-start.8 = (bf16[448,384]{1,0:T(8,128)(2,1)S(1)}, bf16[448,384]{1,0:T(8,128)(2,1)S(1)}, u32[]{:S(2)}, u32[]{:S(2)}) collective-permute-start(bf16[448,384]{1,0:T(8,128)(2,1)S(1)} %slice_bitcast_fusion.1), channel_id=1, source_target_pairs={{0,16},{16,0},{1,17},{17,1},{2,18},{18,2},{3,19},{19,3},{4,20},{20... | collective-permute-start | bytes 1032200 | tf_op jit(solution)/shard_map/ppermute | solution.py:18
  323.4 7.8 %copy-start.16 = (bf16[448,1024]{1,0:T(8,128)(2,1)S(1)}, bf16[448,1024]{1,0:T(8,128)(2,1)}, u32[]{:S(2)}) copy-start(bf16[448,1024]{1,0:T(8,128)(2,1)} %copy-done.15) | copy-start | bytes 2752516
  328.1 6.5 %collective-permute-start.10 = (bf16[448,1024]{1,0:T(8,128)(2,1)S(1)}, bf16[448,1024]{1,0:T(8,128)(2,1)S(1)}, u32[]{:S(2)}, u32[]{:S(2)}) collective-permute-start(bf16[448,1024]{1,0:T(8,128)(2,1)S(1)} %get-tuple-element.40), channel_id=1, source_target_pairs={{0,1},{1,0},{2,3},{3,2},{4,5},{5,4},{6,7},{7,6},{8,9},{9,8},{10,11... | collective-permute-start | bytes 2752520 | tf_op jit(solution)/shard_map/ppermute | solution.py:18
  333.4 22.0 %collective-permute-start.14 = (bf16[448,1024]{1,0:T(8,128)(2,1)S(1)}, bf16[448,1024]{1,0:T(8,128)(2,1)S(1)}, u32[]{:S(2)}, u32[]{:S(2)}) collective-permute-start(bf16[448,1024]{1,0:T(8,128)(2,1)S(1)} %pad_maximum_fusion.2), channel_id=1, source_target_pairs={{0,2},{1,3},{2,0},{3,1},{4,6},{5,7},{6,4},{7,5},{8,10},{9,11},{10,... | collective-permute-start | bytes 2752520 | tf_op jit(solution)/shard_map/ppermute | solution.py:18
  335.1 22.9 %collective-permute-start.17 = (bf16[448,1024]{1,0:T(8,128)(2,1)S(1)}, bf16[448,1024]{1,0:T(8,128)(2,1)S(1)}, u32[]{:S(2)}, u32[]{:S(2)}) collective-permute-start(bf16[448,1024]{1,0:T(8,128)(2,1)S(1)} %pad_maximum_fusion.3), channel_id=1, source_target_pairs={{0,16},{16,0},{1,17},{17,1},{2,18},{18,2},{3,19},{19,3},{4,20},{20... | collective-permute-start | bytes 2752520 | tf_op jit(solution)/shard_map/ppermute | solution.py:18
  336.9 25.8 %collective-permute-start.9 = (bf16[448,1024]{1,0:T(8,128)(2,1)S(1)}, bf16[448,1024]{1,0:T(8,128)(2,1)S(1)}, u32[]{:S(2)}, u32[]{:S(2)}) collective-permute-start(bf16[448,1024]{1,0:T(8,128)(2,1)S(1)} %get-tuple-element.38), channel_id=1, source_target_pairs={{0,1},{1,0},{2,3},{3,2},{4,5},{5,4},{6,7},{7,6},{8,9},{9,8},{10,11... | collective-permute-start | bytes 2752520 | tf_op jit(solution)/shard_map/ppermute | solution.py:18
  337.8 18.8 %collective-permute-start.15 = (bf16[4,128,128]{2,1,0:T(8,128)(2,1)S(1)}, bf16[4,128,128]{2,1,0:T(8,128)(2,1)S(1)}, u32[]{:S(2)}, u32[]{:S(2)}) collective-permute-start(bf16[4,128,128]{2,1,0:T(8,128)(2,1)S(1)} %get-tuple-element.48), channel_id=1, source_target_pairs={{0,4},{4,0},{8,12},{12,8},{1,5},{5,1},{9,13},{13,9},{2,6},{6,2},{1... | collective-permute-start | bytes 393224 | tf_op jit(solution)/shard_map/ppermute | solution.py:18
  337.8 22.4 %collective-permute-start.20 = (bf16[4,128,128]{2,1,0:T(8,128)(2,1)S(1)}, bf16[4,128,128]{2,1,0:T(8,128)(2,1)S(1)}, u32[]{:S(2)}, u32[]{:S(2)}) collective-permute-start(bf16[4,128,128]{2,1,0:T(8,128)(2,1)S(1)} %get-tuple-element.48), channel_id=1, source_target_pairs={{0,12},{4,8},{8,4},{12,0},{1,13},{5,9},{9,5},{13,1},{2,14},{6,10},... | collective-permute-start | bytes 393224 | tf_op jit(solution)/shard_map/ppermute | solution.py:18
  355.4 6.5 %collective-permute-start.19 = (bf16[4,128,128]{2,1,0:T(8,128)(2,1)S(1)}, bf16[4,128,128]{2,1,0:T(8,128)(2,1)S(1)}, u32[]{:S(2)}, u32[]{:S(2)}) collective-permute-start(bf16[4,128,128]{2,1,0:T(8,128)(2,1)S(1)} %get-tuple-element.48), channel_id=1, source_target_pairs={{0,8},{4,12},{8,0},{12,4},{1,9},{5,13},{9,1},{13,5},{2,10},{6,14},... | collective-permute-start | bytes 393224 | tf_op jit(solution)/shard_map/ppermute | solution.py:18
  356.6 11.0 %collective-permute-start.16 = (bf16[224,1024]{1,0:T(8,128)(2,1)S(1)}, bf16[224,1024]{1,0:T(8,128)(2,1)S(1)}, u32[]{:S(2)}, u32[]{:S(2)}) collective-permute-start(bf16[224,1024]{1,0:T(8,128)(2,1)S(1)} %fusion.1), channel_id=1, source_target_pairs={{0,16},{16,0},{1,17},{17,1},{2,18},{18,2},{3,19},{19,3},{4,20},{20... | collective-permute-start | bytes 1376264 | tf_op jit(solution)/shard_map/ppermute | solution.py:18
  358.2 10.3 %collective-permute-start.18 = (bf16[224,1024]{1,0:T(8,128)(2,1)S(1)}, bf16[224,1024]{1,0:T(8,128)(2,1)S(1)}, u32[]{:S(2)}, u32[]{:S(2)}) collective-permute-start(bf16[224,1024]{1,0:T(8,128)(2,1)S(1)} %fusion), channel_id=1, source_target_pairs={{0,2},{1,3},{2,0},{3,1},{4,6},{5,7},{6,4},{7,5},{8,10},{9,11},{10,... | collective-permute-start | bytes 1376264 | tf_op jit(solution)/shard_map/ppermute | solution.py:18
  (20 other events, 53.9 us)
Sparse Core Ops, SparseCore 0:
  11.1 220.8 all-gather.4
  234.2 61.6 all-gather.6

commit v15 on v14

--- a/solution.py
+++ b/solution.py
@@ -10,7 +10,7 @@
 CAP = 2
 BF = jnp.bfloat16
 F32 = jnp.float32
-VMEM_BYTES = 30 * 2**20
+VMEM_BYTES = 25 * 2**20
 
 
 def swap(array, axis, bit):

time: 378 us -> 378 us (level)
  local copies, waits for them, and re-layouts: 46.1 us -> 51.9 us
    unnamed x60 -> x56, local copies, waits for them, and re-layouts: 25.4 us -> 32.4 us
  transfers between devices with their start and end apart: 23 -> 23, of which waited for: 12 -> 12; matrix products, arithmetic and copies ran while one was open for 9% -> 9% of each run, Pallas kernels for 12% -> 11%
where the time goes in v15:
time: 378 us; the launch traced here: 377 us
  waiting for transfers between devices  220 us (58%)
  Pallas kernels  53.6 us (14%)
  local copies, waits for them, and re-layouts  51.9 us (14%)
  starting transfers between devices  21.1 us (6%)
  other arithmetic  16.3 us (4%)
  between operations  14.4 us (4%)
    all_gather x1, waiting for transfers between devices, local(): gather_a = lax.all_gather(shards[0], 'dp')  129 us
    ppermute x21, waiting for transfers between devices, swap(): return lax.ppermute(array, axis, [(i, i ^ bit) for i in range(size)])  88.2 us
    unnamed x56, local copies, waits for them, and re-layouts  32.4 us
    pallas_call x3, Pallas kernels, backward(): pl.pallas_call(functools.partial(backward_kernel, firsts, blocks, bs, acc...  27.7 us
    pallas_call x2, Pallas kernels, forward(): pl.pallas_call(functools.partial(forward_kernel, first, blocks, bs, cuts)...  25.9 us
    ppermute x21, starting transfers between devices, swap(): return lax.ppermute(array, axis, [(i, i ^ bit) for i in range(size)])  21.1 us
  transfers between devices with their start and end apart: 23, of which 12 were waited for; matrix products, arithmetic and copies ran while one was open for 9% of the time, Pallas kernels for 11%

profile of v15, /device:TPU:0, one launch (start us, length us, event | category | flops | bytes accessed | tf_op | source)
XLA Modules:
  0.0 377.4 jit_solution(6143952240180911955)
XLA Ops:
  7.2 3.8 constant_dynamic-slice_fusion.5
  11.1 3.0 collective-permute-start
  15.6 19.2 %collective-permute-done = bf16[448,1024]{1,0:T(8,128)(2,1)} collective-permute-done((bf16[448,1024]{1,0:T(8,128)(2,1)}, bf16[448,1024]{1,0:T(8,128)(2,1)}, u32[]{:S(2)}, u32[]{:S(2)}) %collective-permute-start) | collective-permute-done | bytes 917536 | tf_op jit(solution)/shard_map/ppermute | solution.py:18
  36.5 2.2 constant_dynamic-update-slice_fusion.1
  40.5 2.2 constant_dynamic-update-slice_fusion
  42.7 2.2 constant_dynamic-update-slice_fusion.3
  44.9 11.7 %collective-permute-done.3 = bf16[448,1024]{1,0:T(8,128)(2,1)} collective-permute-done((bf16[448,1024]{1,0:T(8,128)(2,1)}, bf16[448,1024]{1,0:T(8,128)(2,1)}, u32[]{:S(2)}, u32[]{:S(2)}) %collective-permute-start.3) | collective-permute-done | bytes 917536 | tf_op jit(solution)/shard_map/ppermute | solution.py:18
  58.0 2.3 constant_dynamic-update-slice_fusion.2
  61.3 26.1 %collective-permute-done.5 = bf16[448,1536]{1,0:T(8,128)(2,1)} collective-permute-done((bf16[448,1536]{1,0:T(8,128)(2,1)}, bf16[448,1536]{1,0:T(8,128)(2,1)}, u32[]{:S(2)}, u32[]{:S(2)}) %collective-permute-start.5) | collective-permute-done | bytes 1376288 | tf_op jit(solution)/shard_map/ppermute | solution.py:18
  88.5 2.1 constant_dynamic-slice_fusion.2
  92.6 2.4 collective-permute-done.7
  95.9 6.7 %pad_maximum_fusion.x_ref = bf16[4,896,1024]{2,1,0:T(8,128)(2,1)} fusion(bf16[1,896,1024]{2,1,0:T(8,128)(2,1)} %bitcast.7, bf16[1,896,1024]{2,1,0:T(8,128)(2,1)} %bitcast.6, bf16[1,896,1024]{2,1,0:T(8,128)(2,1)} %bitcast.5, bf16[1,896,1024]{2,1,0:T(8,128)(2,1)} %bitcast.4), kind=kLoop, calls=%fused_computation | loop fusion | flops 11010048 | bytes 14680064 | tf_op jit(solution)/shard_map/stack | solution.py:256
  102.6 129.5 %all-gather.5.cloned.1.call-done = bf16[4096,1536]{1,0:T(8,128)(2,1)} async-done(((bf16[1024,1536]{1,0:T(8,128)(2,1)}), bf16[4096,1536]{1,0:T(8,128)(2,1)}) %all-gather.5.cloned.1.call-update) | async-done | bytes 12582928 | tf_op jit(solution)/shard_map/all_gather | solution.py:237
  232.4 3.1 copy-done
  235.5 4.9 %copy-done.5 = bf16[4096,1536]{1,0:T(8,128)(2,1)S(1)} copy-done((bf16[4096,1536]{1,0:T(8,128)(2,1)S(1)}, bf16[4096,1536]{1,0:T(8,128)(2,1)}, u32[]{:S(2)}) %copy-start.5) | copy-done | bytes 12582936
  240.5 20.0 %shard_map.94 = (bf16[2,448,1536]{2,1,0:T(8,128)(2,1)S(1)}, bf16[896,1536]{1,0:T(8,128)(2,1)S(1)}, f32[2,4,128,128]{3,2,1,0:T(8,128)S(1)}) custom-call(s32[20]{0:T(128)S(1)} %pad_add_fusion.1.meta, bf16[4,896,1024]{2,1,0:T(8,128)(2,1)S(1)} %copy-done, bf16[4,1024,1536]{2,1,0:T(8,128)(2,1)S(1)} %bitcast.31, bf16[4,128,128]{2,1,0:T(8,128)(2,1)S(1)} %copy-done.9, ...), custom_call_target="tpu_custom_call" | custom-call | flops 1 | bytes 1 | tf_op jit(solution)/shard_map/pallas_call | solution.py:81
  261.3 4.6 %copy-done.6 = bf16[4096,1536]{1,0:T(8,128)(2,1)S(1)} copy-done((bf16[4096,1536]{1,0:T(8,128)(2,1)S(1)}, bf16[4096,1536]{1,0:T(8,128)(2,1)}, u32[]{:S(2)}) %copy-start.6) | copy-done | bytes 12582936
  265.9 17.9 %shard_map.95.refs_3_ = bf16[4,896,1024]{2,1,0:T(8,128)(2,1)S(1)} custom-call(s32[20]{0:T(128)S(1)} %pad_add_fusion.1.meta, bf16[896,1536]{1,0:T(8,128)(2,1)S(1)} %get-tuple-element.31.refs_0_, bf16[4,1024,1536]{2,1,0:T(8,128)(2,1)S(1)} %bitcast.32, bf16[4,128,128]{2,1,0:T(8,128)(2,1)S(1)} %copy-done.9), custom_call_target="tpu_custom_call" | custom-call | flops 1 | bytes 1 | tf_op jit(solution)/shard_map/pallas_call | solution.py:174
  283.8 2.9 copy-done.2
  289.9 2.6 collective-permute-done.6
  293.6 2.3 all-gather.7.cloned.1.call-done
  295.9 3.1 copy-done.1
  300.9 5.9 %shard_map.96 = (bf16[2,448,384]{2,1,0:T(8,128)(2,1)S(1)}, bf16[896,384]{1,0:T(8,128)(2,1)S(1)}, f32[2,4,128,128]{3,2,1,0:T(8,128)S(1)}) custom-call(s32[20]{0:T(128)S(1)} %pad_add_fusion.1.meta, bf16[4,896,1024]{2,1,0:T(8,128)(2,1)S(1)} %copy-done.1, bf16[4,1024,384]{2,1,0:T(8,128)(2,1)S(1)} %bitcast.33, bf16[4,128,128]{2,1,0:T(8,128)(2,1)S(1)} %copy-done.9, ...), custom_call_target="tpu_custom_call" | custom-call | flops 1 | bytes 1 | tf_op jit(solution)/shard_map/pallas_call | solution.py:81
  307.7 5.1 %shard_map.97 = (bf16[448,1024]{1,0:T(8,128)(2,1)}, bf16[448,1024]{1,0:T(8,128)(2,1)S(1)}, bf16[448,1024]{1,0:T(8,128)(2,1)S(1)}, bf16[448,1024]{1,0:T(8,128)(2,1)S(1)}) custom-call(s32[20]{0:T(128)S(1)} %pad_add_fusion.1.meta, bf16[896,384]{1,0:T(8,128)(2,1)S(1)} %get-tuple-element.34.refs_0_, bf16[4,1024,384]{2,1,0:T(8,128)(2,1)S(1)} %bitcast.34, ...), custom_call_target="tpu_custom_call" | custom-call | flops 1 | bytes 1 | tf_op jit(solution)/shard_map/pallas_call | solution.py:174
  317.5 3.1 collective-permute-start.11
  320.9 3.1 copy-done.4
  323.9 4.7 %shard_map.98 = (bf16[448,1024]{1,0:T(8,128)(2,1)S(1)}, bf16[448,1024]{1,0:T(8,128)(2,1)S(1)}, bf16[448,1024]{1,0:T(8,128)(2,1)S(1)}, bf16[448,1024]{1,0:T(8,128)(2,1)S(1)}) custom-call(s32[20]{0:T(128)S(1)} %pad_add_fusion.1.meta, bf16[896,384]{1,0:T(8,128)(2,1)S(1)} %copy-done.12, bf16[4,1024,384]{2,1,0:T(8,128)(2,1)S(1)} %bitcast.35, ...), custom_call_target="tpu_custom_call" | custom-call | flops 1 | bytes 1 | tf_op jit(solution)/shard_map/pallas_call | solution.py:174
  328.8 2.9 collective-permute-done.8
  337.8 2.5 collective-permute-start.20
  340.3 15.5 %collective-permute-done.14 = bf16[448,1024]{1,0:T(8,128)(2,1)S(1)} collective-permute-done((bf16[448,1024]{1,0:T(8,128)(2,1)S(1)}, bf16[448,1024]{1,0:T(8,128)(2,1)S(1)}, u32[]{:S(2)}, u32[]{:S(2)}) %collective-permute-start.14) | collective-permute-done | bytes 917536 | tf_op jit(solution)/shard_map/ppermute | solution.py:18
  360.1 2.1 collective-permute-done.19
  363.1 4.8 %collective-permute-done.16 = bf16[224,1024]{1,0:T(8,128)(2,1)S(1)} collective-permute-done((bf16[224,1024]{1,0:T(8,128)(2,1)S(1)}, bf16[224,1024]{1,0:T(8,128)(2,1)S(1)}, u32[]{:S(2)}, u32[]{:S(2)}) %collective-permute-start.16) | collective-permute-done | bytes 458784 | tf_op jit(solution)/shard_map/ppermute | solution.py:18
  (122 shorter events, 38.8 us)
Async XLA Ops:
  7.2 224.9 %all-gather.5.cloned.1.call-start = ((), (), s32[]{:S(2)}) async-start(), calls=%async_computation | async-start | bytes 15728640 | tf_op jit(solution)/shard_map/all_gather | solution.py:237
  11.0 27.7 %copy-start.22 = (bf16[448,3840]{1,0:T(8,128)(2,1)S(1)}, bf16[448,3840]{1,0:T(8,128)(2,1)}, u32[]{:S(2)}) copy-start(bf16[448,3840]{1,0:T(8,128)(2,1)} %param.13) | copy-start | bytes 10321924
  11.0 284.9 %all-gather.7.cloned.1.call-start = ((), (), s32[]{:S(2)}) async-start(), calls=%async_computation.1 | async-start | bytes 3932160 | tf_op jit(solution)/shard_map/all_gather | solution.py:267
  11.1 23.7 %collective-permute-start = (bf16[448,1024]{1,0:T(8,128)(2,1)}, bf16[448,1024]{1,0:T(8,128)(2,1)}, u32[]{:S(2)}, u32[]{:S(2)}) collective-permute-start(bf16[448,1024]{1,0:T(8,128)(2,1)} %param.7), channel_id=1, source_target_pairs={{0,16},{16,0},{1,17},{17,1},{2,18},{18,2},{3,19},{19,3},{4,20},{20... | collective-permute-start | bytes 2752520 | tf_op jit(solution)/shard_map/ppermute | solution.py:18
  14.1 28.6 %collective-permute-start.2 = (bf16[448,1024]{1,0:T(8,128)(2,1)}, bf16[448,1024]{1,0:T(8,128)(2,1)}, u32[]{:S(2)}, u32[]{:S(2)}) collective-permute-start(bf16[448,1024]{1,0:T(8,128)(2,1)} %param.7), channel_id=1, source_target_pairs={{0,2},{1,3},{2,0},{3,1},{4,6},{5,7},{6,4},{7,5},{8,10},{9,11},{10,... | collective-permute-start | bytes 2752520 | tf_op jit(solution)/shard_map/ppermute | solution.py:18
  34.8 21.9 %collective-permute-start.3 = (bf16[448,1024]{1,0:T(8,128)(2,1)}, bf16[448,1024]{1,0:T(8,128)(2,1)}, u32[]{:S(2)}, u32[]{:S(2)}) collective-permute-start(bf16[448,1024]{1,0:T(8,128)(2,1)} %collective-permute-done), channel_id=1, source_target_pairs={{0,2},{1,3},{2,0},{3,1},{4,6},{5,7},{6,4},{7,5},{8,10},{9,11},{10,... | collective-permute-start | bytes 2752520 | tf_op jit(solution)/shard_map/ppermute | solution.py:18
  42.7 53.2 %collective-permute-start.1 = (bf16[896,1024]{1,0:T(8,128)(2,1)}, bf16[896,1024]{1,0:T(8,128)(2,1)}, u32[]{:S(2)}, u32[]{:S(2)}) collective-permute-start(bf16[896,1024]{1,0:T(8,128)(2,1)} %constant_dynamic-update-slice_fusion), channel_id=1, source_target_pairs={{0,1},{1,0},{2,3},{3,2},{4,5},{5,4},{6,7},{7,6},{8,9},{9,8},{10,11... | collective-permute-start | bytes 5505032 | tf_op jit(solution)/shard_map/ppermute | solution.py:18
  56.6 30.8 %collective-permute-start.5 = (bf16[448,1536]{1,0:T(8,128)(2,1)}, bf16[448,1536]{1,0:T(8,128)(2,1)}, u32[]{:S(2)}, u32[]{:S(2)}) collective-permute-start(bf16[448,1536]{1,0:T(8,128)(2,1)} %get-tuple-element.27), channel_id=1, source_target_pairs={{0,16},{16,0},{1,17},{17,1},{2,18},{18,2},{3,19},{19,3},{4,20},{20... | collective-permute-start | bytes 4128776 | tf_op jit(solution)/shard_map/ppermute | solution.py:18
  60.3 35.6 %collective-permute-start.4 = (bf16[896,1024]{1,0:T(8,128)(2,1)}, bf16[896,1024]{1,0:T(8,128)(2,1)}, u32[]{:S(2)}, u32[]{:S(2)}) collective-permute-start(bf16[896,1024]{1,0:T(8,128)(2,1)} %constant_dynamic-update-slice_fusion.2), channel_id=1, source_target_pairs={{0,1},{1,0},{2,3},{3,2},{4,5},{5,4},{6,7},{7,6},{8,9},{9,8},{10,11... | collective-permute-start | bytes 5505032 | tf_op jit(solution)/shard_map/ppermute | solution.py:18
  87.4 7.6 %collective-permute-start.7 = (bf16[448,384]{1,0:T(8,128)(2,1)}, bf16[448,384]{1,0:T(8,128)(2,1)S(1)}, u32[]{:S(2)}, u32[]{:S(2)}) collective-permute-start(bf16[448,384]{1,0:T(8,128)(2,1)} %get-tuple-element.29), channel_id=1, source_target_pairs={{0,16},{16,0},{1,17},{17,1},{2,18},{18,2},{3,19},{19,3},{4,20},{20... | collective-permute-start | bytes 1032200 | tf_op jit(solution)/shard_map/ppermute | solution.py:18
  95.9 136.2 %copy-start.24 = (s32[4]{0:T(128)S(1)}, s32[4]{0:T(128)}, u32[]{:S(2)}) copy-start(s32[4]{0:T(128)} %param.10) | copy-start | bytes 52
  95.9 136.2 %copy-start.25 = (s32[4]{0:T(128)S(1)}, s32[4]{0:T(128)}, u32[]{:S(2)}) copy-start(s32[4]{0:T(128)} %param.11) | copy-start | bytes 52
  95.9 136.5 %copy-start.9 = (bf16[4,128,128]{2,1,0:T(8,128)(2,1)S(1)}, bf16[4,128,128]{2,1,0:T(8,128)(2,1)}, u32[]{:S(2)}) copy-start(bf16[4,128,128]{2,1,0:T(8,128)(2,1)} %refs_2_.3) | copy-start | bytes 393220
  260.6 31.9 %collective-permute-start.6 = (bf16[448,1536]{1,0:T(8,128)(2,1)S(1)}, bf16[448,1536]{1,0:T(8,128)(2,1)S(1)}, u32[]{:S(2)}, u32[]{:S(2)}) collective-permute-start(bf16[448,1536]{1,0:T(8,128)(2,1)S(1)} %slice_bitcast_fusion), channel_id=1, source_target_pairs={{0,16},{16,0},{1,17},{17,1},{2,18},{18,2},{3,19},{19,3},{4,20},{20... | collective-permute-start | bytes 4128776 | tf_op jit(solution)/shard_map/ppermute | solution.py:18
  289.9 6.1 %copy-start.10 = (bf16[896,384]{1,0:T(8,128)(2,1)S(1)}, bf16[896,384]{1,0:T(8,128)(2,1)}, u32[]{:S(2)}) copy-start(bf16[896,384]{1,0:T(8,128)(2,1)} %pad_maximum_fusion.4.d_ref) | copy-start | bytes 2064388
  300.9 6.8 %copy-start.3 = (bf16[4,896,1024]{2,1,0:T(8,128)(2,1)S(1)}, bf16[4,896,1024]{2,1,0:T(8,128)(2,1)}, u32[]{:S(2)}) copy-start(bf16[4,896,1024]{2,1,0:T(8,128)(2,1)} %copy-done.2) | copy-start | bytes 22020100
  307.7 13.1 %copy-start.8 = (bf16[4096,384]{1,0:T(8,128)(2,1)S(1)}, bf16[4096,384]{1,0:T(8,128)(2,1)}, u32[]{:S(2)}) copy-start(bf16[4096,384]{1,0:T(8,128)(2,1)} %all-gather.7.cloned.1.call-done) | copy-start | bytes 9437188
  314.7 5.9 %copy-start.26 = (s32[4,1]{0,1:T(1,128)S(1)}, s32[4,1]{0,1:T(1,128)}, u32[]{:S(2)}) copy-start(s32[4,1]{0,1:T(1,128)} %param.12) | copy-start | bytes 52
  315.7 16.0 %collective-permute-start.13 = (bf16[448,1024]{1,0:T(8,128)(2,1)}, bf16[448,1024]{1,0:T(8,128)(2,1)}, u32[]{:S(2)}, u32[]{:S(2)}) collective-permute-start(bf16[448,1024]{1,0:T(8,128)(2,1)} %get-tuple-element.47), channel_id=1, source_target_pairs={{0,1},{1,0},{2,3},{3,2},{4,5},{5,4},{6,7},{7,6},{8,9},{9,8},{10,11... | collective-permute-start | bytes 2752520 | tf_op jit(solution)/shard_map/ppermute | solution.py:18
  315.7 17.7 %collective-permute-start.12 = (bf16[448,1024]{1,0:T(8,128)(2,1)}, bf16[448,1024]{1,0:T(8,128)(2,1)S(1)}, u32[]{:S(2)}, u32[]{:S(2)}) collective-permute-start(bf16[448,1024]{1,0:T(8,128)(2,1)} %copy-done.21), channel_id=1, source_target_pairs={{0,1},{1,0},{2,3},{3,2},{4,5},{5,4},{6,7},{7,6},{8,9},{9,8},{10,11... | collective-permute-start | bytes 2752520 | tf_op jit(solution)/shard_map/ppermute | solution.py:18
  317.5 11.3 %collective-permute-start.11 = (bf16[4,128,128]{2,1,0:T(8,128)(2,1)S(1)}, bf16[4,128,128]{2,1,0:T(8,128)(2,1)S(1)}, u32[]{:S(2)}, u32[]{:S(2)}) collective-permute-start(bf16[4,128,128]{2,1,0:T(8,128)(2,1)S(1)} %fusion.3), channel_id=1, source_target_pairs={{0,16},{16,0},{1,17},{17,1},{2,18},{18,2},{3,19},{19,3},{4,20},{20... | collective-permute-start | bytes 393224 | tf_op jit(solution)/shard_map/ppermute | solution.py:18
  320.6 11.1 %collective-permute-start.8 = (bf16[448,384]{1,0:T(8,128)(2,1)S(1)}, bf16[448,384]{1,0:T(8,128)(2,1)S(1)}, u32[]{:S(2)}, u32[]{:S(2)}) collective-permute-start(bf16[448,384]{1,0:T(8,128)(2,1)S(1)} %slice_bitcast_fusion.1), channel_id=1, source_target_pairs={{0,16},{16,0},{1,17},{17,1},{2,18},{18,2},{3,19},{19,3},{4,20},{20... | collective-permute-start | bytes 1032200 | tf_op jit(solution)/shard_map/ppermute | solution.py:18
  323.9 7.7 %copy-start.14 = (bf16[448,1024]{1,0:T(8,128)(2,1)S(1)}, bf16[448,1024]{1,0:T(8,128)(2,1)}, u32[]{:S(2)}) copy-start(bf16[448,1024]{1,0:T(8,128)(2,1)} %copy-done.13) | copy-start | bytes 2752516
  328.7 6.0 %collective-permute-start.10 = (bf16[448,1024]{1,0:T(8,128)(2,1)S(1)}, bf16[448,1024]{1,0:T(8,128)(2,1)S(1)}, u32[]{:S(2)}, u32[]{:S(2)}) collective-permute-start(bf16[448,1024]{1,0:T(8,128)(2,1)S(1)} %get-tuple-element.40), channel_id=1, source_target_pairs={{0,1},{1,0},{2,3},{3,2},{4,5},{5,4},{6,7},{7,6},{8,9},{9,8},{10,11... | collective-permute-start | bytes 2752520 | tf_op jit(solution)/shard_map/ppermute | solution.py:18
  333.9 21.9 %collective-permute-start.14 = (bf16[448,1024]{1,0:T(8,128)(2,1)S(1)}, bf16[448,1024]{1,0:T(8,128)(2,1)S(1)}, u32[]{:S(2)}, u32[]{:S(2)}) collective-permute-start(bf16[448,1024]{1,0:T(8,128)(2,1)S(1)} %pad_maximum_fusion.2), channel_id=1, source_target_pairs={{0,2},{1,3},{2,0},{3,1},{4,6},{5,7},{6,4},{7,5},{8,10},{9,11},{10,... | collective-permute-start | bytes 2752520 | tf_op jit(solution)/shard_map/ppermute | solution.py:18
  335.1 23.3 %collective-permute-start.17 = (bf16[448,1024]{1,0:T(8,128)(2,1)S(1)}, bf16[448,1024]{1,0:T(8,128)(2,1)S(1)}, u32[]{:S(2)}, u32[]{:S(2)}) collective-permute-start(bf16[448,1024]{1,0:T(8,128)(2,1)S(1)} %pad_maximum_fusion.3), channel_id=1, source_target_pairs={{0,16},{16,0},{1,17},{17,1},{2,18},{18,2},{3,19},{19,3},{4,20},{20... | collective-permute-start | bytes 2752520 | tf_op jit(solution)/shard_map/ppermute | solution.py:18
  336.9 26.2 %collective-permute-start.9 = (bf16[448,1024]{1,0:T(8,128)(2,1)S(1)}, bf16[448,1024]{1,0:T(8,128)(2,1)S(1)}, u32[]{:S(2)}, u32[]{:S(2)}) collective-permute-start(bf16[448,1024]{1,0:T(8,128)(2,1)S(1)} %get-tuple-element.38), channel_id=1, source_target_pairs={{0,1},{1,0},{2,3},{3,2},{4,5},{5,4},{6,7},{7,6},{8,9},{9,8},{10,11... | collective-permute-start | bytes 2752520 | tf_op jit(solution)/shard_map/ppermute | solution.py:18
  337.8 19.2 %collective-permute-start.15 = (bf16[4,128,128]{2,1,0:T(8,128)(2,1)S(1)}, bf16[4,128,128]{2,1,0:T(8,128)(2,1)S(1)}, u32[]{:S(2)}, u32[]{:S(2)}) collective-permute-start(bf16[4,128,128]{2,1,0:T(8,128)(2,1)S(1)} %get-tuple-element.48), channel_id=1, source_target_pairs={{0,4},{4,0},{8,12},{12,8},{1,5},{5,1},{9,13},{13,9},{2,6},{6,2},{1... | collective-permute-start | bytes 393224 | tf_op jit(solution)/shard_map/ppermute | solution.py:18
  337.8 22.3 %collective-permute-start.20 = (bf16[4,128,128]{2,1,0:T(8,128)(2,1)S(1)}, bf16[4,128,128]{2,1,0:T(8,128)(2,1)S(1)}, u32[]{:S(2)}, u32[]{:S(2)}) collective-permute-start(bf16[4,128,128]{2,1,0:T(8,128)(2,1)S(1)} %get-tuple-element.48), channel_id=1, source_target_pairs={{0,12},{4,8},{8,4},{12,0},{1,13},{5,9},{9,5},{13,1},{2,14},{6,10},... | collective-permute-start | bytes 393224 | tf_op jit(solution)/shard_map/ppermute | solution.py:18
  355.8 6.4 %collective-permute-start.19 = (bf16[4,128,128]{2,1,0:T(8,128)(2,1)S(1)}, bf16[4,128,128]{2,1,0:T(8,128)(2,1)S(1)}, u32[]{:S(2)}, u32[]{:S(2)}) collective-permute-start(bf16[4,128,128]{2,1,0:T(8,128)(2,1)S(1)} %get-tuple-element.48), channel_id=1, source_target_pairs={{0,8},{4,12},{8,0},{12,4},{1,9},{5,13},{9,1},{13,5},{2,10},{6,14},... | collective-permute-start | bytes 393224 | tf_op jit(solution)/shard_map/ppermute | solution.py:18
  357.0 10.9 %collective-permute-start.16 = (bf16[224,1024]{1,0:T(8,128)(2,1)S(1)}, bf16[224,1024]{1,0:T(8,128)(2,1)S(1)}, u32[]{:S(2)}, u32[]{:S(2)}) collective-permute-start(bf16[224,1024]{1,0:T(8,128)(2,1)S(1)} %fusion.1), channel_id=1, source_target_pairs={{0,16},{16,0},{1,17},{17,1},{2,18},{18,2},{3,19},{19,3},{4,20},{20... | collective-permute-start | bytes 1376264 | tf_op jit(solution)/shard_map/ppermute | solution.py:18
  358.6 10.3 %collective-permute-start.18 = (bf16[224,1024]{1,0:T(8,128)(2,1)S(1)}, bf16[224,1024]{1,0:T(8,128)(2,1)S(1)}, u32[]{:S(2)}, u32[]{:S(2)}) collective-permute-start(bf16[224,1024]{1,0:T(8,128)(2,1)S(1)} %fusion), channel_id=1, source_target_pairs={{0,2},{1,3},{2,0},{3,1},{4,6},{5,7},{6,4},{7,5},{8,10},{9,11},{10,... | collective-permute-start | bytes 1376264 | tf_op jit(solution)/shard_map/ppermute | solution.py:18
  (18 other events, 54.5 us)
Sparse Core Ops, SparseCore 0:
  11.1 220.8 all-gather.4
  234.2 61.6 all-gather.6
